TPU v7x, 256 devices: a whole 4x4x8 slice. The times are simulated.
256 devices in a mesh: section: 4 (over x_hi, core), seq: 8 (over z), fsdp: 8 (over y, x_lo).
Axes of the slice: x: 4 (x_hi: 2, x_lo: 2; x = x_hi * 2 + x_lo), y: 4, z: 8, core: 2. Of those that a mesh axis runs over, the one named last changes fastest.
Arguments:
- student_input: bfloat16 [2048, 64], P('seq'), may hold values from -6 to 6
- previous_latent: bfloat16 [2048, 64], P('seq'), may hold values from -6 to 6
- score_noise: bfloat16 [2048, 64], P('seq'), may hold values from -6 to 6
- timesteps: int32 [3], replicated, may hold values from 50 to 949
- modulation: float32 [4, 5, 5120], P('section'), may hold values from -3 to 3
- in_weight: bfloat16 [3, 64, 5120], replicated, may hold values from -4 to 4
- qkv_weight: bfloat16 [3, 5120, 3, 3072], P(None, 'seq', None, 'fsdp'), may hold values from -1 to 1
- out_weight: bfloat16 [3, 5120, 3072], P(None, 'seq', 'fsdp'), may hold values from -0.109375 to 0.109375
- head_weight: bfloat16 [3, 5120, 64], replicated, may hold values from -0.078125 to 0.078125
- kv_cache: bfloat16 [4, 2048, 2, 3072], P('section', 'seq', None, 'fsdp'), may hold values from -60 to 60
- saved_features: bfloat16 [2048, 5120], P(('seq', 'fsdp')), may hold values from -6 to 6
Outputs:
- student_group: float32 [2048, 64], P(('seq', 'fsdp'))
- dmd_grad: float32 [2048, 64], P(('seq', 'fsdp'))
- head_grad: float32 [5120, 64], P(('seq', 'fsdp'))
All inputs are finite; a program needn't handle non-finite values.
Results may differ from a plain program's by a relative error of at most 0.015.
Values may be sent and summed in bfloat16 or wider, within the bound.
No kernel may reach another device: no remote copies, remote signals or barrier semaphores. Data moves between devices by JAX's collectives and lax.ppermute only.
A program may use at most 128 MiB of HBM per device.

v0:
```python
import jax
import jax.numpy as jnp
from jax import lax
from jax.sharding import PartitionSpec as P

HEAD_DIM = 128


guidance_scale = 5.0


def noise_levels(steps):
    remain = 1.0 - steps.astype(jnp.float32) / 1000.0
    return 5.0 * remain / (1.0 + 4.0 * remain)


def normalize(values):
    centre = values - jnp.mean(values, axis=-1, keepdims=True)
    spread = jnp.mean(centre * centre, axis=-1, keepdims=True)
    return centre * lax.rsqrt(spread + 1e-06)


def select_model(stacked, model_index):
    return lax.dynamic_index_in_dim(stacked, model_index, 0, keepdims=False)


def per_device(
    student_input,
    previous_latent,
    score_noise,
    timesteps,
    modulation,
    in_weight,
    qkv_weight,
    out_weight,
    head_weight,
    kv_cache,
    saved_features,
):
    section = lax.axis_index("section")
    model_index = section - (section >= 2).astype(jnp.int32)
    levels = noise_levels(timesteps)
    is_student = section == 0
    noised = (
        (1.0 - levels[1]) * previous_latent.astype(jnp.float32)
        + levels[1] * score_noise.astype(jnp.float32)
    ).astype(jnp.bfloat16)
    latent = jnp.where(is_student, student_input, noised)
    noise_level = jnp.where(is_student, levels[0], levels[1])
    shifts = modulation[0]
    embed_weight = select_model(in_weight, model_index)
    attn_weight = select_model(qkv_weight, model_index)
    output_weight = select_model(out_weight, model_index)
    final_weight = select_model(head_weight, model_index)
    hidden = jnp.dot(latent, embed_weight, preferred_element_type=jnp.float32)
    normed = (normalize(hidden) * (1.0 + shifts[1]) + shifts[0]).astype(jnp.bfloat16)
    local_rows = normed.shape[0]
    feat_part = attn_weight.shape[2]
    full_attn, full_output = (
        lax.all_gather(attn_weight, "seq", axis=0, tiled=True),
        lax.all_gather(output_weight, "seq", axis=0, tiled=True),
    )
    projected = jnp.dot(
        normed,
        full_attn.reshape(full_attn.shape[0], 3 * feat_part),
        preferred_element_type=jnp.float32,
    )
    projected = projected.reshape(local_rows, 3, feat_part).astype(jnp.bfloat16)
    heads_here = feat_part // HEAD_DIM
    queries = projected[:, 0].reshape(local_rows, heads_here, HEAD_DIM)
    current = projected[:, 1:]
    running_max = jnp.full((heads_here, local_rows), -1e30, jnp.float32)
    joined = jnp.concatenate(
        (
            lax.all_gather(current, "seq", axis=0, tiled=True),
            lax.all_gather(kv_cache[0], "seq", axis=0, tiled=True),
        ),
        axis=0,
    )
    count_keys = joined.shape[0]
    key_rows = joined[:, 0].reshape(count_keys, heads_here, HEAD_DIM)
    value_rows = joined[:, 1].reshape(count_keys, heads_here, HEAD_DIM)
    scores = jnp.einsum(
        "qhd,khd->hqk", queries, key_rows, preferred_element_type=jnp.float32
    ) * HEAD_DIM ** (-0.5)
    new_max = jnp.maximum(running_max, jnp.max(scores, axis=2))
    weights = jnp.exp(scores - new_max[:, :, None])
    totals = jnp.sum(weights, axis=2)
    weighted = jnp.einsum(
        "hqk,khd->hqd", weights.astype(jnp.bfloat16), value_rows, preferred_element_type=jnp.float32
    )
    running_max, totals, weighted = (new_max, totals, weighted)
    attended = (
        (weighted / totals[:, :, None])
        .transpose(1, 0, 2)
        .reshape(local_rows, feat_part)
        .astype(jnp.bfloat16)
    )
    row_share = local_rows // lax.axis_size("fsdp")
    row_block = attended
    mixed_sum = lax.psum_scatter(
        lax.dot_general(
            row_block, full_output, (((1,), (1,)), ((), ())), preferred_element_type=jnp.float32
        ).astype(jnp.bfloat16),
        "fsdp",
        scatter_dimension=0,
        tiled=True,
    ).astype(jnp.float32)
    offset = lax.axis_index("fsdp") * row_share
    hidden_rows = lax.dynamic_slice_in_dim(hidden, offset, row_share, 0)
    latent_rows = lax.dynamic_slice_in_dim(latent, offset, row_share, 0)
    residual = hidden_rows + shifts[2] * mixed_sum
    head_in = (normalize(residual) * (1.0 + shifts[4]) + shifts[3]).astype(jnp.bfloat16)
    velocity = jnp.dot(head_in, final_weight, preferred_element_type=jnp.float32)
    estimate = latent_rows.astype(jnp.float32) - noise_level * velocity
    gathered = lax.all_gather(estimate[None], "section", axis=0, tiled=True)
    student_group = gathered[0]
    teacher_estimate = gathered[2] + guidance_scale * (gathered[1] - gathered[2])
    dmd_grad = gathered[3] - teacher_estimate
    velocity_grad = (-levels[2] * dmd_grad).astype(jnp.bfloat16)
    row_block = saved_features
    head_grad = lax.psum_scatter(
        lax.dot_general(
            row_block, velocity_grad, (((0,), (0,)), ((), ())), preferred_element_type=jnp.float32
        ),
        ("seq", "fsdp"),
        scatter_dimension=0,
        tiled=True,
    )
    return (student_group, dmd_grad, head_grad)


def solution(mesh):
    placed = (
        P("seq", None),
        P("seq", None),
        P("seq", None),
        P(),
        P("section", None, None),
        P(),
        P(None, "seq", None, "fsdp"),
        P(None, "seq", "fsdp"),
        P(),
        P("section", "seq", None, "fsdp"),
        P(("seq", "fsdp"), None),
    )
    return jax.shard_map(
        per_device,
        mesh=mesh,
        in_specs=placed,
        out_specs=(P(("seq", "fsdp"), None), P(("seq", "fsdp"), None), P(("seq", "fsdp"), None)),
        check_vma=False,
    )
```

profile of v0, /device:TPU:2, one launch (start us, length us, event | category | flops | bytes accessed | tf_op | source)
XLA Modules:
  0.0 690.0 jit_solution(2931873147739295200)
XLA Ops:
  7.3 1.6 constant_dynamic-slice_fusion.1
  8.9 2.1 copy.45
  11.1 1.8 copy.36
  15.3 3.1 fusion.51
  18.4 3.1 multiply_reduce_fusion.1
  21.7 118.6 %all-gather.11.cloned.1.call-done = bf16[1,5120,3,384]{1,3,2,0:T(8,128)(2,1)} async-done(((bf16[1,640,3,384]{1,3,2,0:T(8,128)(2,1)}), bf16[1,5120,3,384]{1,3,2,0:T(8,128)(2,1)}) %all-gather.11.cloned.1.call-update) | async-done | bytes 11796496 | tf_op jit(solution)/shard_map/all_gather | solution.py:60
  140.2 9.8 %fusion.16 = bf16[256,3,384]{2,0,1:T(8,128)(2,1)S(1)} fusion(bf16[1,5120,3,384]{1,3,2,0:T(8,128)(2,1)} %all-gather.11.cloned.1.call-done, f32[256,5120]{1,0:T(8,128)} %get-tuple-element.16, f32[5120]{0:T(1024)S(1)} %bitcast.64, f32[5120]{0:T(1024)S(1)} %bitcast.65, f32[256]{0:T(256)S(1)} %add_rsqrt_fusion, f32[256]{0:T(256)S(1)} %broadcast_multiply_fusion), kind=kOutput, calls=%fused_computation.23 | convolution fusion | flops 3026747392 | bytes 17672192 | tf_op jit(solution)/shard_map/dot_general | solution.py:63
  150.9 1.9 constant_dynamic-slice_fusion
  153.2 32.5 %all-gather.13.cloned.1.call-done = bf16[1,2048,2,384]{3,1,2,0:T(8,128)(2,1)} async-done(((bf16[1,256,2,384]{3,1,2,0:T(8,128)(2,1)}), bf16[1,2048,2,384]{3,1,2,0:T(8,128)(2,1)}) %all-gather.13.cloned.1.call-update) | async-done | bytes 3145744 | tf_op jit(solution)/shard_map/all_gather | solution.py:76
  185.7 45.4 %all-gather.9.cloned.1.call-done = bf16[2048,2,384]{2,0,1:T(8,128)(2,1)} async-done(((bf16[256,2,384]{2,0,1:T(8,128)(2,1)}), bf16[2048,2,384]{2,0,1:T(8,128)(2,1)}) %all-gather.9.cloned.1.call-update) | async-done | bytes 3145744 | tf_op jit(solution)/shard_map/all_gather | solution.py:75
  231.1 5.4 fusion.9
  236.5 4.7 copy.40
  241.2 3.0 copy.37
  244.2 3.8 multiply_reduce_fusion
  248.0 2.2 fusion.2
  250.2 4.5 fusion.28
  254.8 29.0 %all-gather.15.cloned.1.call-done = bf16[1,5120,384]{2,1,0:T(8,128)(2,1)} async-done(((bf16[1,640,384]{2,1,0:T(8,128)(2,1)}), bf16[1,5120,384]{2,1,0:T(8,128)(2,1)}) %all-gather.15.cloned.1.call-update) | async-done | bytes 3932176 | tf_op jit(solution)/shard_map/all_gather | solution.py:61
  283.8 5.2 convolution_convert_fusion
  291.0 59.9 %reduce-scatter.5.cloned.1.call-done = bf16[32,5120]{1,0:T(8,128)(2,1)} async-done(((bf16[256,5120]{1,0:T(8,128)(2,1)}), bf16[32,5120]{1,0:T(8,128)(2,1)}) %reduce-scatter.5.cloned.1.call-update) | async-done | bytes 327696 | tf_op jit(solution)/shard_map/reduce_scatter | solution.py:101
  352.3 1.6 multiply_reduce_fusion.2
  353.9 1.8 fusion.24
  355.7 6.8 all-gather.3
  364.4 2.0 copy.43
  366.4 315.3 %reduce-scatter.7.cloned.1.call-done = f32[80,64]{1,0:T(8,128)} async-done(((f32[5120,64]{1,0:T(8,128)}), f32[80,64]{1,0:T(8,128)}) %reduce-scatter.7.cloned.1.call-update) | async-done | bytes 20496
  (47 shorter events, 8.0 us)
Async XLA Ops:
  7.2 8.2 %copy-start = (bf16[3,64,5120]{2,1,0:T(8,128)(2,1)S(1)}, bf16[3,64,5120]{2,1,0:T(8,128)(2,1)}, u32[]{:S(2)}) copy-start(bf16[3,64,5120]{2,1,0:T(8,128)(2,1)} %param.16) | copy-start | bytes 5898244
  7.2 5.8 copy-start.4
  7.2 5.9 copy-start.5
  7.2 6.0 copy-start.6
  7.2 6.1 copy-start.7
  7.2 133.0 %all-gather.11.cloned.1.call-start = ((), (), s32[]{:S(2)}) async-start(), calls=%async_computation.4 | async-start | bytes 13271040 | tf_op jit(solution)/shard_map/all_gather | solution.py:60
  11.1 174.6 %all-gather.13.cloned.1.call-start = ((), (), s32[]{:S(2)}) async-start(), calls=%async_computation.5 | async-start | bytes 3538944 | tf_op jit(solution)/shard_map/all_gather | solution.py:76
  12.9 218.2 %all-gather.9.cloned.1.call-start = ((), (), s32[]{:S(2)}) async-start(), calls=%async_computation.2 | async-start | bytes 3538944 | tf_op jit(solution)/shard_map/all_gather | solution.py:75
  15.3 6.3 copy-start.2
  150.8 133.0 %all-gather.15.cloned.1.call-start = ((), (), s32[]{:S(2)}) async-start(), calls=%async_computation.6 | async-start | bytes 4423680 | tf_op jit(solution)/shard_map/all_gather | solution.py:61
  152.8 198.1 %reduce-scatter.5.cloned.1.call-start = ((), (), s32[]{:S(2)}) async-start(), calls=%async_computation.3 | async-start | bytes 2949120 | tf_op jit(solution)/shard_map/reduce_scatter | solution.py:101
  289.0 392.7 %reduce-scatter.7.cloned.1.call-start = ((), (), s32[]{:S(2)}) async-start(), calls=%async_computation.7 | async-start | bytes 2662400
  352.3 330.9 %copy-start.1 = (bf16[3,64,5120]{2,1,0:T(8,128)(2,1)S(1)}, bf16[3,64,5120]{2,1,0:T(8,128)(2,1)}, u32[]{:S(2)}) copy-start(bf16[3,64,5120]{2,1,0:T(8,128)(2,1)} %param.16) | copy-start | bytes 5898244
  363.0 320.1 %copy-start.3 = (f32[32,64]{1,0:T(8,128)}, f32[32,64]{1,0:T(8,128)S(1)}, u32[]{:S(2)}) copy-start(f32[32,64]{1,0:T(8,128)S(1)} %get-tuple-element.10) | copy-start | bytes 24580
Sparse Core Ops, SparseCore 0:
  11.2 128.9 all-gather.10
  142.0 43.6 all-gather.12
  187.5 43.6 all-gather.8
  232.8 50.9 all-gather.14
  289.1 61.7 reduce-scatter.4
  366.6 315.0 reduce-scatter.6
where the time goes:
time: 695 us; the launch traced here: 690 us
  waiting for transfers between devices  601 us (86%)
  matrix products  29.5 us (4%)
  local copies, waits for them, and re-layouts  20.6 us (3%)
  between operations  16.9 us (2%)
  other arithmetic  15.1 us (2%)
    unnamed x7, waiting for transfers between devices  315 us
    all_gather x1, waiting for transfers between devices, per_device(): lax.all_gather(attn_weight, 'seq', axis=0, tiled=True)  119 us
    reduce_scatter x1, waiting for transfers between devices, per_device(): lax.psum_scatter(lax.dot_general(row_block, full_output, (((1,), (1,)), (...  59.9 us
    all_gather x1, waiting for transfers between devices, per_device(): lax.all_gather(current, 'seq', axis=0, tiled=True)  45.4 us
    all_gather x1, waiting for transfers between devices, per_device(): lax.all_gather(kv_cache[0], 'seq', axis=0, tiled=True)  32.5 us
    all_gather x1, waiting for transfers between devices, per_device(): lax.all_gather(output_weight, 'seq', axis=0, tiled=True)  29 us
  transfers between devices with their start and end apart: 6, of which 6 were waited for; matrix products, arithmetic and copies ran while one was open for 7% of the time, Pallas kernels for 0%

commit v1 on v0

v1 whole, which is shorter than its diff:
```python
import functools

import jax
import jax.numpy as jnp
from jax import lax
from jax.experimental import pallas as pl
from jax.experimental.pallas import tpu as pltpu
from jax.sharding import PartitionSpec as P

HEAD_DIM = 128
LOG2E = 1.4426950408889634
guidance_scale = 5.0
bf16 = jnp.bfloat16
f32 = jnp.float32


def noise_levels(steps):
    remain = 1.0 - steps.astype(f32) / 1000.0
    return 5.0 * remain / (1.0 + 4.0 * remain)


def select_model(stacked, model_index):
    return lax.dynamic_index_in_dim(stacked, model_index, 0, keepdims=False)


def exchange(blocks, axis):
    return lax.all_to_all(blocks, axis, 0, 0, tiled=True)


def share(block, axis, count):
    return exchange(jnp.broadcast_to(block[None], (count,) + block.shape), axis)


def ring(block, axis, count, split):
    half = count // 2
    up = [(i, (i + 1) % count) for i in range(count)]
    down = [(i, (i - 1) % count) for i in range(count)]
    behind, ahead = [block], [block]
    for _ in range(half - 1):
        behind.append(lax.ppermute(behind[-1], axis, up))
        ahead.append(lax.ppermute(ahead[-1], axis, down))
    size = block.shape[split] // 2
    first = lax.ppermute(lax.slice_in_dim(behind[-1], 0, size, axis=split), axis, up)
    second = lax.ppermute(lax.slice_in_dim(ahead[-1], size, 2 * size, axis=split), axis, down)
    return behind, ahead[1:], first, second


def attention_kernel(heads, where_ref, lat_ref, a_ref, *refs):
    context_refs, out_ref = refs[:-1], refs[-1]
    feat = heads * HEAD_DIM
    factors = a_ref[...].astype(f32)
    count, _, width = factors.shape
    table = factors[:, :8].reshape(count * 8, width).astype(bf16)
    shift = factors[0, 8:9]
    queries_here = out_ref.shape[0]

    def project(block, first, last):
        latents = block[: count * 8]
        scale = jnp.sum(block[count * 8 :].astype(f32).T, axis=1, keepdims=True)
        plain = lax.dot_general(
            latents, table[:, first:last], (((0,), (0,)), ((), ())), preferred_element_type=f32
        )
        return plain * scale + shift[:, first:last]

    queries = (project(lat_ref[where_ref[0]], 0, feat) * (HEAD_DIM ** (-0.5) * LOG2E)).astype(bf16)

    def update(carry, keys, values):
        new = []
        for h in range(heads):
            top, total, weighted = carry[h]
            cols = slice(h * HEAD_DIM, (h + 1) * HEAD_DIM)
            scores = lax.dot_general(
                keys[:, cols], queries[:, cols], (((1,), (1,)), ((), ())), preferred_element_type=f32
            )
            new_top = jnp.maximum(top, jnp.max(scores, axis=0, keepdims=True))
            weights = jnp.exp2(scores - new_top)
            keep = jnp.exp2(top - new_top)
            total = total * keep + jnp.sum(weights, axis=0, keepdims=True)
            weighted = weighted * keep + lax.dot_general(
                values[:, cols], weights.astype(bf16), (((0,), (0,)), ((), ())), preferred_element_type=f32
            )
            new.append((new_top, total, weighted))
        return tuple(new)

    def current_step(i, carry):
        both = project(lat_ref[i], feat, 3 * feat).astype(bf16)
        return update(carry, both[:, :feat], both[:, feat:])

    carry = tuple(
        (
            jnp.full((1, queries_here), -1e30, f32),
            jnp.zeros((1, queries_here), f32),
            jnp.zeros((HEAD_DIM, queries_here), f32),
        )
        for _ in range(heads)
    )
    carry = lax.fori_loop(0, lat_ref.shape[0], current_step, carry)
    for ref in context_refs:
        carry = update(carry, ref[0], ref[1])
    for h in range(heads):
        _, total, weighted = carry[h]
        out_ref[:, h * HEAD_DIM : (h + 1) * HEAD_DIM] = (weighted / total).T.astype(bf16)


def head_kernel(count, where_ref, lat_ref, embed_ref, gate_ref, head_ref, aux_ref, *refs):
    out_ref = refs[-1]
    weight_refs = refs[: count]
    att_refs = refs[count:-1]
    me_seq, me_fsdp = where_ref[0], where_ref[1]
    half = count // 2
    def block_rows(f):
        rows = [att_refs[i][f] for i in range(half)]
        rows += [att_refs[half][f], att_refs[half + 1][f]]
        rows += [att_refs[half + 2 + i][f] for i in range(half - 1)]
        return jnp.concatenate(rows, axis=0)

    distance = list(range(half)) + [half] + [-(i + 1) for i in range(half - 1)]
    owners = [lax.rem(me_seq - d + 2 * count, count) for d in distance]
    mixed = None
    for k in range(count):
        f = lax.rem(me_fsdp - k + count, count)
        part = lax.dot_general(
            block_rows(f), weight_refs[k][...], (((1,), (1,)), ((), ())), preferred_element_type=f32
        )
        mixed = part if mixed is None else mixed + part
    latents = jnp.concatenate([lat_ref[o] for o in owners], axis=0)
    hidden = jnp.dot(latents, embed_ref[...], preferred_element_type=f32)
    residual = hidden + gate_ref[...] * mixed
    centre = jnp.mean(residual, axis=1, keepdims=True)
    residual = residual - centre
    spread = jnp.sum(residual * residual, axis=1, keepdims=True)
    values = lax.dot_general(
        residual.astype(bf16), head_ref[...], (((1,), (1,)), ((), ())), preferred_element_type=f32
    )
    lanes = lax.broadcasted_iota(jnp.int32, values.shape, 1)
    values = jnp.where(lanes == 64, centre, jnp.where(lanes == 65, spread, values))
    size = lat_ref.shape[1]
    for n, o in enumerate(owners):
        out_ref[o, :size] = values[n * size : (n + 1) * size]
        out_ref[o, size:] = aux_ref[...]


def per_device(
    student_input,
    previous_latent,
    score_noise,
    timesteps,
    modulation,
    in_weight,
    qkv_weight,
    out_weight,
    head_weight,
    kv_cache,
    saved_features,
):
    section, me_seq, me_fsdp = (lax.axis_index(a) for a in ("section", "seq", "fsdp"))
    sections, n_seq, n_fsdp = (lax.axis_size(a) for a in ("section", "seq", "fsdp"))
    where = jnp.stack([me_seq, me_fsdp]).astype(jnp.int32)
    model_index = section - (section >= 2).astype(jnp.int32)
    levels = noise_levels(timesteps)
    is_student = section == 0
    noised = (
        (1.0 - levels[1]) * previous_latent.astype(f32) + levels[1] * score_noise.astype(f32)
    ).astype(bf16)
    latent = jnp.where(is_student, student_input, noised)
    rows, latent_dim = latent.shape
    width = in_weight.shape[2]
    shifts = modulation[0]
    part = qkv_weight.shape[1]
    feat = qkv_weight.shape[3]
    heads = feat // HEAD_DIM
    piece = rows // n_fsdp

    context = kv_cache[0].transpose(1, 0, 2)
    ctx_behind, ctx_ahead, ctx_first, ctx_second = ring(context, "seq", n_seq, 1)
    output_weight = select_model(out_weight, model_index)
    output_weights = [output_weight] + [
        lax.ppermute(output_weight, "fsdp", [(i, (i + k) % n_fsdp) for i in range(n_fsdp)])
        for k in range(1, n_fsdp)
    ]

    embed_weight = select_model(in_weight, model_index)
    embed = embed_weight.astype(f32)
    row_mean = jnp.mean(embed, axis=1, keepdims=True)
    embed_here = lax.dynamic_slice_in_dim(embed_weight, me_seq * part, part, 1)
    shifts_here = lax.dynamic_slice_in_dim(shifts, me_seq * part, part, 1)
    centred = ((embed_here.astype(f32) - row_mean) * (1.0 + shifts_here[1])).astype(bf16)
    group = latent_dim // n_seq
    folded = jnp.concatenate(
        [
            centred.reshape(n_seq, group, part),
            jnp.broadcast_to(shifts_here[0].astype(bf16), (n_seq, 1, part)),
            jnp.zeros((n_seq, 15 - group, part), bf16),
        ],
        axis=1,
    ).reshape(n_seq * 16, part)
    attn_weight = select_model(qkv_weight, model_index).transpose(1, 0, 2)
    table = jnp.concatenate(
        [jnp.dot(folded, attn_weight[i], preferred_element_type=f32) for i in range(3)], axis=1
    )
    table = exchange(table.astype(bf16).reshape(n_seq, 16, 3 * feat), "seq")
    table = jnp.sum(table.astype(f32), axis=0).astype(bf16)
    table = share(table, "seq", n_seq)

    hidden = jnp.dot(latent, embed_weight, preferred_element_type=f32)
    hidden = hidden - jnp.mean(hidden, axis=1, keepdims=True)
    inverse = lax.rsqrt(jnp.mean(hidden * hidden, axis=1) + 1e-06)
    inverse_hi = lax.reduce_precision(inverse, 8, 7)
    inverse_mid = lax.reduce_precision(inverse - inverse_hi, 8, 7)
    inverse_lo = inverse - inverse_hi - inverse_mid
    packed = jnp.concatenate(
        [
            latent.T,
            jnp.stack([inverse_hi, inverse_mid, inverse_lo]).astype(bf16),
            jnp.zeros((13, rows), bf16),
        ],
        axis=0,
    )
    latents = share(packed, "seq", n_seq)

    vmem = pl.BlockSpec(memory_space=pltpu.VMEM)
    smem = pl.BlockSpec(memory_space=pltpu.SMEM)
    context_blocks = ctx_behind + [ctx_first, ctx_second] + ctx_ahead
    attended = pl.pallas_call(
        functools.partial(attention_kernel, heads),
        out_shape=jax.ShapeDtypeStruct((rows, feat), bf16),
        in_specs=[smem] + [vmem] * (2 + len(context_blocks)),
        out_specs=vmem,
        compiler_params=pltpu.CompilerParams(vmem_limit_bytes=48 * 1024 * 1024),
    )(where, latents, table, *context_blocks)

    attended = exchange(attended.reshape(n_fsdp, piece, feat), "fsdp")
    att_behind, att_ahead, att_first, att_second = ring(attended, "seq", n_seq, 1)
    att_blocks = att_behind + [att_first, att_second] + att_ahead

    head = select_model(head_weight, model_index)
    head_here = lax.dynamic_slice_in_dim(head, me_seq * part, part, 0).T
    scaled_head = (head_here.astype(f32) * (1.0 + shifts_here[4])).astype(bf16)
    head_sum = jnp.sum(scaled_head.astype(f32), axis=1)
    head_shift = jnp.sum(head_here.astype(f32) * shifts_here[3], axis=1)
    aux = jnp.zeros((8, 128), f32).at[0, :latent_dim].set(head_sum).at[1, :latent_dim].set(head_shift)
    padded_head = jnp.concatenate([scaled_head, jnp.zeros((128 - latent_dim, part), bf16)], axis=0)
    group_latents = lax.dynamic_slice_in_dim(latents, me_fsdp * piece, piece, 2)[
        :, :latent_dim
    ].transpose(0, 2, 1)
    partials = pl.pallas_call(
        functools.partial(head_kernel, n_seq),
        out_shape=jax.ShapeDtypeStruct((n_seq, piece + 8, 128), f32),
        in_specs=[smem] + [vmem] * (5 + n_fsdp + len(att_blocks)),
        out_specs=vmem,
        compiler_params=pltpu.CompilerParams(vmem_limit_bytes=48 * 1024 * 1024),
    )(
        where,
        group_latents,
        embed_here,
        shifts_here[2:3],
        padded_head,
        aux,
        *output_weights,
        *att_blocks,
    )
    partials = jnp.broadcast_to(partials[None], (sections,) + partials.shape)
    partials = exchange(partials.reshape((sections * n_seq,) + partials.shape[2:]), ("section", "seq"))
    partials = partials.reshape(sections, n_seq, piece + 8, 128)
    values = partials[:, :, :piece, :latent_dim]
    means = partials[:, :, :piece, latent_dim]
    spreads = partials[:, :, :piece, latent_dim + 1]
    sums = partials[:, :, piece, :latent_dim]
    consts = jnp.sum(partials[:, :, piece + 1, :latent_dim], axis=1)
    offsets = means - jnp.mean(means, axis=1, keepdims=True)
    linear = jnp.sum(values + offsets[..., None] * sums[:, :, None, :], axis=1)
    variance = (jnp.sum(spreads, axis=1) + part * jnp.sum(offsets * offsets, axis=1)) / width
    velocity = linear * lax.rsqrt(variance + 1e-06)[..., None] + consts[:, None, :]
    own_student = lax.dynamic_slice_in_dim(student_input, me_fsdp * piece, piece, 0).astype(f32)
    own_noised = lax.dynamic_slice_in_dim(noised, me_fsdp * piece, piece, 0).astype(f32)
    student_group = own_student - levels[0] * velocity[0]
    scored = own_noised[None] - levels[1] * velocity[1:]
    teacher_estimate = scored[1] + guidance_scale * (scored[0] - scored[1])
    dmd_grad = scored[2] - teacher_estimate
    velocity_grad = (-levels[2] * dmd_grad).astype(bf16)

    share_width = width // (n_seq * n_fsdp)
    features = saved_features.reshape(piece, n_seq, n_fsdp, share_width).transpose(2, 1, 0, 3)
    features = exchange(features, "fsdp")
    features = features.transpose(1, 0, 2, 3).reshape(n_seq, rows, share_width)
    grads = share(velocity_grad, "fsdp", n_fsdp).reshape(rows, latent_dim)
    partial_grad = lax.dot_general(
        jnp.broadcast_to(grads[None], (n_seq, rows, latent_dim)),
        features,
        (((1,), (1,)), ((0,), (0,))),
        preferred_element_type=f32,
    )
    head_grad = jnp.sum(exchange(partial_grad, "seq"), axis=0).T
    return (student_group, dmd_grad, head_grad)


def solution(mesh):
    placed = (
        P("seq", None),
        P("seq", None),
        P("seq", None),
        P(),
        P("section", None, None),
        P(),
        P(None, "seq", None, "fsdp"),
        P(None, "seq", "fsdp"),
        P(),
        P("section", "seq", None, "fsdp"),
        P(("seq", "fsdp"), None),
    )
    return jax.shard_map(
        per_device,
        mesh=mesh,
        in_specs=placed,
        out_specs=(P(("seq", "fsdp"), None), P(("seq", "fsdp"), None), P(("seq", "fsdp"), None)),
        check_vma=False,
    )
```

time: 695 us -> 260 us (0.37)
  waiting for transfers between devices: 601 us -> 72.6 us
  starting transfers between devices: 0.43 us -> 96.3 us
  matrix products: 29.5 us -> 7.01 us
  Pallas kernels: 0 us -> 20.2 us
  between operations: 16.9 us -> 2.37 us
  local copies, waits for them, and re-layouts: 20.6 us -> 29.8 us
    unnamed x7 -> x0, waiting for transfers between devices: 315 us -> none
    all_gather x4 -> x0, waiting for transfers between devices: 225 us -> none  [the longest x1 119 us: per_device(): lax.all_gather(attn_weight, 'seq', axis=0, tiled=True)]
    reduce_scatter x1 -> x0, waiting for transfers between devices: 59.9 us -> none  [per_device(): lax.psum_scatter(lax.dot_general(row_block, full_output, (((1,), (1,)), (...]
    ppermute x0 -> x23, starting transfers between devices: none -> 58.7 us  [the longest x7 28 us: per_device(): lax.ppermute(output_weight, 'fsdp', [(i, (i + k) % n_fsdp) for i in range...]
    all_to_all x0 -> x7, waiting for transfers between devices: none -> 42.5 us  [exchange(): return lax.all_to_all(blocks, axis, 0, 0, tiled=True)]
    all_to_all x0 -> x7, starting transfers between devices: none -> 37.5 us  [exchange(): return lax.all_to_all(blocks, axis, 0, 0, tiled=True)]
    ppermute x0 -> x23, waiting for transfers between devices: none -> 30.1 us  [the longest x6 20.5 us: ring(): behind.append(lax.ppermute(behind[-1], axis, up))]
    dot_general x7 -> x5, matrix products: 29.5 us -> 7.01 us  [the longest x3 4.04 us: per_device(): jnp.dot(folded, attn_weight[i], preferred_element_type=f32)]
  transfers between devices with their start and end apart: 6 -> 30, of which waited for: 6 -> 13; matrix products, arithmetic and copies ran while one was open for 7% -> 17% of each run, Pallas kernels for 0% -> 0%
where the time goes in v1:
time: 260 us; the launch traced here: 258 us
  starting transfers between devices  96.3 us (37%)
  waiting for transfers between devices  72.6 us (28%)
  local copies, waits for them, and re-layouts  29.8 us (11%)
  Pallas kernels  20.2 us (8%)
  other arithmetic  18.7 us (7%)
  blocking collectives  11.5 us (4%)
  matrix products  7.01 us (3%)
    all_to_all x7, waiting for transfers between devices, exchange(): return lax.all_to_all(blocks, axis, 0, 0, tiled=True)  42.5 us
    all_to_all x7, starting transfers between devices, exchange(): return lax.all_to_all(blocks, axis, 0, 0, tiled=True)  37.5 us
    ppermute x7, starting transfers between devices, per_device(): lax.ppermute(output_weight, 'fsdp', [(i, (i + k) % n_fsdp) for i in range...  28 us
    ppermute x6, waiting for transfers between devices, ring(): behind.append(lax.ppermute(behind[-1], axis, up))  20.5 us
    ppermute x6, starting transfers between devices, ring(): ahead.append(lax.ppermute(ahead[-1], axis, down))  18.2 us
    pallas_call x1, Pallas kernels, per_device(): pl.pallas_call(functools.partial(attention_kernel, heads), out_shape=jax....  15.9 us
    all_to_all x1, blocking collectives, exchange(): return lax.all_to_all(blocks, axis, 0, 0, tiled=True)  11.5 us
    unnamed x43, local copies, waits for them, and re-layouts  10.7 us
  transfers between devices with their start and end apart: 30, of which 13 were waited for; matrix products, arithmetic and copies ran while one was open for 17% of the time, Pallas kernels for 0%

profile of v1, /device:TPU:2, one launch (start us, length us, event | category | flops | bytes accessed | tf_op | source)
XLA Modules:
  0.0 258.4 jit_solution(8847794486416687202)
XLA Ops:
  3.8 4.0 %collective-permute-start.11 = (bf16[2,256,384]{2,1,0:T(8,128)(2,1)S(1)}, bf16[2,256,384]{2,1,0:T(8,128)(2,1)S(1)}, u32[]{:S(2)}, u32[]{:S(2)}) collective-permute-start(bf16[2,256,384]{2,1,0:T(8,128)(2,1)S(1)} %bitcast.92), channel_id=1, source_target_pairs={{0,56},{8,0},{16,8},{24,16},{32,24},{40,32},{48,40},{56,48},{1,57}... | collective-permute-start | bytes 1179656 | tf_op jit(solution)/shard_map/ppermute | solution.py:41
  19.3 5.8 %all-to-all-start.1 = ((bf16[8,16,1152]{2,1,0:T(8,128)(2,1)}), bf16[8,16,1152]{2,1,0:T(8,128)(2,1)S(1)}, u32[]{:S(2)}, u32[]{:S(2)}) async-start(bf16[8,16,1152]{2,1,0:T(8,128)(2,1)} %pad_maximum_fusion), calls=%async_computation.1 | async-start | bytes 589824 | tf_op jit(solution)/shard_map/all_to_all | solution.py:27
  30.0 7.1 %all-to-all-done.1 = bf16[8,16,1152]{2,1,0:T(8,128)(2,1)S(1)} async-done(((bf16[8,16,1152]{2,1,0:T(8,128)(2,1)}), bf16[8,16,1152]{2,1,0:T(8,128)(2,1)S(1)}, u32[]{:S(2)}, u32[]{:S(2)}) %all-to-all-start.1) | async-done | bytes 294944 | tf_op jit(solution)/shard_map/all_to_all | solution.py:27
  37.9 3.4 %all-to-all-start = ((bf16[8,80,256]{2,1,0:T(8,128)(2,1)}), bf16[8,80,256]{2,1,0:T(8,128)(2,1)S(1)}, u32[]{:S(2)}, u32[]{:S(2)}) async-start(bf16[8,80,256]{2,1,0:T(8,128)(2,1)} %broadcast_in_dim.21), calls=%async_computation | async-start | bytes 655360 | tf_op jit(solution)/shard_map/all_to_all | solution.py:27
  46.1 12.3 %collective-permute-done.8.refs_2_ = bf16[2,256,384]{2,1,0:T(8,128)(2,1)} collective-permute-done((bf16[2,256,384]{2,1,0:T(8,128)(2,1)S(1)}, bf16[2,256,384]{2,1,0:T(8,128)(2,1)}, u32[]{:S(2)}, u32[]{:S(2)}) %collective-permute-start.8) | collective-permute-done | bytes 393248 | tf_op jit(solution)/shard_map/ppermute | solution.py:40
  58.4 3.2 %collective-permute-start.13 = (bf16[2,256,384]{2,1,0:T(8,128)(2,1)}, bf16[2,256,384]{2,1,0:T(8,128)(2,1)S(1)}, u32[]{:S(2)}, u32[]{:S(2)}) collective-permute-start(bf16[2,256,384]{2,1,0:T(8,128)(2,1)} %collective-permute-done.12.refs_7_), channel_id=1, source_target_pairs={{0,56},{8,0},{16,8},{24,16},{32,24},{40,32},{48,40},{56,48},{1,57}... | collective-permute-start | bytes 1179656 | tf_op jit(solution)/shard_map/ppermute | solution.py:41
  63.4 4.5 %all-to-all-start.2 = ((bf16[8,16,1152]{2,1,0:T(8,128)(2,1)}), bf16[8,16,1152]{2,1,0:T(8,128)(2,1)S(1)}, u32[]{:S(2)}, u32[]{:S(2)}) async-start(bf16[8,16,1152]{2,1,0:T(8,128)(2,1)} %broadcast_in_dim.24), calls=%async_computation.2 | async-start | bytes 589824 | tf_op jit(solution)/shard_map/all_to_all | solution.py:27
  72.4 3.7 %collective-permute-start.14 = (bf16[2,128,384]{2,1,0:T(8,128)(2,1)}, bf16[2,128,384]{2,1,0:T(8,128)(2,1)}, u32[]{:S(2)}, u32[]{:S(2)}) collective-permute-start(bf16[2,128,384]{2,1,0:T(8,128)(2,1)} %slice.155), channel_id=1, source_target_pairs={{0,56},{8,0},{16,8},{24,16},{32,24},{40,32},{48,40},{56,48},{1,57}... | collective-permute-start | bytes 589832 | tf_op jit(solution)/shard_map/ppermute | solution.py:44
  76.2 4.2 %all-to-all-done.2.a_ref = bf16[8,16,1152]{2,1,0:T(8,128)(2,1)S(1)} async-done(((bf16[8,16,1152]{2,1,0:T(8,128)(2,1)}), bf16[8,16,1152]{2,1,0:T(8,128)(2,1)S(1)}, u32[]{:S(2)}, u32[]{:S(2)}) %all-to-all-start.2) | async-done | bytes 294944 | tf_op jit(solution)/shard_map/all_to_all | solution.py:27
  82.6 15.9 %shard_map.130 = bf16[256,384]{1,0:T(8,128)(2,1)S(1)} custom-call(s32[2]{0:T(128)S(1)} %pad_add_fusion.where_ref, bf16[8,80,256]{2,1,0:T(8,128)(2,1)S(1)} %all-to-all-done.lat_ref, bf16[8,16,1152]{2,1,0:T(8,128)(2,1)S(1)} %all-to-all-done.2.a_ref, bf16[2,256,384]{2,1,0:T(8,128)(2,1)S(1)} %bitcast.93, bf16[2,256,384]{2,1,0:T(8,128)(2,1)S(1)} %copy-done.2, ...), custom_call_target="tpu_custom_call" | custom-call | tf_op jit(solution)/shard_map/pallas_call | solution.py:224
  98.5 11.5 %all_to_all.40.refs_8_ = bf16[8,32,384]{2,1,0:T(8,128)(2,1)S(1)} all-to-all(bf16[8,32,384]{2,1,0:T(8,128)(2,1)S(1)} %bitcast.94), channel_id=1, replica_groups=mesh['section'=4,'seq'=8,'fsdp'=8] {'fsdp'}, dimensions={0} | all-to-all | bytes 393216 | tf_op jit(solution)/shard_map/all_to_all | solution.py:27
  118.6 3.2 %collective-permute-start.20 = (bf16[8,32,384]{2,1,0:T(8,128)(2,1)S(1)}, bf16[8,32,384]{2,1,0:T(8,128)(2,1)}, u32[]{:S(2)}, u32[]{:S(2)}) collective-permute-start(bf16[8,32,384]{2,1,0:T(8,128)(2,1)S(1)} %collective-permute-done.19.refs_14_), channel_id=1, source_target_pairs={{0,56},{8,0},{16,8},{24,16},{32,24},{40,32},{48,40},{56,48},{1,57}... | collective-permute-start | bytes 589832 | tf_op jit(solution)/shard_map/ppermute | solution.py:41
  122.5 4.3 %collective-permute-done.16.refs_10_ = bf16[8,32,384]{2,1,0:T(8,128)(2,1)} collective-permute-done((bf16[8,32,384]{2,1,0:T(8,128)(2,1)S(1)}, bf16[8,32,384]{2,1,0:T(8,128)(2,1)}, u32[]{:S(2)}, u32[]{:S(2)}) %collective-permute-start.16) | collective-permute-done | bytes 196640 | tf_op jit(solution)/shard_map/ppermute | solution.py:40
  127.0 3.8 %collective-permute-start.21 = (bf16[8,32,384]{2,1,0:T(8,128)(2,1)}, bf16[8,32,384]{2,1,0:T(8,128)(2,1)S(1)}, u32[]{:S(2)}, u32[]{:S(2)}) collective-permute-start(bf16[8,32,384]{2,1,0:T(8,128)(2,1)} %collective-permute-done.20.refs_15_), channel_id=1, source_target_pairs={{0,56},{8,0},{16,8},{24,16},{32,24},{40,32},{48,40},{56,48},{1,57}... | collective-permute-start | bytes 589832 | tf_op jit(solution)/shard_map/ppermute | solution.py:41
  134.9 21.0 %collective-permute-start.4 = (bf16[640,384]{1,0:T(8,128)(2,1)S(1)}, bf16[640,384]{1,0:T(8,128)(2,1)}, u32[]{:S(2)}, u32[]{:S(2)}) collective-permute-start(bf16[640,384]{1,0:T(8,128)(2,1)S(1)} %dynamic-slice_bitcast_fusion.1.refs_0_), channel_id=1, source_target_pairs={{0,5},{1,6},{2,7},{3,0},{4,1},{5,2},{6,3},{7,4},{8,13},{9,14},{10,... | collective-permute-start | bytes 1474568 | tf_op jit(solution)/shard_map/ppermute | solution.py:178
  169.6 8.0 %collective-permute-done.5.refs_6_ = bf16[640,384]{1,0:T(8,128)(2,1)} collective-permute-done((bf16[640,384]{1,0:T(8,128)(2,1)S(1)}, bf16[640,384]{1,0:T(8,128)(2,1)}, u32[]{:S(2)}, u32[]{:S(2)}) %collective-permute-start.5) | collective-permute-done | bytes 491552 | tf_op jit(solution)/shard_map/ppermute | solution.py:178
  180.4 4.2 %shard_map.131 = f32[8,40,128]{2,1,0:T(8,128)S(1)} custom-call(s32[2]{0:T(128)S(1)} %pad_add_fusion.where_ref, bf16[8,32,64]{2,1,0:T(8,128)(2,1)S(1)} %bitcast.95, bf16[64,640]{1,0:T(8,128)(2,1)S(1)} %copy-done.5, f32[1,640]{1,0:T(1,128)S(1)} %get-tuple-element.44.gate_ref, bf16[128,640]{1,0:T(8,128)(2,1)S(1)} %concatenate.20.head_ref, ...), custom_call_target="tpu_custom_call" | custom-call | tf_op jit(solution)/shard_map/pallas_call | solution.py:246
  185.6 7.8 %all-to-all-start.4 = ((f32[32,40,128]{2,1,0:T(8,128)}), f32[32,40,128]{2,1,0:T(8,128)S(1)}, u32[]{:S(2)}, u32[]{:S(2)}) async-start(f32[32,40,128]{2,1,0:T(8,128)} %bitcast.30), calls=%async_computation.4 | async-start | bytes 1310720 | tf_op jit(solution)/shard_map/all_to_all | solution.py:27
  196.1 17.4 %all-to-all-done.4 = f32[32,40,128]{2,1,0:T(8,128)S(1)} async-done(((f32[32,40,128]{2,1,0:T(8,128)}), f32[32,40,128]{2,1,0:T(8,128)S(1)}, u32[]{:S(2)}, u32[]{:S(2)}) %all-to-all-start.4) | async-done | bytes 655392 | tf_op jit(solution)/shard_map/all_to_all | solution.py:27
  213.4 5.4 %all-to-all-start.6 = ((bf16[8,8,32,80]{3,2,1,0:T(8,128)(2,1)}), bf16[8,8,32,80]{3,2,1,0:T(8,128)(2,1)S(1)}, u32[]{:S(2)}, u32[]{:S(2)}) async-start(bf16[8,8,32,80]{3,2,1,0:T(8,128)(2,1)} %copy.80), calls=%async_computation.6 | async-start | bytes 1048576 | tf_op jit(solution)/shard_map/all_to_all | solution.py:27
  230.7 5.7 %all-to-all-start.5 = ((bf16[8,2,1024]{2,1,0:T(2,128)(2,1)}), bf16[8,2,1024]{2,1,0:T(2,128)(2,1)S(1)}, u32[]{:S(2)}, u32[]{:S(2)}) async-start(bf16[8,2,1024]{2,1,0:T(2,128)(2,1)} %reshape.221), calls=%async_computation.5 | async-start | bytes 65536 | tf_op jit(solution)/shard_map/all_to_all | solution.py:27
  236.4 4.8 %all-to-all-done.5 = bf16[8,2,1024]{2,1,0:T(2,128)(2,1)S(1)} async-done(((bf16[8,2,1024]{2,1,0:T(2,128)(2,1)}), bf16[8,2,1024]{2,1,0:T(2,128)(2,1)S(1)}, u32[]{:S(2)}, u32[]{:S(2)}) %all-to-all-start.5) | async-done | bytes 32800 | tf_op jit(solution)/shard_map/all_to_all | solution.py:27
  242.4 4.9 %all-to-all-start.7 = ((f32[8,64,80]{2,1,0:T(8,128)}), f32[8,64,80]{2,1,0:T(8,128)S(1)}, u32[]{:S(2)}, u32[]{:S(2)}) async-start(f32[8,64,80]{2,1,0:T(8,128)} %fusion.8), calls=%async_computation.7 | async-start | bytes 524288 | tf_op jit(solution)/shard_map/all_to_all | solution.py:27
  248.7 9.1 %all-to-all-done.7 = f32[8,64,80]{2,1,0:T(8,128)S(1)} async-done(((f32[8,64,80]{2,1,0:T(8,128)}), f32[8,64,80]{2,1,0:T(8,128)S(1)}, u32[]{:S(2)}, u32[]{:S(2)}) %all-to-all-start.7) | async-done | bytes 163872 | tf_op jit(solution)/shard_map/all_to_all | solution.py:27
  (149 shorter events, 80.7 us)
Async XLA Ops:
  1.8 39.5 %collective-permute-start.7 = (bf16[2,256,384]{2,1,0:T(8,128)(2,1)S(1)}, bf16[2,256,384]{2,1,0:T(8,128)(2,1)S(1)}, u32[]{:S(2)}, u32[]{:S(2)}) collective-permute-start(bf16[2,256,384]{2,1,0:T(8,128)(2,1)S(1)} %bitcast.91), channel_id=1, source_target_pairs={{0,8},{8,16},{16,24},{24,32},{32,40},{40,48},{48,56},{56,0},{1,9},... | collective-permute-start | bytes 1179656 | tf_op jit(solution)/shard_map/ppermute | solution.py:40
  3.8 40.2 %collective-permute-start.11 = (bf16[2,256,384]{2,1,0:T(8,128)(2,1)S(1)}, bf16[2,256,384]{2,1,0:T(8,128)(2,1)S(1)}, u32[]{:S(2)}, u32[]{:S(2)}) collective-permute-start(bf16[2,256,384]{2,1,0:T(8,128)(2,1)S(1)} %bitcast.92), channel_id=1, source_target_pairs={{0,56},{8,0},{16,8},{24,16},{32,24},{40,32},{48,40},{56,48},{1,57}... | collective-permute-start | bytes 1179656 | tf_op jit(solution)/shard_map/ppermute | solution.py:41
  19.3 17.8 %all-to-all-start.1 = ((bf16[8,16,1152]{2,1,0:T(8,128)(2,1)}), bf16[8,16,1152]{2,1,0:T(8,128)(2,1)S(1)}, u32[]{:S(2)}, u32[]{:S(2)}) async-start(bf16[8,16,1152]{2,1,0:T(8,128)(2,1)} %pad_maximum_fusion), calls=%async_computation.1 | async-start | bytes 589824 | tf_op jit(solution)/shard_map/all_to_all | solution.py:27
  37.9 24.8 %all-to-all-start = ((bf16[8,80,256]{2,1,0:T(8,128)(2,1)}), bf16[8,80,256]{2,1,0:T(8,128)(2,1)S(1)}, u32[]{:S(2)}, u32[]{:S(2)}) async-start(bf16[8,80,256]{2,1,0:T(8,128)(2,1)} %broadcast_in_dim.21), calls=%async_computation | async-start | bytes 655360 | tf_op jit(solution)/shard_map/all_to_all | solution.py:27
  41.3 17.1 %collective-permute-start.8 = (bf16[2,256,384]{2,1,0:T(8,128)(2,1)S(1)}, bf16[2,256,384]{2,1,0:T(8,128)(2,1)}, u32[]{:S(2)}, u32[]{:S(2)}) collective-permute-start(bf16[2,256,384]{2,1,0:T(8,128)(2,1)S(1)} %collective-permute-done.7.refs_1_), channel_id=1, source_target_pairs={{0,8},{8,16},{16,24},{24,32},{32,40},{40,48},{48,56},{56,0},{1,9},... | collective-permute-start | bytes 1179656 | tf_op jit(solution)/shard_map/ppermute | solution.py:40
  44.0 14.4 %collective-permute-start.12 = (bf16[2,256,384]{2,1,0:T(8,128)(2,1)S(1)}, bf16[2,256,384]{2,1,0:T(8,128)(2,1)}, u32[]{:S(2)}, u32[]{:S(2)}) collective-permute-start(bf16[2,256,384]{2,1,0:T(8,128)(2,1)S(1)} %collective-permute-done.11.refs_6_), channel_id=1, source_target_pairs={{0,56},{8,0},{16,8},{24,16},{32,24},{40,32},{48,40},{56,48},{1,57}... | collective-permute-start | bytes 1179656 | tf_op jit(solution)/shard_map/ppermute | solution.py:41
  58.4 10.7 %collective-permute-start.9 = (bf16[2,256,384]{2,1,0:T(8,128)(2,1)}, bf16[2,256,384]{2,1,0:T(8,128)(2,1)S(1)}, u32[]{:S(2)}, u32[]{:S(2)}) collective-permute-start(bf16[2,256,384]{2,1,0:T(8,128)(2,1)} %collective-permute-done.8.refs_2_), channel_id=1, source_target_pairs={{0,8},{8,16},{16,24},{24,32},{32,40},{40,48},{48,56},{56,0},{1,9},... | collective-permute-start | bytes 1179656 | tf_op jit(solution)/shard_map/ppermute | solution.py:40
  58.4 13.3 %collective-permute-start.13 = (bf16[2,256,384]{2,1,0:T(8,128)(2,1)}, bf16[2,256,384]{2,1,0:T(8,128)(2,1)S(1)}, u32[]{:S(2)}, u32[]{:S(2)}) collective-permute-start(bf16[2,256,384]{2,1,0:T(8,128)(2,1)} %collective-permute-done.12.refs_7_), channel_id=1, source_target_pairs={{0,56},{8,0},{16,8},{24,16},{32,24},{40,32},{48,40},{56,48},{1,57}... | collective-permute-start | bytes 1179656 | tf_op jit(solution)/shard_map/ppermute | solution.py:41
  63.4 17.0 %all-to-all-start.2 = ((bf16[8,16,1152]{2,1,0:T(8,128)(2,1)}), bf16[8,16,1152]{2,1,0:T(8,128)(2,1)S(1)}, u32[]{:S(2)}, u32[]{:S(2)}) async-start(bf16[8,16,1152]{2,1,0:T(8,128)(2,1)} %broadcast_in_dim.24), calls=%async_computation.2 | async-start | bytes 589824 | tf_op jit(solution)/shard_map/all_to_all | solution.py:27
  69.8 10.8 %collective-permute-start.10 = (bf16[2,128,384]{2,1,0:T(8,128)(2,1)}, bf16[2,128,384]{2,1,0:T(8,128)(2,1)}, u32[]{:S(2)}, u32[]{:S(2)}) collective-permute-start(bf16[2,128,384]{2,1,0:T(8,128)(2,1)} %slice.154), channel_id=1, source_target_pairs={{0,8},{8,16},{16,24},{24,32},{32,40},{40,48},{48,56},{56,0},{1,9},... | collective-permute-start | bytes 589832 | tf_op jit(solution)/shard_map/ppermute | solution.py:43
  113.3 19.0 %collective-permute-start = (bf16[640,384]{1,0:T(8,128)(2,1)S(1)}, bf16[640,384]{1,0:T(8,128)(2,1)S(1)}, u32[]{:S(2)}, u32[]{:S(2)}) collective-permute-start(bf16[640,384]{1,0:T(8,128)(2,1)S(1)} %dynamic-slice_bitcast_fusion.1.refs_0_), channel_id=1, source_target_pairs={{0,1},{1,2},{2,3},{3,4},{4,5},{5,6},{6,7},{7,0},{8,9},{9,10},{10,1... | collective-permute-start | bytes 1474568 | tf_op jit(solution)/shard_map/ppermute | solution.py:178
  114.3 20.5 %collective-permute-start.1 = (bf16[640,384]{1,0:T(8,128)(2,1)S(1)}, bf16[640,384]{1,0:T(8,128)(2,1)}, u32[]{:S(2)}, u32[]{:S(2)}) collective-permute-start(bf16[640,384]{1,0:T(8,128)(2,1)S(1)} %dynamic-slice_bitcast_fusion.1.refs_0_), channel_id=1, source_target_pairs={{0,2},{1,3},{2,4},{3,5},{4,6},{5,7},{6,0},{7,1},{8,10},{9,11},{10,... | collective-permute-start | bytes 1474568 | tf_op jit(solution)/shard_map/ppermute | solution.py:178
  126.8 29.0 %collective-permute-start.17 = (bf16[8,32,384]{2,1,0:T(8,128)(2,1)}, bf16[8,32,384]{2,1,0:T(8,128)(2,1)S(1)}, u32[]{:S(2)}, u32[]{:S(2)}) collective-permute-start(bf16[8,32,384]{2,1,0:T(8,128)(2,1)} %collective-permute-done.16.refs_10_), channel_id=1, source_target_pairs={{0,8},{8,16},{16,24},{24,32},{32,40},{40,48},{48,56},{56,0},{1,9},... | collective-permute-start | bytes 589832 | tf_op jit(solution)/shard_map/ppermute | solution.py:40
  127.0 28.8 %collective-permute-start.21 = (bf16[8,32,384]{2,1,0:T(8,128)(2,1)}, bf16[8,32,384]{2,1,0:T(8,128)(2,1)S(1)}, u32[]{:S(2)}, u32[]{:S(2)}) collective-permute-start(bf16[8,32,384]{2,1,0:T(8,128)(2,1)} %collective-permute-done.20.refs_15_), channel_id=1, source_target_pairs={{0,56},{8,0},{16,8},{24,16},{32,24},{40,32},{48,40},{56,48},{1,57}... | collective-permute-start | bytes 589832 | tf_op jit(solution)/shard_map/ppermute | solution.py:41
  130.8 33.8 %collective-permute-start.2 = (bf16[640,384]{1,0:T(8,128)(2,1)S(1)}, bf16[640,384]{1,0:T(8,128)(2,1)}, u32[]{:S(2)}, u32[]{:S(2)}) collective-permute-start(bf16[640,384]{1,0:T(8,128)(2,1)S(1)} %dynamic-slice_bitcast_fusion.1.refs_0_), channel_id=1, source_target_pairs={{0,3},{1,4},{2,5},{3,6},{4,7},{5,0},{6,1},{7,2},{8,11},{9,12},{10,... | collective-permute-start | bytes 1474568 | tf_op jit(solution)/shard_map/ppermute | solution.py:178
  132.4 33.2 %collective-permute-start.3 = (bf16[640,384]{1,0:T(8,128)(2,1)S(1)}, bf16[640,384]{1,0:T(8,128)(2,1)}, u32[]{:S(2)}, u32[]{:S(2)}) collective-permute-start(bf16[640,384]{1,0:T(8,128)(2,1)S(1)} %dynamic-slice_bitcast_fusion.1.refs_0_), channel_id=1, source_target_pairs={{0,4},{1,5},{2,6},{3,7},{4,0},{5,1},{6,2},{7,3},{8,12},{9,13},{10,... | collective-permute-start | bytes 1474568 | tf_op jit(solution)/shard_map/ppermute | solution.py:178
  134.9 34.7 %collective-permute-start.4 = (bf16[640,384]{1,0:T(8,128)(2,1)S(1)}, bf16[640,384]{1,0:T(8,128)(2,1)}, u32[]{:S(2)}, u32[]{:S(2)}) collective-permute-start(bf16[640,384]{1,0:T(8,128)(2,1)S(1)} %dynamic-slice_bitcast_fusion.1.refs_0_), channel_id=1, source_target_pairs={{0,5},{1,6},{2,7},{3,0},{4,1},{5,2},{6,3},{7,4},{8,13},{9,14},{10,... | collective-permute-start | bytes 1474568 | tf_op jit(solution)/shard_map/ppermute | solution.py:178
  155.9 21.8 %collective-permute-start.5 = (bf16[640,384]{1,0:T(8,128)(2,1)S(1)}, bf16[640,384]{1,0:T(8,128)(2,1)}, u32[]{:S(2)}, u32[]{:S(2)}) collective-permute-start(bf16[640,384]{1,0:T(8,128)(2,1)S(1)} %dynamic-slice_bitcast_fusion.1.refs_0_), channel_id=1, source_target_pairs={{0,6},{1,7},{2,0},{3,1},{4,2},{5,3},{6,4},{7,5},{8,14},{9,15},{10,... | collective-permute-start | bytes 1474568 | tf_op jit(solution)/shard_map/ppermute | solution.py:178
  155.9 21.8 %collective-permute-start.6 = (bf16[640,384]{1,0:T(8,128)(2,1)S(1)}, bf16[640,384]{1,0:T(8,128)(2,1)}, u32[]{:S(2)}, u32[]{:S(2)}) collective-permute-start(bf16[640,384]{1,0:T(8,128)(2,1)S(1)} %dynamic-slice_bitcast_fusion.1.refs_0_), channel_id=1, source_target_pairs={{0,7},{1,0},{2,1},{3,2},{4,3},{5,4},{6,5},{7,6},{8,15},{9,8},{10,9... | collective-permute-start | bytes 1474568 | tf_op jit(solution)/shard_map/ppermute | solution.py:178
  164.6 13.1 %collective-permute-start.18 = (bf16[8,16,384]{2,1,0:T(8,128)(2,1)}, bf16[8,16,384]{2,1,0:T(8,128)(2,1)}, u32[]{:S(2)}, u32[]{:S(2)}) collective-permute-start(bf16[8,16,384]{2,1,0:T(8,128)(2,1)} %slice.156), channel_id=1, source_target_pairs={{0,8},{8,16},{16,24},{24,32},{32,40},{40,48},{48,56},{56,0},{1,9},... | collective-permute-start | bytes 294920 | tf_op jit(solution)/shard_map/ppermute | solution.py:43
  165.6 12.1 %collective-permute-start.22 = (bf16[8,16,384]{2,1,0:T(8,128)(2,1)}, bf16[8,16,384]{2,1,0:T(8,128)(2,1)}, u32[]{:S(2)}, u32[]{:S(2)}) collective-permute-start(bf16[8,16,384]{2,1,0:T(8,128)(2,1)} %slice.157), channel_id=1, source_target_pairs={{0,56},{8,0},{16,8},{24,16},{32,24},{40,32},{48,40},{56,48},{1,57}... | collective-permute-start | bytes 294920 | tf_op jit(solution)/shard_map/ppermute | solution.py:44
  185.6 27.8 %all-to-all-start.4 = ((f32[32,40,128]{2,1,0:T(8,128)}), f32[32,40,128]{2,1,0:T(8,128)S(1)}, u32[]{:S(2)}, u32[]{:S(2)}) async-start(f32[32,40,128]{2,1,0:T(8,128)} %bitcast.30), calls=%async_computation.4 | async-start | bytes 1310720 | tf_op jit(solution)/shard_map/all_to_all | solution.py:27
  213.4 17.2 %all-to-all-start.6 = ((bf16[8,8,32,80]{3,2,1,0:T(8,128)(2,1)}), bf16[8,8,32,80]{3,2,1,0:T(8,128)(2,1)S(1)}, u32[]{:S(2)}, u32[]{:S(2)}) async-start(bf16[8,8,32,80]{3,2,1,0:T(8,128)(2,1)} %copy.80), calls=%async_computation.6 | async-start | bytes 1048576 | tf_op jit(solution)/shard_map/all_to_all | solution.py:27
  242.4 15.4 %all-to-all-start.7 = ((f32[8,64,80]{2,1,0:T(8,128)}), f32[8,64,80]{2,1,0:T(8,128)S(1)}, u32[]{:S(2)}, u32[]{:S(2)}) async-start(f32[8,64,80]{2,1,0:T(8,128)} %fusion.8), calls=%async_computation.7 | async-start | bytes 524288 | tf_op jit(solution)/shard_map/all_to_all | solution.py:27
  (25 other events, 252.5 us)

commit v2 on v0

v2 whole, which is shorter than its diff:
```python
import functools

import jax
import jax.numpy as jnp
from jax import lax
from jax.experimental import pallas as pl
from jax.experimental.pallas import tpu as pltpu
from jax.sharding import PartitionSpec as P

HEAD_DIM = 128
LOG2E = 1.4426950408889634
guidance_scale = 5.0
bf16 = jnp.bfloat16
f32 = jnp.float32
VMEM = pl.BlockSpec(memory_space=pltpu.VMEM)
SMEM = pl.BlockSpec(memory_space=pltpu.SMEM)
ROOM = pltpu.CompilerParams(vmem_limit_bytes=48 * 1024 * 1024)


def noise_levels(steps):
    remain = 1.0 - steps.astype(f32) / 1000.0
    return 5.0 * remain / (1.0 + 4.0 * remain)


def select_model(stacked, model_index):
    return lax.dynamic_index_in_dim(stacked, model_index, 0, keepdims=False)


def exchange(blocks, axis):
    return lax.all_to_all(blocks, axis, 0, 0, tiled=True)


def ring(block, axis, count, split):
    up = [(i, (i + 1) % count) for i in range(count)]
    down = [(i, (i - 1) % count) for i in range(count)]
    behind, ahead = [block], [block]
    for _ in range(count // 2 - 1):
        behind.append(lax.ppermute(behind[-1], axis, up))
        ahead.append(lax.ppermute(ahead[-1], axis, down))
    size = block.shape[split] // 2
    first = lax.ppermute(lax.slice_in_dim(behind[-1], 0, size, axis=split), axis, up)
    second = lax.ppermute(lax.slice_in_dim(ahead[-1], size, 2 * size, axis=split), axis, down)
    return behind + ahead[1:] + [first, second]


def dot(a, b, over):
    return lax.dot_general(a, b, ((over[0], over[1]), ((), ())), preferred_element_type=f32)


def prepare_kernel(
    where_ref, levels_ref, embed_ref, weight_ref, shifts_ref, student_ref, previous_ref, noise_ref, out_ref
):
    pieces, size, _ = out_ref.shape
    latent_dim, width = embed_ref.shape[1:]
    parts, depth, feat = weight_ref.shape[1:]
    rows = student_ref.shape[1]
    level = levels_ref[1]
    noised = (1.0 - level) * previous_ref[...].astype(f32) + level * noise_ref[...].astype(f32)
    latents = jnp.where(where_ref[3] == 0, student_ref[...].astype(f32), noised.astype(bf16).astype(f32))

    step = 1024
    row_sum = jnp.zeros((latent_dim, 1), f32)
    for first in range(0, width, step):
        row_sum += jnp.sum(embed_ref[0, :, first : first + step].astype(f32), axis=1, keepdims=True)
    row_mean = row_sum / width

    here = pl.ds(pl.multiple_of(where_ref[1] * depth, 128), depth)
    centred = (embed_ref[0, :, here].astype(f32) - row_mean) * (1.0 + shifts_ref[1:2, here])
    group = latent_dim // pieces
    filler = jnp.concatenate(
        [shifts_ref[0:1, here], jnp.zeros((size - group - 1, depth), f32)], axis=0
    )
    folded = jnp.concatenate(
        [
            x
            for i in range(pieces)
            for x in (centred[i * group : (i + 1) * group], filler)
        ],
        axis=0,
    ).astype(bf16)
    for i in range(parts):
        table = dot(folded, weight_ref[0, i], ((1,), (0,))).astype(bf16)
        out_ref[:, :, i * feat : (i + 1) * feat] = table.reshape(pieces, size, feat)

    mean = jnp.sum(row_mean * latents, axis=0, keepdims=True)
    plain = latents.astype(bf16)
    spread = jnp.zeros((1, rows), f32)
    for first in range(0, width, step):
        hidden = dot(embed_ref[0, :, first : first + step], plain, ((0,), (0,))) - mean
        spread += jnp.sum(hidden * hidden, axis=0, keepdims=True)
    inverse = lax.rsqrt(spread / width + 1e-06)
    high = inverse.astype(bf16).astype(f32)
    middle = (inverse - high).astype(bf16).astype(f32)
    low = inverse - high - middle
    line = lax.broadcasted_iota(jnp.int32, (size, rows), 0)
    tail = jnp.where(line == 0, high, jnp.where(line == 1, middle, jnp.where(line == 2, low, 0.0)))
    blocks = [plain[i * size : (i + 1) * size] for i in range(latent_dim // size)] + [tail.astype(bf16)]
    for n, block in enumerate(blocks):
        first = parts * feat + n * rows
        out_ref[:, :, first : first + rows] = jnp.broadcast_to(block[None], (pieces, size, rows))


def total_kernel(in_ref, out_ref):
    total = jnp.sum(in_ref[:, :, : out_ref.shape[2]].astype(f32), axis=0).astype(bf16)
    out_ref[...] = jnp.broadcast_to(total[None], out_ref.shape)


def fold_keys(heads, carry, queries, keys, values):
    scores = [dot(keys(h), queries[:, h * HEAD_DIM : (h + 1) * HEAD_DIM], ((1,), (1,))) for h in range(heads)]
    new = []
    for h in range(heads):
        top, total, weighted = carry[h]
        new_top = jnp.maximum(top, jnp.max(scores[h], axis=0, keepdims=True))
        weights = jnp.exp2(scores[h] - new_top)
        keep = jnp.exp2(top - new_top)
        total = total * keep + jnp.sum(weights, axis=0, keepdims=True)
        weighted = weighted * keep + dot(values(h), weights.astype(bf16), ((0,), (0,)))
        new.append((new_top, total, weighted))
    return tuple(new)


def current_kernel(heads, where_ref, packed_ref, table_ref, query_ref, state_ref, held_ref):
    feat = heads * HEAD_DIM
    count, size, width = table_ref.shape
    rows = query_ref.shape[0]
    group = 8
    factors = table_ref[...].astype(f32)
    table = factors[:, :group].reshape(count * group, width).astype(bf16)
    shift = factors[0, group : group + 1]
    lines = count * group // size

    def project(i, first, last):
        latents = jnp.concatenate(
            [packed_ref[i, :, width + n * rows : width + (n + 1) * rows] for n in range(lines)], axis=0
        )
        scale = packed_ref[i, :, width + lines * rows : width + (lines + 1) * rows].astype(f32)
        scale = jnp.sum(scale.T, axis=1, keepdims=True)
        return dot(latents, table[:, first:last], ((0,), (0,))) * scale + shift[:, first:last]

    queries = (project(where_ref[1], 0, feat) * (HEAD_DIM ** (-0.5) * LOG2E)).astype(bf16)
    query_ref[...] = queries

    def fill(i, _):
        at = pl.ds(pl.multiple_of(i * rows, rows), rows)
        held_ref[at, :] = project(i, feat, 3 * feat).astype(bf16)
        return 0

    lax.fori_loop(0, count, fill, 0)
    carry = tuple(
        (jnp.full((1, rows), -1e30, f32), jnp.zeros((1, rows), f32), jnp.zeros((HEAD_DIM, rows), f32))
        for _ in range(heads)
    )
    step = 2 * rows

    def current(i, carry):
        at = pl.ds(pl.multiple_of(i * step, step), step)
        return fold_keys(
            heads,
            carry,
            queries,
            lambda h: held_ref[at, h * HEAD_DIM : (h + 1) * HEAD_DIM],
            lambda h: held_ref[at, feat + h * HEAD_DIM : feat + (h + 1) * HEAD_DIM],
        )

    carry = lax.fori_loop(0, count * rows // step, current, carry)
    for h in range(heads):
        state_ref[h, :HEAD_DIM] = carry[h][2]
        state_ref[h, HEAD_DIM : HEAD_DIM + 8] = jnp.broadcast_to(carry[h][0], (8, rows))
        state_ref[h, HEAD_DIM + 8 : HEAD_DIM + 16] = jnp.broadcast_to(carry[h][1], (8, rows))


def context_kernel(heads, query_ref, state_ref, *refs):
    context_refs, out_ref = refs[:-1], refs[-1]
    rows = query_ref.shape[0]
    queries = query_ref[...]
    carry = tuple(
        (
            state_ref[h, HEAD_DIM : HEAD_DIM + 1],
            state_ref[h, HEAD_DIM + 8 : HEAD_DIM + 9],
            state_ref[h, :HEAD_DIM],
        )
        for h in range(heads)
    )
    taken, held = [], 0
    for ref in context_refs:
        taken.append(ref)
        held += ref.shape[1]
        if held == 2 * rows:
            carry = fold_keys(
                heads,
                carry,
                queries,
                lambda h: jnp.concatenate([r[0, :, h * HEAD_DIM : (h + 1) * HEAD_DIM] for r in taken], axis=0),
                lambda h: jnp.concatenate([r[1, :, h * HEAD_DIM : (h + 1) * HEAD_DIM] for r in taken], axis=0),
            )
            taken, held = [], 0
    for h in range(heads):
        _, total, weighted = carry[h]
        attended = (weighted / total).T.astype(bf16)
        out_ref[:, :, h * HEAD_DIM : (h + 1) * HEAD_DIM] = jnp.broadcast_to(
            attended[None], (out_ref.shape[0], rows, HEAD_DIM)
        )


def halves(value):
    high = value.astype(bf16).astype(f32)
    return high, value - high


def head_kernel(sections, where_ref, packed_ref, embed_ref, shifts_ref, head_ref, att_ref, *refs):
    weight_refs, out_ref = refs[:-1], refs[-1]
    n_fsdp, rows = att_ref.shape[:2]
    latent_dim = embed_ref.shape[0]
    size = packed_ref.shape[1]
    width = packed_ref.shape[2] - rows * (latent_dim // size + 1)
    mixed = None
    for f in range(n_fsdp):
        whole = [ref[f] for ref in weight_refs[:-2]]
        whole.append(weight_refs[-2][f] if f < n_fsdp // 2 else weight_refs[-1][f - n_fsdp // 2])
        part = dot(att_ref[f], jnp.concatenate(whole, axis=0), ((1,), (1,)))
        mixed = part if mixed is None else mixed + part
    latents = jnp.concatenate(
        [
            packed_ref[where_ref[1], :, width + n * rows : width + (n + 1) * rows]
            for n in range(latent_dim // size)
        ],
        axis=0,
    )
    residual = dot(latents, embed_ref[...], ((0,), (0,))) + shifts_ref[2:3] * mixed
    centre = jnp.mean(residual, axis=1, keepdims=True)
    residual = residual - centre
    spread = jnp.sum(residual * residual, axis=1, keepdims=True)
    plain_head = head_ref[...].astype(f32)
    head = (plain_head * (1.0 + shifts_ref[4:5])).astype(bf16)
    padded = jnp.concatenate([head, jnp.zeros_like(head)], axis=0)
    values = dot(residual.astype(bf16), padded, ((1,), (1,)))
    lanes = lax.broadcasted_iota(jnp.int32, values.shape, 1)
    for n, column in enumerate(halves(centre) + halves(spread)):
        values = jnp.where(lanes == latent_dim + n, column, values)
    values = values.astype(bf16)
    sums = jnp.sum(head.astype(f32), axis=1, keepdims=True)
    consts = jnp.sum(plain_head * shifts_ref[3:4], axis=1, keepdims=True)
    place = lax.broadcasted_iota(jnp.int32, (latent_dim, 128), 1)
    extra = jnp.zeros((latent_dim, 128), f32)
    for n, column in enumerate(halves(sums) + halves(consts)):
        extra = jnp.where(place == n, column, extra)
    extra = jnp.concatenate([extra, jnp.zeros_like(extra)], axis=0).T[:16].astype(bf16)
    piece = rows // n_fsdp
    for f in range(n_fsdp):
        for s in range(sections):
            out_ref[s * n_fsdp + f, :piece] = values[f * piece : (f + 1) * piece]
            out_ref[s * n_fsdp + f, piece:] = extra


def estimate_kernel(sections, width, levels_ref, partial_ref, student_ref, noised_ref, group_ref, grad_ref, out_ref):
    piece, latent_dim = student_ref.shape
    count = partial_ref.shape[0] // sections
    estimates = []
    for p in range(sections):
        blocks = [partial_ref[p * count + i].astype(f32) for i in range(count)]

        def column(b, n):
            at = latent_dim + n
            return b[:piece, at : at + 1] + b[:piece, at + 1 : at + 2]

        def line(b, n):
            at = piece + n
            return b[at : at + 1, :latent_dim] + b[at + 1 : at + 2, :latent_dim]

        means = [column(b, 0) for b in blocks]
        mean = sum(means) / count
        linear, spread, shift = 0.0, 0.0, 0.0
        for b, m in zip(blocks, means):
            offset = m - mean
            linear += b[:piece, :latent_dim] + offset * line(b, 0)
            spread += column(b, 2) + (width // count) * (offset * offset)
            shift += line(b, 2)
        velocity = linear * lax.rsqrt(spread / width + 1e-06) + shift
        latent = (student_ref if p == 0 else noised_ref)[...].astype(f32)
        estimates.append(latent - levels_ref[0 if p == 0 else 1] * velocity)
    group_ref[...] = estimates[0]
    teacher = estimates[2] + guidance_scale * (estimates[1] - estimates[2])
    grad = estimates[3] - teacher
    grad_ref[...] = grad
    velocity_grad = -levels_ref[2] * grad
    padded = jnp.concatenate([velocity_grad, jnp.zeros_like(velocity_grad)], axis=1).astype(bf16)
    out_ref[...] = jnp.broadcast_to(padded[None], out_ref.shape)


def gradient_kernel(grad_ref, feature_ref, out_ref):
    count, latent_dim, width = out_ref.shape
    grads = grad_ref[...].reshape(-1, grad_ref.shape[2])
    for first, last in ((0, feature_ref.shape[2]), (feature_ref.shape[2], count * width)):
        rows = feature_ref.shape[1] // 2
        part = feature_ref[:, :rows] if first == 0 else feature_ref[:, rows:]
        part = part.reshape(-1, feature_ref.shape[2])
        product = dot(grads, part, ((0,), (0,)))[:latent_dim]
        if first == 0:
            joined = product
        else:
            joined = jnp.concatenate([joined, product], axis=1)
    for i in range(count):
        out_ref[i] = joined[:, i * width : (i + 1) * width]


def per_device(
    student_input,
    previous_latent,
    score_noise,
    timesteps,
    modulation,
    in_weight,
    qkv_weight,
    out_weight,
    head_weight,
    kv_cache,
    saved_features,
):
    section, me_seq, me_fsdp = (lax.axis_index(a) for a in ("section", "seq", "fsdp"))
    sections, n_seq, n_fsdp = (lax.axis_size(a) for a in ("section", "seq", "fsdp"))
    model_index = section - (section >= 2).astype(jnp.int32)
    where = jnp.stack([model_index, me_seq, me_fsdp, section]).astype(jnp.int32)
    levels = noise_levels(timesteps)
    rows, latent_dim = student_input.shape
    width = in_weight.shape[2]
    depth, feat = qkv_weight.shape[1], qkv_weight.shape[3]
    heads = feat // HEAD_DIM
    piece = rows // n_fsdp
    shifts = modulation[0]
    slot = depth // n_fsdp

    context_blocks = ring(kv_cache[0].transpose(1, 0, 2), "seq", n_seq, 1)

    packed_width = 3 * feat + (latent_dim // 16 + 1) * rows
    packed = pl.pallas_call(
        prepare_kernel,
        grid_spec=pltpu.PrefetchScalarGridSpec(
            num_scalar_prefetch=1,
            grid=(1,),
            in_specs=[
                SMEM,
                pl.BlockSpec((1, latent_dim, width), lambda i, w: (w[0], 0, 0)),
                pl.BlockSpec((1, 3, depth, feat), lambda i, w: (w[0], 0, 0, 0)),
                VMEM,
                VMEM,
                VMEM,
                VMEM,
            ],
            out_specs=VMEM,
        ),
        out_shape=jax.ShapeDtypeStruct((n_seq, 16, packed_width), bf16),
        compiler_params=ROOM,
    )(
        where,
        levels,
        in_weight,
        qkv_weight.transpose(0, 2, 1, 3),
        shifts,
        student_input.T,
        previous_latent.T,
        score_noise.T,
    )
    weight_blocks = select_model(out_weight, model_index).reshape(n_fsdp, slot, feat)
    feature_blocks = saved_features.reshape(piece, n_seq, n_fsdp, slot).transpose(2, 0, 1, 3)
    feature_blocks = feature_blocks.reshape(n_fsdp, piece, n_seq * slot)
    spare = jnp.zeros((n_fsdp, piece, 2 * feat - n_seq * slot), bf16)
    aside = jnp.concatenate(
        [
            weight_blocks,
            feature_blocks[:, :, :feat],
            jnp.concatenate([feature_blocks[:, :, feat:], spare], axis=2),
        ],
        axis=1,
    )
    aside, packed = lax.optimization_barrier((aside, packed))
    aside = exchange(aside, "fsdp")
    features = aside[:, slot:]
    weight_ring = ring(aside[:, :slot], "seq", n_seq, 0)
    packed = exchange(packed, "seq")
    table = pl.pallas_call(
        total_kernel,
        in_specs=[VMEM],
        out_specs=VMEM,
        out_shape=jax.ShapeDtypeStruct((n_seq, 16, 3 * feat), bf16),
        compiler_params=ROOM,
    )(packed)
    table = exchange(table, "seq")
    queries, state = pl.pallas_call(
        functools.partial(current_kernel, heads),
        out_shape=(
            jax.ShapeDtypeStruct((rows, feat), bf16),
            jax.ShapeDtypeStruct((heads, HEAD_DIM + 16, rows), f32),
        ),
        in_specs=[SMEM] + [VMEM] * 2,
        out_specs=(VMEM, VMEM),
        scratch_shapes=[pltpu.VMEM((n_seq * rows, 2 * feat), bf16)],
        compiler_params=ROOM,
    )(where, packed, table)
    attended = pl.pallas_call(
        functools.partial(context_kernel, heads),
        out_shape=jax.ShapeDtypeStruct((n_fsdp, rows, feat), bf16),
        in_specs=[VMEM] * (2 + len(context_blocks)),
        out_specs=VMEM,
        compiler_params=ROOM,
    )(queries, state, *context_blocks)
    attended = exchange(attended, "fsdp")

    def columns(array):
        cut = array.reshape(array.shape[0], n_seq, n_fsdp, slot)
        cut = lax.dynamic_index_in_dim(cut, me_fsdp, 2, keepdims=False)
        cut = lax.dynamic_slice_in_dim(jnp.concatenate([cut, cut], axis=1), me_seq, n_seq, 1)
        half = n_seq // 2
        order = [0] + [n_seq - d for d in range(1, half)] + list(range(1, half + 1))
        return jnp.concatenate([cut[:, d] for d in order], axis=1)

    embed_here = columns(select_model(in_weight, model_index))
    head_here = columns(select_model(head_weight.transpose(0, 2, 1), model_index))
    shifts_here = columns(shifts)
    partials = pl.pallas_call(
        functools.partial(head_kernel, sections),
        out_shape=jax.ShapeDtypeStruct((sections * n_fsdp, piece + 16, 128), bf16),
        in_specs=[SMEM] + [VMEM] * (5 + len(weight_ring)),
        out_specs=VMEM,
        compiler_params=ROOM,
    )(where, packed, embed_here, shifts_here, head_here, attended, *weight_ring)
    partials = exchange(partials, ("section", "fsdp"))

    noised = (
        (1.0 - levels[1]) * previous_latent.astype(f32) + levels[1] * score_noise.astype(f32)
    ).astype(bf16)
    own_student = lax.dynamic_slice_in_dim(student_input, me_fsdp * piece, piece, 0)
    own_noised = lax.dynamic_slice_in_dim(noised, me_fsdp * piece, piece, 0)
    student_group, dmd_grad, grads = pl.pallas_call(
        functools.partial(estimate_kernel, sections, width),
        out_shape=(
            jax.ShapeDtypeStruct((piece, latent_dim), f32),
            jax.ShapeDtypeStruct((piece, latent_dim), f32),
            jax.ShapeDtypeStruct((n_fsdp, piece, 2 * latent_dim), bf16),
        ),
        in_specs=[SMEM] + [VMEM] * 3,
        out_specs=(VMEM, VMEM, VMEM),
    )(levels, partials, own_student, own_noised)
    grads = exchange(grads, "fsdp")
    partial_grad = pl.pallas_call(
        gradient_kernel,
        out_shape=jax.ShapeDtypeStruct((n_seq, latent_dim, slot), f32),
        in_specs=[VMEM] * 2,
        out_specs=VMEM,
    )(grads, features)
    head_grad = jnp.sum(exchange(partial_grad, "seq"), axis=0).T
    return (student_group, dmd_grad, head_grad)


def solution(mesh):
    placed = (
        P("seq", None),
        P("seq", None),
        P("seq", None),
        P(),
        P("section", None, None),
        P(),
        P(None, "seq", None, "fsdp"),
        P(None, "seq", "fsdp"),
        P(),
        P("section", "seq", None, "fsdp"),
        P(("seq", "fsdp"), None),
    )
    return jax.shard_map(
        per_device,
        mesh=mesh,
        in_specs=placed,
        out_specs=(P(("seq", "fsdp"), None), P(("seq", "fsdp"), None), P(("seq", "fsdp"), None)),
        check_vma=False,
    )
```

time: 695 us -> 205 us (0.29)
  waiting for transfers between devices: 601 us -> 46.5 us
  starting transfers between devices: 0.43 us -> 65.7 us
  matrix products: 29.5 us -> 0 us
  Pallas kernels: 0 us -> 24.9 us
  local copies, waits for them, and re-layouts: 20.6 us -> 41.8 us
  between operations: 16.9 us -> 1.69 us
  blocking collectives: 6.75 us -> 17 us
  other arithmetic: 15.1 us -> 5.79 us
    unnamed x7 -> x0, waiting for transfers between devices: 315 us -> none
    all_gather x4 -> x0, waiting for transfers between devices: 225 us -> none  [the longest x1 119 us: per_device(): lax.all_gather(attn_weight, 'seq', axis=0, tiled=True)]
    reduce_scatter x1 -> x0, waiting for transfers between devices: 59.9 us -> none  [per_device(): lax.psum_scatter(lax.dot_general(row_block, full_output, (((1,), (1,)), (...]
    all_to_all x0 -> x6, starting transfers between devices: none -> 36.6 us  [exchange(): return lax.all_to_all(blocks, axis, 0, 0, tiled=True)]
    ppermute x0 -> x16, waiting for transfers between devices: none -> 31 us  [the longest x6 31 us: ring(): behind.append(lax.ppermute(behind[-1], axis, up))]
    dot_general x7 -> x0, matrix products: 29.5 us -> none  [the longest x1 9.77 us: per_device(): jnp.dot(normed, full_attn.reshape(full_attn.shape[0], 3 * feat_part), pre...]
    ppermute x0 -> x16, starting transfers between devices: none -> 29 us  [the longest x6 16 us: ring(): ahead.append(lax.ppermute(ahead[-1], axis, down))]
    pallas_call x0 -> x7, Pallas kernels: none -> 24.9 us  [the longest x1 6.87 us: per_device(): pl.pallas_call(functools.partial(current_kernel, heads), out_shape=(jax.S...]
  transfers between devices with their start and end apart: 6 -> 22, of which waited for: 6 -> 8; matrix products, arithmetic and copies ran while one was open for 7% -> 17% of each run, Pallas kernels for 0% -> 5%
where the time goes in v2:
time: 205 us; the launch traced here: 203 us
  starting transfers between devices  65.7 us (32%)
  waiting for transfers between devices  46.5 us (23%)
  local copies, waits for them, and re-layouts  41.8 us (20%)
  Pallas kernels  24.9 us (12%)
  blocking collectives  17 us (8%)
  other arithmetic  5.79 us (3%)
    all_to_all x6, starting transfers between devices, exchange(): return lax.all_to_all(blocks, axis, 0, 0, tiled=True)  36.6 us
    ppermute x6, waiting for transfers between devices, ring(): behind.append(lax.ppermute(behind[-1], axis, up))  31 us
    all_to_all x1, blocking collectives, exchange(): return lax.all_to_all(blocks, axis, 0, 0, tiled=True)  17 us
    ppermute x6, starting transfers between devices, ring(): ahead.append(lax.ppermute(ahead[-1], axis, down))  16 us
    all_to_all x6, waiting for transfers between devices, exchange(): return lax.all_to_all(blocks, axis, 0, 0, tiled=True)  15.5 us
    unnamed x45, local copies, waits for them, and re-layouts  9.62 us
    pallas_call x1, Pallas kernels, per_device(): pl.pallas_call(functools.partial(current_kernel, heads), out_shape=(jax.S...  6.87 us
    ppermute x6, starting transfers between devices, ring(): behind.append(lax.ppermute(behind[-1], axis, up))  6.57 us
  transfers between devices with their start and end apart: 22, of which 8 were waited for; matrix products, arithmetic and copies ran while one was open for 17% of the time, Pallas kernels for 5%

profile of v2, /device:TPU:2, one launch (start us, length us, event | category | flops | bytes accessed | tf_op | source)
XLA Modules:
  0.0 203.5 jit_solution(11764552365883178665)
XLA Ops:
  5.4 4.1 %shard_map.130 = bf16[8,16,2432]{2,1,0:T(8,128)(2,1)} custom-call(s32[4]{0:T(128)S(1)} %pad_add_fusion.where_ref, f32[3]{0:T(128)S(1)} %add_divide_fusion.levels_ref, bf16[3,64,5120]{2,1,0:T(8,128)(2,1)S(1)} %copy-done.2, bf16[3,3,640,384]{3,2,1,0:T(8,128)(2,1)} %bitcast.90, f32[5,5120]{1,0:T(8,128)S(1)} %bitcast.86, bf16[64,256]{1,0:T(8,128)(2,1)S(1)} %bitcast.87, ...), custom_call_target="tpu_custom_call" | custom-call | tf_op jit(solution)/shard_map/pallas_call | solution.py:335
  9.5 6.5 %all-to-all-start.3 = ((bf16[8,144,384]{2,1,0:T(8,128)(2,1)}), bf16[8,144,384]{2,1,0:T(8,128)(2,1)}, u32[]{:S(2)}, u32[]{:S(2)}) async-start(bf16[8,144,384]{2,1,0:T(8,128)(2,1)} %fusion.1), calls=%async_computation.3 | async-start | bytes 1769472 | tf_op jit(solution)/shard_map/all_to_all | solution.py:30
  17.6 4.0 %collective-permute-start.3 = (bf16[2,256,384]{2,1,0:T(8,128)(2,1)S(1)}, bf16[2,256,384]{2,1,0:T(8,128)(2,1)}, u32[]{:S(2)}, u32[]{:S(2)}) collective-permute-start(bf16[2,256,384]{2,1,0:T(8,128)(2,1)S(1)} %bitcast.84), channel_id=1, source_target_pairs={{0,56},{8,0},{16,8},{24,16},{32,24},{40,32},{48,40},{56,48},{1,57}... | collective-permute-start | bytes 1179656 | tf_op jit(solution)/shard_map/ppermute | solution.py:39
  21.6 6.8 %all-to-all-done.3 = bf16[8,144,384]{2,1,0:T(8,128)(2,1)} async-done(((bf16[8,144,384]{2,1,0:T(8,128)(2,1)}), bf16[8,144,384]{2,1,0:T(8,128)(2,1)}, u32[]{:S(2)}, u32[]{:S(2)}) %all-to-all-start.3) | async-done | bytes 884768 | tf_op jit(solution)/shard_map/all_to_all | solution.py:30
  28.4 8.5 %all-to-all-start = ((bf16[8,16,2432]{2,1,0:T(8,128)(2,1)}), bf16[8,16,2432]{2,1,0:T(8,128)(2,1)S(1)}, u32[]{:S(2)}, u32[]{:S(2)}) async-start(bf16[8,16,2432]{2,1,0:T(8,128)(2,1)} %shard_map.130), calls=%async_computation | async-start | bytes 1245184 | tf_op jit(solution)/shard_map/all_to_all | solution.py:30
  41.0 19.9 %collective-permute-done.1.refs_2_ = bf16[2,256,384]{2,1,0:T(8,128)(2,1)} collective-permute-done((bf16[2,256,384]{2,1,0:T(8,128)(2,1)S(1)}, bf16[2,256,384]{2,1,0:T(8,128)(2,1)}, u32[]{:S(2)}, u32[]{:S(2)}) %collective-permute-start.1) | collective-permute-done | bytes 393248 | tf_op jit(solution)/shard_map/ppermute | solution.py:38
  60.8 3.2 %collective-permute-start.5 = (bf16[2,256,384]{2,1,0:T(8,128)(2,1)}, bf16[2,256,384]{2,1,0:T(8,128)(2,1)}, u32[]{:S(2)}, u32[]{:S(2)}) collective-permute-start(bf16[2,256,384]{2,1,0:T(8,128)(2,1)} %collective-permute-done.4.refs_5_), channel_id=1, source_target_pairs={{0,56},{8,0},{16,8},{24,16},{32,24},{40,32},{48,40},{56,48},{1,57}... | collective-permute-start | bytes 1179656 | tf_op jit(solution)/shard_map/ppermute | solution.py:39
  65.2 3.2 %collective-permute-start.11 = (bf16[8,80,384]{2,1,0:T(8,128)(2,1)S(1)}, bf16[8,80,384]{2,1,0:T(8,128)(2,1)}, u32[]{:S(2)}, u32[]{:S(2)}) collective-permute-start(bf16[8,80,384]{2,1,0:T(8,128)(2,1)S(1)} %slice.161.refs_0_), channel_id=1, source_target_pairs={{0,56},{8,0},{16,8},{24,16},{32,24},{40,32},{48,40},{56,48},{1,57}... | collective-permute-start | bytes 1474568 | tf_op jit(solution)/shard_map/ppermute | solution.py:39
  69.2 4.5 %all-to-all-start.1 = ((bf16[8,16,1152]{2,1,0:T(8,128)(2,1)}), bf16[8,16,1152]{2,1,0:T(8,128)(2,1)}, u32[]{:S(2)}, u32[]{:S(2)}) async-start(bf16[8,16,1152]{2,1,0:T(8,128)(2,1)} %copy-done.3), calls=%async_computation.1 | async-start | bytes 589824 | tf_op jit(solution)/shard_map/all_to_all | solution.py:30
  82.9 4.8 %collective-permute-done.8.refs_1_ = bf16[8,80,384]{2,1,0:T(8,128)(2,1)} collective-permute-done((bf16[8,80,384]{2,1,0:T(8,128)(2,1)S(1)}, bf16[8,80,384]{2,1,0:T(8,128)(2,1)}, u32[]{:S(2)}, u32[]{:S(2)}) %collective-permute-start.8) | collective-permute-done | bytes 491552 | tf_op jit(solution)/shard_map/ppermute | solution.py:38
  87.6 3.8 %collective-permute-start.12 = (bf16[8,80,384]{2,1,0:T(8,128)(2,1)}, bf16[8,80,384]{2,1,0:T(8,128)(2,1)}, u32[]{:S(2)}, u32[]{:S(2)}) collective-permute-start(bf16[8,80,384]{2,1,0:T(8,128)(2,1)} %collective-permute-done.11.refs_4_), channel_id=1, source_target_pairs={{0,56},{8,0},{16,8},{24,16},{32,24},{40,32},{48,40},{56,48},{1,57}... | collective-permute-start | bytes 1474568 | tf_op jit(solution)/shard_map/ppermute | solution.py:39
  92.3 6.9 %shard_map.132 = (bf16[256,384]{1,0:T(8,128)(2,1)S(1)}, f32[3,144,256]{2,1,0:T(8,128)S(1)}) custom-call(s32[4]{0:T(128)S(1)} %pad_add_fusion.where_ref, bf16[8,16,2432]{2,1,0:T(8,128)(2,1)S(1)} %all-to-all-done.in_ref.packed_ref, bf16[8,16,1152]{2,1,0:T(8,128)(2,1)} %all-to-all-done.1.table_ref), custom_call_target="tpu_custom_call" | custom-call | tf_op jit(solution)/shard_map/pallas_call | solution.py:388
  100.2 4.2 %shard_map.133 = bf16[8,256,384]{2,1,0:T(8,128)(2,1)S(1)} custom-call(bf16[256,384]{1,0:T(8,128)(2,1)S(1)} %get-tuple-element.11.query_ref, f32[3,144,256]{2,1,0:T(8,128)S(1)} %get-tuple-element.12.state_ref, bf16[2,256,384]{2,1,0:T(8,128)(2,1)S(1)} %bitcast.85, bf16[2,256,384]{2,1,0:T(8,128)(2,1)S(1)} %copy-done.9, ...), custom_call_target="tpu_custom_call" | custom-call | tf_op jit(solution)/shard_map/pallas_call | solution.py:399
  105.6 5.4 %all-to-all-start.2 = ((bf16[8,256,384]{2,1,0:T(8,128)(2,1)}), bf16[8,256,384]{2,1,0:T(8,128)(2,1)}, u32[]{:S(2)}, u32[]{:S(2)}) async-start(bf16[8,256,384]{2,1,0:T(8,128)(2,1)} %copy-done.1), calls=%async_computation.2 | async-start | bytes 3145728 | tf_op jit(solution)/shard_map/all_to_all | solution.py:30
  111.8 3.1 %reshape.28 = bf16[64,8,8,80]{3,2,1,0:T(8,128)(2,1)} reshape(bf16[1,64,5120]{2,1,0:T(8,128)(2,1)} %dynamic-slice_bitcast_fusion) | data formatting | bytes 1310720 | tf_op jit(solution)/shard_map/reshape | solution.py:409
  116.5 3.1 %reshape.27 = bf16[64,8,8,80]{3,2,1,0:T(8,128)(2,1)} reshape(bf16[1,64,5120]{2,1,0:T(8,128)(2,1)} %constant_dynamic-slice_fusion.6) | data formatting | bytes 1310720 | tf_op jit(solution)/shard_map/reshape | solution.py:409
  124.8 2.9 %collective-permute-start.10 = (bf16[8,80,384]{2,1,0:T(8,128)(2,1)}, bf16[8,80,384]{2,1,0:T(8,128)(2,1)S(1)}, u32[]{:S(2)}, u32[]{:S(2)}) collective-permute-start(bf16[8,80,384]{2,1,0:T(8,128)(2,1)} %collective-permute-done.9.refs_2_), channel_id=1, source_target_pairs={{0,8},{8,16},{16,24},{24,32},{32,40},{40,48},{48,56},{56,0},{1,9},... | collective-permute-start | bytes 1474568 | tf_op jit(solution)/shard_map/ppermute | solution.py:38
  130.3 5.7 %collective-permute-done.10.refs_3_ = bf16[8,80,384]{2,1,0:T(8,128)(2,1)S(1)} collective-permute-done((bf16[8,80,384]{2,1,0:T(8,128)(2,1)}, bf16[8,80,384]{2,1,0:T(8,128)(2,1)S(1)}, u32[]{:S(2)}, u32[]{:S(2)}) %collective-permute-start.10) | collective-permute-done | bytes 491552 | tf_op jit(solution)/shard_map/ppermute | solution.py:38
  149.0 5.1 %shard_map.134 = bf16[32,48,128]{2,1,0:T(8,128)(2,1)} custom-call(s32[4]{0:T(128)S(1)} %pad_add_fusion.where_ref, bf16[8,16,2432]{2,1,0:T(8,128)(2,1)S(1)} %all-to-all-done.in_ref.packed_ref, bf16[64,640]{1,0:T(8,128)(2,1)S(1)} %concatenate.27.embed_ref, f32[5,640]{1,0:T(8,128)S(1)} %concatenate.29.shifts_ref, bf16[64,640]{1,0:T(8,128)(2,1)S(1)} %concatenate.31.head_ref, ...), custom_call_target="tpu_custom_call" | custom-call | tf_op jit(solution)/shard_map/pallas_call | solution.py:419
  154.1 7.1 %all-to-all-start.4 = ((bf16[32,48,128]{2,1,0:T(8,128)(2,1)}), bf16[32,48,128]{2,1,0:T(8,128)(2,1)S(1)}, u32[]{:S(2)}, u32[]{:S(2)}) async-start(bf16[32,48,128]{2,1,0:T(8,128)(2,1)} %shard_map.134), calls=%async_computation.4 | async-start | bytes 786432 | tf_op jit(solution)/shard_map/all_to_all | solution.py:30
  165.5 4.5 %all-to-all-done.4.partial_ref = bf16[32,48,128]{2,1,0:T(8,128)(2,1)S(1)} async-done(((bf16[32,48,128]{2,1,0:T(8,128)(2,1)}), bf16[32,48,128]{2,1,0:T(8,128)(2,1)S(1)}, u32[]{:S(2)}, u32[]{:S(2)}) %all-to-all-start.4) | async-done | bytes 393248 | tf_op jit(solution)/shard_map/all_to_all | solution.py:30
  173.4 4.6 %all-to-all-start.5 = ((bf16[8,32,128]{2,1,0:T(8,128)(2,1)}), bf16[8,32,128]{2,1,0:T(8,128)(2,1)S(1)}, u32[]{:S(2)}, u32[]{:S(2)}) async-start(bf16[8,32,128]{2,1,0:T(8,128)(2,1)} %get-tuple-element.16), calls=%async_computation.5 | async-start | bytes 131072 | tf_op jit(solution)/shard_map/all_to_all | solution.py:30
  179.8 3.3 %all-to-all-done.5.grad_ref = bf16[8,32,128]{2,1,0:T(8,128)(2,1)S(1)} async-done(((bf16[8,32,128]{2,1,0:T(8,128)(2,1)}), bf16[8,32,128]{2,1,0:T(8,128)(2,1)S(1)}, u32[]{:S(2)}, u32[]{:S(2)}) %all-to-all-start.5) | async-done | bytes 65568 | tf_op jit(solution)/shard_map/all_to_all | solution.py:30
  185.8 17.0 %all_to_all.35 = f32[8,64,80]{2,1,0:T(8,128)S(1)} all-to-all(f32[8,64,80]{2,1,0:T(8,128)} %shard_map.136), channel_id=1, replica_groups=mesh['section'=4,'seq'=8,'fsdp'=8] {'seq'}, dimensions={0} | all-to-all | bytes 327680 | tf_op jit(solution)/shard_map/all_to_all | solution.py:30
  (111 shorter events, 59.6 us)
Async XLA Ops:
  0.6 110.3 %copy-start = (bf16[3,5120,64]{1,2,0:T(8,128)(2,1)S(1)}, bf16[3,5120,64]{1,2,0:T(8,128)(2,1)}, u32[]{:S(2)}) copy-start(bf16[3,5120,64]{1,2,0:T(8,128)(2,1)} %param.19) | copy-start | bytes 5898244
  3.0 159.1 %copy-start.13 = (f32[3]{0:T(128)}, f32[3]{0:T(128)S(1)}, u32[]{:S(2)}) copy-start(f32[3]{0:T(128)S(1)} %add_divide_fusion.levels_ref) | copy-start | bytes 40
  9.5 18.9 %all-to-all-start.3 = ((bf16[8,144,384]{2,1,0:T(8,128)(2,1)}), bf16[8,144,384]{2,1,0:T(8,128)(2,1)}, u32[]{:S(2)}, u32[]{:S(2)}) async-start(bf16[8,144,384]{2,1,0:T(8,128)(2,1)} %fusion.1), calls=%async_computation.3 | async-start | bytes 1769472 | tf_op jit(solution)/shard_map/all_to_all | solution.py:30
  16.0 20.9 %collective-permute-start = (bf16[2,256,384]{2,1,0:T(8,128)(2,1)S(1)}, bf16[2,256,384]{2,1,0:T(8,128)(2,1)S(1)}, u32[]{:S(2)}, u32[]{:S(2)}) collective-permute-start(bf16[2,256,384]{2,1,0:T(8,128)(2,1)S(1)} %bitcast.83), channel_id=1, source_target_pairs={{0,8},{8,16},{16,24},{24,32},{32,40},{40,48},{48,56},{56,0},{1,9},... | collective-permute-start | bytes 1179656 | tf_op jit(solution)/shard_map/ppermute | solution.py:38
  17.6 22.1 %collective-permute-start.3 = (bf16[2,256,384]{2,1,0:T(8,128)(2,1)S(1)}, bf16[2,256,384]{2,1,0:T(8,128)(2,1)}, u32[]{:S(2)}, u32[]{:S(2)}) collective-permute-start(bf16[2,256,384]{2,1,0:T(8,128)(2,1)S(1)} %bitcast.84), channel_id=1, source_target_pairs={{0,56},{8,0},{16,8},{24,16},{32,24},{40,32},{48,40},{56,48},{1,57}... | collective-permute-start | bytes 1179656 | tf_op jit(solution)/shard_map/ppermute | solution.py:39
  28.4 40.1 %all-to-all-start = ((bf16[8,16,2432]{2,1,0:T(8,128)(2,1)}), bf16[8,16,2432]{2,1,0:T(8,128)(2,1)S(1)}, u32[]{:S(2)}, u32[]{:S(2)}) async-start(bf16[8,16,2432]{2,1,0:T(8,128)(2,1)} %shard_map.130), calls=%async_computation | async-start | bytes 1245184 | tf_op jit(solution)/shard_map/all_to_all | solution.py:30
  36.9 23.9 %collective-permute-start.1 = (bf16[2,256,384]{2,1,0:T(8,128)(2,1)S(1)}, bf16[2,256,384]{2,1,0:T(8,128)(2,1)}, u32[]{:S(2)}, u32[]{:S(2)}) collective-permute-start(bf16[2,256,384]{2,1,0:T(8,128)(2,1)S(1)} %collective-permute-done.refs_1_), channel_id=1, source_target_pairs={{0,8},{8,16},{16,24},{24,32},{32,40},{40,48},{48,56},{56,0},{1,9},... | collective-permute-start | bytes 1179656 | tf_op jit(solution)/shard_map/ppermute | solution.py:38
  39.7 21.2 %collective-permute-start.4 = (bf16[2,256,384]{2,1,0:T(8,128)(2,1)}, bf16[2,256,384]{2,1,0:T(8,128)(2,1)}, u32[]{:S(2)}, u32[]{:S(2)}) collective-permute-start(bf16[2,256,384]{2,1,0:T(8,128)(2,1)} %collective-permute-done.3.refs_4_), channel_id=1, source_target_pairs={{0,56},{8,0},{16,8},{24,16},{32,24},{40,32},{48,40},{56,48},{1,57}... | collective-permute-start | bytes 1179656 | tf_op jit(solution)/shard_map/ppermute | solution.py:39
  60.8 13.6 %collective-permute-start.2 = (bf16[2,256,384]{2,1,0:T(8,128)(2,1)}, bf16[2,256,384]{2,1,0:T(8,128)(2,1)}, u32[]{:S(2)}, u32[]{:S(2)}) collective-permute-start(bf16[2,256,384]{2,1,0:T(8,128)(2,1)} %collective-permute-done.1.refs_2_), channel_id=1, source_target_pairs={{0,8},{8,16},{16,24},{24,32},{32,40},{40,48},{48,56},{56,0},{1,9},... | collective-permute-start | bytes 1179656 | tf_op jit(solution)/shard_map/ppermute | solution.py:38
  60.8 16.6 %collective-permute-start.5 = (bf16[2,256,384]{2,1,0:T(8,128)(2,1)}, bf16[2,256,384]{2,1,0:T(8,128)(2,1)}, u32[]{:S(2)}, u32[]{:S(2)}) collective-permute-start(bf16[2,256,384]{2,1,0:T(8,128)(2,1)} %collective-permute-done.4.refs_5_), channel_id=1, source_target_pairs={{0,56},{8,0},{16,8},{24,16},{32,24},{40,32},{48,40},{56,48},{1,57}... | collective-permute-start | bytes 1179656 | tf_op jit(solution)/shard_map/ppermute | solution.py:39
  65.1 22.5 %collective-permute-start.8 = (bf16[8,80,384]{2,1,0:T(8,128)(2,1)S(1)}, bf16[8,80,384]{2,1,0:T(8,128)(2,1)}, u32[]{:S(2)}, u32[]{:S(2)}) collective-permute-start(bf16[8,80,384]{2,1,0:T(8,128)(2,1)S(1)} %slice.161.refs_0_), channel_id=1, source_target_pairs={{0,8},{8,16},{16,24},{24,32},{32,40},{40,48},{48,56},{56,0},{1,9},... | collective-permute-start | bytes 1474568 | tf_op jit(solution)/shard_map/ppermute | solution.py:38
  65.2 22.4 %collective-permute-start.11 = (bf16[8,80,384]{2,1,0:T(8,128)(2,1)S(1)}, bf16[8,80,384]{2,1,0:T(8,128)(2,1)}, u32[]{:S(2)}, u32[]{:S(2)}) collective-permute-start(bf16[8,80,384]{2,1,0:T(8,128)(2,1)S(1)} %slice.161.refs_0_), channel_id=1, source_target_pairs={{0,56},{8,0},{16,8},{24,16},{32,24},{40,32},{48,40},{56,48},{1,57}... | collective-permute-start | bytes 1474568 | tf_op jit(solution)/shard_map/ppermute | solution.py:39
  69.2 23.1 %all-to-all-start.1 = ((bf16[8,16,1152]{2,1,0:T(8,128)(2,1)}), bf16[8,16,1152]{2,1,0:T(8,128)(2,1)}, u32[]{:S(2)}, u32[]{:S(2)}) async-start(bf16[8,16,1152]{2,1,0:T(8,128)(2,1)} %copy-done.3), calls=%async_computation.1 | async-start | bytes 589824 | tf_op jit(solution)/shard_map/all_to_all | solution.py:30
  76.0 23.2 %collective-permute-start.6 = (bf16[2,128,384]{2,1,0:T(8,128)(2,1)}, bf16[2,128,384]{2,1,0:T(8,128)(2,1)}, u32[]{:S(2)}, u32[]{:S(2)}) collective-permute-start(bf16[2,128,384]{2,1,0:T(8,128)(2,1)} %slice.159), channel_id=1, source_target_pairs={{0,8},{8,16},{16,24},{24,32},{32,40},{40,48},{48,56},{56,0},{1,9},... | collective-permute-start | bytes 589832 | tf_op jit(solution)/shard_map/ppermute | solution.py:41
  79.0 20.2 %collective-permute-start.7 = (bf16[2,128,384]{2,1,0:T(8,128)(2,1)}, bf16[2,128,384]{2,1,0:T(8,128)(2,1)}, u32[]{:S(2)}, u32[]{:S(2)}) collective-permute-start(bf16[2,128,384]{2,1,0:T(8,128)(2,1)} %slice.160), channel_id=1, source_target_pairs={{0,56},{8,0},{16,8},{24,16},{32,24},{40,32},{48,40},{56,48},{1,57}... | collective-permute-start | bytes 589832 | tf_op jit(solution)/shard_map/ppermute | solution.py:42
  87.6 37.1 %collective-permute-start.9 = (bf16[8,80,384]{2,1,0:T(8,128)(2,1)}, bf16[8,80,384]{2,1,0:T(8,128)(2,1)}, u32[]{:S(2)}, u32[]{:S(2)}) collective-permute-start(bf16[8,80,384]{2,1,0:T(8,128)(2,1)} %collective-permute-done.8.refs_1_), channel_id=1, source_target_pairs={{0,8},{8,16},{16,24},{24,32},{32,40},{40,48},{48,56},{56,0},{1,9},... | collective-permute-start | bytes 1474568 | tf_op jit(solution)/shard_map/ppermute | solution.py:38
  87.6 40.0 %collective-permute-start.12 = (bf16[8,80,384]{2,1,0:T(8,128)(2,1)}, bf16[8,80,384]{2,1,0:T(8,128)(2,1)}, u32[]{:S(2)}, u32[]{:S(2)}) collective-permute-start(bf16[8,80,384]{2,1,0:T(8,128)(2,1)} %collective-permute-done.11.refs_4_), channel_id=1, source_target_pairs={{0,56},{8,0},{16,8},{24,16},{32,24},{40,32},{48,40},{56,48},{1,57}... | collective-permute-start | bytes 1474568 | tf_op jit(solution)/shard_map/ppermute | solution.py:39
  105.6 41.4 %all-to-all-start.2 = ((bf16[8,256,384]{2,1,0:T(8,128)(2,1)}), bf16[8,256,384]{2,1,0:T(8,128)(2,1)}, u32[]{:S(2)}, u32[]{:S(2)}) async-start(bf16[8,256,384]{2,1,0:T(8,128)(2,1)} %copy-done.1), calls=%async_computation.2 | async-start | bytes 3145728 | tf_op jit(solution)/shard_map/all_to_all | solution.py:30
  124.8 11.2 %collective-permute-start.10 = (bf16[8,80,384]{2,1,0:T(8,128)(2,1)}, bf16[8,80,384]{2,1,0:T(8,128)(2,1)S(1)}, u32[]{:S(2)}, u32[]{:S(2)}) collective-permute-start(bf16[8,80,384]{2,1,0:T(8,128)(2,1)} %collective-permute-done.9.refs_2_), channel_id=1, source_target_pairs={{0,8},{8,16},{16,24},{24,32},{32,40},{40,48},{48,56},{56,0},{1,9},... | collective-permute-start | bytes 1474568 | tf_op jit(solution)/shard_map/ppermute | solution.py:38
  127.7 10.9 %collective-permute-start.13 = (bf16[8,80,384]{2,1,0:T(8,128)(2,1)}, bf16[8,80,384]{2,1,0:T(8,128)(2,1)S(1)}, u32[]{:S(2)}, u32[]{:S(2)}) collective-permute-start(bf16[8,80,384]{2,1,0:T(8,128)(2,1)} %collective-permute-done.12.refs_5_), channel_id=1, source_target_pairs={{0,56},{8,0},{16,8},{24,16},{32,24},{40,32},{48,40},{56,48},{1,57}... | collective-permute-start | bytes 1474568 | tf_op jit(solution)/shard_map/ppermute | solution.py:39
  137.5 9.5 %collective-permute-start.14 = (bf16[4,80,384]{2,1,0:T(8,128)(2,1)}, bf16[4,80,384]{2,1,0:T(8,128)(2,1)S(1)}, u32[]{:S(2)}, u32[]{:S(2)}) collective-permute-start(bf16[4,80,384]{2,1,0:T(8,128)(2,1)} %slice.162), channel_id=1, source_target_pairs={{0,8},{8,16},{16,24},{24,32},{32,40},{40,48},{48,56},{56,0},{1,9},... | collective-permute-start | bytes 737288 | tf_op jit(solution)/shard_map/ppermute | solution.py:41
  140.1 6.8 %collective-permute-start.15 = (bf16[4,80,384]{2,1,0:T(8,128)(2,1)}, bf16[4,80,384]{2,1,0:T(8,128)(2,1)}, u32[]{:S(2)}, u32[]{:S(2)}) collective-permute-start(bf16[4,80,384]{2,1,0:T(8,128)(2,1)} %slice.163), channel_id=1, source_target_pairs={{0,56},{8,0},{16,8},{24,16},{32,24},{40,32},{48,40},{56,48},{1,57}... | collective-permute-start | bytes 737288 | tf_op jit(solution)/shard_map/ppermute | solution.py:42
  154.1 15.9 %all-to-all-start.4 = ((bf16[32,48,128]{2,1,0:T(8,128)(2,1)}), bf16[32,48,128]{2,1,0:T(8,128)(2,1)S(1)}, u32[]{:S(2)}, u32[]{:S(2)}) async-start(bf16[32,48,128]{2,1,0:T(8,128)(2,1)} %shard_map.134), calls=%async_computation.4 | async-start | bytes 786432 | tf_op jit(solution)/shard_map/all_to_all | solution.py:30
  173.4 9.7 %all-to-all-start.5 = ((bf16[8,32,128]{2,1,0:T(8,128)(2,1)}), bf16[8,32,128]{2,1,0:T(8,128)(2,1)S(1)}, u32[]{:S(2)}, u32[]{:S(2)}) async-start(bf16[8,32,128]{2,1,0:T(8,128)(2,1)} %get-tuple-element.16), calls=%async_computation.5 | async-start | bytes 131072 | tf_op jit(solution)/shard_map/all_to_all | solution.py:30
  (17 other events, 29.6 us)

commit v3 on v2

v3 whole, which is shorter than its diff:
```python
import functools

import jax
import jax.numpy as jnp
from jax import lax
from jax.experimental import pallas as pl
from jax.experimental.pallas import tpu as pltpu
from jax.sharding import PartitionSpec as P

HEAD_DIM = 128
LOG2E = 1.4426950408889634
guidance_scale = 5.0
bf16 = jnp.bfloat16
f32 = jnp.float32


def run(kernel, where, outs, *operands, picked=(), scratch=(), raw=False):
    def spec(shape, pick=False):
        zeros = (0,) * (len(shape) - 1)
        if pick:
            return pl.BlockSpec((1,) + tuple(shape[1:]), lambda i, w: (w[0],) + zeros)
        return pl.BlockSpec(tuple(shape), lambda i, w: (0,) + zeros)

    in_specs = [
        pl.BlockSpec(memory_space=pltpu.SMEM)
        if x.ndim == 1
        else pl.BlockSpec(memory_space=pl.ANY)
        if raw
        else spec(x.shape, n in picked)
        for n, x in enumerate(operands)
    ]
    result = pl.pallas_call(
        kernel,
        grid_spec=pltpu.PrefetchScalarGridSpec(
            num_scalar_prefetch=1,
            grid=(1,),
            in_specs=in_specs,
            out_specs=tuple(spec(shape) for shape, _ in outs),
            scratch_shapes=list(scratch),
        ),
        out_shape=tuple(jax.ShapeDtypeStruct(shape, dtype) for shape, dtype in outs),
        compiler_params=pltpu.CompilerParams(vmem_limit_bytes=52 * 1024 * 1024),
    )(where, *operands)
    return result[0] if len(outs) == 1 else result


def together(value, *others):
    return lax.optimization_barrier((value,) + others)[0]


def noise_levels(steps):
    remain = 1.0 - steps.astype(f32) / 1000.0
    return 5.0 * remain / (1.0 + 4.0 * remain)


def select_model(stacked, model_index):
    return lax.dynamic_index_in_dim(stacked, model_index, 0, keepdims=False)


def exchange(blocks, axis):
    return lax.all_to_all(blocks, axis, 0, 0, tiled=True)


class Ring:
    def __init__(self, block, axis, count, split, split_at=None):
        self.split_at = split_at
        self.axis, self.split, self.half = axis, split, count // 2
        self.up = [(i, (i + 1) % count) for i in range(count)]
        self.down = [(i, (i - 1) % count) for i in range(count)]
        self.behind, self.ahead, self.last = [block], [block], []

    def step(self):
        self.behind.append(lax.ppermute(self.behind[-1], self.axis, self.up))
        self.ahead.append(lax.ppermute(self.ahead[-1], self.axis, self.down))

    def ends(self):
        return self.behind[-1], self.ahead[-1]

    def finish(self):
        while len(self.behind) < self.half:
            self.step()
        total = self.behind[0].shape[self.split]
        size = total // 2 if self.split_at is None else self.split_at
        first = lax.slice_in_dim(self.behind[-1], 0, size, axis=self.split)
        second = lax.slice_in_dim(self.ahead[-1], size, total, axis=self.split)
        self.last = [lax.ppermute(first, self.axis, self.up), lax.ppermute(second, self.axis, self.down)]

    def blocks(self):
        return self.behind + self.ahead[1:] + self.last


def dot(a, b, over):
    return lax.dot_general(a, b, ((over[0], over[1]), ((), ())), preferred_element_type=f32)


def prepare_kernel(
    where_ref, steps_ref, embed_ref, weight_ref, shifts_ref, student_ref, previous_ref, noise_ref, context_ref, out_ref
):
    latent_dim, width = embed_ref.shape[1:]
    parts, depth, feat = weight_ref.shape[1:]
    rows = student_ref.shape[1]
    out_ref[: 2 * rows] = context_ref[...].reshape(2 * rows, feat)
    level = noise_levels(jnp.full((1, rows), steps_ref[1], jnp.int32))
    noised = (1.0 - level) * previous_ref[...].astype(f32) + level * noise_ref[...].astype(f32)
    latents = jnp.where(where_ref[3] == 0, student_ref[...].astype(f32), noised.astype(bf16).astype(f32))

    step = 1024
    row_sum = jnp.zeros((latent_dim, 1), f32)
    for first in range(0, width, step):
        row_sum += jnp.sum(embed_ref[0, :, first : first + step].astype(f32), axis=1, keepdims=True)
    row_mean = row_sum / width

    here = pl.ds(pl.multiple_of(where_ref[1] * depth, 128), depth)
    centred = (embed_ref[0, :, here].astype(f32) - row_mean) * (1.0 + shifts_ref[1, :, here])
    shift = jnp.broadcast_to(shifts_ref[0, :, here], (16, depth))
    folded = jnp.concatenate([centred, shift], axis=0).astype(bf16)
    tail = 2 * rows + parts * latent_dim
    lines = []
    for i in range(parts):
        table = dot(folded, weight_ref[0, i], ((1,), (0,)))
        at = 2 * rows + i * latent_dim
        out_ref[at : at + latent_dim] = table[:latent_dim].astype(bf16)
        lines += [table[latent_dim : latent_dim + 1, n : n + 128] for n in range(0, feat, 128)]

    mean = jnp.sum(row_mean * latents, axis=0, keepdims=True)
    plain = latents.astype(bf16)
    spread = jnp.zeros((1, rows), f32)
    for first in range(0, width, step):
        hidden = dot(embed_ref[0, :, first : first + step], plain, ((0,), (0,))) - mean
        spread += jnp.sum(hidden * hidden, axis=0, keepdims=True)
    inverse = lax.rsqrt(spread / width + 1e-06)
    high = inverse.astype(bf16).astype(f32)
    middle = (inverse - high).astype(bf16).astype(f32)
    low = inverse - high - middle
    line = lax.broadcasted_iota(jnp.int32, (16, rows), 0)
    scales = jnp.where(line == 0, high, jnp.where(line == 1, middle, jnp.where(line == 2, low, 0.0)))
    out_ref[tail : tail + latent_dim, :rows] = plain
    out_ref[tail + latent_dim :, :rows] = scales.astype(bf16)
    spare = jnp.zeros((latent_dim + 16 - len(lines), 128), f32)
    out_ref[tail:, rows:] = jnp.concatenate(lines + [spare], axis=0).astype(bf16)


def aside_kernel(where_ref, weight_ref, feature_ref, out_ref):
    count, lines, feat = out_ref.shape
    rows, width = feature_ref.shape
    slot = weight_ref.shape[1] // count
    part = width // count
    out_ref[:, :slot] = weight_ref[0].reshape(count, slot, feat)
    spare = jnp.zeros((rows, 2 * feat - part), bf16)
    for j in range(count):
        pieces = [feature_ref[:, s * part + j * slot : s * part + (j + 1) * slot] for s in range(count)]
        joined = jnp.concatenate(pieces + [spare], axis=1)
        out_ref[j, slot : slot + rows] = joined[:, :feat]
        out_ref[j, slot + rows :] = joined[:, feat:]


def columns_kernel(where_ref, embed_ref, head_ref, shifts_ref, embed_out, head_out, shifts_out):
    count = 8
    part = embed_ref.shape[2] // count
    slot = part // count
    half = count // 2
    order = [0] + [count - d for d in range(1, half)] + list(range(1, half + 1))
    for f in range(count):

        @pl.when(where_ref[2] == f)
        def _(f=f):
            sources = [(embed_ref.at[0], embed_out), (head_ref.at[0], head_out)]
            sources += [(shifts_ref.at[i], shifts_out.at[i]) for i in range(shifts_ref.shape[0])]
            for source, target in sources:
                pieces = []
                for d in order:
                    owner = lax.rem(where_ref[1] + d, count)
                    block = source[:, pl.ds(pl.multiple_of(owner * part, 128), part)]
                    pieces.append(block[:, f * slot : (f + 1) * slot])
                target[...] = jnp.concatenate(pieces, axis=1)


def fold_keys(heads, carry, queries, keys, values):
    scores = [dot(keys(h), queries[:, h * HEAD_DIM : (h + 1) * HEAD_DIM], ((1,), (1,))) for h in range(heads)]
    new = []
    for h in range(heads):
        top, total, weighted = carry[h]
        new_top = jnp.maximum(top, jnp.max(scores[h], axis=0, keepdims=True))
        weights = jnp.exp2(scores[h] - new_top)
        keep = jnp.exp2(top - new_top)
        total = total * keep + jnp.sum(weights, axis=0, keepdims=True)
        weighted = weighted * keep + dot(values(h), weights.astype(bf16), ((0,), (0,)))
        new.append((new_top, total, weighted))
    return tuple(new)


def attention_kernel(heads, latent_dim, where_ref, *refs):
    n_blocks = len(refs) - 4
    block_refs, (out_ref, all_ref, held_ref, sems) = refs[:n_blocks], refs[n_blocks:]
    count, lines, feat = all_ref.shape
    rows = out_ref.shape[1]
    copies = []
    for n, ref in enumerate(block_refs):
        if n < count:
            target = all_ref.at[n, pl.ds(0, ref.shape[0])]
        else:
            target = all_ref.at[count - 1, pl.ds(lines - ref.shape[0], ref.shape[0])]
        copies.append(pltpu.make_async_copy(ref, target, sems.at[n]))
    for copy in copies:
        copy.start()
    for copy in copies:
        copy.wait()

    tail = 2 * rows + 3 * latent_dim
    parts = [slice(2 * rows + i * latent_dim, 2 * rows + (i + 1) * latent_dim) for i in range(3)]
    tables = [sum(all_ref[n, at].astype(f32) for n in range(count)).astype(bf16) for at in parts]
    shift = sum(all_ref[n, tail : tail + 16, rows:].astype(f32) for n in range(count))
    shifts = [
        jnp.concatenate([shift[i * heads + h : i * heads + h + 1] for h in range(heads)], axis=1) for i in range(3)
    ]

    def project(n, which):
        latents = all_ref[n, tail : tail + latent_dim, :rows]
        scale = all_ref[n, tail + latent_dim :, :rows].astype(f32)
        scale = jnp.sum(scale.T, axis=1, keepdims=True)
        return [dot(latents, tables[i], ((0,), (0,))) * scale + shifts[i] for i in which]

    queries = (project(0, (0,))[0] * (HEAD_DIM ** (-0.5) * LOG2E)).astype(bf16)

    def fill(n, _):
        keys, values = project(n, (1, 2))
        held_ref[n, :rows] = keys.astype(bf16)
        held_ref[n, rows:] = values.astype(bf16)
        return 0

    lax.fori_loop(0, count, fill, 0)
    carry = tuple(
        (jnp.full((1, rows), -1e30, f32), jnp.zeros((1, rows), f32), jnp.zeros((HEAD_DIM, rows), f32))
        for _ in range(heads)
    )

    def pair(ref, i, carry):
        def both(first, h):
            cols = slice(h * HEAD_DIM, (h + 1) * HEAD_DIM)
            return jnp.concatenate([ref[2 * i + n, first : first + rows, cols] for n in range(2)], axis=0)

        return fold_keys(heads, carry, queries, lambda h: both(0, h), lambda h: both(rows, h))

    carry = lax.fori_loop(0, count // 2, lambda i, c: pair(held_ref, i, c), carry)
    carry = lax.fori_loop(0, count // 2, lambda i, c: pair(all_ref, i, c), carry)
    for h in range(heads):
        _, total, weighted = carry[h]
        attended = (weighted / total).T.astype(bf16)
        out_ref[:, :, h * HEAD_DIM : (h + 1) * HEAD_DIM] = jnp.broadcast_to(
            attended[None], (out_ref.shape[0], rows, HEAD_DIM)
        )


def halves(value):
    high = value.astype(bf16).astype(f32)
    return high, value - high


def head_kernel(sections, where_ref, own_ref, embed_ref, shifts_ref, head_ref, att_ref, *refs):
    weight_refs, out_ref = refs[:-1], refs[-1]
    n_fsdp, rows = att_ref.shape[:2]
    latent_dim = embed_ref.shape[0]
    mixed = None
    for f in range(n_fsdp):
        whole = [ref[f] for ref in weight_refs[:-2]]
        whole.append(weight_refs[-2][f] if f < n_fsdp // 2 else weight_refs[-1][f - n_fsdp // 2])
        part = dot(att_ref[f], jnp.concatenate(whole, axis=0), ((1,), (1,)))
        mixed = part if mixed is None else mixed + part
    latents = own_ref[own_ref.shape[0] - latent_dim - 16 : own_ref.shape[0] - 16, :rows]
    residual = dot(latents, embed_ref[...], ((0,), (0,))) + shifts_ref[2] * mixed
    centre = jnp.mean(residual, axis=1, keepdims=True)
    residual = residual - centre
    spread = jnp.sum(residual * residual, axis=1, keepdims=True)
    plain_head = head_ref[...].astype(f32)
    head = (plain_head * (1.0 + shifts_ref[4])).astype(bf16)
    padded = jnp.concatenate([head, jnp.zeros_like(head)], axis=0)
    values = dot(residual.astype(bf16), padded, ((1,), (1,)))
    lanes = lax.broadcasted_iota(jnp.int32, values.shape, 1)
    for n, column in enumerate(halves(centre) + halves(spread)):
        values = jnp.where(lanes == latent_dim + n, column, values)
    values = values.astype(bf16)
    sums = jnp.sum(head.astype(f32), axis=1, keepdims=True)
    consts = jnp.sum(plain_head * shifts_ref[3], axis=1, keepdims=True)
    place = lax.broadcasted_iota(jnp.int32, (latent_dim, 128), 1)
    extra = jnp.zeros((latent_dim, 128), f32)
    for n, column in enumerate(halves(sums) + halves(consts)):
        extra = jnp.where(place == n, column, extra)
    extra = jnp.concatenate([extra, jnp.zeros_like(extra)], axis=0).T[:16].astype(bf16)
    piece = rows // n_fsdp
    for f in range(n_fsdp):
        for s in range(sections):
            out_ref[s * n_fsdp + f, :piece] = values[f * piece : (f + 1) * piece]
            out_ref[s * n_fsdp + f, piece:] = extra


def estimate_kernel(sections, width, where_ref, levels_ref, partial_ref, student_ref, noised_ref, group_ref, grad_ref, out_ref):
    piece, latent_dim = student_ref.shape
    count = partial_ref.shape[0] // sections
    estimates = []
    for p in range(sections):
        blocks = [partial_ref[p * count + i].astype(f32) for i in range(count)]

        def column(b, n):
            at = latent_dim + n
            return b[:piece, at : at + 1] + b[:piece, at + 1 : at + 2]

        def line(b, n):
            at = piece + n
            return b[at : at + 1, :latent_dim] + b[at + 1 : at + 2, :latent_dim]

        means = [column(b, 0) for b in blocks]
        mean = sum(means) / count
        linear, spread, shift = 0.0, 0.0, 0.0
        for b, m in zip(blocks, means):
            offset = m - mean
            linear += b[:piece, :latent_dim] + offset * line(b, 0)
            spread += column(b, 2) + (width // count) * (offset * offset)
            shift += line(b, 2)
        velocity = linear * lax.rsqrt(spread / width + 1e-06) + shift
        latent = (student_ref if p == 0 else noised_ref)[...].astype(f32)
        estimates.append(latent - levels_ref[0 if p == 0 else 1] * velocity)
    group_ref[...] = estimates[0]
    teacher = estimates[2] + guidance_scale * (estimates[1] - estimates[2])
    grad = estimates[3] - teacher
    grad_ref[...] = grad
    velocity_grad = -levels_ref[2] * grad
    padded = jnp.concatenate([velocity_grad, jnp.zeros_like(velocity_grad)], axis=1).astype(bf16)
    out_ref[...] = jnp.broadcast_to(padded[None], out_ref.shape)


def gradient_kernel(where_ref, grad_ref, feature_ref, out_ref):
    count, latent_dim, width = out_ref.shape
    rows = grad_ref.shape[1]
    grads = grad_ref[...].reshape(-1, grad_ref.shape[2])
    first, second = (
        dot(grads, feature_ref[:, at : at + rows].reshape(count * rows, -1), ((0,), (0,)))[:latent_dim]
        for at in (width, width + rows)
    )
    joined = jnp.concatenate([first, second], axis=1)
    for i in range(count):
        out_ref[i] = joined[:, i * width : (i + 1) * width]


def per_device(
    student_input,
    previous_latent,
    score_noise,
    timesteps,
    modulation,
    in_weight,
    qkv_weight,
    out_weight,
    head_weight,
    kv_cache,
    saved_features,
):
    section, me_seq, me_fsdp = (lax.axis_index(a) for a in ("section", "seq", "fsdp"))
    sections, n_seq, n_fsdp = (lax.axis_size(a) for a in ("section", "seq", "fsdp"))
    model_index = section - (section >= 2).astype(jnp.int32)
    where = jnp.stack([model_index, me_seq, me_fsdp, section]).astype(jnp.int32)
    levels = noise_levels(timesteps)
    rows, latent_dim = student_input.shape
    width = in_weight.shape[2]
    depth, feat = qkv_weight.shape[1], qkv_weight.shape[3]
    heads = feat // HEAD_DIM
    piece = rows // n_fsdp
    shifts = modulation.transpose(1, 0, 2)
    slot = depth // n_fsdp

    cut = run(aside_kernel, where, [((n_fsdp, slot + 2 * piece, feat), bf16)], out_weight, saved_features, picked=(0,))
    lines = 2 * rows + 3 * latent_dim + latent_dim + 16
    own = run(
        prepare_kernel,
        where,
        [((lines, feat), bf16)],
        timesteps,
        in_weight,
        qkv_weight.transpose(0, 2, 1, 3),
        shifts,
        student_input.T,
        previous_latent.T,
        score_noise.T,
        kv_cache[0].transpose(1, 0, 2),
        picked=(1, 2),
    )
    aside = exchange(cut, "fsdp")
    around = Ring(own, "seq", n_seq, 0, lines // 32 * 16)
    around.step()
    around.step()
    block, *_ = lax.optimization_barrier((aside[:, :slot],) + around.ends())
    weights = Ring(block, "seq", n_seq, 0)
    weights.step()
    around.finish()
    blocks = around.blocks()
    attended = run(
        functools.partial(attention_kernel, heads, latent_dim),
        together(where, *weights.ends()),
        [((n_fsdp, rows, feat), bf16)],
        *blocks,
        scratch=[
            pltpu.VMEM((n_seq, lines, feat), bf16),
            pltpu.VMEM((n_seq, 2 * rows, feat), bf16),
            pltpu.SemaphoreType.DMA((n_seq + 1,)),
        ],
        raw=True,
    )
    weights.step()
    attended = exchange(together(attended, *weights.ends()), "fsdp")
    weights.step()
    weights.finish()
    embed_here, head_here, shifts_here = run(
        columns_kernel,
        together(where, own),
        [((latent_dim, depth), bf16), ((latent_dim, depth), bf16), ((shifts.shape[0], 1, depth), f32)],
        in_weight,
        head_weight.transpose(0, 2, 1),
        shifts,
        picked=(0, 1),
    )
    partials = run(
        functools.partial(head_kernel, sections),
        where,
        [((sections * n_fsdp, piece + 16, 128), bf16)],
        own,
        embed_here,
        shifts_here,
        head_here,
        attended,
        *weights.blocks(),
    )
    partials = exchange(partials, ("section", "fsdp"))

    noised = (
        (1.0 - levels[1]) * previous_latent.astype(f32) + levels[1] * score_noise.astype(f32)
    ).astype(bf16)
    own_student = lax.dynamic_slice_in_dim(student_input, me_fsdp * piece, piece, 0)
    own_noised = lax.dynamic_slice_in_dim(noised, me_fsdp * piece, piece, 0)
    student_group, dmd_grad, grads = run(
        functools.partial(estimate_kernel, sections, width),
        where,
        [((piece, latent_dim), f32), ((piece, latent_dim), f32), ((n_fsdp, piece, 2 * latent_dim), bf16)],
        levels,
        partials,
        own_student,
        own_noised,
    )
    grads = exchange(grads, "fsdp")
    partial_grad = run(gradient_kernel, where, [((n_seq, latent_dim, slot), f32)], grads, aside)
    head_grad = jnp.sum(exchange(partial_grad, "seq"), axis=0).T
    return (student_group, dmd_grad, head_grad)


def solution(mesh):
    placed = (
        P("seq", None),
        P("seq", None),
        P("seq", None),
        P(),
        P("section", None, None),
        P(),
        P(None, "seq", None, "fsdp"),
        P(None, "seq", "fsdp"),
        P(),
        P("section", "seq", None, "fsdp"),
        P(("seq", "fsdp"), None),
    )
    return jax.shard_map(
        per_device,
        mesh=mesh,
        in_specs=placed,
        out_specs=(P(("seq", "fsdp"), None), P(("seq", "fsdp"), None), P(("seq", "fsdp"), None)),
        check_vma=False,
    )
```

time: 205 us -> 179 us (0.87)
  local copies, waits for them, and re-layouts: 41.8 us -> 6.87 us
  starting transfers between devices: 65.7 us -> 47.2 us
  waiting for transfers between devices: 46.5 us -> 64.6 us
  blocking collectives: 17 us -> 25 us
  Pallas kernels: 24.9 us -> 31.4 us
  other arithmetic: 5.79 us -> 1.38 us
    ppermute x16, waiting for transfers between devices: 31 us -> 53.7 us  [the longest x6 31.5 us: step(): self.behind.append(lax.ppermute(self.behind[-1], self.axis, self.up))]
    all_to_all x6 -> x3, starting transfers between devices: 36.6 us -> 19 us  [exchange(): return lax.all_to_all(blocks, axis, 0, 0, tiled=True)]
    dynamic_slice x7 -> x0, local copies, waits for them, and re-layouts: 8.73 us -> none  [the longest x4 4.64 us: columns(): cut = lax.dynamic_index_in_dim(cut, me_fsdp, 2, keepdims=False)]
    reshape x5 -> x0, local copies, waits for them, and re-layouts: 8.35 us -> none  [the longest x2 6.17 us: columns(): cut = array.reshape(array.shape[0], n_seq, n_fsdp, slot)]
    all_to_all x1 -> x2, blocking collectives: 17 us -> 25 us  [exchange(): return lax.all_to_all(blocks, axis, 0, 0, tiled=True)]
    slice x8 -> x5, local copies, waits for them, and re-layouts: 7.57 us -> 0.93 us  [the longest x2 0.82 us: finish(): second = lax.slice_in_dim(self.ahead[-1], size, total, axis=self.split)]
    pallas_call x7, Pallas kernels: 24.9 us -> 31.4 us  [run(): pl.pallas_call(kernel, grid_spec=pltpu.PrefetchScalarGridSpec(num_scalar_...]
    all_to_all x6 -> x3, waiting for transfers between devices: 15.5 us -> 10.9 us  [exchange(): return lax.all_to_all(blocks, axis, 0, 0, tiled=True)]
  transfers between devices with their start and end apart: 22 -> 19, of which waited for: 8 -> 10; matrix products, arithmetic and copies ran while one was open for 17% -> 1% of each run, Pallas kernels for 5% -> 10%
where the time goes in v3:
time: 179 us; the launch traced here: 178 us
  waiting for transfers between devices  64.6 us (36%)
  starting transfers between devices  47.2 us (26%)
  Pallas kernels  31.4 us (18%)
  blocking collectives  25 us (14%)
  local copies, waits for them, and re-layouts  6.87 us (4%)
    ppermute x6, waiting for transfers between devices, step(): self.behind.append(lax.ppermute(self.behind[-1], self.axis, self.up))  31.5 us
    pallas_call x7, Pallas kernels, run(): pl.pallas_call(kernel, grid_spec=pltpu.PrefetchScalarGridSpec(num_scalar_...  31.4 us
    all_to_all x2, blocking collectives, exchange(): return lax.all_to_all(blocks, axis, 0, 0, tiled=True)  25 us
    all_to_all x3, starting transfers between devices, exchange(): return lax.all_to_all(blocks, axis, 0, 0, tiled=True)  19 us
    ppermute x6, starting transfers between devices, step(): self.ahead.append(lax.ppermute(self.ahead[-1], self.axis, self.down))  16.9 us
    ppermute x2, waiting for transfers between devices, finish(): lax.ppermute(first, self.axis, self.up)  11.7 us
    all_to_all x3, waiting for transfers between devices, exchange(): return lax.all_to_all(blocks, axis, 0, 0, tiled=True)  10.9 us
    ppermute x6, waiting for transfers between devices, step(): self.ahead.append(lax.ppermute(self.ahead[-1], self.axis, self.down))  9.32 us
  transfers between devices with their start and end apart: 19, of which 10 were waited for; matrix products, arithmetic and copies ran while one was open for 1% of the time, Pallas kernels for 10%

profile of v3, /device:TPU:2, one launch (start us, length us, event | category | flops | bytes accessed | tf_op | source)
XLA Modules:
  0.0 178.1 jit_solution(325618119016460553)
XLA Ops:
  5.6 3.4 %shard_map.130.refs_0_.own_ref = bf16[784,384]{1,0:T(8,128)(2,1)S(1)} custom-call(s32[4]{0:T(128)S(1)} %pad_add_fusion.where_ref, s32[3]{0:T(128)S(1)} %copy-done.10, bf16[3,64,5120]{2,1,0:T(8,128)(2,1)} %embed_ref.3, bf16[3,3,640,384]{3,2,1,0:T(8,128)(2,1)} %bitcast.23, f32[5,1,5120]{2,1,0:T(1,128)S(1)} %bitcast.18, bf16[64,256]{1,0:T(8,128)(2,1)S(1)} %bitcast.20, ...), custom_call_target="tpu_custom_call" | custom-call | tf_op jit(solution)/shard_map/pallas_call | solution.py:32
  11.0 4.0 %collective-permute-start.2 = (bf16[784,384]{1,0:T(8,128)(2,1)S(1)}, bf16[784,384]{1,0:T(8,128)(2,1)S(1)}, u32[]{:S(2)}, u32[]{:S(2)}) collective-permute-start(bf16[784,384]{1,0:T(8,128)(2,1)S(1)} %shard_map.130.refs_0_.own_ref), channel_id=1, source_target_pairs={{0,56},{8,0},{16,8},{24,16},{32,24},{40,32},{48,40},{56,48},{1,57}... | collective-permute-start | bytes 1806344 | tf_op jit(solution)/shard_map/ppermute | solution.py:74
  15.0 2.8 %shard_map.132 = bf16[8,144,384]{2,1,0:T(8,128)(2,1)} custom-call(s32[4]{0:T(128)S(1)} %pad_add_fusion.where_ref, bf16[3,640,384]{2,1,0:T(8,128)(2,1)} %weight_ref.1, bf16[32,5120]{1,0:T(8,128)(2,1)S(1)} %copy-done.3), custom_call_target="tpu_custom_call" | custom-call | tf_op jit(solution)/shard_map/pallas_call | solution.py:32
  17.8 5.9 %all-to-all-start = ((bf16[8,144,384]{2,1,0:T(8,128)(2,1)}), bf16[8,144,384]{2,1,0:T(8,128)(2,1)S(1)}, u32[]{:S(2)}, u32[]{:S(2)}) async-start(bf16[8,144,384]{2,1,0:T(8,128)(2,1)} %shard_map.132), calls=%async_computation | async-start | bytes 1769472 | tf_op jit(solution)/shard_map/all_to_all | solution.py:61
  23.7 4.8 %collective-permute-done.refs_1_ = bf16[784,384]{1,0:T(8,128)(2,1)S(1)} collective-permute-done((bf16[784,384]{1,0:T(8,128)(2,1)S(1)}, bf16[784,384]{1,0:T(8,128)(2,1)S(1)}, u32[]{:S(2)}, u32[]{:S(2)}) %collective-permute-start) | collective-permute-done | bytes 602144 | tf_op jit(solution)/shard_map/ppermute | solution.py:73
  28.5 3.2 %collective-permute-start.3 = (bf16[784,384]{1,0:T(8,128)(2,1)S(1)}, bf16[784,384]{1,0:T(8,128)(2,1)}, u32[]{:S(2)}, u32[]{:S(2)}) collective-permute-start(bf16[784,384]{1,0:T(8,128)(2,1)S(1)} %collective-permute-done.2.refs_4_), channel_id=1, source_target_pairs={{0,56},{8,0},{16,8},{24,16},{32,24},{40,32},{48,40},{56,48},{1,57}... | collective-permute-start | bytes 1806344 | tf_op jit(solution)/shard_map/ppermute | solution.py:74
  31.8 4.5 %all-to-all-done.feature_ref = bf16[8,144,384]{2,1,0:T(8,128)(2,1)S(1)} async-done(((bf16[8,144,384]{2,1,0:T(8,128)(2,1)}), bf16[8,144,384]{2,1,0:T(8,128)(2,1)S(1)}, u32[]{:S(2)}, u32[]{:S(2)}) %all-to-all-start) | async-done | bytes 884768 | tf_op jit(solution)/shard_map/all_to_all | solution.py:61
  36.3 8.3 %collective-permute-done.1.refs_2_ = bf16[784,384]{1,0:T(8,128)(2,1)} collective-permute-done((bf16[784,384]{1,0:T(8,128)(2,1)S(1)}, bf16[784,384]{1,0:T(8,128)(2,1)}, u32[]{:S(2)}, u32[]{:S(2)}) %collective-permute-start.1) | collective-permute-done | bytes 602144 | tf_op jit(solution)/shard_map/ppermute | solution.py:73
  44.6 3.2 %collective-permute-start.5 = (bf16[8,80,384]{2,1,0:T(8,128)(2,1)S(1)}, bf16[8,80,384]{2,1,0:T(8,128)(2,1)S(1)}, u32[]{:S(2)}, u32[]{:S(2)}) collective-permute-start(bf16[8,80,384]{2,1,0:T(8,128)(2,1)S(1)} %slice.25.refs_0_), channel_id=1, source_target_pairs={{0,56},{8,0},{16,8},{24,16},{32,24},{40,32},{48,40},{56,48},{1,57}... | collective-permute-start | bytes 1474568 | tf_op jit(solution)/shard_map/ppermute | solution.py:74
  49.9 10.1 %collective-permute-done.4.refs_1_ = bf16[8,80,384]{2,1,0:T(8,128)(2,1)S(1)} collective-permute-done((bf16[8,80,384]{2,1,0:T(8,128)(2,1)S(1)}, bf16[8,80,384]{2,1,0:T(8,128)(2,1)S(1)}, u32[]{:S(2)}, u32[]{:S(2)}) %collective-permute-start.4) | collective-permute-done | bytes 491552 | tf_op jit(solution)/shard_map/ppermute | solution.py:73
  60.0 3.2 %collective-permute-start.11 = (bf16[8,80,384]{2,1,0:T(8,128)(2,1)S(1)}, bf16[8,80,384]{2,1,0:T(8,128)(2,1)}, u32[]{:S(2)}, u32[]{:S(2)}) collective-permute-start(bf16[8,80,384]{2,1,0:T(8,128)(2,1)S(1)} %collective-permute-done.5.refs_4_), channel_id=1, source_target_pairs={{0,56},{8,0},{16,8},{24,16},{32,24},{40,32},{48,40},{56,48},{1,57}... | collective-permute-start | bytes 1474568 | tf_op jit(solution)/shard_map/ppermute | solution.py:74
  63.2 9.3 %collective-permute-done.7.refs_6_ = bf16[784,384]{1,0:T(8,128)(2,1)S(1)} collective-permute-done((bf16[784,384]{1,0:T(8,128)(2,1)}, bf16[784,384]{1,0:T(8,128)(2,1)S(1)}, u32[]{:S(2)}, u32[]{:S(2)}) %collective-permute-start.7) | collective-permute-done | bytes 602144 | tf_op jit(solution)/shard_map/ppermute | solution.py:74
  72.6 3.7 %collective-permute-start.9 = (bf16[400,384]{1,0:T(8,128)(2,1)S(1)}, bf16[400,384]{1,0:T(8,128)(2,1)S(1)}, u32[]{:S(2)}, u32[]{:S(2)}) collective-permute-start(bf16[400,384]{1,0:T(8,128)(2,1)S(1)} %slice.27), channel_id=1, source_target_pairs={{0,56},{8,0},{16,8},{24,16},{32,24},{40,32},{48,40},{56,48},{1,57}... | collective-permute-start | bytes 921608 | tf_op jit(solution)/shard_map/ppermute | solution.py:86
  76.6 10.5 %collective-permute-done.8.refs_7_ = bf16[384,384]{1,0:T(8,128)(2,1)S(1)} collective-permute-done((bf16[384,384]{1,0:T(8,128)(2,1)S(1)}, bf16[384,384]{1,0:T(8,128)(2,1)S(1)}, u32[]{:S(2)}, u32[]{:S(2)}) %collective-permute-start.8) | collective-permute-done | bytes 294944 | tf_op jit(solution)/shard_map/ppermute | solution.py:86
  87.1 13.6 %shard_map.133 = bf16[8,256,384]{2,1,0:T(8,128)(2,1)} custom-call(s32[4]{0:T(128)S(1)} %pad_add_fusion.where_ref, bf16[784,384]{1,0:T(8,128)(2,1)S(1)} %shard_map.130.refs_0_.own_ref, bf16[784,384]{1,0:T(8,128)(2,1)S(1)} %collective-permute-done.refs_1_, bf16[784,384]{1,0:T(8,128)(2,1)} %collective-permute-done.1.refs_2_, bf16[784,384]{1,0:T(8,128)(2,1)} %copy-done.13, ...), custom_call_target="tpu_custom_call" | custom-call | tf_op jit(solution)/shard_map/pallas_call | solution.py:32
  100.7 5.9 %all-to-all-start.1 = ((bf16[8,256,384]{2,1,0:T(8,128)(2,1)}), bf16[8,256,384]{2,1,0:T(8,128)(2,1)}, u32[]{:S(2)}, u32[]{:S(2)}) async-start(bf16[8,256,384]{2,1,0:T(8,128)(2,1)} %shard_map.133), calls=%async_computation.1 | async-start | bytes 3145728 | tf_op jit(solution)/shard_map/all_to_all | solution.py:61
  109.9 8.2 %collective-permute-done.12.refs_3_ = bf16[8,80,384]{2,1,0:T(8,128)(2,1)S(1)} collective-permute-done((bf16[8,80,384]{2,1,0:T(8,128)(2,1)}, bf16[8,80,384]{2,1,0:T(8,128)(2,1)S(1)}, u32[]{:S(2)}, u32[]{:S(2)}) %collective-permute-start.12) | collective-permute-done | bytes 491552 | tf_op jit(solution)/shard_map/ppermute | solution.py:73
  122.3 2.1 %shard_map.131 = (bf16[64,640]{1,0:T(8,128)(2,1)S(1)}, bf16[64,640]{1,0:T(8,128)(2,1)S(1)}, f32[5,1,640]{2,1,0:T(1,128)S(1)}) custom-call(s32[4]{0:T(128)S(1)} %pad_add_fusion.where_ref, bf16[3,64,5120]{2,1,0:T(8,128)(2,1)} %embed_ref.3, bf16[3,64,5120]{2,1,0:T(8,128)(2,1)} %bitcast.24, f32[5,1,5120]{2,1,0:T(1,128)S(1)} %bitcast.19), custom_call_target="tpu_custom_call" | custom-call | tf_op jit(solution)/shard_map/pallas_call | solution.py:32
  126.9 6.0 %shard_map.134 = bf16[32,48,128]{2,1,0:T(8,128)(2,1)} custom-call(s32[4]{0:T(128)S(1)} %pad_add_fusion.where_ref, bf16[784,384]{1,0:T(8,128)(2,1)} %copy-done, bf16[64,640]{1,0:T(8,128)(2,1)S(1)} %get-tuple-element.14.embed_ref, f32[5,1,640]{2,1,0:T(1,128)S(1)} %get-tuple-element.15.shifts_ref, bf16[64,640]{1,0:T(8,128)(2,1)S(1)} %get-tuple-element.16.head_ref, ...), custom_call_target="tpu_custom_call" | custom-call | tf_op jit(solution)/shard_map/pallas_call | solution.py:32
  132.9 7.1 %all-to-all-start.2 = ((bf16[32,48,128]{2,1,0:T(8,128)(2,1)}), bf16[32,48,128]{2,1,0:T(8,128)(2,1)S(1)}, u32[]{:S(2)}, u32[]{:S(2)}) async-start(bf16[32,48,128]{2,1,0:T(8,128)(2,1)} %shard_map.134), calls=%async_computation.2 | async-start | bytes 786432 | tf_op jit(solution)/shard_map/all_to_all | solution.py:61
  142.4 6.4 %all-to-all-done.2.partial_ref = bf16[32,48,128]{2,1,0:T(8,128)(2,1)S(1)} async-done(((bf16[32,48,128]{2,1,0:T(8,128)(2,1)}), bf16[32,48,128]{2,1,0:T(8,128)(2,1)S(1)}, u32[]{:S(2)}, u32[]{:S(2)}) %all-to-all-start.2) | async-done | bytes 393248 | tf_op jit(solution)/shard_map/all_to_all | solution.py:61
  148.8 2.7 %shard_map.135 = (f32[32,64]{1,0:T(8,128)}, f32[32,64]{1,0:T(8,128)}, bf16[8,32,128]{2,1,0:T(8,128)(2,1)S(1)}) custom-call(s32[4]{0:T(128)S(1)} %pad_add_fusion.where_ref, f32[3]{0:T(128)S(1)} %add_divide_fusion.levels_ref, bf16[32,48,128]{2,1,0:T(8,128)(2,1)S(1)} %all-to-all-done.2.partial_ref, bf16[32,64]{1,0:T(8,128)(2,1)S(1)} %copy.23.student_ref, ...), custom_call_target="tpu_custom_call" | custom-call | tf_op jit(solution)/shard_map/pallas_call | solution.py:32
  151.5 9.2 %all_to_all.25.grad_ref = bf16[8,32,128]{2,1,0:T(8,128)(2,1)S(1)} all-to-all(bf16[8,32,128]{2,1,0:T(8,128)(2,1)S(1)} %get-tuple-element.22), channel_id=1, replica_groups=mesh['section'=4,'seq'=8,'fsdp'=8] {'fsdp'}, dimensions={0} | all-to-all | bytes 131072 | tf_op jit(solution)/shard_map/all_to_all | solution.py:61
  161.6 15.9 %all_to_all.26 = f32[8,64,80]{2,1,0:T(8,128)S(1)} all-to-all(f32[8,64,80]{2,1,0:T(8,128)S(1)} %shard_map.136), channel_id=1, replica_groups=mesh['section'=4,'seq'=8,'fsdp'=8] {'seq'}, dimensions={0} | all-to-all | bytes 327680 | tf_op jit(solution)/shard_map/all_to_all | solution.py:61
  (77 shorter events, 22.4 us)
Async XLA Ops:
  9.0 78.1 %copy-start = (bf16[784,384]{1,0:T(8,128)(2,1)}, bf16[784,384]{1,0:T(8,128)(2,1)S(1)}, u32[]{:S(2)}) copy-start(bf16[784,384]{1,0:T(8,128)(2,1)S(1)} %shard_map.130.refs_0_.own_ref) | copy-start | bytes 1806340
  9.0 19.5 %collective-permute-start = (bf16[784,384]{1,0:T(8,128)(2,1)S(1)}, bf16[784,384]{1,0:T(8,128)(2,1)S(1)}, u32[]{:S(2)}, u32[]{:S(2)}) collective-permute-start(bf16[784,384]{1,0:T(8,128)(2,1)S(1)} %shard_map.130.refs_0_.own_ref), channel_id=1, source_target_pairs={{0,8},{8,16},{16,24},{24,32},{32,40},{40,48},{48,56},{56,0},{1,9},... | collective-permute-start | bytes 1806344 | tf_op jit(solution)/shard_map/ppermute | solution.py:73
  11.0 17.5 %collective-permute-start.2 = (bf16[784,384]{1,0:T(8,128)(2,1)S(1)}, bf16[784,384]{1,0:T(8,128)(2,1)S(1)}, u32[]{:S(2)}, u32[]{:S(2)}) collective-permute-start(bf16[784,384]{1,0:T(8,128)(2,1)S(1)} %shard_map.130.refs_0_.own_ref), channel_id=1, source_target_pairs={{0,56},{8,0},{16,8},{24,16},{32,24},{40,32},{48,40},{56,48},{1,57}... | collective-permute-start | bytes 1806344 | tf_op jit(solution)/shard_map/ppermute | solution.py:74
  17.8 18.4 %all-to-all-start = ((bf16[8,144,384]{2,1,0:T(8,128)(2,1)}), bf16[8,144,384]{2,1,0:T(8,128)(2,1)S(1)}, u32[]{:S(2)}, u32[]{:S(2)}) async-start(bf16[8,144,384]{2,1,0:T(8,128)(2,1)} %shard_map.132), calls=%async_computation | async-start | bytes 1769472 | tf_op jit(solution)/shard_map/all_to_all | solution.py:61
  28.5 16.1 %collective-permute-start.1 = (bf16[784,384]{1,0:T(8,128)(2,1)S(1)}, bf16[784,384]{1,0:T(8,128)(2,1)}, u32[]{:S(2)}, u32[]{:S(2)}) collective-permute-start(bf16[784,384]{1,0:T(8,128)(2,1)S(1)} %collective-permute-done.refs_1_), channel_id=1, source_target_pairs={{0,8},{8,16},{16,24},{24,32},{32,40},{40,48},{48,56},{56,0},{1,9},... | collective-permute-start | bytes 1806344 | tf_op jit(solution)/shard_map/ppermute | solution.py:73
  28.5 58.6 %copy-start.16 = (bf16[784,384]{1,0:T(8,128)(2,1)}, bf16[784,384]{1,0:T(8,128)(2,1)S(1)}, u32[]{:S(2)}) copy-start(bf16[784,384]{1,0:T(8,128)(2,1)S(1)} %collective-permute-done.2.refs_4_) | copy-start | bytes 1806340
  28.5 16.1 %collective-permute-start.3 = (bf16[784,384]{1,0:T(8,128)(2,1)S(1)}, bf16[784,384]{1,0:T(8,128)(2,1)}, u32[]{:S(2)}, u32[]{:S(2)}) collective-permute-start(bf16[784,384]{1,0:T(8,128)(2,1)S(1)} %collective-permute-done.2.refs_4_), channel_id=1, source_target_pairs={{0,56},{8,0},{16,8},{24,16},{32,24},{40,32},{48,40},{56,48},{1,57}... | collective-permute-start | bytes 1806344 | tf_op jit(solution)/shard_map/ppermute | solution.py:74
  44.6 15.4 %collective-permute-start.4 = (bf16[8,80,384]{2,1,0:T(8,128)(2,1)S(1)}, bf16[8,80,384]{2,1,0:T(8,128)(2,1)S(1)}, u32[]{:S(2)}, u32[]{:S(2)}) collective-permute-start(bf16[8,80,384]{2,1,0:T(8,128)(2,1)S(1)} %slice.25.refs_0_), channel_id=1, source_target_pairs={{0,8},{8,16},{16,24},{24,32},{32,40},{40,48},{48,56},{56,0},{1,9},... | collective-permute-start | bytes 1474568 | tf_op jit(solution)/shard_map/ppermute | solution.py:73
  44.6 15.4 %collective-permute-start.5 = (bf16[8,80,384]{2,1,0:T(8,128)(2,1)S(1)}, bf16[8,80,384]{2,1,0:T(8,128)(2,1)S(1)}, u32[]{:S(2)}, u32[]{:S(2)}) collective-permute-start(bf16[8,80,384]{2,1,0:T(8,128)(2,1)S(1)} %slice.25.refs_0_), channel_id=1, source_target_pairs={{0,56},{8,0},{16,8},{24,16},{32,24},{40,32},{48,40},{56,48},{1,57}... | collective-permute-start | bytes 1474568 | tf_op jit(solution)/shard_map/ppermute | solution.py:74
  47.9 24.7 %collective-permute-start.7 = (bf16[784,384]{1,0:T(8,128)(2,1)}, bf16[784,384]{1,0:T(8,128)(2,1)S(1)}, u32[]{:S(2)}, u32[]{:S(2)}) collective-permute-start(bf16[784,384]{1,0:T(8,128)(2,1)} %collective-permute-done.3.refs_5_), channel_id=1, source_target_pairs={{0,56},{8,0},{16,8},{24,16},{32,24},{40,32},{48,40},{56,48},{1,57}... | collective-permute-start | bytes 1806344 | tf_op jit(solution)/shard_map/ppermute | solution.py:74
  49.6 26.6 %collective-permute-start.6 = (bf16[784,384]{1,0:T(8,128)(2,1)}, bf16[784,384]{1,0:T(8,128)(2,1)S(1)}, u32[]{:S(2)}, u32[]{:S(2)}) collective-permute-start(bf16[784,384]{1,0:T(8,128)(2,1)} %collective-permute-done.1.refs_2_), channel_id=1, source_target_pairs={{0,8},{8,16},{16,24},{24,32},{32,40},{40,48},{48,56},{56,0},{1,9},... | collective-permute-start | bytes 1806344 | tf_op jit(solution)/shard_map/ppermute | solution.py:73
  60.0 40.7 %copy-start.17 = (bf16[8,80,384]{2,1,0:T(8,128)(2,1)}, bf16[8,80,384]{2,1,0:T(8,128)(2,1)S(1)}, u32[]{:S(2)}) copy-start(bf16[8,80,384]{2,1,0:T(8,128)(2,1)S(1)} %collective-permute-done.4.refs_1_) | copy-start | bytes 1474564
  60.0 40.7 %collective-permute-start.10 = (bf16[8,80,384]{2,1,0:T(8,128)(2,1)S(1)}, bf16[8,80,384]{2,1,0:T(8,128)(2,1)}, u32[]{:S(2)}, u32[]{:S(2)}) collective-permute-start(bf16[8,80,384]{2,1,0:T(8,128)(2,1)S(1)} %collective-permute-done.4.refs_1_), channel_id=1, source_target_pairs={{0,8},{8,16},{16,24},{24,32},{32,40},{40,48},{48,56},{56,0},{1,9},... | collective-permute-start | bytes 1474568 | tf_op jit(solution)/shard_map/ppermute | solution.py:73
  60.0 40.7 %copy-start.18 = (bf16[8,80,384]{2,1,0:T(8,128)(2,1)}, bf16[8,80,384]{2,1,0:T(8,128)(2,1)S(1)}, u32[]{:S(2)}) copy-start(bf16[8,80,384]{2,1,0:T(8,128)(2,1)S(1)} %collective-permute-done.5.refs_4_) | copy-start | bytes 1474564
  60.0 40.7 %collective-permute-start.11 = (bf16[8,80,384]{2,1,0:T(8,128)(2,1)S(1)}, bf16[8,80,384]{2,1,0:T(8,128)(2,1)}, u32[]{:S(2)}, u32[]{:S(2)}) collective-permute-start(bf16[8,80,384]{2,1,0:T(8,128)(2,1)S(1)} %collective-permute-done.5.refs_4_), channel_id=1, source_target_pairs={{0,56},{8,0},{16,8},{24,16},{32,24},{40,32},{48,40},{56,48},{1,57}... | collective-permute-start | bytes 1474568 | tf_op jit(solution)/shard_map/ppermute | solution.py:74
  72.6 14.5 %collective-permute-start.9 = (bf16[400,384]{1,0:T(8,128)(2,1)S(1)}, bf16[400,384]{1,0:T(8,128)(2,1)S(1)}, u32[]{:S(2)}, u32[]{:S(2)}) collective-permute-start(bf16[400,384]{1,0:T(8,128)(2,1)S(1)} %slice.27), channel_id=1, source_target_pairs={{0,56},{8,0},{16,8},{24,16},{32,24},{40,32},{48,40},{56,48},{1,57}... | collective-permute-start | bytes 921608 | tf_op jit(solution)/shard_map/ppermute | solution.py:86
  76.3 10.8 %collective-permute-start.8 = (bf16[384,384]{1,0:T(8,128)(2,1)S(1)}, bf16[384,384]{1,0:T(8,128)(2,1)S(1)}, u32[]{:S(2)}, u32[]{:S(2)}) collective-permute-start(bf16[384,384]{1,0:T(8,128)(2,1)S(1)} %slice.26), channel_id=1, source_target_pairs={{0,8},{8,16},{16,24},{24,32},{32,40},{40,48},{48,56},{56,0},{1,9},... | collective-permute-start | bytes 884744 | tf_op jit(solution)/shard_map/ppermute | solution.py:86
  100.7 21.6 %copy-start.2 = (f32[1,5,5120]{2,0,1:T(1,128)S(1)}, f32[1,5,5120]{2,0,1:T(1,128)}, u32[]{:S(2)}) copy-start(f32[1,5,5120]{2,0,1:T(1,128)} %param.15) | copy-start | bytes 307204
  100.7 26.2 %all-to-all-start.1 = ((bf16[8,256,384]{2,1,0:T(8,128)(2,1)}), bf16[8,256,384]{2,1,0:T(8,128)(2,1)}, u32[]{:S(2)}, u32[]{:S(2)}) async-start(bf16[8,256,384]{2,1,0:T(8,128)(2,1)} %shard_map.133), calls=%async_computation.1 | async-start | bytes 3145728 | tf_op jit(solution)/shard_map/all_to_all | solution.py:61
  106.7 11.4 %collective-permute-start.12 = (bf16[8,80,384]{2,1,0:T(8,128)(2,1)}, bf16[8,80,384]{2,1,0:T(8,128)(2,1)S(1)}, u32[]{:S(2)}, u32[]{:S(2)}) collective-permute-start(bf16[8,80,384]{2,1,0:T(8,128)(2,1)} %collective-permute-done.10.refs_2_), channel_id=1, source_target_pairs={{0,8},{8,16},{16,24},{24,32},{32,40},{40,48},{48,56},{56,0},{1,9},... | collective-permute-start | bytes 1474568 | tf_op jit(solution)/shard_map/ppermute | solution.py:73
  108.5 10.8 %collective-permute-start.13 = (bf16[8,80,384]{2,1,0:T(8,128)(2,1)}, bf16[8,80,384]{2,1,0:T(8,128)(2,1)S(1)}, u32[]{:S(2)}, u32[]{:S(2)}) collective-permute-start(bf16[8,80,384]{2,1,0:T(8,128)(2,1)} %collective-permute-done.11.refs_5_), channel_id=1, source_target_pairs={{0,56},{8,0},{16,8},{24,16},{32,24},{40,32},{48,40},{56,48},{1,57}... | collective-permute-start | bytes 1474568 | tf_op jit(solution)/shard_map/ppermute | solution.py:74
  118.1 7.5 %collective-permute-start.14 = (bf16[4,80,384]{2,1,0:T(8,128)(2,1)S(1)}, bf16[4,80,384]{2,1,0:T(8,128)(2,1)S(1)}, u32[]{:S(2)}, u32[]{:S(2)}) collective-permute-start(bf16[4,80,384]{2,1,0:T(8,128)(2,1)S(1)} %slice.28), channel_id=1, source_target_pairs={{0,8},{8,16},{16,24},{24,32},{32,40},{40,48},{48,56},{56,0},{1,9},... | collective-permute-start | bytes 737288 | tf_op jit(solution)/shard_map/ppermute | solution.py:86
  120.1 6.8 %collective-permute-start.15 = (bf16[4,80,384]{2,1,0:T(8,128)(2,1)}, bf16[4,80,384]{2,1,0:T(8,128)(2,1)S(1)}, u32[]{:S(2)}, u32[]{:S(2)}) collective-permute-start(bf16[4,80,384]{2,1,0:T(8,128)(2,1)} %slice.29), channel_id=1, source_target_pairs={{0,56},{8,0},{16,8},{24,16},{32,24},{40,32},{48,40},{56,48},{1,57}... | collective-permute-start | bytes 737288 | tf_op jit(solution)/shard_map/ppermute | solution.py:86
  132.9 15.9 %all-to-all-start.2 = ((bf16[32,48,128]{2,1,0:T(8,128)(2,1)}), bf16[32,48,128]{2,1,0:T(8,128)(2,1)S(1)}, u32[]{:S(2)}, u32[]{:S(2)}) async-start(bf16[32,48,128]{2,1,0:T(8,128)(2,1)} %shard_map.134), calls=%async_computation.2 | async-start | bytes 786432 | tf_op jit(solution)/shard_map/all_to_all | solution.py:61
  (14 other events, 92.5 us)

commit v4 on v3

--- a/solution.py
+++ b/solution.py
@@ -14,7 +14,7 @@
 f32 = jnp.float32
 
 
-def run(kernel, where, outs, *operands, picked=(), scratch=(), raw=False):
+def run(kernel, where, outs, *operands, picked=(), scratch=(), raw=(), cost=None):
     def spec(shape, pick=False):
         zeros = (0,) * (len(shape) - 1)
         if pick:
@@ -24,8 +24,8 @@
     in_specs = [
         pl.BlockSpec(memory_space=pltpu.SMEM)
         if x.ndim == 1
-        else pl.BlockSpec(memory_space=pl.ANY)
-        if raw
+        else pl.BlockSpec(memory_space=pltpu.HBM)
+        if n in raw
         else spec(x.shape, n in picked)
         for n, x in enumerate(operands)
     ]
@@ -40,6 +40,7 @@
         ),
         out_shape=tuple(jax.ShapeDtypeStruct(shape, dtype) for shape, dtype in outs),
         compiler_params=pltpu.CompilerParams(vmem_limit_bytes=52 * 1024 * 1024),
+        cost_estimate=cost,
     )(where, *operands)
     return result[0] if len(outs) == 1 else result
 
@@ -94,13 +95,20 @@
 
 
 def prepare_kernel(
-    where_ref, steps_ref, embed_ref, weight_ref, shifts_ref, student_ref, previous_ref, noise_ref, context_ref, out_ref
+    where_ref, embed_ref, weight_ref, shifts_hbm, student_hbm, previous_hbm, noise_hbm, context_hbm, *refs
 ):
+    first_ref, second_ref, shifts_ref, student_ref, previous_ref, noise_ref, out_ref, sems = refs
     latent_dim, width = embed_ref.shape[1:]
     parts, depth, feat = weight_ref.shape[1:]
     rows = student_ref.shape[1]
-    out_ref[: 2 * rows] = context_ref[...].reshape(2 * rows, feat)
-    level = noise_levels(jnp.full((1, rows), steps_ref[1], jnp.int32))
+    sources = (shifts_hbm, student_hbm, previous_hbm, noise_hbm, context_hbm)
+    targets = (shifts_ref, student_ref, previous_ref, noise_ref, out_ref.at[pl.ds(0, 2 * rows)])
+    copies = [pltpu.make_async_copy(a, b, sems.at[n]) for n, (a, b) in enumerate(zip(sources, targets))]
+    for copy in copies:
+        copy.start()
+    for copy in copies:
+        copy.wait()
+    level = noise_levels(jnp.full((1, rows), where_ref[5], jnp.int32))
     noised = (1.0 - level) * previous_ref[...].astype(f32) + level * noise_ref[...].astype(f32)
     latents = jnp.where(where_ref[3] == 0, student_ref[...].astype(f32), noised.astype(bf16).astype(f32))
 
@@ -138,6 +146,9 @@
     out_ref[tail + latent_dim :, :rows] = scales.astype(bf16)
     spare = jnp.zeros((latent_dim + 16 - len(lines), 128), f32)
     out_ref[tail:, rows:] = jnp.concatenate(lines + [spare], axis=0).astype(bf16)
+    cut = first_ref.shape[0]
+    first_ref[...] = out_ref[:cut]
+    second_ref[...] = out_ref[cut:]
 
 
 def aside_kernel(where_ref, weight_ref, feature_ref, out_ref):
@@ -189,21 +200,27 @@
     return tuple(new)
 
 
-def attention_kernel(heads, latent_dim, where_ref, *refs):
+def attention_kernel(heads, latent_dim, group_start, where_ref, *refs):
     n_blocks = len(refs) - 4
     block_refs, (out_ref, all_ref, held_ref, sems) = refs[:n_blocks], refs[n_blocks:]
     count, lines, feat = all_ref.shape
     rows = out_ref.shape[1]
+    half = n_blocks // 2
     copies = []
-    for n, ref in enumerate(block_refs):
-        if n < count:
-            target = all_ref.at[n, pl.ds(0, ref.shape[0])]
-        else:
-            target = all_ref.at[count - 1, pl.ds(lines - ref.shape[0], ref.shape[0])]
-        copies.append(pltpu.make_async_copy(ref, target, sems.at[n]))
-    for copy in copies:
+    for start, group in ((0, block_refs[:half]), (group_start, block_refs[half:])):
+        at = [(n, start) for n in range(count)] + [(count - 1, start + group[count - 1].shape[0])]
+        copies.append(
+            [
+                pltpu.make_async_copy(
+                    ref, all_ref.at[n, pl.ds(place, ref.shape[0])], sems.at[(half if start else 0) + i]
+                )
+                for i, ((n, place), ref) in enumerate(zip(at, group))
+            ]
+        )
+    early, late = copies[1], copies[0]
+    for copy in early + late:
         copy.start()
-    for copy in copies:
+    for copy in early:
         copy.wait()
 
     tail = 2 * rows + 3 * latent_dim
@@ -241,8 +258,10 @@
 
         return fold_keys(heads, carry, queries, lambda h: both(0, h), lambda h: both(rows, h))
 
-    carry = lax.fori_loop(0, count // 2, lambda i, c: pair(held_ref, i, c), carry)
-    carry = lax.fori_loop(0, count // 2, lambda i, c: pair(all_ref, i, c), carry)
+    carry = lax.fori_loop(0, count // 2, lambda i, c: pair(held_ref, i, c), carry, unroll=2)
+    for copy in late:
+        copy.wait()
+    carry = lax.fori_loop(0, count // 2, lambda i, c: pair(all_ref, i, c), carry, unroll=2)
     for h in range(heads):
         _, total, weighted = carry[h]
         attended = (weighted / total).T.astype(bf16)
@@ -261,9 +280,12 @@
     n_fsdp, rows = att_ref.shape[:2]
     latent_dim = embed_ref.shape[0]
     mixed = None
+    middle = len(weight_refs) // 2
     for f in range(n_fsdp):
-        whole = [ref[f] for ref in weight_refs[:-2]]
-        whole.append(weight_refs[-2][f] if f < n_fsdp // 2 else weight_refs[-1][f - n_fsdp // 2])
+        group = weight_refs[:middle] if f < n_fsdp // 2 else weight_refs[middle:]
+        g = f % (n_fsdp // 2)
+        whole = [ref[g] for ref in group[:-2]]
+        whole.append(group[-2][g] if g < n_fsdp // 4 else group[-1][g - n_fsdp // 4])
         part = dot(att_ref[f], jnp.concatenate(whole, axis=0), ((1,), (1,)))
         mixed = part if mixed is None else mixed + part
     latents = own_ref[own_ref.shape[0] - latent_dim - 16 : own_ref.shape[0] - 16, :rows]
@@ -357,7 +379,7 @@
     section, me_seq, me_fsdp = (lax.axis_index(a) for a in ("section", "seq", "fsdp"))
     sections, n_seq, n_fsdp = (lax.axis_size(a) for a in ("section", "seq", "fsdp"))
     model_index = section - (section >= 2).astype(jnp.int32)
-    where = jnp.stack([model_index, me_seq, me_fsdp, section]).astype(jnp.int32)
+    where = jnp.concatenate([jnp.stack([model_index, me_seq, me_fsdp, section]).astype(jnp.int32), timesteps])
     levels = noise_levels(timesteps)
     rows, latent_dim = student_input.shape
     width = in_weight.shape[2]
@@ -369,45 +391,61 @@
 
     cut = run(aside_kernel, where, [((n_fsdp, slot + 2 * piece, feat), bf16)], out_weight, saved_features, picked=(0,))
     lines = 2 * rows + 3 * latent_dim + latent_dim + 16
-    own = run(
+    first = lines // 32 * 16
+    own, second = run(
         prepare_kernel,
         where,
-        [((lines, feat), bf16)],
-        timesteps,
+        [((first, feat), bf16), ((lines - first, feat), bf16)],
         in_weight,
         qkv_weight.transpose(0, 2, 1, 3),
         shifts,
         student_input.T,
         previous_latent.T,
         score_noise.T,
-        kv_cache[0].transpose(1, 0, 2),
-        picked=(1, 2),
+        kv_cache[0].transpose(1, 0, 2).reshape(2 * rows, feat),
+        picked=(0, 1),
+        raw=(2, 3, 4, 5, 6),
+        scratch=[
+            pltpu.VMEM(shifts.shape, f32),
+            pltpu.VMEM((latent_dim, rows), bf16),
+            pltpu.VMEM((latent_dim, rows), bf16),
+            pltpu.VMEM((latent_dim, rows), bf16),
+            pltpu.VMEM((lines, feat), bf16),
+            pltpu.SemaphoreType.DMA((5,)),
+        ],
     )
     aside = exchange(cut, "fsdp")
-    around = Ring(own, "seq", n_seq, 0, lines // 32 * 16)
-    around.step()
-    around.step()
-    block, *_ = lax.optimization_barrier((aside[:, :slot],) + around.ends())
-    weights = Ring(block, "seq", n_seq, 0)
-    weights.step()
-    around.finish()
-    blocks = around.blocks()
+    around = [Ring(x, "seq", n_seq, 0, x.shape[0] // 32 * 16) for x in (own, second)]
+    for _ in range(n_seq // 2 - 1):
+        for r in around:
+            r.step()
+    ends = around[0].ends() + around[1].ends()
+    block, *_ = lax.optimization_barrier((aside[:, :slot],) + ends)
+    weights = [Ring(block[i : i + n_fsdp // 2], "seq", n_seq, 0) for i in (0, n_fsdp // 2)]
+    for r in around:
+        r.finish()
+    for r in weights:
+        r.step()
+    blocks = around[0].blocks() + around[1].blocks()
     attended = run(
-        functools.partial(attention_kernel, heads, latent_dim),
-        together(where, *weights.ends()),
+        functools.partial(attention_kernel, heads, latent_dim, first),
+        where,
         [((n_fsdp, rows, feat), bf16)],
         *blocks,
         scratch=[
             pltpu.VMEM((n_seq, lines, feat), bf16),
             pltpu.VMEM((n_seq, 2 * rows, feat), bf16),
-            pltpu.SemaphoreType.DMA((n_seq + 1,)),
+            pltpu.SemaphoreType.DMA((len(blocks),)),
         ],
-        raw=True,
-    )
-    weights.step()
-    attended = exchange(together(attended, *weights.ends()), "fsdp")
-    weights.step()
-    weights.finish()
+        raw=range(len(blocks)),
+        cost=pl.CostEstimate(flops=11 * 10**9, bytes_accessed=20 * 10**6, transcendentals=3 * 10**6),
+    )
+    attended = exchange(together(attended, *weights[0].ends(), *weights[1].ends()), "fsdp")
+    for _ in range(n_seq // 2 - 2):
+        for r in weights:
+            r.step()
+    for r in weights:
+        r.finish()
     embed_here, head_here, shifts_here = run(
         columns_kernel,
         together(where, own),
@@ -421,12 +459,13 @@
         functools.partial(head_kernel, sections),
         where,
         [((sections * n_fsdp, piece + 16, 128), bf16)],
-        own,
+        second,
         embed_here,
         shifts_here,
         head_here,
         attended,
-        *weights.blocks(),
+        *weights[0].blocks(),
+        *weights[1].blocks(),
     )
     partials = exchange(partials, ("section", "fsdp"))
 

time: 179 us -> 172 us (0.961)
  waiting for transfers between devices: 64.6 us -> 36.2 us
  starting transfers between devices: 47.2 us -> 68.5 us
    ppermute x6 -> x12, starting transfers between devices: 16.9 us -> 34.4 us  [step(): self.ahead.append(lax.ppermute(self.ahead[-1], self.axis, self.down))]
    ppermute x6 -> x12, waiting for transfers between devices: 31.5 us -> 22.4 us  [step(): self.behind.append(lax.ppermute(self.behind[-1], self.axis, self.up))]
    ppermute x6 -> x12, waiting for transfers between devices: 9.32 us -> 1.81 us  [step(): self.ahead.append(lax.ppermute(self.ahead[-1], self.axis, self.down))]
    ppermute x2 -> x4, waiting for transfers between devices: 11.7 us -> 4.88 us  [finish(): lax.ppermute(first, self.axis, self.up)]
    ppermute x2 -> x4, starting transfers between devices: 5.78 us -> 10.2 us  [finish(): lax.ppermute(second, self.axis, self.down)]
    all_to_all x3, waiting for transfers between devices: 10.9 us -> 6.42 us  [exchange(): return lax.all_to_all(blocks, axis, 0, 0, tiled=True)]
    unnamed x42 -> x43, local copies, waits for them, and re-layouts: 5.16 us -> 3.48 us
    ppermute x6 -> x12, starting transfers between devices: 4.09 us -> 2.48 us  [step(): self.behind.append(lax.ppermute(self.behind[-1], self.axis, self.up))]
  transfers between devices with their start and end apart: 19 -> 35, of which waited for: 10 -> 12; matrix products, arithmetic and copies ran while one was open for 1% -> 2% of each run, Pallas kernels for 10% -> 10%
where the time goes in v4:
time: 172 us; the launch traced here: 171 us
  starting transfers between devices  68.5 us (40%)
  waiting for transfers between devices  36.2 us (21%)
  Pallas kernels  30.5 us (18%)
  blocking collectives  24.7 us (14%)
  local copies, waits for them, and re-layouts  8.07 us (5%)
    ppermute x12, starting transfers between devices, step(): self.ahead.append(lax.ppermute(self.ahead[-1], self.axis, self.down))  34.4 us
    pallas_call x7, Pallas kernels, run(): pl.pallas_call(kernel, grid_spec=pltpu.PrefetchScalarGridSpec(num_scalar_...  30.5 us
    all_to_all x2, blocking collectives, exchange(): return lax.all_to_all(blocks, axis, 0, 0, tiled=True)  24.7 us
    ppermute x12, waiting for transfers between devices, step(): self.behind.append(lax.ppermute(self.behind[-1], self.axis, self.up))  22.4 us
    all_to_all x3, starting transfers between devices, exchange(): return lax.all_to_all(blocks, axis, 0, 0, tiled=True)  19 us
    ppermute x4, starting transfers between devices, finish(): lax.ppermute(second, self.axis, self.down)  10.2 us
    all_to_all x3, waiting for transfers between devices, exchange(): return lax.all_to_all(blocks, axis, 0, 0, tiled=True)  6.42 us
    ppermute x4, waiting for transfers between devices, finish(): lax.ppermute(first, self.axis, self.up)  4.88 us
  transfers between devices with their start and end apart: 35, of which 12 were waited for; matrix products, arithmetic and copies ran while one was open for 2% of the time, Pallas kernels for 10%

profile of v4, /device:TPU:2, one launch (start us, length us, event | category | flops | bytes accessed | tf_op | source)
XLA Modules:
  0.0 171.0 jit_solution(8761500499550327744)
XLA Ops:
  5.6 3.9 %shard_map.130 = (bf16[384,384]{1,0:T(8,128)(2,1)S(1)}, bf16[400,384]{1,0:T(8,128)(2,1)S(1)}) custom-call(s32[7]{0:T(128)S(1)} %concatenate.3.where_ref, bf16[3,64,5120]{2,1,0:T(8,128)(2,1)} %embed_ref.3, bf16[3,3,640,384]{3,2,1,0:T(8,128)(2,1)} %bitcast.22, f32[5,1,5120]{2,1,0:T(1,128)S(1)} %bitcast.17, bf16[64,256]{1,0:T(8,128)(2,1)S(1)} %bitcast.19, ...), custom_call_target="tpu_custom_call" | custom-call | tf_op jit(solution)/shard_map/pallas_call | solution.py:32
  9.5 5.9 %collective-permute-start.11 = (bf16[400,384]{1,0:T(8,128)(2,1)S(1)}, bf16[400,384]{1,0:T(8,128)(2,1)S(1)}, u32[]{:S(2)}, u32[]{:S(2)}) collective-permute-start(bf16[400,384]{1,0:T(8,128)(2,1)S(1)} %get-tuple-element.14.refs_9_.own_ref), channel_id=1, source_target_pairs={{0,56},{8,0},{16,8},{24,16},{32,24},{40,32},{48,40},{56,48},{1,57}... | collective-permute-start | bytes 921608 | tf_op jit(solution)/shard_map/ppermute | solution.py:75
  15.4 3.3 %collective-permute-start.3 = (bf16[384,384]{1,0:T(8,128)(2,1)S(1)}, bf16[384,384]{1,0:T(8,128)(2,1)}, u32[]{:S(2)}, u32[]{:S(2)}) collective-permute-start(bf16[384,384]{1,0:T(8,128)(2,1)S(1)} %get-tuple-element.15.refs_0_), channel_id=1, source_target_pairs={{0,56},{8,0},{16,8},{24,16},{32,24},{40,32},{48,40},{56,48},{1,57}... | collective-permute-start | bytes 884744 | tf_op jit(solution)/shard_map/ppermute | solution.py:75
  18.7 2.8 %shard_map.133 = bf16[8,144,384]{2,1,0:T(8,128)(2,1)} custom-call(s32[7]{0:T(128)S(1)} %concatenate.3.where_ref, bf16[3,640,384]{2,1,0:T(8,128)(2,1)} %weight_ref.1, bf16[32,5120]{1,0:T(8,128)(2,1)S(1)} %copy-done.2), custom_call_target="tpu_custom_call" | custom-call | tf_op jit(solution)/shard_map/pallas_call | solution.py:32
  21.5 5.9 %all-to-all-start = ((bf16[8,144,384]{2,1,0:T(8,128)(2,1)}), bf16[8,144,384]{2,1,0:T(8,128)(2,1)S(1)}, u32[]{:S(2)}, u32[]{:S(2)}) async-start(bf16[8,144,384]{2,1,0:T(8,128)(2,1)} %shard_map.133), calls=%async_computation | async-start | bytes 1769472 | tf_op jit(solution)/shard_map/all_to_all | solution.py:62
  32.1 3.2 %collective-permute-start.4 = (bf16[384,384]{1,0:T(8,128)(2,1)}, bf16[384,384]{1,0:T(8,128)(2,1)}, u32[]{:S(2)}, u32[]{:S(2)}) collective-permute-start(bf16[384,384]{1,0:T(8,128)(2,1)} %collective-permute-done.3.refs_4_), channel_id=1, source_target_pairs={{0,56},{8,0},{16,8},{24,16},{32,24},{40,32},{48,40},{56,48},{1,57}... | collective-permute-start | bytes 884744 | tf_op jit(solution)/shard_map/ppermute | solution.py:75
  37.1 2.7 %collective-permute-start.13 = (bf16[400,384]{1,0:T(8,128)(2,1)}, bf16[400,384]{1,0:T(8,128)(2,1)S(1)}, u32[]{:S(2)}, u32[]{:S(2)}) collective-permute-start(bf16[400,384]{1,0:T(8,128)(2,1)} %collective-permute-done.12.refs_14_), channel_id=1, source_target_pairs={{0,56},{8,0},{16,8},{24,16},{32,24},{40,32},{48,40},{56,48},{1,57}... | collective-permute-start | bytes 921608 | tf_op jit(solution)/shard_map/ppermute | solution.py:75
  41.0 6.2 %collective-permute-done.1.refs_2_ = bf16[384,384]{1,0:T(8,128)(2,1)S(1)} collective-permute-done((bf16[384,384]{1,0:T(8,128)(2,1)S(1)}, bf16[384,384]{1,0:T(8,128)(2,1)S(1)}, u32[]{:S(2)}, u32[]{:S(2)}) %collective-permute-start.1) | collective-permute-done | bytes 294944 | tf_op jit(solution)/shard_map/ppermute | solution.py:74
  47.3 3.2 %collective-permute-start.5 = (bf16[384,384]{1,0:T(8,128)(2,1)}, bf16[384,384]{1,0:T(8,128)(2,1)S(1)}, u32[]{:S(2)}, u32[]{:S(2)}) collective-permute-start(bf16[384,384]{1,0:T(8,128)(2,1)} %collective-permute-done.4.refs_5_), channel_id=1, source_target_pairs={{0,56},{8,0},{16,8},{24,16},{32,24},{40,32},{48,40},{56,48},{1,57}... | collective-permute-start | bytes 884744 | tf_op jit(solution)/shard_map/ppermute | solution.py:75
  50.6 6.9 %collective-permute-done.2.refs_3_ = bf16[384,384]{1,0:T(8,128)(2,1)S(1)} collective-permute-done((bf16[384,384]{1,0:T(8,128)(2,1)S(1)}, bf16[384,384]{1,0:T(8,128)(2,1)S(1)}, u32[]{:S(2)}, u32[]{:S(2)}) %collective-permute-start.2) | collective-permute-done | bytes 294944 | tf_op jit(solution)/shard_map/ppermute | solution.py:74
  57.7 3.5 %collective-permute-start.7 = (bf16[192,384]{1,0:T(8,128)(2,1)S(1)}, bf16[192,384]{1,0:T(8,128)(2,1)S(1)}, u32[]{:S(2)}, u32[]{:S(2)}) collective-permute-start(bf16[192,384]{1,0:T(8,128)(2,1)S(1)} %slice.50), channel_id=1, source_target_pairs={{0,56},{8,0},{16,8},{24,16},{32,24},{40,32},{48,40},{56,48},{1,57}... | collective-permute-start | bytes 442376 | tf_op jit(solution)/shard_map/ppermute | solution.py:87
  70.9 12.3 %shard_map.132 = bf16[8,256,384]{2,1,0:T(8,128)(2,1)} custom-call(s32[7]{0:T(128)S(1)} %concatenate.3.where_ref, bf16[384,384]{1,0:T(8,128)(2,1)S(1)} %get-tuple-element.15.refs_0_, bf16[384,384]{1,0:T(8,128)(2,1)S(1)} %collective-permute-done.refs_1_, bf16[384,384]{1,0:T(8,128)(2,1)S(1)} %collective-permute-done.1.refs_2_, ...), custom_call_target="tpu_custom_call" | custom-call | flops 11000000512 | bytes 20000000 | tf_op jit(solution)/shard_map/pallas_call | solution.py:32
  83.3 5.9 %all-to-all-start.1 = ((bf16[8,256,384]{2,1,0:T(8,128)(2,1)}), bf16[8,256,384]{2,1,0:T(8,128)(2,1)}, u32[]{:S(2)}, u32[]{:S(2)}) async-start(bf16[8,256,384]{2,1,0:T(8,128)(2,1)} %shard_map.132), calls=%async_computation.1 | async-start | bytes 3145728 | tf_op jit(solution)/shard_map/all_to_all | solution.py:62
  92.7 3.0 %collective-permute-start.28 = (bf16[4,80,384]{2,1,0:T(8,128)(2,1)}, bf16[4,80,384]{2,1,0:T(8,128)(2,1)}, u32[]{:S(2)}, u32[]{:S(2)}) collective-permute-start(bf16[4,80,384]{2,1,0:T(8,128)(2,1)} %collective-permute-done.19.refs_13_), channel_id=1, source_target_pairs={{0,56},{8,0},{16,8},{24,16},{32,24},{40,32},{48,40},{56,48},{1,57}... | collective-permute-start | bytes 737288 | tf_op jit(solution)/shard_map/ppermute | solution.py:75
  95.7 3.4 %collective-permute-done.20.refs_2_ = bf16[4,80,384]{2,1,0:T(8,128)(2,1)S(1)} collective-permute-done((bf16[4,80,384]{2,1,0:T(8,128)(2,1)S(1)}, bf16[4,80,384]{2,1,0:T(8,128)(2,1)S(1)}, u32[]{:S(2)}, u32[]{:S(2)}) %collective-permute-start.20) | collective-permute-done | bytes 245792 | tf_op jit(solution)/shard_map/ppermute | solution.py:74
  99.5 2.9 %collective-permute-start.23 = (bf16[4,80,384]{2,1,0:T(8,128)(2,1)S(1)}, bf16[4,80,384]{2,1,0:T(8,128)(2,1)S(1)}, u32[]{:S(2)}, u32[]{:S(2)}) collective-permute-start(bf16[4,80,384]{2,1,0:T(8,128)(2,1)S(1)} %collective-permute-done.22.refs_5_), channel_id=1, source_target_pairs={{0,56},{8,0},{16,8},{24,16},{32,24},{40,32},{48,40},{56,48},{1,57}... | collective-permute-start | bytes 737288 | tf_op jit(solution)/shard_map/ppermute | solution.py:75
  104.9 2.9 %collective-permute-start.29 = (bf16[4,80,384]{2,1,0:T(8,128)(2,1)}, bf16[4,80,384]{2,1,0:T(8,128)(2,1)}, u32[]{:S(2)}, u32[]{:S(2)}) collective-permute-start(bf16[4,80,384]{2,1,0:T(8,128)(2,1)} %collective-permute-done.28.refs_14_), channel_id=1, source_target_pairs={{0,56},{8,0},{16,8},{24,16},{32,24},{40,32},{48,40},{56,48},{1,57}... | collective-permute-start | bytes 737288 | tf_op jit(solution)/shard_map/ppermute | solution.py:75
  110.1 3.3 %collective-permute-start.25 = (bf16[2,80,384]{2,1,0:T(8,128)(2,1)S(1)}, bf16[2,80,384]{2,1,0:T(8,128)(2,1)S(1)}, u32[]{:S(2)}, u32[]{:S(2)}) collective-permute-start(bf16[2,80,384]{2,1,0:T(8,128)(2,1)S(1)} %slice.55), channel_id=1, source_target_pairs={{0,56},{8,0},{16,8},{24,16},{32,24},{40,32},{48,40},{56,48},{1,57}... | collective-permute-start | bytes 368648 | tf_op jit(solution)/shard_map/ppermute | solution.py:87
  114.4 3.4 %collective-permute-start.31 = (bf16[2,80,384]{2,1,0:T(8,128)(2,1)S(1)}, bf16[2,80,384]{2,1,0:T(8,128)(2,1)S(1)}, u32[]{:S(2)}, u32[]{:S(2)}) collective-permute-start(bf16[2,80,384]{2,1,0:T(8,128)(2,1)S(1)} %slice.57), channel_id=1, source_target_pairs={{0,56},{8,0},{16,8},{24,16},{32,24},{40,32},{48,40},{56,48},{1,57}... | collective-permute-start | bytes 368648 | tf_op jit(solution)/shard_map/ppermute | solution.py:87
  120.3 5.8 %shard_map.134 = bf16[32,48,128]{2,1,0:T(8,128)(2,1)} custom-call(s32[7]{0:T(128)S(1)} %concatenate.3.where_ref, bf16[400,384]{1,0:T(8,128)(2,1)} %copy-done.3, bf16[64,640]{1,0:T(8,128)(2,1)S(1)} %get-tuple-element.17.embed_ref, f32[5,1,640]{2,1,0:T(1,128)S(1)} %get-tuple-element.18.shifts_ref, bf16[64,640]{1,0:T(8,128)(2,1)S(1)} %get-tuple-element.19.head_ref, ...), custom_call_target="tpu_custom_call" | custom-call | tf_op jit(solution)/shard_map/pallas_call | solution.py:32
  126.1 7.2 %all-to-all-start.2 = ((bf16[32,48,128]{2,1,0:T(8,128)(2,1)}), bf16[32,48,128]{2,1,0:T(8,128)(2,1)S(1)}, u32[]{:S(2)}, u32[]{:S(2)}) async-start(bf16[32,48,128]{2,1,0:T(8,128)(2,1)} %shard_map.134), calls=%async_computation.2 | async-start | bytes 786432 | tf_op jit(solution)/shard_map/all_to_all | solution.py:62
  135.7 6.4 %all-to-all-done.2.partial_ref = bf16[32,48,128]{2,1,0:T(8,128)(2,1)S(1)} async-done(((bf16[32,48,128]{2,1,0:T(8,128)(2,1)}), bf16[32,48,128]{2,1,0:T(8,128)(2,1)S(1)}, u32[]{:S(2)}, u32[]{:S(2)}) %all-to-all-start.2) | async-done | bytes 393248 | tf_op jit(solution)/shard_map/all_to_all | solution.py:62
  144.7 9.2 %all_to_all.25.grad_ref = bf16[8,32,128]{2,1,0:T(8,128)(2,1)S(1)} all-to-all(bf16[8,32,128]{2,1,0:T(8,128)(2,1)S(1)} %get-tuple-element.24), channel_id=1, replica_groups=mesh['section'=4,'seq'=8,'fsdp'=8] {'fsdp'}, dimensions={0} | all-to-all | bytes 131072 | tf_op jit(solution)/shard_map/all_to_all | solution.py:62
  154.8 15.5 %all_to_all.26 = f32[8,64,80]{2,1,0:T(8,128)S(1)} all-to-all(f32[8,64,80]{2,1,0:T(8,128)S(1)} %shard_map.136), channel_id=1, replica_groups=mesh['section'=4,'seq'=8,'fsdp'=8] {'seq'}, dimensions={0} | all-to-all | bytes 327680 | tf_op jit(solution)/shard_map/all_to_all | solution.py:62
  (116 shorter events, 40.4 us)
Async XLA Ops:
  9.5 17.9 %collective-permute-start.11 = (bf16[400,384]{1,0:T(8,128)(2,1)S(1)}, bf16[400,384]{1,0:T(8,128)(2,1)S(1)}, u32[]{:S(2)}, u32[]{:S(2)}) collective-permute-start(bf16[400,384]{1,0:T(8,128)(2,1)S(1)} %get-tuple-element.14.refs_9_.own_ref), channel_id=1, source_target_pairs={{0,56},{8,0},{16,8},{24,16},{32,24},{40,32},{48,40},{56,48},{1,57}... | collective-permute-start | bytes 921608 | tf_op jit(solution)/shard_map/ppermute | solution.py:75
  15.4 14.1 %collective-permute-start.8 = (bf16[400,384]{1,0:T(8,128)(2,1)S(1)}, bf16[400,384]{1,0:T(8,128)(2,1)S(1)}, u32[]{:S(2)}, u32[]{:S(2)}) collective-permute-start(bf16[400,384]{1,0:T(8,128)(2,1)S(1)} %get-tuple-element.14.refs_9_.own_ref), channel_id=1, source_target_pairs={{0,8},{8,16},{16,24},{24,32},{32,40},{40,48},{48,56},{56,0},{1,9},... | collective-permute-start | bytes 921608 | tf_op jit(solution)/shard_map/ppermute | solution.py:74
  15.4 16.7 %collective-permute-start = (bf16[384,384]{1,0:T(8,128)(2,1)S(1)}, bf16[384,384]{1,0:T(8,128)(2,1)S(1)}, u32[]{:S(2)}, u32[]{:S(2)}) collective-permute-start(bf16[384,384]{1,0:T(8,128)(2,1)S(1)} %get-tuple-element.15.refs_0_), channel_id=1, source_target_pairs={{0,8},{8,16},{16,24},{24,32},{32,40},{40,48},{48,56},{56,0},{1,9},... | collective-permute-start | bytes 884744 | tf_op jit(solution)/shard_map/ppermute | solution.py:74
  15.4 16.7 %collective-permute-start.3 = (bf16[384,384]{1,0:T(8,128)(2,1)S(1)}, bf16[384,384]{1,0:T(8,128)(2,1)}, u32[]{:S(2)}, u32[]{:S(2)}) collective-permute-start(bf16[384,384]{1,0:T(8,128)(2,1)S(1)} %get-tuple-element.15.refs_0_), channel_id=1, source_target_pairs={{0,56},{8,0},{16,8},{24,16},{32,24},{40,32},{48,40},{56,48},{1,57}... | collective-permute-start | bytes 884744 | tf_op jit(solution)/shard_map/ppermute | solution.py:75
  21.5 29.0 %all-to-all-start = ((bf16[8,144,384]{2,1,0:T(8,128)(2,1)}), bf16[8,144,384]{2,1,0:T(8,128)(2,1)S(1)}, u32[]{:S(2)}, u32[]{:S(2)}) async-start(bf16[8,144,384]{2,1,0:T(8,128)(2,1)} %shard_map.133), calls=%async_computation | async-start | bytes 1769472 | tf_op jit(solution)/shard_map/all_to_all | solution.py:62
  29.5 11.5 %collective-permute-start.9 = (bf16[400,384]{1,0:T(8,128)(2,1)S(1)}, bf16[400,384]{1,0:T(8,128)(2,1)}, u32[]{:S(2)}, u32[]{:S(2)}) collective-permute-start(bf16[400,384]{1,0:T(8,128)(2,1)S(1)} %collective-permute-done.8.refs_10_), channel_id=1, source_target_pairs={{0,8},{8,16},{16,24},{24,32},{32,40},{40,48},{48,56},{56,0},{1,9},... | collective-permute-start | bytes 921608 | tf_op jit(solution)/shard_map/ppermute | solution.py:74
  32.1 15.1 %collective-permute-start.1 = (bf16[384,384]{1,0:T(8,128)(2,1)S(1)}, bf16[384,384]{1,0:T(8,128)(2,1)S(1)}, u32[]{:S(2)}, u32[]{:S(2)}) collective-permute-start(bf16[384,384]{1,0:T(8,128)(2,1)S(1)} %collective-permute-done.refs_1_), channel_id=1, source_target_pairs={{0,8},{8,16},{16,24},{24,32},{32,40},{40,48},{48,56},{56,0},{1,9},... | collective-permute-start | bytes 884744 | tf_op jit(solution)/shard_map/ppermute | solution.py:74
  32.1 15.1 %collective-permute-start.4 = (bf16[384,384]{1,0:T(8,128)(2,1)}, bf16[384,384]{1,0:T(8,128)(2,1)}, u32[]{:S(2)}, u32[]{:S(2)}) collective-permute-start(bf16[384,384]{1,0:T(8,128)(2,1)} %collective-permute-done.3.refs_4_), channel_id=1, source_target_pairs={{0,56},{8,0},{16,8},{24,16},{32,24},{40,32},{48,40},{56,48},{1,57}... | collective-permute-start | bytes 884744 | tf_op jit(solution)/shard_map/ppermute | solution.py:75
  37.1 24.0 %collective-permute-start.13 = (bf16[400,384]{1,0:T(8,128)(2,1)}, bf16[400,384]{1,0:T(8,128)(2,1)S(1)}, u32[]{:S(2)}, u32[]{:S(2)}) collective-permute-start(bf16[400,384]{1,0:T(8,128)(2,1)} %collective-permute-done.12.refs_14_), channel_id=1, source_target_pairs={{0,56},{8,0},{16,8},{24,16},{32,24},{40,32},{48,40},{56,48},{1,57}... | collective-permute-start | bytes 921608 | tf_op jit(solution)/shard_map/ppermute | solution.py:75
  41.0 20.2 %collective-permute-start.10 = (bf16[400,384]{1,0:T(8,128)(2,1)}, bf16[400,384]{1,0:T(8,128)(2,1)}, u32[]{:S(2)}, u32[]{:S(2)}) collective-permute-start(bf16[400,384]{1,0:T(8,128)(2,1)} %collective-permute-done.9.refs_11_), channel_id=1, source_target_pairs={{0,8},{8,16},{16,24},{24,32},{32,40},{40,48},{48,56},{56,0},{1,9},... | collective-permute-start | bytes 921608 | tf_op jit(solution)/shard_map/ppermute | solution.py:74
  47.3 10.2 %collective-permute-start.2 = (bf16[384,384]{1,0:T(8,128)(2,1)S(1)}, bf16[384,384]{1,0:T(8,128)(2,1)S(1)}, u32[]{:S(2)}, u32[]{:S(2)}) collective-permute-start(bf16[384,384]{1,0:T(8,128)(2,1)S(1)} %collective-permute-done.1.refs_2_), channel_id=1, source_target_pairs={{0,8},{8,16},{16,24},{24,32},{32,40},{40,48},{48,56},{56,0},{1,9},... | collective-permute-start | bytes 884744 | tf_op jit(solution)/shard_map/ppermute | solution.py:74
  47.3 10.3 %collective-permute-start.5 = (bf16[384,384]{1,0:T(8,128)(2,1)}, bf16[384,384]{1,0:T(8,128)(2,1)S(1)}, u32[]{:S(2)}, u32[]{:S(2)}) collective-permute-start(bf16[384,384]{1,0:T(8,128)(2,1)} %collective-permute-done.4.refs_5_), channel_id=1, source_target_pairs={{0,56},{8,0},{16,8},{24,16},{32,24},{40,32},{48,40},{56,48},{1,57}... | collective-permute-start | bytes 884744 | tf_op jit(solution)/shard_map/ppermute | solution.py:75
  57.7 10.0 %collective-permute-start.7 = (bf16[192,384]{1,0:T(8,128)(2,1)S(1)}, bf16[192,384]{1,0:T(8,128)(2,1)S(1)}, u32[]{:S(2)}, u32[]{:S(2)}) collective-permute-start(bf16[192,384]{1,0:T(8,128)(2,1)S(1)} %slice.50), channel_id=1, source_target_pairs={{0,56},{8,0},{16,8},{24,16},{32,24},{40,32},{48,40},{56,48},{1,57}... | collective-permute-start | bytes 442376 | tf_op jit(solution)/shard_map/ppermute | solution.py:87
  64.3 18.9 %collective-permute-start.16 = (bf16[4,80,384]{2,1,0:T(8,128)(2,1)S(1)}, bf16[4,80,384]{2,1,0:T(8,128)(2,1)S(1)}, u32[]{:S(2)}, u32[]{:S(2)}) collective-permute-start(bf16[4,80,384]{2,1,0:T(8,128)(2,1)S(1)} %get-tuple-element.26.refs_0_), channel_id=1, source_target_pairs={{0,8},{8,16},{16,24},{24,32},{32,40},{40,48},{48,56},{56,0},{1,9},... | collective-permute-start | bytes 737288 | tf_op jit(solution)/shard_map/ppermute | solution.py:74
  65.0 18.3 %collective-permute-start.17 = (bf16[4,80,384]{2,1,0:T(8,128)(2,1)S(1)}, bf16[4,80,384]{2,1,0:T(8,128)(2,1)S(1)}, u32[]{:S(2)}, u32[]{:S(2)}) collective-permute-start(bf16[4,80,384]{2,1,0:T(8,128)(2,1)S(1)} %get-tuple-element.26.refs_0_), channel_id=1, source_target_pairs={{0,56},{8,0},{16,8},{24,16},{32,24},{40,32},{48,40},{56,48},{1,57}... | collective-permute-start | bytes 737288 | tf_op jit(solution)/shard_map/ppermute | solution.py:75
  67.7 15.6 %collective-permute-start.18 = (bf16[4,80,384]{2,1,0:T(8,128)(2,1)S(1)}, bf16[4,80,384]{2,1,0:T(8,128)(2,1)S(1)}, u32[]{:S(2)}, u32[]{:S(2)}) collective-permute-start(bf16[4,80,384]{2,1,0:T(8,128)(2,1)S(1)} %get-tuple-element.25.refs_9_), channel_id=1, source_target_pairs={{0,8},{8,16},{16,24},{24,32},{32,40},{40,48},{48,56},{56,0},{1,9},... | collective-permute-start | bytes 737288 | tf_op jit(solution)/shard_map/ppermute | solution.py:74
  70.3 13.0 %collective-permute-start.19 = (bf16[4,80,384]{2,1,0:T(8,128)(2,1)S(1)}, bf16[4,80,384]{2,1,0:T(8,128)(2,1)}, u32[]{:S(2)}, u32[]{:S(2)}) collective-permute-start(bf16[4,80,384]{2,1,0:T(8,128)(2,1)S(1)} %get-tuple-element.25.refs_9_), channel_id=1, source_target_pairs={{0,56},{8,0},{16,8},{24,16},{32,24},{40,32},{48,40},{56,48},{1,57}... | collective-permute-start | bytes 737288 | tf_op jit(solution)/shard_map/ppermute | solution.py:75
  83.3 36.9 %all-to-all-start.1 = ((bf16[8,256,384]{2,1,0:T(8,128)(2,1)}), bf16[8,256,384]{2,1,0:T(8,128)(2,1)}, u32[]{:S(2)}, u32[]{:S(2)}) async-start(bf16[8,256,384]{2,1,0:T(8,128)(2,1)} %shard_map.132), calls=%async_computation.1 | async-start | bytes 3145728 | tf_op jit(solution)/shard_map/all_to_all | solution.py:62
  89.3 9.9 %collective-permute-start.20 = (bf16[4,80,384]{2,1,0:T(8,128)(2,1)S(1)}, bf16[4,80,384]{2,1,0:T(8,128)(2,1)S(1)}, u32[]{:S(2)}, u32[]{:S(2)}) collective-permute-start(bf16[4,80,384]{2,1,0:T(8,128)(2,1)S(1)} %collective-permute-done.16.refs_1_), channel_id=1, source_target_pairs={{0,8},{8,16},{16,24},{24,32},{32,40},{40,48},{48,56},{56,0},{1,9},... | collective-permute-start | bytes 737288 | tf_op jit(solution)/shard_map/ppermute | solution.py:74
  92.5 12.0 %collective-permute-start.26 = (bf16[4,80,384]{2,1,0:T(8,128)(2,1)S(1)}, bf16[4,80,384]{2,1,0:T(8,128)(2,1)}, u32[]{:S(2)}, u32[]{:S(2)}) collective-permute-start(bf16[4,80,384]{2,1,0:T(8,128)(2,1)S(1)} %collective-permute-done.18.refs_10_), channel_id=1, source_target_pairs={{0,8},{8,16},{16,24},{24,32},{32,40},{40,48},{48,56},{56,0},{1,9},... | collective-permute-start | bytes 737288 | tf_op jit(solution)/shard_map/ppermute | solution.py:74
  92.7 12.2 %collective-permute-start.28 = (bf16[4,80,384]{2,1,0:T(8,128)(2,1)}, bf16[4,80,384]{2,1,0:T(8,128)(2,1)}, u32[]{:S(2)}, u32[]{:S(2)}) collective-permute-start(bf16[4,80,384]{2,1,0:T(8,128)(2,1)} %collective-permute-done.19.refs_13_), channel_id=1, source_target_pairs={{0,56},{8,0},{16,8},{24,16},{32,24},{40,32},{48,40},{56,48},{1,57}... | collective-permute-start | bytes 737288 | tf_op jit(solution)/shard_map/ppermute | solution.py:75
  99.1 10.8 %collective-permute-start.21 = (bf16[4,80,384]{2,1,0:T(8,128)(2,1)S(1)}, bf16[4,80,384]{2,1,0:T(8,128)(2,1)S(1)}, u32[]{:S(2)}, u32[]{:S(2)}) collective-permute-start(bf16[4,80,384]{2,1,0:T(8,128)(2,1)S(1)} %collective-permute-done.20.refs_2_), channel_id=1, source_target_pairs={{0,8},{8,16},{16,24},{24,32},{32,40},{40,48},{48,56},{56,0},{1,9},... | collective-permute-start | bytes 737288 | tf_op jit(solution)/shard_map/ppermute | solution.py:74
  99.5 10.5 %collective-permute-start.23 = (bf16[4,80,384]{2,1,0:T(8,128)(2,1)S(1)}, bf16[4,80,384]{2,1,0:T(8,128)(2,1)S(1)}, u32[]{:S(2)}, u32[]{:S(2)}) collective-permute-start(bf16[4,80,384]{2,1,0:T(8,128)(2,1)S(1)} %collective-permute-done.22.refs_5_), channel_id=1, source_target_pairs={{0,56},{8,0},{16,8},{24,16},{32,24},{40,32},{48,40},{56,48},{1,57}... | collective-permute-start | bytes 737288 | tf_op jit(solution)/shard_map/ppermute | solution.py:75
  126.1 16.0 %all-to-all-start.2 = ((bf16[32,48,128]{2,1,0:T(8,128)(2,1)}), bf16[32,48,128]{2,1,0:T(8,128)(2,1)S(1)}, u32[]{:S(2)}, u32[]{:S(2)}) async-start(bf16[32,48,128]{2,1,0:T(8,128)(2,1)} %shard_map.134), calls=%async_computation.2 | async-start | bytes 786432 | tf_op jit(solution)/shard_map/all_to_all | solution.py:62
  (31 other events, 303.7 us)

commit v5 on v4

--- a/solution.py
+++ b/solution.py
@@ -97,7 +97,7 @@
 def prepare_kernel(
     where_ref, embed_ref, weight_ref, shifts_hbm, student_hbm, previous_hbm, noise_hbm, context_hbm, *refs
 ):
-    first_ref, second_ref, shifts_ref, student_ref, previous_ref, noise_ref, out_ref, sems = refs
+    out_ref, plain_ref, shifts_ref, student_ref, previous_ref, noise_ref, sems = refs
     latent_dim, width = embed_ref.shape[1:]
     parts, depth, feat = weight_ref.shape[1:]
     rows = student_ref.shape[1]
@@ -137,18 +137,10 @@
         hidden = dot(embed_ref[0, :, first : first + step], plain, ((0,), (0,))) - mean
         spread += jnp.sum(hidden * hidden, axis=0, keepdims=True)
     inverse = lax.rsqrt(spread / width + 1e-06)
-    high = inverse.astype(bf16).astype(f32)
-    middle = (inverse - high).astype(bf16).astype(f32)
-    low = inverse - high - middle
-    line = lax.broadcasted_iota(jnp.int32, (16, rows), 0)
-    scales = jnp.where(line == 0, high, jnp.where(line == 1, middle, jnp.where(line == 2, low, 0.0)))
-    out_ref[tail : tail + latent_dim, :rows] = plain
-    out_ref[tail + latent_dim :, :rows] = scales.astype(bf16)
-    spare = jnp.zeros((latent_dim + 16 - len(lines), 128), f32)
+    out_ref[tail:, :rows] = (latents * inverse).astype(bf16)
+    plain_ref[...] = plain
+    spare = jnp.zeros((latent_dim - len(lines), 128), f32)
     out_ref[tail:, rows:] = jnp.concatenate(lines + [spare], axis=0).astype(bf16)
-    cut = first_ref.shape[0]
-    first_ref[...] = out_ref[:cut]
-    second_ref[...] = out_ref[cut:]
 
 
 def aside_kernel(where_ref, weight_ref, feature_ref, out_ref):
@@ -200,24 +192,26 @@
     return tuple(new)
 
 
-def attention_kernel(heads, latent_dim, group_start, where_ref, *refs):
+def attention_kernel(heads, latent_dim, where_ref, *refs):
     n_blocks = len(refs) - 4
     block_refs, (out_ref, all_ref, held_ref, sems) = refs[:n_blocks], refs[n_blocks:]
     count, lines, feat = all_ref.shape
     rows = out_ref.shape[1]
-    half = n_blocks // 2
-    copies = []
-    for start, group in ((0, block_refs[:half]), (group_start, block_refs[half:])):
-        at = [(n, start) for n in range(count)] + [(count - 1, start + group[count - 1].shape[0])]
-        copies.append(
-            [
-                pltpu.make_async_copy(
-                    ref, all_ref.at[n, pl.ds(place, ref.shape[0])], sems.at[(half if start else 0) + i]
+    at = [(n, 0, ref.shape[0]) for n, ref in enumerate(block_refs[:-1])]
+    at.append((count - 1, block_refs[-2].shape[0], block_refs[-1].shape[0]))
+    early, late = [], []
+    for ref, (n, place, size) in zip(block_refs, at):
+        for first, last, group in ((0, 2 * rows, late), (2 * rows, lines, early)):
+            first, last = max(first, place), min(last, place + size)
+            if first < last:
+                copies = len(early) + len(late)
+                group.append(
+                    pltpu.make_async_copy(
+                        ref.at[pl.ds(first - place, last - first)],
+                        all_ref.at[n, pl.ds(first, last - first)],
+                        sems.at[copies],
+                    )
                 )
-                for i, ((n, place), ref) in enumerate(zip(at, group))
-            ]
-        )
-    early, late = copies[1], copies[0]
     for copy in early + late:
         copy.start()
     for copy in early:
@@ -233,9 +227,7 @@
 
     def project(n, which):
         latents = all_ref[n, tail : tail + latent_dim, :rows]
-        scale = all_ref[n, tail + latent_dim :, :rows].astype(f32)
-        scale = jnp.sum(scale.T, axis=1, keepdims=True)
-        return [dot(latents, tables[i], ((0,), (0,))) * scale + shifts[i] for i in which]
+        return [dot(latents, tables[i], ((0,), (0,))) + shifts[i] for i in which]
 
     queries = (project(0, (0,))[0] * (HEAD_DIM ** (-0.5) * LOG2E)).astype(bf16)
 
@@ -245,23 +237,23 @@
         held_ref[n, rows:] = values.astype(bf16)
         return 0
 
-    lax.fori_loop(0, count, fill, 0)
+    lax.fori_loop(0, count, fill, 0, unroll=4)
     carry = tuple(
         (jnp.full((1, rows), -1e30, f32), jnp.zeros((1, rows), f32), jnp.zeros((HEAD_DIM, rows), f32))
         for _ in range(heads)
     )
 
-    def pair(ref, i, carry):
+    def four(ref, i, carry):
         def both(first, h):
             cols = slice(h * HEAD_DIM, (h + 1) * HEAD_DIM)
-            return jnp.concatenate([ref[2 * i + n, first : first + rows, cols] for n in range(2)], axis=0)
+            return jnp.concatenate([ref[4 * i + n, first : first + rows, cols] for n in range(4)], axis=0)
 
         return fold_keys(heads, carry, queries, lambda h: both(0, h), lambda h: both(rows, h))
 
-    carry = lax.fori_loop(0, count // 2, lambda i, c: pair(held_ref, i, c), carry, unroll=2)
+    carry = lax.fori_loop(0, count // 4, lambda i, c: four(held_ref, i, c), carry, unroll=2)
     for copy in late:
         copy.wait()
-    carry = lax.fori_loop(0, count // 2, lambda i, c: pair(all_ref, i, c), carry, unroll=2)
+    carry = lax.fori_loop(0, count // 4, lambda i, c: four(all_ref, i, c), carry, unroll=2)
     for h in range(heads):
         _, total, weighted = carry[h]
         attended = (weighted / total).T.astype(bf16)
@@ -280,16 +272,12 @@
     n_fsdp, rows = att_ref.shape[:2]
     latent_dim = embed_ref.shape[0]
     mixed = None
-    middle = len(weight_refs) // 2
     for f in range(n_fsdp):
-        group = weight_refs[:middle] if f < n_fsdp // 2 else weight_refs[middle:]
-        g = f % (n_fsdp // 2)
-        whole = [ref[g] for ref in group[:-2]]
-        whole.append(group[-2][g] if g < n_fsdp // 4 else group[-1][g - n_fsdp // 4])
+        whole = [ref[f] for ref in weight_refs[:-2]]
+        whole.append(weight_refs[-2][f] if f < n_fsdp // 2 else weight_refs[-1][f - n_fsdp // 2])
         part = dot(att_ref[f], jnp.concatenate(whole, axis=0), ((1,), (1,)))
         mixed = part if mixed is None else mixed + part
-    latents = own_ref[own_ref.shape[0] - latent_dim - 16 : own_ref.shape[0] - 16, :rows]
-    residual = dot(latents, embed_ref[...], ((0,), (0,))) + shifts_ref[2] * mixed
+    residual = dot(own_ref[...], embed_ref[...], ((0,), (0,))) + shifts_ref[2] * mixed
     centre = jnp.mean(residual, axis=1, keepdims=True)
     residual = residual - centre
     spread = jnp.sum(residual * residual, axis=1, keepdims=True)
@@ -351,16 +339,32 @@
 
 
 def gradient_kernel(where_ref, grad_ref, feature_ref, out_ref):
-    count, latent_dim, width = out_ref.shape
+    count, lines, pair = out_ref.shape
     rows = grad_ref.shape[1]
+    slot = feature_ref.shape[1] - 2 * rows
+    latent_dim, half = pair // 2, slot // 2
     grads = grad_ref[...].reshape(-1, grad_ref.shape[2])
-    first, second = (
-        dot(grads, feature_ref[:, at : at + rows].reshape(count * rows, -1), ((0,), (0,)))[:latent_dim]
-        for at in (width, width + rows)
-    )
-    joined = jnp.concatenate([first, second], axis=1)
+    joined = jnp.concatenate(
+        [
+            dot(feature_ref[:, at : at + rows].reshape(count * rows, -1), grads, ((0,), (0,)))[:, :latent_dim]
+            for at in (slot, slot + rows)
+        ],
+        axis=0,
+    )
+    spare = jnp.zeros((lines - half, pair), f32)
     for i in range(count):
-        out_ref[i] = joined[:, i * width : (i + 1) * width]
+        at = i * slot
+        block = jnp.concatenate([joined[at : at + half], joined[at + half : at + slot]], axis=1)
+        out_ref[i] = jnp.concatenate([block, spare], axis=0).astype(bf16)
+
+
+def sum_kernel(where_ref, part_ref, out_ref):
+    latent_dim, slot = out_ref.shape
+    total = part_ref[0].astype(f32)
+    for i in range(1, part_ref.shape[0]):
+        total += part_ref[i].astype(f32)
+    half = slot // 2
+    out_ref[...] = jnp.concatenate([total[:half, :latent_dim], total[:half, latent_dim:]], axis=0).T
 
 
 def per_device(
@@ -389,13 +393,11 @@
     shifts = modulation.transpose(1, 0, 2)
     slot = depth // n_fsdp
 
-    cut = run(aside_kernel, where, [((n_fsdp, slot + 2 * piece, feat), bf16)], out_weight, saved_features, picked=(0,))
-    lines = 2 * rows + 3 * latent_dim + latent_dim + 16
-    first = lines // 32 * 16
-    own, second = run(
+    lines = 2 * rows + 4 * latent_dim
+    own, plain = run(
         prepare_kernel,
         where,
-        [((first, feat), bf16), ((lines - first, feat), bf16)],
+        [((lines, feat), bf16), ((latent_dim, rows), bf16)],
         in_weight,
         qkv_weight.transpose(0, 2, 1, 3),
         shifts,
@@ -410,42 +412,11 @@
             pltpu.VMEM((latent_dim, rows), bf16),
             pltpu.VMEM((latent_dim, rows), bf16),
             pltpu.VMEM((latent_dim, rows), bf16),
-            pltpu.VMEM((lines, feat), bf16),
             pltpu.SemaphoreType.DMA((5,)),
         ],
     )
+    cut = run(aside_kernel, together(where, own), [((n_fsdp, slot + 2 * piece, feat), bf16)], out_weight, saved_features, picked=(0,))
     aside = exchange(cut, "fsdp")
-    around = [Ring(x, "seq", n_seq, 0, x.shape[0] // 32 * 16) for x in (own, second)]
-    for _ in range(n_seq // 2 - 1):
-        for r in around:
-            r.step()
-    ends = around[0].ends() + around[1].ends()
-    block, *_ = lax.optimization_barrier((aside[:, :slot],) + ends)
-    weights = [Ring(block[i : i + n_fsdp // 2], "seq", n_seq, 0) for i in (0, n_fsdp // 2)]
-    for r in around:
-        r.finish()
-    for r in weights:
-        r.step()
-    blocks = around[0].blocks() + around[1].blocks()
-    attended = run(
-        functools.partial(attention_kernel, heads, latent_dim, first),
-        where,
-        [((n_fsdp, rows, feat), bf16)],
-        *blocks,
-        scratch=[
-            pltpu.VMEM((n_seq, lines, feat), bf16),
-            pltpu.VMEM((n_seq, 2 * rows, feat), bf16),
-            pltpu.SemaphoreType.DMA((len(blocks),)),
-        ],
-        raw=range(len(blocks)),
-        cost=pl.CostEstimate(flops=11 * 10**9, bytes_accessed=20 * 10**6, transcendentals=3 * 10**6),
-    )
-    attended = exchange(together(attended, *weights[0].ends(), *weights[1].ends()), "fsdp")
-    for _ in range(n_seq // 2 - 2):
-        for r in weights:
-            r.step()
-    for r in weights:
-        r.finish()
     embed_here, head_here, shifts_here = run(
         columns_kernel,
         together(where, own),
@@ -455,17 +426,42 @@
         shifts,
         picked=(0, 1),
     )
+    around = Ring(own, "seq", n_seq, 0)
+    around.step()
+    around.step()
+    block, *_ = lax.optimization_barrier((aside[:, :slot],) + around.ends())
+    weights = Ring(block, "seq", n_seq, 0)
+    around.step()
+    weights.step()
+    around.finish()
+    weights.step()
+    blocks = around.blocks()
+    attended = run(
+        functools.partial(attention_kernel, heads, latent_dim),
+        together(where, embed_here, *weights.ends()),
+        [((n_fsdp, rows, feat), bf16)],
+        *blocks,
+        scratch=[
+            pltpu.VMEM((n_seq, lines, feat), bf16),
+            pltpu.VMEM((n_seq, 2 * rows, feat), bf16),
+            pltpu.SemaphoreType.DMA((2 * len(blocks),)),
+        ],
+        raw=range(len(blocks)),
+        cost=pl.CostEstimate(flops=11 * 10**9, bytes_accessed=20 * 10**6, transcendentals=3 * 10**6),
+    )
+    weights.step()
+    attended = exchange(together(attended, *weights.ends()), "fsdp")
+    weights.finish()
     partials = run(
         functools.partial(head_kernel, sections),
         where,
         [((sections * n_fsdp, piece + 16, 128), bf16)],
-        second,
+        plain,
         embed_here,
         shifts_here,
         head_here,
         attended,
-        *weights[0].blocks(),
-        *weights[1].blocks(),
+        *weights.blocks(),
     )
     partials = exchange(partials, ("section", "fsdp"))
 
@@ -484,8 +480,10 @@
         own_noised,
     )
     grads = exchange(grads, "fsdp")
-    partial_grad = run(gradient_kernel, where, [((n_seq, latent_dim, slot), f32)], grads, aside)
-    head_grad = jnp.sum(exchange(partial_grad, "seq"), axis=0).T
+    partial_grad = run(
+        gradient_kernel, where, [((n_seq, (slot // 2 + 15) // 16 * 16, 2 * latent_dim), bf16)], grads, aside
+    )
+    head_grad = run(sum_kernel, where, [((latent_dim, slot), f32)], exchange(partial_grad, "seq")).T
     return (student_group, dmd_grad, head_grad)
 
 

time: 172 us -> 170 us (0.988)
  waiting for transfers between devices: 36.2 us -> 60.8 us
  starting transfers between devices: 68.5 us -> 47.3 us
  blocking collectives: 24.7 us -> 22.5 us
    ppermute x12 -> x6, starting transfers between devices: 34.4 us -> 18.1 us  [step(): self.ahead.append(lax.ppermute(self.ahead[-1], self.axis, self.down))]
    ppermute x12 -> x6, waiting for transfers between devices: 22.4 us -> 35.1 us  [step(): self.behind.append(lax.ppermute(self.behind[-1], self.axis, self.up))]
    all_to_all x3, waiting for transfers between devices: 6.42 us -> 17.6 us  [exchange(): return lax.all_to_all(blocks, axis, 0, 0, tiled=True)]
    ppermute x4 -> x2, starting transfers between devices: 10.2 us -> 4.46 us  [finish(): lax.ppermute(second, self.axis, self.down)]
    all_to_all x2, blocking collectives: 24.7 us -> 22.5 us  [exchange(): return lax.all_to_all(blocks, axis, 0, 0, tiled=True)]
    ppermute x12 -> x6, waiting for transfers between devices: 1.81 us -> 0.02 us  [step(): self.ahead.append(lax.ppermute(self.ahead[-1], self.axis, self.down))]
    ppermute x12 -> x6, starting transfers between devices: 2.48 us -> 4.12 us  [step(): self.behind.append(lax.ppermute(self.behind[-1], self.axis, self.up))]
    ppermute x4 -> x2, waiting for transfers between devices: 4.88 us -> 6.1 us  [finish(): lax.ppermute(first, self.axis, self.up)]
  transfers between devices with their start and end apart: 35 -> 19, of which waited for: 12 -> 11; matrix products, arithmetic and copies ran while one was open for 2% -> 2% of each run, Pallas kernels for 10% -> 9%
where the time goes in v5:
time: 170 us; the launch traced here: 169 us
  waiting for transfers between devices  60.8 us (36%)
  starting transfers between devices  47.3 us (28%)
  Pallas kernels  29.4 us (17%)
  blocking collectives  22.5 us (13%)
  local copies, waits for them, and re-layouts  7.13 us (4%)
    ppermute x6, waiting for transfers between devices, step(): self.behind.append(lax.ppermute(self.behind[-1], self.axis, self.up))  35.1 us
    pallas_call x8, Pallas kernels, run(): pl.pallas_call(kernel, grid_spec=pltpu.PrefetchScalarGridSpec(num_scalar_...  29.4 us
    all_to_all x2, blocking collectives, exchange(): return lax.all_to_all(blocks, axis, 0, 0, tiled=True)  22.5 us
    all_to_all x3, starting transfers between devices, exchange(): return lax.all_to_all(blocks, axis, 0, 0, tiled=True)  18.3 us
    ppermute x6, starting transfers between devices, step(): self.ahead.append(lax.ppermute(self.ahead[-1], self.axis, self.down))  18.1 us
    all_to_all x3, waiting for transfers between devices, exchange(): return lax.all_to_all(blocks, axis, 0, 0, tiled=True)  17.6 us
    ppermute x2, waiting for transfers between devices, finish(): lax.ppermute(first, self.axis, self.up)  6.1 us
    ppermute x2, starting transfers between devices, finish(): lax.ppermute(second, self.axis, self.down)  4.46 us
  transfers between devices with their start and end apart: 19, of which 11 were waited for; matrix products, arithmetic and copies ran while one was open for 2% of the time, Pallas kernels for 9%

profile of v5, /device:TPU:2, one launch (start us, length us, event | category | flops | bytes accessed | tf_op | source)
XLA Modules:
  0.0 169.3 jit_solution(144878066930859239)
XLA Ops:
  5.6 3.8 %shard_map.130 = (bf16[768,384]{1,0:T(8,128)(2,1)S(1)}, bf16[64,256]{1,0:T(8,128)(2,1)S(1)}) custom-call(s32[7]{0:T(128)S(1)} %concatenate.3.where_ref, bf16[3,64,5120]{2,1,0:T(8,128)(2,1)} %embed_ref.3, bf16[3,3,640,384]{3,2,1,0:T(8,128)(2,1)} %bitcast.22, f32[5,1,5120]{2,1,0:T(1,128)S(1)} %bitcast.17, bf16[64,256]{1,0:T(8,128)(2,1)S(1)} %bitcast.19, ...), custom_call_target="tpu_custom_call" | custom-call | tf_op jit(solution)/shard_map/pallas_call | solution.py:32
  11.4 4.0 %collective-permute-start.2 = (bf16[768,384]{1,0:T(8,128)(2,1)S(1)}, bf16[768,384]{1,0:T(8,128)(2,1)S(1)}, u32[]{:S(2)}, u32[]{:S(2)}) collective-permute-start(bf16[768,384]{1,0:T(8,128)(2,1)S(1)} %get-tuple-element.16.refs_0_), channel_id=1, source_target_pairs={{0,56},{8,0},{16,8},{24,16},{32,24},{40,32},{48,40},{56,48},{1,57}... | collective-permute-start | bytes 1769480 | tf_op jit(solution)/shard_map/ppermute | solution.py:75
  18.2 6.1 %all-to-all-start = ((bf16[8,144,384]{2,1,0:T(8,128)(2,1)}), bf16[8,144,384]{2,1,0:T(8,128)(2,1)S(1)}, u32[]{:S(2)}, u32[]{:S(2)}) async-start(bf16[8,144,384]{2,1,0:T(8,128)(2,1)} %shard_map.132), calls=%async_computation | async-start | bytes 1769472 | tf_op jit(solution)/shard_map/all_to_all | solution.py:62
  24.3 4.4 %collective-permute-done.refs_1_ = bf16[768,384]{1,0:T(8,128)(2,1)S(1)} collective-permute-done((bf16[768,384]{1,0:T(8,128)(2,1)S(1)}, bf16[768,384]{1,0:T(8,128)(2,1)S(1)}, u32[]{:S(2)}, u32[]{:S(2)}) %collective-permute-start) | collective-permute-done | bytes 589856 | tf_op jit(solution)/shard_map/ppermute | solution.py:74
  28.7 3.2 %collective-permute-start.3 = (bf16[768,384]{1,0:T(8,128)(2,1)S(1)}, bf16[768,384]{1,0:T(8,128)(2,1)}, u32[]{:S(2)}, u32[]{:S(2)}) collective-permute-start(bf16[768,384]{1,0:T(8,128)(2,1)S(1)} %collective-permute-done.2.refs_4_), channel_id=1, source_target_pairs={{0,56},{8,0},{16,8},{24,16},{32,24},{40,32},{48,40},{56,48},{1,57}... | collective-permute-start | bytes 1769480 | tf_op jit(solution)/shard_map/ppermute | solution.py:75
  31.9 4.8 %all-to-all-done.feature_ref = bf16[8,144,384]{2,1,0:T(8,128)(2,1)S(1)} async-done(((bf16[8,144,384]{2,1,0:T(8,128)(2,1)}), bf16[8,144,384]{2,1,0:T(8,128)(2,1)S(1)}, u32[]{:S(2)}, u32[]{:S(2)}) %all-to-all-start) | async-done | bytes 884768 | tf_op jit(solution)/shard_map/all_to_all | solution.py:62
  36.8 7.7 %collective-permute-done.1.refs_2_ = bf16[768,384]{1,0:T(8,128)(2,1)} collective-permute-done((bf16[768,384]{1,0:T(8,128)(2,1)S(1)}, bf16[768,384]{1,0:T(8,128)(2,1)}, u32[]{:S(2)}, u32[]{:S(2)}) %collective-permute-start.1) | collective-permute-done | bytes 589856 | tf_op jit(solution)/shard_map/ppermute | solution.py:74
  44.5 3.2 %collective-permute-start.6 = (bf16[8,80,384]{2,1,0:T(8,128)(2,1)S(1)}, bf16[8,80,384]{2,1,0:T(8,128)(2,1)S(1)}, u32[]{:S(2)}, u32[]{:S(2)}) collective-permute-start(bf16[8,80,384]{2,1,0:T(8,128)(2,1)S(1)} %slice.25.refs_0_), channel_id=1, source_target_pairs={{0,56},{8,0},{16,8},{24,16},{32,24},{40,32},{48,40},{56,48},{1,57}... | collective-permute-start | bytes 1474568 | tf_op jit(solution)/shard_map/ppermute | solution.py:75
  47.8 3.2 %collective-permute-start.9 = (bf16[768,384]{1,0:T(8,128)(2,1)}, bf16[768,384]{1,0:T(8,128)(2,1)S(1)}, u32[]{:S(2)}, u32[]{:S(2)}) collective-permute-start(bf16[768,384]{1,0:T(8,128)(2,1)} %collective-permute-done.3.refs_5_), channel_id=1, source_target_pairs={{0,56},{8,0},{16,8},{24,16},{32,24},{40,32},{48,40},{56,48},{1,57}... | collective-permute-start | bytes 1769480 | tf_op jit(solution)/shard_map/ppermute | solution.py:75
  51.0 8.9 %collective-permute-done.4.refs_1_ = bf16[8,80,384]{2,1,0:T(8,128)(2,1)S(1)} collective-permute-done((bf16[8,80,384]{2,1,0:T(8,128)(2,1)S(1)}, bf16[8,80,384]{2,1,0:T(8,128)(2,1)S(1)}, u32[]{:S(2)}, u32[]{:S(2)}) %collective-permute-start.4) | collective-permute-done | bytes 491552 | tf_op jit(solution)/shard_map/ppermute | solution.py:74
  59.9 3.2 %collective-permute-start.7 = (bf16[8,80,384]{2,1,0:T(8,128)(2,1)S(1)}, bf16[8,80,384]{2,1,0:T(8,128)(2,1)S(1)}, u32[]{:S(2)}, u32[]{:S(2)}) collective-permute-start(bf16[8,80,384]{2,1,0:T(8,128)(2,1)S(1)} %collective-permute-done.6.refs_4_), channel_id=1, source_target_pairs={{0,56},{8,0},{16,8},{24,16},{32,24},{40,32},{48,40},{56,48},{1,57}... | collective-permute-start | bytes 1474568 | tf_op jit(solution)/shard_map/ppermute | solution.py:75
  63.1 9.4 %collective-permute-done.8.refs_3_ = bf16[768,384]{1,0:T(8,128)(2,1)S(1)} collective-permute-done((bf16[768,384]{1,0:T(8,128)(2,1)}, bf16[768,384]{1,0:T(8,128)(2,1)S(1)}, u32[]{:S(2)}, u32[]{:S(2)}) %collective-permute-start.8) | collective-permute-done | bytes 589856 | tf_op jit(solution)/shard_map/ppermute | solution.py:74
  72.7 3.3 %collective-permute-start.11 = (bf16[384,384]{1,0:T(8,128)(2,1)S(1)}, bf16[384,384]{1,0:T(8,128)(2,1)S(1)}, u32[]{:S(2)}, u32[]{:S(2)}) collective-permute-start(bf16[384,384]{1,0:T(8,128)(2,1)S(1)} %slice.27), channel_id=1, source_target_pairs={{0,56},{8,0},{16,8},{24,16},{32,24},{40,32},{48,40},{56,48},{1,57}... | collective-permute-start | bytes 884744 | tf_op jit(solution)/shard_map/ppermute | solution.py:87
  78.4 4.7 %collective-permute-done.5.refs_2_ = bf16[8,80,384]{2,1,0:T(8,128)(2,1)S(1)} collective-permute-done((bf16[8,80,384]{2,1,0:T(8,128)(2,1)S(1)}, bf16[8,80,384]{2,1,0:T(8,128)(2,1)S(1)}, u32[]{:S(2)}, u32[]{:S(2)}) %collective-permute-start.5) | collective-permute-done | bytes 491552 | tf_op jit(solution)/shard_map/ppermute | solution.py:74
  86.4 3.0 %collective-permute-done.10.refs_7_ = bf16[384,384]{1,0:T(8,128)(2,1)S(1)} collective-permute-done((bf16[384,384]{1,0:T(8,128)(2,1)S(1)}, bf16[384,384]{1,0:T(8,128)(2,1)S(1)}, u32[]{:S(2)}, u32[]{:S(2)}) %collective-permute-start.10) | collective-permute-done | bytes 294944 | tf_op jit(solution)/shard_map/ppermute | solution.py:87
  89.4 9.8 %shard_map.133 = bf16[8,256,384]{2,1,0:T(8,128)(2,1)} custom-call(s32[7]{0:T(128)S(1)} %concatenate.3.where_ref, bf16[768,384]{1,0:T(8,128)(2,1)S(1)} %get-tuple-element.16.refs_0_, bf16[768,384]{1,0:T(8,128)(2,1)S(1)} %collective-permute-done.refs_1_, bf16[768,384]{1,0:T(8,128)(2,1)} %collective-permute-done.1.refs_2_, bf16[768,384]{1,0:T(8,128)(2,1)} %copy-done.14, ...), custom_call_target="tpu_custom_call" | custom-call | flops 11000000512 | bytes 20000000 | tf_op jit(solution)/shard_map/pallas_call | solution.py:32
  99.3 5.9 %all-to-all-start.1 = ((bf16[8,256,384]{2,1,0:T(8,128)(2,1)}), bf16[8,256,384]{2,1,0:T(8,128)(2,1)}, u32[]{:S(2)}, u32[]{:S(2)}) async-start(bf16[8,256,384]{2,1,0:T(8,128)(2,1)} %shard_map.133), calls=%async_computation.1 | async-start | bytes 3145728 | tf_op jit(solution)/shard_map/all_to_all | solution.py:62
  109.6 3.1 %collective-permute-done.14.refs_7_ = bf16[4,80,384]{2,1,0:T(8,128)(2,1)S(1)} collective-permute-done((bf16[4,80,384]{2,1,0:T(8,128)(2,1)S(1)}, bf16[4,80,384]{2,1,0:T(8,128)(2,1)S(1)}, u32[]{:S(2)}, u32[]{:S(2)}) %collective-permute-start.14) | collective-permute-done | bytes 245792 | tf_op jit(solution)/shard_map/ppermute | solution.py:87
  114.7 6.3 %all-to-all-done.1.att_ref = bf16[8,256,384]{2,1,0:T(8,128)(2,1)} async-done(((bf16[8,256,384]{2,1,0:T(8,128)(2,1)}), bf16[8,256,384]{2,1,0:T(8,128)(2,1)}, u32[]{:S(2)}, u32[]{:S(2)}) %all-to-all-start.1) | async-done | bytes 1572896 | tf_op jit(solution)/shard_map/all_to_all | solution.py:62
  121.1 5.9 %shard_map.134 = bf16[32,48,128]{2,1,0:T(8,128)(2,1)} custom-call(s32[7]{0:T(128)S(1)} %concatenate.3.where_ref, bf16[64,256]{1,0:T(8,128)(2,1)S(1)} %get-tuple-element.15.own_ref, bf16[64,640]{1,0:T(8,128)(2,1)S(1)} %get-tuple-element.18.embed_ref, f32[5,1,640]{2,1,0:T(1,128)S(1)} %get-tuple-element.19.shifts_ref, ...), custom_call_target="tpu_custom_call" | custom-call | tf_op jit(solution)/shard_map/pallas_call | solution.py:32
  126.9 6.3 %all-to-all-start.2 = ((bf16[32,48,128]{2,1,0:T(8,128)(2,1)}), bf16[32,48,128]{2,1,0:T(8,128)(2,1)S(1)}, u32[]{:S(2)}, u32[]{:S(2)}) async-start(bf16[32,48,128]{2,1,0:T(8,128)(2,1)} %shard_map.134), calls=%async_computation.2 | async-start | bytes 786432 | tf_op jit(solution)/shard_map/all_to_all | solution.py:62
  135.5 6.4 %all-to-all-done.2.partial_ref = bf16[32,48,128]{2,1,0:T(8,128)(2,1)S(1)} async-done(((bf16[32,48,128]{2,1,0:T(8,128)(2,1)}), bf16[32,48,128]{2,1,0:T(8,128)(2,1)S(1)}, u32[]{:S(2)}, u32[]{:S(2)}) %all-to-all-start.2) | async-done | bytes 393248 | tf_op jit(solution)/shard_map/all_to_all | solution.py:62
  144.6 9.2 %all_to_all.25.grad_ref = bf16[8,32,128]{2,1,0:T(8,128)(2,1)S(1)} all-to-all(bf16[8,32,128]{2,1,0:T(8,128)(2,1)S(1)} %get-tuple-element.26), channel_id=1, replica_groups=mesh['section'=4,'seq'=8,'fsdp'=8] {'fsdp'}, dimensions={0} | all-to-all | bytes 131072 | tf_op jit(solution)/shard_map/all_to_all | solution.py:62
  154.7 13.3 %all_to_all.26.part_ref = bf16[8,48,128]{2,1,0:T(8,128)(2,1)S(1)} all-to-all(bf16[8,48,128]{2,1,0:T(8,128)(2,1)S(1)} %shard_map.136), channel_id=1, replica_groups=mesh['section'=4,'seq'=8,'fsdp'=8] {'seq'}, dimensions={0} | all-to-all | bytes 196608 | tf_op jit(solution)/shard_map/all_to_all | solution.py:62
  (75 shorter events, 28.5 us)
Async XLA Ops:
  9.4 19.3 %collective-permute-start = (bf16[768,384]{1,0:T(8,128)(2,1)S(1)}, bf16[768,384]{1,0:T(8,128)(2,1)S(1)}, u32[]{:S(2)}, u32[]{:S(2)}) collective-permute-start(bf16[768,384]{1,0:T(8,128)(2,1)S(1)} %get-tuple-element.16.refs_0_), channel_id=1, source_target_pairs={{0,8},{8,16},{16,24},{24,32},{32,40},{40,48},{48,56},{56,0},{1,9},... | collective-permute-start | bytes 1769480 | tf_op jit(solution)/shard_map/ppermute | solution.py:74
  11.4 17.3 %collective-permute-start.2 = (bf16[768,384]{1,0:T(8,128)(2,1)S(1)}, bf16[768,384]{1,0:T(8,128)(2,1)S(1)}, u32[]{:S(2)}, u32[]{:S(2)}) collective-permute-start(bf16[768,384]{1,0:T(8,128)(2,1)S(1)} %get-tuple-element.16.refs_0_), channel_id=1, source_target_pairs={{0,56},{8,0},{16,8},{24,16},{32,24},{40,32},{48,40},{56,48},{1,57}... | collective-permute-start | bytes 1769480 | tf_op jit(solution)/shard_map/ppermute | solution.py:75
  18.2 57.8 %copy-start.1 = (f32[1,5,5120]{2,0,1:T(1,128)S(1)}, f32[1,5,5120]{2,0,1:T(1,128)}, u32[]{:S(2)}) copy-start(f32[1,5,5120]{2,0,1:T(1,128)} %param.15) | copy-start | bytes 307204
  18.2 18.6 %all-to-all-start = ((bf16[8,144,384]{2,1,0:T(8,128)(2,1)}), bf16[8,144,384]{2,1,0:T(8,128)(2,1)S(1)}, u32[]{:S(2)}, u32[]{:S(2)}) async-start(bf16[8,144,384]{2,1,0:T(8,128)(2,1)} %shard_map.132), calls=%async_computation | async-start | bytes 1769472 | tf_op jit(solution)/shard_map/all_to_all | solution.py:62
  28.7 15.8 %collective-permute-start.1 = (bf16[768,384]{1,0:T(8,128)(2,1)S(1)}, bf16[768,384]{1,0:T(8,128)(2,1)}, u32[]{:S(2)}, u32[]{:S(2)}) collective-permute-start(bf16[768,384]{1,0:T(8,128)(2,1)S(1)} %collective-permute-done.refs_1_), channel_id=1, source_target_pairs={{0,8},{8,16},{16,24},{24,32},{32,40},{40,48},{48,56},{56,0},{1,9},... | collective-permute-start | bytes 1769480 | tf_op jit(solution)/shard_map/ppermute | solution.py:74
  28.7 49.6 %copy-start.17 = (bf16[768,384]{1,0:T(8,128)(2,1)}, bf16[768,384]{1,0:T(8,128)(2,1)S(1)}, u32[]{:S(2)}) copy-start(bf16[768,384]{1,0:T(8,128)(2,1)S(1)} %collective-permute-done.2.refs_4_) | copy-start | bytes 1769476
  28.7 15.8 %collective-permute-start.3 = (bf16[768,384]{1,0:T(8,128)(2,1)S(1)}, bf16[768,384]{1,0:T(8,128)(2,1)}, u32[]{:S(2)}, u32[]{:S(2)}) collective-permute-start(bf16[768,384]{1,0:T(8,128)(2,1)S(1)} %collective-permute-done.2.refs_4_), channel_id=1, source_target_pairs={{0,56},{8,0},{16,8},{24,16},{32,24},{40,32},{48,40},{56,48},{1,57}... | collective-permute-start | bytes 1769480 | tf_op jit(solution)/shard_map/ppermute | solution.py:75
  44.5 15.4 %collective-permute-start.4 = (bf16[8,80,384]{2,1,0:T(8,128)(2,1)S(1)}, bf16[8,80,384]{2,1,0:T(8,128)(2,1)S(1)}, u32[]{:S(2)}, u32[]{:S(2)}) collective-permute-start(bf16[8,80,384]{2,1,0:T(8,128)(2,1)S(1)} %slice.25.refs_0_), channel_id=1, source_target_pairs={{0,8},{8,16},{16,24},{24,32},{32,40},{40,48},{48,56},{56,0},{1,9},... | collective-permute-start | bytes 1474568 | tf_op jit(solution)/shard_map/ppermute | solution.py:74
  44.5 15.4 %collective-permute-start.6 = (bf16[8,80,384]{2,1,0:T(8,128)(2,1)S(1)}, bf16[8,80,384]{2,1,0:T(8,128)(2,1)S(1)}, u32[]{:S(2)}, u32[]{:S(2)}) collective-permute-start(bf16[8,80,384]{2,1,0:T(8,128)(2,1)S(1)} %slice.25.refs_0_), channel_id=1, source_target_pairs={{0,56},{8,0},{16,8},{24,16},{32,24},{40,32},{48,40},{56,48},{1,57}... | collective-permute-start | bytes 1474568 | tf_op jit(solution)/shard_map/ppermute | solution.py:75
  47.8 24.8 %collective-permute-start.8 = (bf16[768,384]{1,0:T(8,128)(2,1)}, bf16[768,384]{1,0:T(8,128)(2,1)S(1)}, u32[]{:S(2)}, u32[]{:S(2)}) collective-permute-start(bf16[768,384]{1,0:T(8,128)(2,1)} %collective-permute-done.1.refs_2_), channel_id=1, source_target_pairs={{0,8},{8,16},{16,24},{24,32},{32,40},{40,48},{48,56},{56,0},{1,9},... | collective-permute-start | bytes 1769480 | tf_op jit(solution)/shard_map/ppermute | solution.py:74
  47.8 24.9 %collective-permute-start.9 = (bf16[768,384]{1,0:T(8,128)(2,1)}, bf16[768,384]{1,0:T(8,128)(2,1)S(1)}, u32[]{:S(2)}, u32[]{:S(2)}) collective-permute-start(bf16[768,384]{1,0:T(8,128)(2,1)} %collective-permute-done.3.refs_5_), channel_id=1, source_target_pairs={{0,56},{8,0},{16,8},{24,16},{32,24},{40,32},{48,40},{56,48},{1,57}... | collective-permute-start | bytes 1769480 | tf_op jit(solution)/shard_map/ppermute | solution.py:75
  59.9 18.4 %copy-start.10 = (bf16[8,80,384]{2,1,0:T(8,128)(2,1)}, bf16[8,80,384]{2,1,0:T(8,128)(2,1)S(1)}, u32[]{:S(2)}) copy-start(bf16[8,80,384]{2,1,0:T(8,128)(2,1)S(1)} %collective-permute-done.4.refs_1_) | copy-start | bytes 1474564
  59.9 23.2 %collective-permute-start.5 = (bf16[8,80,384]{2,1,0:T(8,128)(2,1)S(1)}, bf16[8,80,384]{2,1,0:T(8,128)(2,1)S(1)}, u32[]{:S(2)}, u32[]{:S(2)}) collective-permute-start(bf16[8,80,384]{2,1,0:T(8,128)(2,1)S(1)} %collective-permute-done.4.refs_1_), channel_id=1, source_target_pairs={{0,8},{8,16},{16,24},{24,32},{32,40},{40,48},{48,56},{56,0},{1,9},... | collective-permute-start | bytes 1474568 | tf_op jit(solution)/shard_map/ppermute | solution.py:74
  59.9 18.4 %copy-start.11 = (bf16[8,80,384]{2,1,0:T(8,128)(2,1)}, bf16[8,80,384]{2,1,0:T(8,128)(2,1)S(1)}, u32[]{:S(2)}) copy-start(bf16[8,80,384]{2,1,0:T(8,128)(2,1)S(1)} %collective-permute-done.6.refs_4_) | copy-start | bytes 1474564
  59.9 23.2 %collective-permute-start.7 = (bf16[8,80,384]{2,1,0:T(8,128)(2,1)S(1)}, bf16[8,80,384]{2,1,0:T(8,128)(2,1)S(1)}, u32[]{:S(2)}, u32[]{:S(2)}) collective-permute-start(bf16[8,80,384]{2,1,0:T(8,128)(2,1)S(1)} %collective-permute-done.6.refs_4_), channel_id=1, source_target_pairs={{0,56},{8,0},{16,8},{24,16},{32,24},{40,32},{48,40},{56,48},{1,57}... | collective-permute-start | bytes 1474568 | tf_op jit(solution)/shard_map/ppermute | solution.py:75
  72.6 16.8 %collective-permute-start.10 = (bf16[384,384]{1,0:T(8,128)(2,1)S(1)}, bf16[384,384]{1,0:T(8,128)(2,1)S(1)}, u32[]{:S(2)}, u32[]{:S(2)}) collective-permute-start(bf16[384,384]{1,0:T(8,128)(2,1)S(1)} %slice.26), channel_id=1, source_target_pairs={{0,8},{8,16},{16,24},{24,32},{32,40},{40,48},{48,56},{56,0},{1,9},... | collective-permute-start | bytes 884744 | tf_op jit(solution)/shard_map/ppermute | solution.py:87
  72.7 16.7 %collective-permute-start.11 = (bf16[384,384]{1,0:T(8,128)(2,1)S(1)}, bf16[384,384]{1,0:T(8,128)(2,1)S(1)}, u32[]{:S(2)}, u32[]{:S(2)}) collective-permute-start(bf16[384,384]{1,0:T(8,128)(2,1)S(1)} %slice.27), channel_id=1, source_target_pairs={{0,56},{8,0},{16,8},{24,16},{32,24},{40,32},{48,40},{56,48},{1,57}... | collective-permute-start | bytes 884744 | tf_op jit(solution)/shard_map/ppermute | solution.py:87
  83.1 16.1 %copy-start.13 = (bf16[8,80,384]{2,1,0:T(8,128)(2,1)}, bf16[8,80,384]{2,1,0:T(8,128)(2,1)S(1)}, u32[]{:S(2)}) copy-start(bf16[8,80,384]{2,1,0:T(8,128)(2,1)S(1)} %collective-permute-done.7.refs_5_) | copy-start | bytes 1474564
  83.1 16.2 %collective-permute-start.12 = (bf16[8,80,384]{2,1,0:T(8,128)(2,1)S(1)}, bf16[8,80,384]{2,1,0:T(8,128)(2,1)S(1)}, u32[]{:S(2)}, u32[]{:S(2)}) collective-permute-start(bf16[8,80,384]{2,1,0:T(8,128)(2,1)S(1)} %collective-permute-done.5.refs_2_), channel_id=1, source_target_pairs={{0,8},{8,16},{16,24},{24,32},{32,40},{40,48},{48,56},{56,0},{1,9},... | collective-permute-start | bytes 1474568 | tf_op jit(solution)/shard_map/ppermute | solution.py:74
  85.2 14.1 %collective-permute-start.13 = (bf16[8,80,384]{2,1,0:T(8,128)(2,1)S(1)}, bf16[8,80,384]{2,1,0:T(8,128)(2,1)}, u32[]{:S(2)}, u32[]{:S(2)}) collective-permute-start(bf16[8,80,384]{2,1,0:T(8,128)(2,1)S(1)} %collective-permute-done.7.refs_5_), channel_id=1, source_target_pairs={{0,56},{8,0},{16,8},{24,16},{32,24},{40,32},{48,40},{56,48},{1,57}... | collective-permute-start | bytes 1474568 | tf_op jit(solution)/shard_map/ppermute | solution.py:75
  99.3 21.8 %all-to-all-start.1 = ((bf16[8,256,384]{2,1,0:T(8,128)(2,1)}), bf16[8,256,384]{2,1,0:T(8,128)(2,1)}, u32[]{:S(2)}, u32[]{:S(2)}) async-start(bf16[8,256,384]{2,1,0:T(8,128)(2,1)} %shard_map.133), calls=%async_computation.1 | async-start | bytes 3145728 | tf_op jit(solution)/shard_map/all_to_all | solution.py:62
  105.2 7.5 %collective-permute-start.14 = (bf16[4,80,384]{2,1,0:T(8,128)(2,1)S(1)}, bf16[4,80,384]{2,1,0:T(8,128)(2,1)S(1)}, u32[]{:S(2)}, u32[]{:S(2)}) collective-permute-start(bf16[4,80,384]{2,1,0:T(8,128)(2,1)S(1)} %slice.28), channel_id=1, source_target_pairs={{0,8},{8,16},{16,24},{24,32},{32,40},{40,48},{48,56},{56,0},{1,9},... | collective-permute-start | bytes 737288 | tf_op jit(solution)/shard_map/ppermute | solution.py:87
  108.4 6.3 %collective-permute-start.15 = (bf16[4,80,384]{2,1,0:T(8,128)(2,1)S(1)}, bf16[4,80,384]{2,1,0:T(8,128)(2,1)S(1)}, u32[]{:S(2)}, u32[]{:S(2)}) collective-permute-start(bf16[4,80,384]{2,1,0:T(8,128)(2,1)S(1)} %slice.29), channel_id=1, source_target_pairs={{0,56},{8,0},{16,8},{24,16},{32,24},{40,32},{48,40},{56,48},{1,57}... | collective-permute-start | bytes 737288 | tf_op jit(solution)/shard_map/ppermute | solution.py:87
  126.9 15.0 %all-to-all-start.2 = ((bf16[32,48,128]{2,1,0:T(8,128)(2,1)}), bf16[32,48,128]{2,1,0:T(8,128)(2,1)S(1)}, u32[]{:S(2)}, u32[]{:S(2)}) async-start(bf16[32,48,128]{2,1,0:T(8,128)(2,1)} %shard_map.134), calls=%async_computation.2 | async-start | bytes 786432 | tf_op jit(solution)/shard_map/all_to_all | solution.py:62
  (13 other events, 97.5 us)

commit v6 on v5

--- a/solution.py
+++ b/solution.py
@@ -76,6 +76,9 @@
 
     def ends(self):
         return self.behind[-1], self.ahead[-1]
+
+    def after(self, other):
+        self.behind[-1], self.ahead[-1], *_ = lax.optimization_barrier(self.ends() + other.ends())
 
     def finish(self):
         while len(self.behind) < self.half:
@@ -428,17 +431,18 @@
     )
     around = Ring(own, "seq", n_seq, 0)
     around.step()
-    around.step()
     block, *_ = lax.optimization_barrier((aside[:, :slot],) + around.ends())
     weights = Ring(block, "seq", n_seq, 0)
+    weights.step()
     around.step()
-    weights.step()
+    around.step()
+    weights.after(around)
     around.finish()
     weights.step()
     blocks = around.blocks()
     attended = run(
         functools.partial(attention_kernel, heads, latent_dim),
-        together(where, embed_here, *weights.ends()),
+        together(where, embed_here),
         [((n_fsdp, rows, feat), bf16)],
         *blocks,
         scratch=[
@@ -449,7 +453,6 @@
         raw=range(len(blocks)),
         cost=pl.CostEstimate(flops=11 * 10**9, bytes_accessed=20 * 10**6, transcendentals=3 * 10**6),
     )
-    weights.step()
     attended = exchange(together(attended, *weights.ends()), "fsdp")
     weights.finish()
     partials = run(

time: 170 us -> 167 us (0.982)
  waiting for transfers between devices: 60.8 us -> 54.4 us
  blocking collectives: 22.5 us -> 24.3 us
    all_to_all x3, waiting for transfers between devices: 17.6 us -> 11.5 us  [exchange(): return lax.all_to_all(blocks, axis, 0, 0, tiled=True)]
    ppermute x2, starting transfers between devices: 2.29 us -> 0.17 us  [finish(): lax.ppermute(first, self.axis, self.up)]
    ppermute x6, starting transfers between devices: 18.1 us -> 20.2 us  [step(): self.ahead.append(lax.ppermute(self.ahead[-1], self.axis, self.down))]
    ppermute x2, starting transfers between devices: 4.46 us -> 6.38 us  [finish(): lax.ppermute(second, self.axis, self.down)]
    all_to_all x2, blocking collectives: 22.5 us -> 24.3 us  [exchange(): return lax.all_to_all(blocks, axis, 0, 0, tiled=True)]
    ppermute x6, starting transfers between devices: 4.12 us -> 2.34 us  [step(): self.behind.append(lax.ppermute(self.behind[-1], self.axis, self.up))]
    unnamed x39 -> x35, local copies, waits for them, and re-layouts: 3.46 us -> 3.47 us
  transfers between devices with their start and end apart: 19 -> 19, of which waited for: 11 -> 10; matrix products, arithmetic and copies ran while one was open for 2% -> 2% of each run, Pallas kernels for 9% -> 9%
where the time goes in v6:
time: 167 us; the launch traced here: 166 us
  waiting for transfers between devices  54.4 us (33%)
  starting transfers between devices  48.3 us (29%)
  Pallas kernels  29.2 us (17%)
  blocking collectives  24.3 us (15%)
  local copies, waits for them, and re-layouts  7.99 us (5%)
    ppermute x6, waiting for transfers between devices, step(): self.behind.append(lax.ppermute(self.behind[-1], self.axis, self.up))  36.3 us
    pallas_call x8, Pallas kernels, run(): pl.pallas_call(kernel, grid_spec=pltpu.PrefetchScalarGridSpec(num_scalar_...  29.2 us
    all_to_all x2, blocking collectives, exchange(): return lax.all_to_all(blocks, axis, 0, 0, tiled=True)  24.3 us
    ppermute x6, starting transfers between devices, step(): self.ahead.append(lax.ppermute(self.ahead[-1], self.axis, self.down))  20.2 us
    all_to_all x3, starting transfers between devices, exchange(): return lax.all_to_all(blocks, axis, 0, 0, tiled=True)  19.3 us
    all_to_all x3, waiting for transfers between devices, exchange(): return lax.all_to_all(blocks, axis, 0, 0, tiled=True)  11.5 us
    ppermute x2, starting transfers between devices, finish(): lax.ppermute(second, self.axis, self.down)  6.38 us
    ppermute x2, waiting for transfers between devices, finish(): lax.ppermute(first, self.axis, self.up)  5.79 us
  transfers between devices with their start and end apart: 19, of which 10 were waited for; matrix products, arithmetic and copies ran while one was open for 2% of the time, Pallas kernels for 9%

profile of v6, /device:TPU:2, one launch (start us, length us, event | category | flops | bytes accessed | tf_op | source)
XLA Modules:
  0.0 166.4 jit_solution(11660582441704015046)
XLA Ops:
  5.6 3.8 %shard_map.130 = (bf16[768,384]{1,0:T(8,128)(2,1)S(1)}, bf16[64,256]{1,0:T(8,128)(2,1)S(1)}) custom-call(s32[7]{0:T(128)S(1)} %concatenate.3.where_ref, bf16[3,64,5120]{2,1,0:T(8,128)(2,1)} %embed_ref.3, bf16[3,3,640,384]{3,2,1,0:T(8,128)(2,1)} %bitcast.22, f32[5,1,5120]{2,1,0:T(1,128)S(1)} %bitcast.17, bf16[64,256]{1,0:T(8,128)(2,1)S(1)} %bitcast.19, ...), custom_call_target="tpu_custom_call" | custom-call | tf_op jit(solution)/shard_map/pallas_call | solution.py:32
  11.4 4.0 %collective-permute-start.3 = (bf16[768,384]{1,0:T(8,128)(2,1)S(1)}, bf16[768,384]{1,0:T(8,128)(2,1)S(1)}, u32[]{:S(2)}, u32[]{:S(2)}) collective-permute-start(bf16[768,384]{1,0:T(8,128)(2,1)S(1)} %get-tuple-element.18.refs_0_), channel_id=1, source_target_pairs={{0,56},{8,0},{16,8},{24,16},{32,24},{40,32},{48,40},{56,48},{1,57}... | collective-permute-start | bytes 1769480 | tf_op jit(solution)/shard_map/ppermute | solution.py:75
  15.4 13.2 %collective-permute-done.refs_1_ = bf16[768,384]{1,0:T(8,128)(2,1)S(1)} collective-permute-done((bf16[768,384]{1,0:T(8,128)(2,1)S(1)}, bf16[768,384]{1,0:T(8,128)(2,1)S(1)}, u32[]{:S(2)}, u32[]{:S(2)}) %collective-permute-start) | collective-permute-done | bytes 589856 | tf_op jit(solution)/shard_map/ppermute | solution.py:74
  28.7 3.2 %collective-permute-start.4 = (bf16[768,384]{1,0:T(8,128)(2,1)S(1)}, bf16[768,384]{1,0:T(8,128)(2,1)}, u32[]{:S(2)}, u32[]{:S(2)}) collective-permute-start(bf16[768,384]{1,0:T(8,128)(2,1)S(1)} %collective-permute-done.3.refs_4_), channel_id=1, source_target_pairs={{0,56},{8,0},{16,8},{24,16},{32,24},{40,32},{48,40},{56,48},{1,57}... | collective-permute-start | bytes 1769480 | tf_op jit(solution)/shard_map/ppermute | solution.py:75
  34.7 6.1 %all-to-all-start = ((bf16[8,144,384]{2,1,0:T(8,128)(2,1)}), bf16[8,144,384]{2,1,0:T(8,128)(2,1)S(1)}, u32[]{:S(2)}, u32[]{:S(2)}) async-start(bf16[8,144,384]{2,1,0:T(8,128)(2,1)} %shard_map.133), calls=%async_computation | async-start | bytes 1769472 | tf_op jit(solution)/shard_map/all_to_all | solution.py:62
  40.8 3.8 %collective-permute-done.1.refs_2_ = bf16[768,384]{1,0:T(8,128)(2,1)} collective-permute-done((bf16[768,384]{1,0:T(8,128)(2,1)S(1)}, bf16[768,384]{1,0:T(8,128)(2,1)}, u32[]{:S(2)}, u32[]{:S(2)}) %collective-permute-start.1) | collective-permute-done | bytes 589856 | tf_op jit(solution)/shard_map/ppermute | solution.py:74
  44.5 3.2 %collective-permute-start.5 = (bf16[768,384]{1,0:T(8,128)(2,1)}, bf16[768,384]{1,0:T(8,128)(2,1)}, u32[]{:S(2)}, u32[]{:S(2)}) collective-permute-start(bf16[768,384]{1,0:T(8,128)(2,1)} %collective-permute-done.4.refs_5_), channel_id=1, source_target_pairs={{0,56},{8,0},{16,8},{24,16},{32,24},{40,32},{48,40},{56,48},{1,57}... | collective-permute-start | bytes 1769480 | tf_op jit(solution)/shard_map/ppermute | solution.py:75
  47.8 4.7 %all-to-all-done.feature_ref = bf16[8,144,384]{2,1,0:T(8,128)(2,1)S(1)} async-done(((bf16[8,144,384]{2,1,0:T(8,128)(2,1)}), bf16[8,144,384]{2,1,0:T(8,128)(2,1)S(1)}, u32[]{:S(2)}, u32[]{:S(2)}) %all-to-all-start) | async-done | bytes 884768 | tf_op jit(solution)/shard_map/all_to_all | solution.py:62
  52.6 3.2 %collective-permute-start.9 = (bf16[8,80,384]{2,1,0:T(8,128)(2,1)S(1)}, bf16[8,80,384]{2,1,0:T(8,128)(2,1)S(1)}, u32[]{:S(2)}, u32[]{:S(2)}) collective-permute-start(bf16[8,80,384]{2,1,0:T(8,128)(2,1)S(1)} %slice.27.refs_0_), channel_id=1, source_target_pairs={{0,56},{8,0},{16,8},{24,16},{32,24},{40,32},{48,40},{56,48},{1,57}... | collective-permute-start | bytes 1474568 | tf_op jit(solution)/shard_map/ppermute | solution.py:75
  55.8 6.4 %collective-permute-done.2.refs_3_ = bf16[768,384]{1,0:T(8,128)(2,1)S(1)} collective-permute-done((bf16[768,384]{1,0:T(8,128)(2,1)}, bf16[768,384]{1,0:T(8,128)(2,1)S(1)}, u32[]{:S(2)}, u32[]{:S(2)}) %collective-permute-start.2) | collective-permute-done | bytes 589856 | tf_op jit(solution)/shard_map/ppermute | solution.py:74
  63.4 3.2 %collective-permute-start.7 = (bf16[384,384]{1,0:T(8,128)(2,1)S(1)}, bf16[384,384]{1,0:T(8,128)(2,1)S(1)}, u32[]{:S(2)}, u32[]{:S(2)}) collective-permute-start(bf16[384,384]{1,0:T(8,128)(2,1)S(1)} %slice.26), channel_id=1, source_target_pairs={{0,56},{8,0},{16,8},{24,16},{32,24},{40,32},{48,40},{56,48},{1,57}... | collective-permute-start | bytes 884744 | tf_op jit(solution)/shard_map/ppermute | solution.py:90
  68.8 3.9 %collective-permute-done.8.refs_1_ = bf16[8,80,384]{2,1,0:T(8,128)(2,1)S(1)} collective-permute-done((bf16[8,80,384]{2,1,0:T(8,128)(2,1)S(1)}, bf16[8,80,384]{2,1,0:T(8,128)(2,1)S(1)}, u32[]{:S(2)}, u32[]{:S(2)}) %collective-permute-start.8) | collective-permute-done | bytes 491552 | tf_op jit(solution)/shard_map/ppermute | solution.py:74
  73.0 3.2 %collective-permute-start.11 = (bf16[8,80,384]{2,1,0:T(8,128)(2,1)S(1)}, bf16[8,80,384]{2,1,0:T(8,128)(2,1)}, u32[]{:S(2)}, u32[]{:S(2)}) collective-permute-start(bf16[8,80,384]{2,1,0:T(8,128)(2,1)S(1)} %collective-permute-done.9.refs_4_), channel_id=1, source_target_pairs={{0,56},{8,0},{16,8},{24,16},{32,24},{40,32},{48,40},{56,48},{1,57}... | collective-permute-start | bytes 1474568 | tf_op jit(solution)/shard_map/ppermute | solution.py:75
  79.1 9.8 %shard_map.132 = bf16[8,256,384]{2,1,0:T(8,128)(2,1)} custom-call(s32[7]{0:T(128)S(1)} %concatenate.3.where_ref, bf16[768,384]{1,0:T(8,128)(2,1)S(1)} %get-tuple-element.18.refs_0_, bf16[768,384]{1,0:T(8,128)(2,1)S(1)} %collective-permute-done.refs_1_, bf16[768,384]{1,0:T(8,128)(2,1)} %collective-permute-done.1.refs_2_, bf16[768,384]{1,0:T(8,128)(2,1)} %copy-done.13, ...), custom_call_target="tpu_custom_call" | custom-call | flops 11000000512 | bytes 20000000 | tf_op jit(solution)/shard_map/pallas_call | solution.py:32
  88.9 5.9 %all-to-all-start.1 = ((bf16[8,256,384]{2,1,0:T(8,128)(2,1)}), bf16[8,256,384]{2,1,0:T(8,128)(2,1)}, u32[]{:S(2)}, u32[]{:S(2)}) async-start(bf16[8,256,384]{2,1,0:T(8,128)(2,1)} %shard_map.132), calls=%async_computation.1 | async-start | bytes 3145728 | tf_op jit(solution)/shard_map/all_to_all | solution.py:62
  94.9 3.2 %collective-permute-start.13 = (bf16[8,80,384]{2,1,0:T(8,128)(2,1)}, bf16[8,80,384]{2,1,0:T(8,128)(2,1)S(1)}, u32[]{:S(2)}, u32[]{:S(2)}) collective-permute-start(bf16[8,80,384]{2,1,0:T(8,128)(2,1)} %collective-permute-done.11.refs_5_), channel_id=1, source_target_pairs={{0,56},{8,0},{16,8},{24,16},{32,24},{40,32},{48,40},{56,48},{1,57}... | collective-permute-start | bytes 1474568 | tf_op jit(solution)/shard_map/ppermute | solution.py:75
  98.1 9.0 %collective-permute-done.12.refs_3_ = bf16[8,80,384]{2,1,0:T(8,128)(2,1)S(1)} collective-permute-done((bf16[8,80,384]{2,1,0:T(8,128)(2,1)}, bf16[8,80,384]{2,1,0:T(8,128)(2,1)S(1)}, u32[]{:S(2)}, u32[]{:S(2)}) %collective-permute-start.12) | collective-permute-done | bytes 491552 | tf_op jit(solution)/shard_map/ppermute | solution.py:74
  108.0 3.2 %collective-permute-start.15 = (bf16[4,80,384]{2,1,0:T(8,128)(2,1)}, bf16[4,80,384]{2,1,0:T(8,128)(2,1)S(1)}, u32[]{:S(2)}, u32[]{:S(2)}) collective-permute-start(bf16[4,80,384]{2,1,0:T(8,128)(2,1)} %slice.29), channel_id=1, source_target_pairs={{0,56},{8,0},{16,8},{24,16},{32,24},{40,32},{48,40},{56,48},{1,57}... | collective-permute-start | bytes 737288 | tf_op jit(solution)/shard_map/ppermute | solution.py:90
  111.6 3.0 %collective-permute-done.14.refs_7_ = bf16[4,80,384]{2,1,0:T(8,128)(2,1)S(1)} collective-permute-done((bf16[4,80,384]{2,1,0:T(8,128)(2,1)S(1)}, bf16[4,80,384]{2,1,0:T(8,128)(2,1)S(1)}, u32[]{:S(2)}, u32[]{:S(2)}) %collective-permute-start.14) | collective-permute-done | bytes 245792 | tf_op jit(solution)/shard_map/ppermute | solution.py:90
  115.3 5.9 %shard_map.134 = bf16[32,48,128]{2,1,0:T(8,128)(2,1)} custom-call(s32[7]{0:T(128)S(1)} %concatenate.3.where_ref, bf16[64,256]{1,0:T(8,128)(2,1)S(1)} %get-tuple-element.17.own_ref, bf16[64,640]{1,0:T(8,128)(2,1)S(1)} %get-tuple-element.20.embed_ref, f32[5,1,640]{2,1,0:T(1,128)S(1)} %get-tuple-element.21.shifts_ref, ...), custom_call_target="tpu_custom_call" | custom-call | tf_op jit(solution)/shard_map/pallas_call | solution.py:32
  121.2 7.3 %all-to-all-start.2 = ((bf16[32,48,128]{2,1,0:T(8,128)(2,1)}), bf16[32,48,128]{2,1,0:T(8,128)(2,1)S(1)}, u32[]{:S(2)}, u32[]{:S(2)}) async-start(bf16[32,48,128]{2,1,0:T(8,128)(2,1)} %shard_map.134), calls=%async_computation.2 | async-start | bytes 786432 | tf_op jit(solution)/shard_map/all_to_all | solution.py:62
  130.4 6.9 %all-to-all-done.2.partial_ref = bf16[32,48,128]{2,1,0:T(8,128)(2,1)S(1)} async-done(((bf16[32,48,128]{2,1,0:T(8,128)(2,1)}), bf16[32,48,128]{2,1,0:T(8,128)(2,1)S(1)}, u32[]{:S(2)}, u32[]{:S(2)}) %all-to-all-start.2) | async-done | bytes 393248 | tf_op jit(solution)/shard_map/all_to_all | solution.py:62
  139.9 9.2 %all_to_all.25.grad_ref = bf16[8,32,128]{2,1,0:T(8,128)(2,1)S(1)} all-to-all(bf16[8,32,128]{2,1,0:T(8,128)(2,1)S(1)} %get-tuple-element.30), channel_id=1, replica_groups=mesh['section'=4,'seq'=8,'fsdp'=8] {'fsdp'}, dimensions={0} | all-to-all | bytes 131072 | tf_op jit(solution)/shard_map/all_to_all | solution.py:62
  150.0 15.1 %all_to_all.26.part_ref = bf16[8,48,128]{2,1,0:T(8,128)(2,1)S(1)} all-to-all(bf16[8,48,128]{2,1,0:T(8,128)(2,1)S(1)} %shard_map.136), channel_id=1, replica_groups=mesh['section'=4,'seq'=8,'fsdp'=8] {'seq'}, dimensions={0} | all-to-all | bytes 196608 | tf_op jit(solution)/shard_map/all_to_all | solution.py:62
  (71 shorter events, 24.5 us)
Async XLA Ops:
  5.6 26.3 %copy-start.2 = (bf16[32,5120]{1,0:T(8,128)(2,1)S(1)}, bf16[32,5120]{1,0:T(8,128)(2,1)}, u32[]{:S(2)}) copy-start(bf16[32,5120]{1,0:T(8,128)(2,1)} %feature_ref.1) | copy-start | bytes 983044
  9.4 19.3 %collective-permute-start = (bf16[768,384]{1,0:T(8,128)(2,1)S(1)}, bf16[768,384]{1,0:T(8,128)(2,1)S(1)}, u32[]{:S(2)}, u32[]{:S(2)}) collective-permute-start(bf16[768,384]{1,0:T(8,128)(2,1)S(1)} %get-tuple-element.18.refs_0_), channel_id=1, source_target_pairs={{0,8},{8,16},{16,24},{24,32},{32,40},{40,48},{48,56},{56,0},{1,9},... | collective-permute-start | bytes 1769480 | tf_op jit(solution)/shard_map/ppermute | solution.py:74
  11.4 17.3 %collective-permute-start.3 = (bf16[768,384]{1,0:T(8,128)(2,1)S(1)}, bf16[768,384]{1,0:T(8,128)(2,1)S(1)}, u32[]{:S(2)}, u32[]{:S(2)}) collective-permute-start(bf16[768,384]{1,0:T(8,128)(2,1)S(1)} %get-tuple-element.18.refs_0_), channel_id=1, source_target_pairs={{0,56},{8,0},{16,8},{24,16},{32,24},{40,32},{48,40},{56,48},{1,57}... | collective-permute-start | bytes 1769480 | tf_op jit(solution)/shard_map/ppermute | solution.py:75
  28.7 15.8 %collective-permute-start.1 = (bf16[768,384]{1,0:T(8,128)(2,1)S(1)}, bf16[768,384]{1,0:T(8,128)(2,1)}, u32[]{:S(2)}, u32[]{:S(2)}) collective-permute-start(bf16[768,384]{1,0:T(8,128)(2,1)S(1)} %collective-permute-done.refs_1_), channel_id=1, source_target_pairs={{0,8},{8,16},{16,24},{24,32},{32,40},{40,48},{48,56},{56,0},{1,9},... | collective-permute-start | bytes 1769480 | tf_op jit(solution)/shard_map/ppermute | solution.py:74
  28.7 15.8 %collective-permute-start.4 = (bf16[768,384]{1,0:T(8,128)(2,1)S(1)}, bf16[768,384]{1,0:T(8,128)(2,1)}, u32[]{:S(2)}, u32[]{:S(2)}) collective-permute-start(bf16[768,384]{1,0:T(8,128)(2,1)S(1)} %collective-permute-done.3.refs_4_), channel_id=1, source_target_pairs={{0,56},{8,0},{16,8},{24,16},{32,24},{40,32},{48,40},{56,48},{1,57}... | collective-permute-start | bytes 1769480 | tf_op jit(solution)/shard_map/ppermute | solution.py:75
  34.7 32.0 %copy-start.1 = (f32[1,5,5120]{2,0,1:T(1,128)S(1)}, f32[1,5,5120]{2,0,1:T(1,128)}, u32[]{:S(2)}) copy-start(f32[1,5,5120]{2,0,1:T(1,128)} %param.15) | copy-start | bytes 307204
  34.7 17.7 %all-to-all-start = ((bf16[8,144,384]{2,1,0:T(8,128)(2,1)}), bf16[8,144,384]{2,1,0:T(8,128)(2,1)S(1)}, u32[]{:S(2)}, u32[]{:S(2)}) async-start(bf16[8,144,384]{2,1,0:T(8,128)(2,1)} %shard_map.133), calls=%async_computation | async-start | bytes 1769472 | tf_op jit(solution)/shard_map/all_to_all | solution.py:62
  44.5 17.7 %collective-permute-start.2 = (bf16[768,384]{1,0:T(8,128)(2,1)}, bf16[768,384]{1,0:T(8,128)(2,1)S(1)}, u32[]{:S(2)}, u32[]{:S(2)}) collective-permute-start(bf16[768,384]{1,0:T(8,128)(2,1)} %collective-permute-done.1.refs_2_), channel_id=1, source_target_pairs={{0,8},{8,16},{16,24},{24,32},{32,40},{40,48},{48,56},{56,0},{1,9},... | collective-permute-start | bytes 1769480 | tf_op jit(solution)/shard_map/ppermute | solution.py:74
  44.5 17.8 %collective-permute-start.5 = (bf16[768,384]{1,0:T(8,128)(2,1)}, bf16[768,384]{1,0:T(8,128)(2,1)}, u32[]{:S(2)}, u32[]{:S(2)}) collective-permute-start(bf16[768,384]{1,0:T(8,128)(2,1)} %collective-permute-done.4.refs_5_), channel_id=1, source_target_pairs={{0,56},{8,0},{16,8},{24,16},{32,24},{40,32},{48,40},{56,48},{1,57}... | collective-permute-start | bytes 1769480 | tf_op jit(solution)/shard_map/ppermute | solution.py:75
  52.5 20.3 %collective-permute-start.8 = (bf16[8,80,384]{2,1,0:T(8,128)(2,1)S(1)}, bf16[8,80,384]{2,1,0:T(8,128)(2,1)S(1)}, u32[]{:S(2)}, u32[]{:S(2)}) collective-permute-start(bf16[8,80,384]{2,1,0:T(8,128)(2,1)S(1)} %slice.27.refs_0_), channel_id=1, source_target_pairs={{0,8},{8,16},{16,24},{24,32},{32,40},{40,48},{48,56},{56,0},{1,9},... | collective-permute-start | bytes 1474568 | tf_op jit(solution)/shard_map/ppermute | solution.py:74
  52.6 20.2 %collective-permute-start.9 = (bf16[8,80,384]{2,1,0:T(8,128)(2,1)S(1)}, bf16[8,80,384]{2,1,0:T(8,128)(2,1)S(1)}, u32[]{:S(2)}, u32[]{:S(2)}) collective-permute-start(bf16[8,80,384]{2,1,0:T(8,128)(2,1)S(1)} %slice.27.refs_0_), channel_id=1, source_target_pairs={{0,56},{8,0},{16,8},{24,16},{32,24},{40,32},{48,40},{56,48},{1,57}... | collective-permute-start | bytes 1474568 | tf_op jit(solution)/shard_map/ppermute | solution.py:75
  62.2 16.8 %collective-permute-start.6 = (bf16[384,384]{1,0:T(8,128)(2,1)S(1)}, bf16[384,384]{1,0:T(8,128)(2,1)S(1)}, u32[]{:S(2)}, u32[]{:S(2)}) collective-permute-start(bf16[384,384]{1,0:T(8,128)(2,1)S(1)} %slice.25), channel_id=1, source_target_pairs={{0,8},{8,16},{16,24},{24,32},{32,40},{40,48},{48,56},{56,0},{1,9},... | collective-permute-start | bytes 884744 | tf_op jit(solution)/shard_map/ppermute | solution.py:90
  63.4 15.6 %collective-permute-start.7 = (bf16[384,384]{1,0:T(8,128)(2,1)S(1)}, bf16[384,384]{1,0:T(8,128)(2,1)S(1)}, u32[]{:S(2)}, u32[]{:S(2)}) collective-permute-start(bf16[384,384]{1,0:T(8,128)(2,1)S(1)} %slice.26), channel_id=1, source_target_pairs={{0,56},{8,0},{16,8},{24,16},{32,24},{40,32},{48,40},{56,48},{1,57}... | collective-permute-start | bytes 884744 | tf_op jit(solution)/shard_map/ppermute | solution.py:90
  72.8 16.1 %collective-permute-start.10 = (bf16[8,80,384]{2,1,0:T(8,128)(2,1)S(1)}, bf16[8,80,384]{2,1,0:T(8,128)(2,1)}, u32[]{:S(2)}, u32[]{:S(2)}) collective-permute-start(bf16[8,80,384]{2,1,0:T(8,128)(2,1)S(1)} %collective-permute-done.8.refs_1_), channel_id=1, source_target_pairs={{0,8},{8,16},{16,24},{24,32},{32,40},{40,48},{48,56},{56,0},{1,9},... | collective-permute-start | bytes 1474568 | tf_op jit(solution)/shard_map/ppermute | solution.py:74
  73.0 15.9 %collective-permute-start.11 = (bf16[8,80,384]{2,1,0:T(8,128)(2,1)S(1)}, bf16[8,80,384]{2,1,0:T(8,128)(2,1)}, u32[]{:S(2)}, u32[]{:S(2)}) collective-permute-start(bf16[8,80,384]{2,1,0:T(8,128)(2,1)S(1)} %collective-permute-done.9.refs_4_), channel_id=1, source_target_pairs={{0,56},{8,0},{16,8},{24,16},{32,24},{40,32},{48,40},{56,48},{1,57}... | collective-permute-start | bytes 1474568 | tf_op jit(solution)/shard_map/ppermute | solution.py:75
  88.9 22.3 %copy-start.4 = (bf16[256,64]{0,1:T(8,128)(2,1)S(1)}, bf16[256,64]{0,1:T(8,128)(2,1)}, u32[]{:S(2)}) copy-start(bf16[256,64]{0,1:T(8,128)(2,1)} %param.11) | copy-start | bytes 98308
  88.9 22.5 %copy-start.6 = (bf16[256,64]{0,1:T(8,128)(2,1)S(1)}, bf16[256,64]{0,1:T(8,128)(2,1)}, u32[]{:S(2)}) copy-start(bf16[256,64]{0,1:T(8,128)(2,1)} %param.12) | copy-start | bytes 98308
  88.9 22.5 %copy-start.8 = (bf16[256,64]{0,1:T(8,128)(2,1)S(1)}, bf16[256,64]{0,1:T(8,128)(2,1)}, u32[]{:S(2)}) copy-start(bf16[256,64]{0,1:T(8,128)(2,1)} %param.13) | copy-start | bytes 98308
  88.9 26.4 %all-to-all-start.1 = ((bf16[8,256,384]{2,1,0:T(8,128)(2,1)}), bf16[8,256,384]{2,1,0:T(8,128)(2,1)}, u32[]{:S(2)}, u32[]{:S(2)}) async-start(bf16[8,256,384]{2,1,0:T(8,128)(2,1)} %shard_map.132), calls=%async_computation.1 | async-start | bytes 3145728 | tf_op jit(solution)/shard_map/all_to_all | solution.py:62
  94.8 12.2 %collective-permute-start.12 = (bf16[8,80,384]{2,1,0:T(8,128)(2,1)}, bf16[8,80,384]{2,1,0:T(8,128)(2,1)S(1)}, u32[]{:S(2)}, u32[]{:S(2)}) collective-permute-start(bf16[8,80,384]{2,1,0:T(8,128)(2,1)} %collective-permute-done.10.refs_2_), channel_id=1, source_target_pairs={{0,8},{8,16},{16,24},{24,32},{32,40},{40,48},{48,56},{56,0},{1,9},... | collective-permute-start | bytes 1474568 | tf_op jit(solution)/shard_map/ppermute | solution.py:74
  94.9 12.3 %collective-permute-start.13 = (bf16[8,80,384]{2,1,0:T(8,128)(2,1)}, bf16[8,80,384]{2,1,0:T(8,128)(2,1)S(1)}, u32[]{:S(2)}, u32[]{:S(2)}) collective-permute-start(bf16[8,80,384]{2,1,0:T(8,128)(2,1)} %collective-permute-done.11.refs_5_), channel_id=1, source_target_pairs={{0,56},{8,0},{16,8},{24,16},{32,24},{40,32},{48,40},{56,48},{1,57}... | collective-permute-start | bytes 1474568 | tf_op jit(solution)/shard_map/ppermute | solution.py:75
  107.1 7.5 %collective-permute-start.14 = (bf16[4,80,384]{2,1,0:T(8,128)(2,1)S(1)}, bf16[4,80,384]{2,1,0:T(8,128)(2,1)S(1)}, u32[]{:S(2)}, u32[]{:S(2)}) collective-permute-start(bf16[4,80,384]{2,1,0:T(8,128)(2,1)S(1)} %slice.28), channel_id=1, source_target_pairs={{0,8},{8,16},{16,24},{24,32},{32,40},{40,48},{48,56},{56,0},{1,9},... | collective-permute-start | bytes 737288 | tf_op jit(solution)/shard_map/ppermute | solution.py:90
  108.0 7.3 %collective-permute-start.15 = (bf16[4,80,384]{2,1,0:T(8,128)(2,1)}, bf16[4,80,384]{2,1,0:T(8,128)(2,1)S(1)}, u32[]{:S(2)}, u32[]{:S(2)}) collective-permute-start(bf16[4,80,384]{2,1,0:T(8,128)(2,1)} %slice.29), channel_id=1, source_target_pairs={{0,56},{8,0},{16,8},{24,16},{32,24},{40,32},{48,40},{56,48},{1,57}... | collective-permute-start | bytes 737288 | tf_op jit(solution)/shard_map/ppermute | solution.py:90
  121.2 16.0 %all-to-all-start.2 = ((bf16[32,48,128]{2,1,0:T(8,128)(2,1)}), bf16[32,48,128]{2,1,0:T(8,128)(2,1)S(1)}, u32[]{:S(2)}, u32[]{:S(2)}) async-start(bf16[32,48,128]{2,1,0:T(8,128)(2,1)} %shard_map.134), calls=%async_computation.2 | async-start | bytes 786432 | tf_op jit(solution)/shard_map/all_to_all | solution.py:62
  (11 other events, 77.5 us)

commit v7 on v6

--- a/solution.py
+++ b/solution.py
@@ -14,7 +14,7 @@
 f32 = jnp.float32
 
 
-def run(kernel, where, outs, *operands, picked=(), scratch=(), raw=(), cost=None):
+def run(kernel, where, outs, *operands, picked=(), scratch=(), raw=(), inside=(), held=False, cost=None, room=52):
     def spec(shape, pick=False):
         zeros = (0,) * (len(shape) - 1)
         if pick:
@@ -24,6 +24,8 @@
     in_specs = [
         pl.BlockSpec(memory_space=pltpu.SMEM)
         if x.ndim == 1
+        else pl.BlockSpec(memory_space=pltpu.VMEM)
+        if n in inside
         else pl.BlockSpec(memory_space=pltpu.HBM)
         if n in raw
         else spec(x.shape, n in picked)
@@ -35,11 +37,11 @@
             num_scalar_prefetch=1,
             grid=(1,),
             in_specs=in_specs,
-            out_specs=tuple(spec(shape) for shape, _ in outs),
+            out_specs=tuple(pl.BlockSpec(memory_space=pltpu.VMEM) if held else spec(shape) for shape, _ in outs),
             scratch_shapes=list(scratch),
         ),
         out_shape=tuple(jax.ShapeDtypeStruct(shape, dtype) for shape, dtype in outs),
-        compiler_params=pltpu.CompilerParams(vmem_limit_bytes=52 * 1024 * 1024),
+        compiler_params=pltpu.CompilerParams(vmem_limit_bytes=room * 1024 * 1024),
         cost_estimate=cost,
     )(where, *operands)
     return result[0] if len(outs) == 1 else result
@@ -98,18 +100,19 @@
 
 
 def prepare_kernel(
-    where_ref, embed_ref, weight_ref, shifts_hbm, student_hbm, previous_hbm, noise_hbm, context_hbm, *refs
+    where_ref, embed_hbm, weight_hbm, shifts_hbm, student_hbm, previous_hbm, noise_hbm, context_hbm, *refs
 ):
-    out_ref, plain_ref, shifts_ref, student_ref, previous_ref, noise_ref, sems = refs
+    out_ref, plain_ref, embed_ref, weight_ref, shifts_ref, student_ref, previous_ref, noise_ref, context_ref, sems = refs
     latent_dim, width = embed_ref.shape[1:]
     parts, depth, feat = weight_ref.shape[1:]
     rows = student_ref.shape[1]
-    sources = (shifts_hbm, student_hbm, previous_hbm, noise_hbm, context_hbm)
-    targets = (shifts_ref, student_ref, previous_ref, noise_ref, out_ref.at[pl.ds(0, 2 * rows)])
+    model = pl.ds(where_ref[0], 1)
+    sources = (embed_hbm.at[model], shifts_hbm, student_hbm, previous_hbm, noise_hbm, weight_hbm.at[model], context_hbm)
+    targets = (embed_ref, shifts_ref, student_ref, previous_ref, noise_ref, weight_ref, context_ref)
     copies = [pltpu.make_async_copy(a, b, sems.at[n]) for n, (a, b) in enumerate(zip(sources, targets))]
     for copy in copies:
         copy.start()
-    for copy in copies:
+    for copy in copies[:5]:
         copy.wait()
     level = noise_levels(jnp.full((1, rows), where_ref[5], jnp.int32))
     noised = (1.0 - level) * previous_ref[...].astype(f32) + level * noise_ref[...].astype(f32)
@@ -120,18 +123,6 @@
     for first in range(0, width, step):
         row_sum += jnp.sum(embed_ref[0, :, first : first + step].astype(f32), axis=1, keepdims=True)
     row_mean = row_sum / width
-
-    here = pl.ds(pl.multiple_of(where_ref[1] * depth, 128), depth)
-    centred = (embed_ref[0, :, here].astype(f32) - row_mean) * (1.0 + shifts_ref[1, :, here])
-    shift = jnp.broadcast_to(shifts_ref[0, :, here], (16, depth))
-    folded = jnp.concatenate([centred, shift], axis=0).astype(bf16)
-    tail = 2 * rows + parts * latent_dim
-    lines = []
-    for i in range(parts):
-        table = dot(folded, weight_ref[0, i], ((1,), (0,)))
-        at = 2 * rows + i * latent_dim
-        out_ref[at : at + latent_dim] = table[:latent_dim].astype(bf16)
-        lines += [table[latent_dim : latent_dim + 1, n : n + 128] for n in range(0, feat, 128)]
 
     mean = jnp.sum(row_mean * latents, axis=0, keepdims=True)
     plain = latents.astype(bf16)
@@ -140,10 +131,34 @@
         hidden = dot(embed_ref[0, :, first : first + step], plain, ((0,), (0,))) - mean
         spread += jnp.sum(hidden * hidden, axis=0, keepdims=True)
     inverse = lax.rsqrt(spread / width + 1e-06)
-    out_ref[tail:, :rows] = (latents * inverse).astype(bf16)
+    heads = feat // HEAD_DIM
+    scaled = (latents * inverse).astype(bf16)
+    tail = (2 * rows + parts * latent_dim) * heads
+    for n in range(rows // 128):
+        out_ref[tail + n * latent_dim : tail + (n + 1) * latent_dim] = scaled[:, n * 128 : (n + 1) * 128]
     plain_ref[...] = plain
-    spare = jnp.zeros((latent_dim - len(lines), 128), f32)
-    out_ref[tail:, rows:] = jnp.concatenate(lines + [spare], axis=0).astype(bf16)
+    for copy in copies[5:]:
+        copy.wait()
+    here = pl.ds(pl.multiple_of(where_ref[1] * depth, 128), depth)
+    centred = (embed_ref[0, :, here].astype(f32) - row_mean) * (1.0 + shifts_ref[1, :, here])
+    shift = jnp.broadcast_to(shifts_ref[0, :, here], (16, depth))
+    folded = jnp.concatenate([centred, shift], axis=0).astype(bf16)
+    lines = []
+    for i in range(parts):
+        table = dot(folded, weight_ref[0, i], ((1,), (0,)))
+        for h in range(heads):
+            at = 2 * rows * heads + (i * heads + h) * latent_dim
+            out_ref[at : at + latent_dim] = table[:latent_dim, h * 128 : (h + 1) * 128].astype(bf16)
+        lines += [table[latent_dim : latent_dim + 1, n : n + 128] for n in range(0, feat, 128)]
+    spare = jnp.zeros((16 - len(lines), 128), f32)
+    out_ref[tail + rows // 128 * latent_dim :] = jnp.concatenate(lines + [spare], axis=0).astype(bf16)
+    for h in range(heads):
+        cols = slice(h * 128, (h + 1) * 128)
+        out_ref[h * rows : (h + 1) * rows] = context_ref[:rows, cols]
+        values = context_ref[rows:, cols].astype(f32).T.astype(bf16)
+        for n in range(rows // 128):
+            at = heads * rows + h * rows + n * 128
+            out_ref[at : at + 128] = values[:, n * 128 : (n + 1) * 128]
 
 
 def aside_kernel(where_ref, weight_ref, feature_ref, out_ref):
@@ -182,7 +197,7 @@
 
 
 def fold_keys(heads, carry, queries, keys, values):
-    scores = [dot(keys(h), queries[:, h * HEAD_DIM : (h + 1) * HEAD_DIM], ((1,), (1,))) for h in range(heads)]
+    scores = [dot(keys(h), queries[h], ((1,), (0,))) for h in range(heads)]
     new = []
     for h in range(heads):
         top, total, weighted = carry[h]
@@ -190,29 +205,28 @@
         weights = jnp.exp2(scores[h] - new_top)
         keep = jnp.exp2(top - new_top)
         total = total * keep + jnp.sum(weights, axis=0, keepdims=True)
-        weighted = weighted * keep + dot(values(h), weights.astype(bf16), ((0,), (0,)))
+        weighted = weighted * keep + dot(values(h), weights.astype(bf16), ((1,), (0,)))
         new.append((new_top, total, weighted))
     return tuple(new)
 
 
 def attention_kernel(heads, latent_dim, where_ref, *refs):
-    n_blocks = len(refs) - 4
-    block_refs, (out_ref, all_ref, held_ref, sems) = refs[:n_blocks], refs[n_blocks:]
-    count, lines, feat = all_ref.shape
-    rows = out_ref.shape[1]
+    block_refs, (out_ref, all_ref, key_ref, value_ref, sems) = refs[:-5], refs[-5:]
+    count, lines, _ = all_ref.shape
+    rows = out_ref.shape[2]
+    size = heads * rows
     at = [(n, 0, ref.shape[0]) for n, ref in enumerate(block_refs[:-1])]
     at.append((count - 1, block_refs[-2].shape[0], block_refs[-1].shape[0]))
     early, late = [], []
-    for ref, (n, place, size) in zip(block_refs, at):
-        for first, last, group in ((0, 2 * rows, late), (2 * rows, lines, early)):
-            first, last = max(first, place), min(last, place + size)
+    for ref, (n, place, length) in zip(block_refs, at):
+        for first, last, group in ((0, 2 * size, late), (2 * size, lines, early)):
+            first, last = max(first, place), min(last, place + length)
             if first < last:
-                copies = len(early) + len(late)
                 group.append(
                     pltpu.make_async_copy(
                         ref.at[pl.ds(first - place, last - first)],
                         all_ref.at[n, pl.ds(first, last - first)],
-                        sems.at[copies],
+                        sems.at[len(early) + len(late)],
                     )
                 )
     for copy in early + late:
@@ -220,48 +234,64 @@
     for copy in early:
         copy.wait()
 
-    tail = 2 * rows + 3 * latent_dim
-    parts = [slice(2 * rows + i * latent_dim, 2 * rows + (i + 1) * latent_dim) for i in range(3)]
-    tables = [sum(all_ref[n, at].astype(f32) for n in range(count)).astype(bf16) for at in parts]
-    shift = sum(all_ref[n, tail : tail + 16, rows:].astype(f32) for n in range(count))
-    shifts = [
-        jnp.concatenate([shift[i * heads + h : i * heads + h + 1] for h in range(heads)], axis=1) for i in range(3)
+    tables, base = [], 2 * size
+    for i in range(3):
+        at = slice(base + i * heads * latent_dim, base + (i + 1) * heads * latent_dim)
+        total = sum(all_ref[n, at].astype(f32) for n in range(count)).astype(bf16)
+        tables.append([total[h * latent_dim : (h + 1) * latent_dim] for h in range(heads)])
+    tail = base + 3 * heads * latent_dim
+    ends = tail + rows // 128 * latent_dim
+    shift = sum(all_ref[n, ends:].astype(f32) for n in range(count))
+    columns = jnp.concatenate([shift, jnp.zeros((112, 128), f32)], axis=0).T
+    latents = jnp.concatenate(
+        [
+            all_ref[n, tail + i * latent_dim : tail + (i + 1) * latent_dim]
+            for n in range(count)
+            for i in range(rows // 128)
+        ],
+        axis=1,
+    )
+    scale = HEAD_DIM ** (-0.5) * LOG2E
+    queries = [
+        ((dot(tables[0][h], latents[:, :rows], ((0,), (0,))) + columns[:, h : h + 1]) * scale).astype(bf16)
+        for h in range(heads)
     ]
-
-    def project(n, which):
-        latents = all_ref[n, tail : tail + latent_dim, :rows]
-        return [dot(latents, tables[i], ((0,), (0,))) + shifts[i] for i in which]
-
-    queries = (project(0, (0,))[0] * (HEAD_DIM ** (-0.5) * LOG2E)).astype(bf16)
-
-    def fill(n, _):
-        keys, values = project(n, (1, 2))
-        held_ref[n, :rows] = keys.astype(bf16)
-        held_ref[n, rows:] = values.astype(bf16)
-        return 0
-
-    lax.fori_loop(0, count, fill, 0, unroll=4)
+    for h in range(heads):
+        at = heads + h
+        key_ref[h] = (dot(latents, tables[1][h], ((0,), (0,))) + shift[at : at + 1]).astype(bf16)
+        at = 2 * heads + h
+        value_ref[h] = (dot(tables[2][h], latents, ((0,), (0,))) + columns[:, at : at + 1]).astype(bf16)
     carry = tuple(
         (jnp.full((1, rows), -1e30, f32), jnp.zeros((1, rows), f32), jnp.zeros((HEAD_DIM, rows), f32))
         for _ in range(heads)
     )
-
-    def four(ref, i, carry):
-        def both(first, h):
-            cols = slice(h * HEAD_DIM, (h + 1) * HEAD_DIM)
-            return jnp.concatenate([ref[4 * i + n, first : first + rows, cols] for n in range(4)], axis=0)
-
-        return fold_keys(heads, carry, queries, lambda h: both(0, h), lambda h: both(rows, h))
-
-    carry = lax.fori_loop(0, count // 4, lambda i, c: four(held_ref, i, c), carry, unroll=2)
+    step = 4 * rows
+    for i in range(count // 4):
+        at = slice(i * step, (i + 1) * step)
+        carry = fold_keys(heads, carry, queries, lambda h: key_ref[h, at], lambda h: value_ref[h, :, at])
     for copy in late:
         copy.wait()
-    carry = lax.fori_loop(0, count // 4, lambda i, c: four(all_ref, i, c), carry, unroll=2)
+    for i in range(count // 4):
+        here = range(4 * i, 4 * i + 4)
+        carry = fold_keys(
+            heads,
+            carry,
+            queries,
+            lambda h: jnp.concatenate([all_ref[n, h * rows : (h + 1) * rows] for n in here], axis=0),
+            lambda h: jnp.concatenate(
+                [
+                    all_ref[n, size + h * rows + j : size + h * rows + j + 128]
+                    for n in here
+                    for j in range(0, rows, 128)
+                ],
+                axis=1,
+            ),
+        )
     for h in range(heads):
         _, total, weighted = carry[h]
-        attended = (weighted / total).T.astype(bf16)
-        out_ref[:, :, h * HEAD_DIM : (h + 1) * HEAD_DIM] = jnp.broadcast_to(
-            attended[None], (out_ref.shape[0], rows, HEAD_DIM)
+        attended = (weighted / total).astype(bf16)
+        out_ref[:, h * HEAD_DIM : (h + 1) * HEAD_DIM] = jnp.broadcast_to(
+            attended[None], (out_ref.shape[0], HEAD_DIM, rows)
         )
 
 
@@ -272,26 +302,24 @@
 
 def head_kernel(sections, where_ref, own_ref, embed_ref, shifts_ref, head_ref, att_ref, *refs):
     weight_refs, out_ref = refs[:-1], refs[-1]
-    n_fsdp, rows = att_ref.shape[:2]
+    n_fsdp, _, rows = att_ref.shape
     latent_dim = embed_ref.shape[0]
     mixed = None
     for f in range(n_fsdp):
         whole = [ref[f] for ref in weight_refs[:-2]]
         whole.append(weight_refs[-2][f] if f < n_fsdp // 2 else weight_refs[-1][f - n_fsdp // 2])
-        part = dot(att_ref[f], jnp.concatenate(whole, axis=0), ((1,), (1,)))
+        part = dot(jnp.concatenate(whole, axis=0), att_ref[f], ((1,), (0,)))
         mixed = part if mixed is None else mixed + part
-    residual = dot(own_ref[...], embed_ref[...], ((0,), (0,))) + shifts_ref[2] * mixed
-    centre = jnp.mean(residual, axis=1, keepdims=True)
+    gate = jnp.broadcast_to(shifts_ref[2], (8, embed_ref.shape[1])).T[:, :1]
+    residual = dot(embed_ref[...], own_ref[...], ((0,), (0,))) + gate * mixed
+    centre = jnp.mean(residual, axis=0, keepdims=True)
     residual = residual - centre
-    spread = jnp.sum(residual * residual, axis=1, keepdims=True)
+    spread = jnp.sum(residual * residual, axis=0, keepdims=True)
     plain_head = head_ref[...].astype(f32)
     head = (plain_head * (1.0 + shifts_ref[4])).astype(bf16)
-    padded = jnp.concatenate([head, jnp.zeros_like(head)], axis=0)
-    values = dot(residual.astype(bf16), padded, ((1,), (1,)))
-    lanes = lax.broadcasted_iota(jnp.int32, values.shape, 1)
-    for n, column in enumerate(halves(centre) + halves(spread)):
-        values = jnp.where(lanes == latent_dim + n, column, values)
-    values = values.astype(bf16)
+    values = dot(head, residual.astype(bf16), ((1,), (0,)))
+    spare = jnp.zeros((latent_dim - 4, rows), f32)
+    values = jnp.concatenate([values, *halves(centre), *halves(spread), spare], axis=0).T.astype(bf16)
     sums = jnp.sum(head.astype(f32), axis=1, keepdims=True)
     consts = jnp.sum(plain_head * shifts_ref[3], axis=1, keepdims=True)
     place = lax.broadcasted_iota(jnp.int32, (latent_dim, 128), 1)
@@ -396,11 +424,11 @@
     shifts = modulation.transpose(1, 0, 2)
     slot = depth // n_fsdp
 
-    lines = 2 * rows + 4 * latent_dim
+    lines = (2 * rows + 3 * latent_dim) * heads + rows // 128 * latent_dim + 16
     own, plain = run(
         prepare_kernel,
         where,
-        [((lines, feat), bf16), ((latent_dim, rows), bf16)],
+        [((lines, HEAD_DIM), bf16), ((latent_dim, rows), bf16)],
         in_weight,
         qkv_weight.transpose(0, 2, 1, 3),
         shifts,
@@ -408,15 +436,18 @@
         previous_latent.T,
         score_noise.T,
         kv_cache[0].transpose(1, 0, 2).reshape(2 * rows, feat),
-        picked=(0, 1),
-        raw=(2, 3, 4, 5, 6),
+        raw=range(7),
         scratch=[
+            pltpu.VMEM((1, latent_dim, width), bf16),
+            pltpu.VMEM((1, 3, depth, feat), bf16),
             pltpu.VMEM(shifts.shape, f32),
             pltpu.VMEM((latent_dim, rows), bf16),
             pltpu.VMEM((latent_dim, rows), bf16),
             pltpu.VMEM((latent_dim, rows), bf16),
-            pltpu.SemaphoreType.DMA((5,)),
+            pltpu.VMEM((2 * rows, feat), bf16),
+            pltpu.SemaphoreType.DMA((7,)),
         ],
+        room=60,
     )
     cut = run(aside_kernel, together(where, own), [((n_fsdp, slot + 2 * piece, feat), bf16)], out_weight, saved_features, picked=(0,))
     aside = exchange(cut, "fsdp")
@@ -429,7 +460,7 @@
         shifts,
         picked=(0, 1),
     )
-    around = Ring(own, "seq", n_seq, 0)
+    around = Ring(own, "seq", n_seq, 0, lines // 32 * 16)
     around.step()
     block, *_ = lax.optimization_barrier((aside[:, :slot],) + around.ends())
     weights = Ring(block, "seq", n_seq, 0)
@@ -443,11 +474,12 @@
     attended = run(
         functools.partial(attention_kernel, heads, latent_dim),
         together(where, embed_here),
-        [((n_fsdp, rows, feat), bf16)],
+        [((n_fsdp, feat, rows), bf16)],
         *blocks,
         scratch=[
-            pltpu.VMEM((n_seq, lines, feat), bf16),
-            pltpu.VMEM((n_seq, 2 * rows, feat), bf16),
+            pltpu.VMEM((n_seq, lines, HEAD_DIM), bf16),
+            pltpu.VMEM((heads, n_seq * rows, HEAD_DIM), bf16),
+            pltpu.VMEM((heads, HEAD_DIM, n_seq * rows), bf16),
             pltpu.SemaphoreType.DMA((2 * len(blocks),)),
         ],
         raw=range(len(blocks)),

time: 167 us -> 166 us (level)
  local copies, waits for them, and re-layouts: 7.99 us -> 5.06 us
  waiting for transfers between devices: 54.4 us -> 56.5 us
  blocking collectives: 24.3 us -> 22.6 us
    ppermute x6, waiting for transfers between devices: 0.02 us -> 20.5 us  [step(): self.ahead.append(lax.ppermute(self.ahead[-1], self.axis, self.down))]
    ppermute x6, waiting for transfers between devices: 36.3 us -> 17.7 us  [step(): self.behind.append(lax.ppermute(self.behind[-1], self.axis, self.up))]
    unnamed x35, local copies, waits for them, and re-layouts: 3.47 us -> 0.32 us
    ppermute x6, starting transfers between devices: 20.2 us -> 23 us  [step(): self.ahead.append(lax.ppermute(self.ahead[-1], self.axis, self.down))]
    ppermute x6, starting transfers between devices: 2.34 us -> 0.35 us  [step(): self.behind.append(lax.ppermute(self.behind[-1], self.axis, self.up))]
    all_to_all x2, blocking collectives: 24.3 us -> 22.6 us  [exchange(): return lax.all_to_all(blocks, axis, 0, 0, tiled=True)]
where the time goes in v7:
time: 166 us; the launch traced here: 165 us
  waiting for transfers between devices  56.5 us (34%)
  starting transfers between devices  49.6 us (30%)
  Pallas kernels  29 us (17%)
  blocking collectives  22.6 us (14%)
  local copies, waits for them, and re-layouts  5.06 us (3%)
    pallas_call x8, Pallas kernels, run(): pl.pallas_call(kernel, grid_spec=pltpu.PrefetchScalarGridSpec(num_scalar_...  29 us
    ppermute x6, starting transfers between devices, step(): self.ahead.append(lax.ppermute(self.ahead[-1], self.axis, self.down))  23 us
    all_to_all x2, blocking collectives, exchange(): return lax.all_to_all(blocks, axis, 0, 0, tiled=True)  22.6 us
    ppermute x6, waiting for transfers between devices, step(): self.ahead.append(lax.ppermute(self.ahead[-1], self.axis, self.down))  20.5 us
    all_to_all x3, starting transfers between devices, exchange(): return lax.all_to_all(blocks, axis, 0, 0, tiled=True)  19.2 us
    ppermute x6, waiting for transfers between devices, step(): self.behind.append(lax.ppermute(self.behind[-1], self.axis, self.up))  17.7 us
    all_to_all x3, waiting for transfers between devices, exchange(): return lax.all_to_all(blocks, axis, 0, 0, tiled=True)  12.1 us
    ppermute x2, starting transfers between devices, finish(): lax.ppermute(second, self.axis, self.down)  6.81 us
  transfers between devices with their start and end apart: 19, of which 10 were waited for; matrix products, arithmetic and copies ran while one was open for 2% of the time, Pallas kernels for 9%

profile of v7, /device:TPU:2, one launch (start us, length us, event | category | flops | bytes accessed | tf_op | source)
XLA Modules:
  0.0 164.9 jit_solution(12079040901677292223)
XLA Ops:
  3.7 4.5 %shard_map.130 = (bf16[2256,128]{1,0:T(8,128)(2,1)}, bf16[64,256]{1,0:T(8,128)(2,1)}) custom-call(s32[7]{0:T(128)} %concatenate.3.where_ref, bf16[3,64,5120]{2,1,0:T(8,128)(2,1)} %embed_ref.1, bf16[3,3,640,384]{3,2,1,0:T(8,128)(2,1)} %bitcast.18, f32[5,1,5120]{2,1,0:T(1,128)} %bitcast.16, bf16[64,256]{1,0:T(8,128)(2,1)} %bitcast.22, ...), custom_call_target="tpu_custom_call" | custom-call | tf_op jit(solution)/shard_map/pallas_call | solution.py:34
  8.2 5.9 %collective-permute-start.3 = (bf16[2256,128]{1,0:T(8,128)(2,1)}, bf16[2256,128]{1,0:T(8,128)(2,1)S(1)}, u32[]{:S(2)}, u32[]{:S(2)}) collective-permute-start(bf16[2256,128]{1,0:T(8,128)(2,1)} %get-tuple-element.18.refs_0_), channel_id=1, source_target_pairs={{0,56},{8,0},{16,8},{24,16},{32,24},{40,32},{48,40},{56,48},{1,57}... | collective-permute-start | bytes 1732616 | tf_op jit(solution)/shard_map/ppermute | solution.py:77
  14.1 12.6 %collective-permute-done.3.refs_4_ = bf16[2256,128]{1,0:T(8,128)(2,1)S(1)} collective-permute-done((bf16[2256,128]{1,0:T(8,128)(2,1)}, bf16[2256,128]{1,0:T(8,128)(2,1)S(1)}, u32[]{:S(2)}, u32[]{:S(2)}) %collective-permute-start.3) | collective-permute-done | bytes 577568 | tf_op jit(solution)/shard_map/ppermute | solution.py:77
  26.8 3.6 %collective-permute-start.4 = (bf16[2256,128]{1,0:T(8,128)(2,1)S(1)}, bf16[2256,128]{1,0:T(8,128)(2,1)}, u32[]{:S(2)}, u32[]{:S(2)}) collective-permute-start(bf16[2256,128]{1,0:T(8,128)(2,1)S(1)} %collective-permute-done.3.refs_4_), channel_id=1, source_target_pairs={{0,56},{8,0},{16,8},{24,16},{32,24},{40,32},{48,40},{56,48},{1,57}... | collective-permute-start | bytes 1732616 | tf_op jit(solution)/shard_map/ppermute | solution.py:77
  30.4 2.8 %shard_map.133 = bf16[8,144,384]{2,1,0:T(8,128)(2,1)} custom-call(s32[7]{0:T(128)S(1)} %copy-done.3, bf16[3,640,384]{2,1,0:T(8,128)(2,1)} %weight_ref.1, bf16[32,5120]{1,0:T(8,128)(2,1)S(1)} %copy-done.1), custom_call_target="tpu_custom_call" | custom-call | tf_op jit(solution)/shard_map/pallas_call | solution.py:34
  33.1 6.1 %all-to-all-start = ((bf16[8,144,384]{2,1,0:T(8,128)(2,1)}), bf16[8,144,384]{2,1,0:T(8,128)(2,1)S(1)}, u32[]{:S(2)}, u32[]{:S(2)}) async-start(bf16[8,144,384]{2,1,0:T(8,128)(2,1)} %shard_map.133), calls=%async_computation | async-start | bytes 1769472 | tf_op jit(solution)/shard_map/all_to_all | solution.py:64
  41.8 3.8 %collective-permute-start.5 = (bf16[2256,128]{1,0:T(8,128)(2,1)}, bf16[2256,128]{1,0:T(8,128)(2,1)S(1)}, u32[]{:S(2)}, u32[]{:S(2)}) collective-permute-start(bf16[2256,128]{1,0:T(8,128)(2,1)} %collective-permute-done.4.refs_5_), channel_id=1, source_target_pairs={{0,56},{8,0},{16,8},{24,16},{32,24},{40,32},{48,40},{56,48},{1,57}... | collective-permute-start | bytes 1732616 | tf_op jit(solution)/shard_map/ppermute | solution.py:77
  45.6 5.2 %all-to-all-done.feature_ref = bf16[8,144,384]{2,1,0:T(8,128)(2,1)S(1)} async-done(((bf16[8,144,384]{2,1,0:T(8,128)(2,1)}), bf16[8,144,384]{2,1,0:T(8,128)(2,1)S(1)}, u32[]{:S(2)}, u32[]{:S(2)}) %all-to-all-start) | async-done | bytes 884768 | tf_op jit(solution)/shard_map/all_to_all | solution.py:64
  51.0 3.2 %collective-permute-start.9 = (bf16[8,80,384]{2,1,0:T(8,128)(2,1)S(1)}, bf16[8,80,384]{2,1,0:T(8,128)(2,1)S(1)}, u32[]{:S(2)}, u32[]{:S(2)}) collective-permute-start(bf16[8,80,384]{2,1,0:T(8,128)(2,1)S(1)} %slice.27.refs_0_), channel_id=1, source_target_pairs={{0,56},{8,0},{16,8},{24,16},{32,24},{40,32},{48,40},{56,48},{1,57}... | collective-permute-start | bytes 1474568 | tf_op jit(solution)/shard_map/ppermute | solution.py:77
  54.2 5.2 %collective-permute-done.5.refs_6_ = bf16[2256,128]{1,0:T(8,128)(2,1)S(1)} collective-permute-done((bf16[2256,128]{1,0:T(8,128)(2,1)}, bf16[2256,128]{1,0:T(8,128)(2,1)S(1)}, u32[]{:S(2)}, u32[]{:S(2)}) %collective-permute-start.5) | collective-permute-done | bytes 577568 | tf_op jit(solution)/shard_map/ppermute | solution.py:77
  59.5 3.7 %collective-permute-start.7 = (bf16[1136,128]{1,0:T(8,128)(2,1)S(1)}, bf16[1136,128]{1,0:T(8,128)(2,1)S(1)}, u32[]{:S(2)}, u32[]{:S(2)}) collective-permute-start(bf16[1136,128]{1,0:T(8,128)(2,1)S(1)} %slice.26), channel_id=1, source_target_pairs={{0,56},{8,0},{16,8},{24,16},{32,24},{40,32},{48,40},{56,48},{1,57}... | collective-permute-start | bytes 872456 | tf_op jit(solution)/shard_map/ppermute | solution.py:92
  65.5 8.1 %collective-permute-done.8.refs_1_ = bf16[8,80,384]{2,1,0:T(8,128)(2,1)S(1)} collective-permute-done((bf16[8,80,384]{2,1,0:T(8,128)(2,1)S(1)}, bf16[8,80,384]{2,1,0:T(8,128)(2,1)S(1)}, u32[]{:S(2)}, u32[]{:S(2)}) %collective-permute-start.8) | collective-permute-done | bytes 491552 | tf_op jit(solution)/shard_map/ppermute | solution.py:76
  73.9 3.2 %collective-permute-start.11 = (bf16[8,80,384]{2,1,0:T(8,128)(2,1)S(1)}, bf16[8,80,384]{2,1,0:T(8,128)(2,1)}, u32[]{:S(2)}, u32[]{:S(2)}) collective-permute-start(bf16[8,80,384]{2,1,0:T(8,128)(2,1)S(1)} %collective-permute-done.9.refs_4_), channel_id=1, source_target_pairs={{0,56},{8,0},{16,8},{24,16},{32,24},{40,32},{48,40},{56,48},{1,57}... | collective-permute-start | bytes 1474568 | tf_op jit(solution)/shard_map/ppermute | solution.py:77
  79.7 9.1 %shard_map.132 = bf16[8,384,256]{2,1,0:T(8,128)(2,1)} custom-call(s32[7]{0:T(128)S(1)} %copy-done.3, bf16[2256,128]{1,0:T(8,128)(2,1)S(1)} %copy-done.4, bf16[2256,128]{1,0:T(8,128)(2,1)S(1)} %collective-permute-done.refs_1_, bf16[2256,128]{1,0:T(8,128)(2,1)} %collective-permute-done.1.refs_2_, bf16[2256,128]{1,0:T(8,128)(2,1)} %copy-done.10, ...), custom_call_target="tpu_custom_call" | custom-call | flops 11000000512 | bytes 20000000 | tf_op jit(solution)/shard_map/pallas_call | solution.py:34
  89.0 5.9 %all-to-all-start.1 = ((bf16[8,384,256]{2,1,0:T(8,128)(2,1)}), bf16[8,384,256]{2,1,0:T(8,128)(2,1)}, u32[]{:S(2)}, u32[]{:S(2)}) async-start(bf16[8,384,256]{2,1,0:T(8,128)(2,1)} %shard_map.132), calls=%async_computation.1 | async-start | bytes 3145728 | tf_op jit(solution)/shard_map/all_to_all | solution.py:64
  94.9 3.2 %collective-permute-start.13 = (bf16[8,80,384]{2,1,0:T(8,128)(2,1)}, bf16[8,80,384]{2,1,0:T(8,128)(2,1)S(1)}, u32[]{:S(2)}, u32[]{:S(2)}) collective-permute-start(bf16[8,80,384]{2,1,0:T(8,128)(2,1)} %collective-permute-done.11.refs_5_), channel_id=1, source_target_pairs={{0,56},{8,0},{16,8},{24,16},{32,24},{40,32},{48,40},{56,48},{1,57}... | collective-permute-start | bytes 1474568 | tf_op jit(solution)/shard_map/ppermute | solution.py:77
  98.2 9.5 %collective-permute-done.12.refs_3_ = bf16[8,80,384]{2,1,0:T(8,128)(2,1)S(1)} collective-permute-done((bf16[8,80,384]{2,1,0:T(8,128)(2,1)}, bf16[8,80,384]{2,1,0:T(8,128)(2,1)S(1)}, u32[]{:S(2)}, u32[]{:S(2)}) %collective-permute-start.12) | collective-permute-done | bytes 491552 | tf_op jit(solution)/shard_map/ppermute | solution.py:76
  108.7 3.2 %collective-permute-start.15 = (bf16[4,80,384]{2,1,0:T(8,128)(2,1)}, bf16[4,80,384]{2,1,0:T(8,128)(2,1)S(1)}, u32[]{:S(2)}, u32[]{:S(2)}) collective-permute-start(bf16[4,80,384]{2,1,0:T(8,128)(2,1)} %slice.29), channel_id=1, source_target_pairs={{0,56},{8,0},{16,8},{24,16},{32,24},{40,32},{48,40},{56,48},{1,57}... | collective-permute-start | bytes 737288 | tf_op jit(solution)/shard_map/ppermute | solution.py:92
  112.3 3.0 %collective-permute-done.14.refs_7_ = bf16[4,80,384]{2,1,0:T(8,128)(2,1)S(1)} collective-permute-done((bf16[4,80,384]{2,1,0:T(8,128)(2,1)S(1)}, bf16[4,80,384]{2,1,0:T(8,128)(2,1)S(1)}, u32[]{:S(2)}, u32[]{:S(2)}) %collective-permute-start.14) | collective-permute-done | bytes 245792 | tf_op jit(solution)/shard_map/ppermute | solution.py:92
  115.9 5.6 %shard_map.134 = bf16[32,48,128]{2,1,0:T(8,128)(2,1)} custom-call(s32[7]{0:T(128)S(1)} %copy-done.3, bf16[64,256]{1,0:T(8,128)(2,1)S(1)} %copy-done.2, bf16[64,640]{1,0:T(8,128)(2,1)S(1)} %get-tuple-element.20.embed_ref, f32[5,1,640]{2,1,0:T(1,128)S(1)} %get-tuple-element.21.shifts_ref, bf16[64,640]{1,0:T(8,128)(2,1)S(1)} %get-tuple-element.22.head_ref, ...), custom_call_target="tpu_custom_call" | custom-call | tf_op jit(solution)/shard_map/pallas_call | solution.py:34
  121.4 7.2 %all-to-all-start.2 = ((bf16[32,48,128]{2,1,0:T(8,128)(2,1)}), bf16[32,48,128]{2,1,0:T(8,128)(2,1)S(1)}, u32[]{:S(2)}, u32[]{:S(2)}) async-start(bf16[32,48,128]{2,1,0:T(8,128)(2,1)} %shard_map.134), calls=%async_computation.2 | async-start | bytes 786432 | tf_op jit(solution)/shard_map/all_to_all | solution.py:64
  130.6 6.9 %all-to-all-done.2.partial_ref = bf16[32,48,128]{2,1,0:T(8,128)(2,1)S(1)} async-done(((bf16[32,48,128]{2,1,0:T(8,128)(2,1)}), bf16[32,48,128]{2,1,0:T(8,128)(2,1)S(1)}, u32[]{:S(2)}, u32[]{:S(2)}) %all-to-all-start.2) | async-done | bytes 393248 | tf_op jit(solution)/shard_map/all_to_all | solution.py:64
  140.1 9.2 %all_to_all.25.grad_ref = bf16[8,32,128]{2,1,0:T(8,128)(2,1)S(1)} all-to-all(bf16[8,32,128]{2,1,0:T(8,128)(2,1)S(1)} %get-tuple-element.30), channel_id=1, replica_groups=mesh['section'=4,'seq'=8,'fsdp'=8] {'fsdp'}, dimensions={0} | all-to-all | bytes 131072 | tf_op jit(solution)/shard_map/all_to_all | solution.py:64
  150.2 13.4 %all_to_all.26.part_ref = bf16[8,48,128]{2,1,0:T(8,128)(2,1)S(1)} all-to-all(bf16[8,48,128]{2,1,0:T(8,128)(2,1)S(1)} %shard_map.136), channel_id=1, replica_groups=mesh['section'=4,'seq'=8,'fsdp'=8] {'seq'}, dimensions={0} | all-to-all | bytes 196608 | tf_op jit(solution)/shard_map/all_to_all | solution.py:64
  (71 shorter events, 19.2 us)
Async XLA Ops:
  3.7 26.7 %copy-start.1 = (bf16[32,5120]{1,0:T(8,128)(2,1)S(1)}, bf16[32,5120]{1,0:T(8,128)(2,1)}, u32[]{:S(2)}) copy-start(bf16[32,5120]{1,0:T(8,128)(2,1)} %feature_ref.1) | copy-start | bytes 983044
  3.7 26.7 %copy-start.3 = (s32[7]{0:T(128)S(1)}, s32[7]{0:T(128)}, u32[]{:S(2)}) copy-start(s32[7]{0:T(128)} %concatenate.3.where_ref) | copy-start | bytes 88
  8.2 18.6 %collective-permute-start.3 = (bf16[2256,128]{1,0:T(8,128)(2,1)}, bf16[2256,128]{1,0:T(8,128)(2,1)S(1)}, u32[]{:S(2)}, u32[]{:S(2)}) collective-permute-start(bf16[2256,128]{1,0:T(8,128)(2,1)} %get-tuple-element.18.refs_0_), channel_id=1, source_target_pairs={{0,56},{8,0},{16,8},{24,16},{32,24},{40,32},{48,40},{56,48},{1,57}... | collective-permute-start | bytes 1732616 | tf_op jit(solution)/shard_map/ppermute | solution.py:77
  14.1 16.2 %collective-permute-start = (bf16[2256,128]{1,0:T(8,128)(2,1)}, bf16[2256,128]{1,0:T(8,128)(2,1)S(1)}, u32[]{:S(2)}, u32[]{:S(2)}) collective-permute-start(bf16[2256,128]{1,0:T(8,128)(2,1)} %get-tuple-element.18.refs_0_), channel_id=1, source_target_pairs={{0,8},{8,16},{16,24},{24,32},{32,40},{40,48},{48,56},{56,0},{1,9},... | collective-permute-start | bytes 1732616 | tf_op jit(solution)/shard_map/ppermute | solution.py:76
  26.8 15.0 %collective-permute-start.4 = (bf16[2256,128]{1,0:T(8,128)(2,1)S(1)}, bf16[2256,128]{1,0:T(8,128)(2,1)}, u32[]{:S(2)}, u32[]{:S(2)}) collective-permute-start(bf16[2256,128]{1,0:T(8,128)(2,1)S(1)} %collective-permute-done.3.refs_4_), channel_id=1, source_target_pairs={{0,56},{8,0},{16,8},{24,16},{32,24},{40,32},{48,40},{56,48},{1,57}... | collective-permute-start | bytes 1732616 | tf_op jit(solution)/shard_map/ppermute | solution.py:77
  30.4 15.2 %collective-permute-start.1 = (bf16[2256,128]{1,0:T(8,128)(2,1)S(1)}, bf16[2256,128]{1,0:T(8,128)(2,1)}, u32[]{:S(2)}, u32[]{:S(2)}) collective-permute-start(bf16[2256,128]{1,0:T(8,128)(2,1)S(1)} %collective-permute-done.refs_1_), channel_id=1, source_target_pairs={{0,8},{8,16},{16,24},{24,32},{32,40},{40,48},{48,56},{56,0},{1,9},... | collective-permute-start | bytes 1732616 | tf_op jit(solution)/shard_map/ppermute | solution.py:76
  33.1 30.1 %copy-start = (f32[1,5,5120]{2,0,1:T(1,128)S(1)}, f32[1,5,5120]{2,0,1:T(1,128)}, u32[]{:S(2)}) copy-start(f32[1,5,5120]{2,0,1:T(1,128)} %param.15) | copy-start | bytes 307204
  33.1 17.7 %all-to-all-start = ((bf16[8,144,384]{2,1,0:T(8,128)(2,1)}), bf16[8,144,384]{2,1,0:T(8,128)(2,1)S(1)}, u32[]{:S(2)}, u32[]{:S(2)}) async-start(bf16[8,144,384]{2,1,0:T(8,128)(2,1)} %shard_map.133), calls=%async_computation | async-start | bytes 1769472 | tf_op jit(solution)/shard_map/all_to_all | solution.py:64
  41.8 17.6 %collective-permute-start.5 = (bf16[2256,128]{1,0:T(8,128)(2,1)}, bf16[2256,128]{1,0:T(8,128)(2,1)S(1)}, u32[]{:S(2)}, u32[]{:S(2)}) collective-permute-start(bf16[2256,128]{1,0:T(8,128)(2,1)} %collective-permute-done.4.refs_5_), channel_id=1, source_target_pairs={{0,56},{8,0},{16,8},{24,16},{32,24},{40,32},{48,40},{56,48},{1,57}... | collective-permute-start | bytes 1732616 | tf_op jit(solution)/shard_map/ppermute | solution.py:77
  45.6 17.5 %collective-permute-start.2 = (bf16[2256,128]{1,0:T(8,128)(2,1)}, bf16[2256,128]{1,0:T(8,128)(2,1)S(1)}, u32[]{:S(2)}, u32[]{:S(2)}) collective-permute-start(bf16[2256,128]{1,0:T(8,128)(2,1)} %collective-permute-done.1.refs_2_), channel_id=1, source_target_pairs={{0,8},{8,16},{16,24},{24,32},{32,40},{40,48},{48,56},{56,0},{1,9},... | collective-permute-start | bytes 1732616 | tf_op jit(solution)/shard_map/ppermute | solution.py:76
  50.9 22.7 %collective-permute-start.8 = (bf16[8,80,384]{2,1,0:T(8,128)(2,1)S(1)}, bf16[8,80,384]{2,1,0:T(8,128)(2,1)S(1)}, u32[]{:S(2)}, u32[]{:S(2)}) collective-permute-start(bf16[8,80,384]{2,1,0:T(8,128)(2,1)S(1)} %slice.27.refs_0_), channel_id=1, source_target_pairs={{0,8},{8,16},{16,24},{24,32},{32,40},{40,48},{48,56},{56,0},{1,9},... | collective-permute-start | bytes 1474568 | tf_op jit(solution)/shard_map/ppermute | solution.py:76
  51.0 22.6 %collective-permute-start.9 = (bf16[8,80,384]{2,1,0:T(8,128)(2,1)S(1)}, bf16[8,80,384]{2,1,0:T(8,128)(2,1)S(1)}, u32[]{:S(2)}, u32[]{:S(2)}) collective-permute-start(bf16[8,80,384]{2,1,0:T(8,128)(2,1)S(1)} %slice.27.refs_0_), channel_id=1, source_target_pairs={{0,56},{8,0},{16,8},{24,16},{32,24},{40,32},{48,40},{56,48},{1,57}... | collective-permute-start | bytes 1474568 | tf_op jit(solution)/shard_map/ppermute | solution.py:77
  59.5 20.2 %collective-permute-start.7 = (bf16[1136,128]{1,0:T(8,128)(2,1)S(1)}, bf16[1136,128]{1,0:T(8,128)(2,1)S(1)}, u32[]{:S(2)}, u32[]{:S(2)}) collective-permute-start(bf16[1136,128]{1,0:T(8,128)(2,1)S(1)} %slice.26), channel_id=1, source_target_pairs={{0,56},{8,0},{16,8},{24,16},{32,24},{40,32},{48,40},{56,48},{1,57}... | collective-permute-start | bytes 872456 | tf_op jit(solution)/shard_map/ppermute | solution.py:92
  63.2 16.5 %collective-permute-start.6 = (bf16[1120,128]{1,0:T(8,128)(2,1)S(1)}, bf16[1120,128]{1,0:T(8,128)(2,1)S(1)}, u32[]{:S(2)}, u32[]{:S(2)}) collective-permute-start(bf16[1120,128]{1,0:T(8,128)(2,1)S(1)} %slice.25), channel_id=1, source_target_pairs={{0,8},{8,16},{16,24},{24,32},{32,40},{40,48},{48,56},{56,0},{1,9},... | collective-permute-start | bytes 860168 | tf_op jit(solution)/shard_map/ppermute | solution.py:92
  73.6 15.4 %collective-permute-start.10 = (bf16[8,80,384]{2,1,0:T(8,128)(2,1)S(1)}, bf16[8,80,384]{2,1,0:T(8,128)(2,1)}, u32[]{:S(2)}, u32[]{:S(2)}) collective-permute-start(bf16[8,80,384]{2,1,0:T(8,128)(2,1)S(1)} %collective-permute-done.8.refs_1_), channel_id=1, source_target_pairs={{0,8},{8,16},{16,24},{24,32},{32,40},{40,48},{48,56},{56,0},{1,9},... | collective-permute-start | bytes 1474568 | tf_op jit(solution)/shard_map/ppermute | solution.py:76
  73.9 15.1 %collective-permute-start.11 = (bf16[8,80,384]{2,1,0:T(8,128)(2,1)S(1)}, bf16[8,80,384]{2,1,0:T(8,128)(2,1)}, u32[]{:S(2)}, u32[]{:S(2)}) collective-permute-start(bf16[8,80,384]{2,1,0:T(8,128)(2,1)S(1)} %collective-permute-done.9.refs_4_), channel_id=1, source_target_pairs={{0,56},{8,0},{16,8},{24,16},{32,24},{40,32},{48,40},{56,48},{1,57}... | collective-permute-start | bytes 1474568 | tf_op jit(solution)/shard_map/ppermute | solution.py:77
  88.9 23.1 %copy-start.12 = (bf16[256,64]{0,1:T(8,128)(2,1)S(1)}, bf16[256,64]{0,1:T(8,128)(2,1)}, u32[]{:S(2)}) copy-start(bf16[256,64]{0,1:T(8,128)(2,1)} %param.12) | copy-start | bytes 98308
  88.9 26.9 %copy-start.2 = (bf16[64,256]{1,0:T(8,128)(2,1)S(1)}, bf16[64,256]{1,0:T(8,128)(2,1)}, u32[]{:S(2)}) copy-start(bf16[64,256]{1,0:T(8,128)(2,1)} %get-tuple-element.17.own_ref) | copy-start | bytes 98308
  89.0 26.9 %all-to-all-start.1 = ((bf16[8,384,256]{2,1,0:T(8,128)(2,1)}), bf16[8,384,256]{2,1,0:T(8,128)(2,1)}, u32[]{:S(2)}, u32[]{:S(2)}) async-start(bf16[8,384,256]{2,1,0:T(8,128)(2,1)} %shard_map.132), calls=%async_computation.1 | async-start | bytes 3145728 | tf_op jit(solution)/shard_map/all_to_all | solution.py:64
  94.9 12.8 %collective-permute-start.12 = (bf16[8,80,384]{2,1,0:T(8,128)(2,1)}, bf16[8,80,384]{2,1,0:T(8,128)(2,1)S(1)}, u32[]{:S(2)}, u32[]{:S(2)}) collective-permute-start(bf16[8,80,384]{2,1,0:T(8,128)(2,1)} %collective-permute-done.10.refs_2_), channel_id=1, source_target_pairs={{0,8},{8,16},{16,24},{24,32},{32,40},{40,48},{48,56},{56,0},{1,9},... | collective-permute-start | bytes 1474568 | tf_op jit(solution)/shard_map/ppermute | solution.py:76
  94.9 12.9 %collective-permute-start.13 = (bf16[8,80,384]{2,1,0:T(8,128)(2,1)}, bf16[8,80,384]{2,1,0:T(8,128)(2,1)S(1)}, u32[]{:S(2)}, u32[]{:S(2)}) collective-permute-start(bf16[8,80,384]{2,1,0:T(8,128)(2,1)} %collective-permute-done.11.refs_5_), channel_id=1, source_target_pairs={{0,56},{8,0},{16,8},{24,16},{32,24},{40,32},{48,40},{56,48},{1,57}... | collective-permute-start | bytes 1474568 | tf_op jit(solution)/shard_map/ppermute | solution.py:77
  107.7 7.5 %collective-permute-start.14 = (bf16[4,80,384]{2,1,0:T(8,128)(2,1)S(1)}, bf16[4,80,384]{2,1,0:T(8,128)(2,1)S(1)}, u32[]{:S(2)}, u32[]{:S(2)}) collective-permute-start(bf16[4,80,384]{2,1,0:T(8,128)(2,1)S(1)} %slice.28), channel_id=1, source_target_pairs={{0,8},{8,16},{16,24},{24,32},{32,40},{40,48},{48,56},{56,0},{1,9},... | collective-permute-start | bytes 737288 | tf_op jit(solution)/shard_map/ppermute | solution.py:92
  108.7 7.2 %collective-permute-start.15 = (bf16[4,80,384]{2,1,0:T(8,128)(2,1)}, bf16[4,80,384]{2,1,0:T(8,128)(2,1)S(1)}, u32[]{:S(2)}, u32[]{:S(2)}) collective-permute-start(bf16[4,80,384]{2,1,0:T(8,128)(2,1)} %slice.29), channel_id=1, source_target_pairs={{0,56},{8,0},{16,8},{24,16},{32,24},{40,32},{48,40},{56,48},{1,57}... | collective-permute-start | bytes 737288 | tf_op jit(solution)/shard_map/ppermute | solution.py:92
  121.4 16.0 %all-to-all-start.2 = ((bf16[32,48,128]{2,1,0:T(8,128)(2,1)}), bf16[32,48,128]{2,1,0:T(8,128)(2,1)S(1)}, u32[]{:S(2)}, u32[]{:S(2)}) async-start(bf16[32,48,128]{2,1,0:T(8,128)(2,1)} %shard_map.134), calls=%async_computation.2 | async-start | bytes 786432 | tf_op jit(solution)/shard_map/all_to_all | solution.py:64
  (11 other events, 136.7 us)

commit v8 on v7

--- a/solution.py
+++ b/solution.py
@@ -56,10 +56,6 @@
     return 5.0 * remain / (1.0 + 4.0 * remain)
 
 
-def select_model(stacked, model_index):
-    return lax.dynamic_index_in_dim(stacked, model_index, 0, keepdims=False)
-
-
 def exchange(blocks, axis):
     return lax.all_to_all(blocks, axis, 0, 0, tiled=True)
 
@@ -100,13 +96,14 @@
 
 
 def prepare_kernel(
-    where_ref, embed_hbm, weight_hbm, shifts_hbm, student_hbm, previous_hbm, noise_hbm, context_hbm, *refs
+    steps_ref, embed_hbm, weight_hbm, shifts_hbm, student_hbm, previous_hbm, noise_hbm, context_hbm, *refs
 ):
     out_ref, plain_ref, embed_ref, weight_ref, shifts_ref, student_ref, previous_ref, noise_ref, context_ref, sems = refs
     latent_dim, width = embed_ref.shape[1:]
     parts, depth, feat = weight_ref.shape[1:]
     rows = student_ref.shape[1]
-    model = pl.ds(where_ref[0], 1)
+    section, me_seq = lax.axis_index("section"), lax.axis_index("seq")
+    model = pl.ds(jnp.where(section >= 2, section - 1, section), 1)
     sources = (embed_hbm.at[model], shifts_hbm, student_hbm, previous_hbm, noise_hbm, weight_hbm.at[model], context_hbm)
     targets = (embed_ref, shifts_ref, student_ref, previous_ref, noise_ref, weight_ref, context_ref)
     copies = [pltpu.make_async_copy(a, b, sems.at[n]) for n, (a, b) in enumerate(zip(sources, targets))]
@@ -114,9 +111,9 @@
         copy.start()
     for copy in copies[:5]:
         copy.wait()
-    level = noise_levels(jnp.full((1, rows), where_ref[5], jnp.int32))
+    level = noise_levels(jnp.full((1, rows), steps_ref[1], jnp.int32))
     noised = (1.0 - level) * previous_ref[...].astype(f32) + level * noise_ref[...].astype(f32)
-    latents = jnp.where(where_ref[3] == 0, student_ref[...].astype(f32), noised.astype(bf16).astype(f32))
+    latents = jnp.where(section == 0, student_ref[...].astype(f32), noised.astype(bf16).astype(f32))
 
     step = 1024
     row_sum = jnp.zeros((latent_dim, 1), f32)
@@ -139,7 +136,7 @@
     plain_ref[...] = plain
     for copy in copies[5:]:
         copy.wait()
-    here = pl.ds(pl.multiple_of(where_ref[1] * depth, 128), depth)
+    here = pl.ds(pl.multiple_of(me_seq * depth, 128), depth)
     centred = (embed_ref[0, :, here].astype(f32) - row_mean) * (1.0 + shifts_ref[1, :, here])
     shift = jnp.broadcast_to(shifts_ref[0, :, here], (16, depth))
     folded = jnp.concatenate([centred, shift], axis=0).astype(bf16)
@@ -154,8 +151,8 @@
     out_ref[tail + rows // 128 * latent_dim :] = jnp.concatenate(lines + [spare], axis=0).astype(bf16)
     for h in range(heads):
         cols = slice(h * 128, (h + 1) * 128)
-        out_ref[h * rows : (h + 1) * rows] = context_ref[:rows, cols]
-        values = context_ref[rows:, cols].astype(f32).T.astype(bf16)
+        out_ref[h * rows : (h + 1) * rows] = context_ref[:, 0, cols]
+        values = context_ref[:, 1, cols].astype(f32).T.astype(bf16)
         for n in range(rows // 128):
             at = heads * rows + h * rows + n * 128
             out_ref[at : at + 128] = values[:, n * 128 : (n + 1) * 128]
@@ -427,7 +424,7 @@
     lines = (2 * rows + 3 * latent_dim) * heads + rows // 128 * latent_dim + 16
     own, plain = run(
         prepare_kernel,
-        where,
+        timesteps,
         [((lines, HEAD_DIM), bf16), ((latent_dim, rows), bf16)],
         in_weight,
         qkv_weight.transpose(0, 2, 1, 3),
@@ -435,7 +432,7 @@
         student_input.T,
         previous_latent.T,
         score_noise.T,
-        kv_cache[0].transpose(1, 0, 2).reshape(2 * rows, feat),
+        kv_cache[0],
         raw=range(7),
         scratch=[
             pltpu.VMEM((1, latent_dim, width), bf16),
@@ -444,7 +441,7 @@
             pltpu.VMEM((latent_dim, rows), bf16),
             pltpu.VMEM((latent_dim, rows), bf16),
             pltpu.VMEM((latent_dim, rows), bf16),
-            pltpu.VMEM((2 * rows, feat), bf16),
+            pltpu.VMEM((rows, 2, feat), bf16),
             pltpu.SemaphoreType.DMA((7,)),
         ],
         room=60,

time: 166 us -> 164 us (0.988)
  local copies, waits for them, and re-layouts: 5.06 us -> 2.1 us
    transpose x1 -> x0, local copies, waits for them, and re-layouts: 1.78 us -> none  [per_device(): kv_cache[0].transpose(1, 0, 2).reshape(2 * rows, feat)]
where the time goes in v8:
time: 164 us; the launch traced here: 163 us
  waiting for transfers between devices  56.3 us (34%)
  starting transfers between devices  49.5 us (30%)
  Pallas kernels  30.3 us (18%)
  blocking collectives  22.6 us (14%)
  local copies, waits for them, and re-layouts  2.1 us (1%)
    pallas_call x8, Pallas kernels, run(): pl.pallas_call(kernel, grid_spec=pltpu.PrefetchScalarGridSpec(num_scalar_...  30.3 us
    ppermute x6, starting transfers between devices, step(): self.ahead.append(lax.ppermute(self.ahead[-1], self.axis, self.down))  23 us
    all_to_all x2, blocking collectives, exchange(): return lax.all_to_all(blocks, axis, 0, 0, tiled=True)  22.6 us
    ppermute x6, waiting for transfers between devices, step(): self.ahead.append(lax.ppermute(self.ahead[-1], self.axis, self.down))  20.4 us
    all_to_all x3, starting transfers between devices, exchange(): return lax.all_to_all(blocks, axis, 0, 0, tiled=True)  19.3 us
    ppermute x6, waiting for transfers between devices, step(): self.behind.append(lax.ppermute(self.behind[-1], self.axis, self.up))  17.4 us
    all_to_all x3, waiting for transfers between devices, exchange(): return lax.all_to_all(blocks, axis, 0, 0, tiled=True)  11.7 us
    ppermute x2, starting transfers between devices, finish(): lax.ppermute(second, self.axis, self.down)  6.83 us
  transfers between devices with their start and end apart: 19, of which 10 were waited for; matrix products, arithmetic and copies ran while one was open for 2% of the time, Pallas kernels for 9%

profile of v8, /device:TPU:2, one launch (start us, length us, event | category | flops | bytes accessed | tf_op | source)
XLA Modules:
  0.0 163.0 jit_solution(11401146881630653268)
XLA Ops:
  0.7 5.7 %shard_map.130 = (bf16[2256,128]{1,0:T(8,128)(2,1)}, bf16[64,256]{1,0:T(8,128)(2,1)}) custom-call(s32[3]{0:T(128)} %steps_ref.1, bf16[3,64,5120]{2,1,0:T(8,128)(2,1)} %embed_ref.1, bf16[3,3,640,384]{3,2,1,0:T(8,128)(2,1)} %bitcast.15, f32[5,1,5120]{2,1,0:T(1,128)} %bitcast.13, bf16[64,256]{1,0:T(8,128)(2,1)} %bitcast.18, bf16[64,256]{1,0:T(8,128)(2,1)} %bitcast.19, ...), custom_call_target="tpu_custom_call" | custom-call | tf_op jit(solution)/shard_map/pallas_call | solution.py:34
  6.4 5.9 %collective-permute-start.3 = (bf16[2256,128]{1,0:T(8,128)(2,1)}, bf16[2256,128]{1,0:T(8,128)(2,1)S(1)}, u32[]{:S(2)}, u32[]{:S(2)}) collective-permute-start(bf16[2256,128]{1,0:T(8,128)(2,1)} %get-tuple-element.18.refs_0_), channel_id=1, source_target_pairs={{0,56},{8,0},{16,8},{24,16},{32,24},{40,32},{48,40},{56,48},{1,57}... | collective-permute-start | bytes 1732616 | tf_op jit(solution)/shard_map/ppermute | solution.py:73
  12.3 12.6 %collective-permute-done.3.refs_4_ = bf16[2256,128]{1,0:T(8,128)(2,1)S(1)} collective-permute-done((bf16[2256,128]{1,0:T(8,128)(2,1)}, bf16[2256,128]{1,0:T(8,128)(2,1)S(1)}, u32[]{:S(2)}, u32[]{:S(2)}) %collective-permute-start.3) | collective-permute-done | bytes 577568 | tf_op jit(solution)/shard_map/ppermute | solution.py:73
  24.9 3.6 %collective-permute-start.4 = (bf16[2256,128]{1,0:T(8,128)(2,1)S(1)}, bf16[2256,128]{1,0:T(8,128)(2,1)}, u32[]{:S(2)}, u32[]{:S(2)}) collective-permute-start(bf16[2256,128]{1,0:T(8,128)(2,1)S(1)} %collective-permute-done.3.refs_4_), channel_id=1, source_target_pairs={{0,56},{8,0},{16,8},{24,16},{32,24},{40,32},{48,40},{56,48},{1,57}... | collective-permute-start | bytes 1732616 | tf_op jit(solution)/shard_map/ppermute | solution.py:73
  31.4 6.1 %all-to-all-start = ((bf16[8,144,384]{2,1,0:T(8,128)(2,1)}), bf16[8,144,384]{2,1,0:T(8,128)(2,1)S(1)}, u32[]{:S(2)}, u32[]{:S(2)}) async-start(bf16[8,144,384]{2,1,0:T(8,128)(2,1)} %shard_map.133), calls=%async_computation | async-start | bytes 1769472 | tf_op jit(solution)/shard_map/all_to_all | solution.py:60
  40.0 3.8 %collective-permute-start.5 = (bf16[2256,128]{1,0:T(8,128)(2,1)}, bf16[2256,128]{1,0:T(8,128)(2,1)S(1)}, u32[]{:S(2)}, u32[]{:S(2)}) collective-permute-start(bf16[2256,128]{1,0:T(8,128)(2,1)} %collective-permute-done.4.refs_5_), channel_id=1, source_target_pairs={{0,56},{8,0},{16,8},{24,16},{32,24},{40,32},{48,40},{56,48},{1,57}... | collective-permute-start | bytes 1732616 | tf_op jit(solution)/shard_map/ppermute | solution.py:73
  43.8 5.3 %all-to-all-done.feature_ref = bf16[8,144,384]{2,1,0:T(8,128)(2,1)S(1)} async-done(((bf16[8,144,384]{2,1,0:T(8,128)(2,1)}), bf16[8,144,384]{2,1,0:T(8,128)(2,1)S(1)}, u32[]{:S(2)}, u32[]{:S(2)}) %all-to-all-start) | async-done | bytes 884768 | tf_op jit(solution)/shard_map/all_to_all | solution.py:60
  49.2 3.2 %collective-permute-start.9 = (bf16[8,80,384]{2,1,0:T(8,128)(2,1)S(1)}, bf16[8,80,384]{2,1,0:T(8,128)(2,1)S(1)}, u32[]{:S(2)}, u32[]{:S(2)}) collective-permute-start(bf16[8,80,384]{2,1,0:T(8,128)(2,1)S(1)} %slice.27.refs_0_), channel_id=1, source_target_pairs={{0,56},{8,0},{16,8},{24,16},{32,24},{40,32},{48,40},{56,48},{1,57}... | collective-permute-start | bytes 1474568 | tf_op jit(solution)/shard_map/ppermute | solution.py:73
  52.4 5.2 %collective-permute-done.5.refs_6_ = bf16[2256,128]{1,0:T(8,128)(2,1)S(1)} collective-permute-done((bf16[2256,128]{1,0:T(8,128)(2,1)}, bf16[2256,128]{1,0:T(8,128)(2,1)S(1)}, u32[]{:S(2)}, u32[]{:S(2)}) %collective-permute-start.5) | collective-permute-done | bytes 577568 | tf_op jit(solution)/shard_map/ppermute | solution.py:73
  57.6 3.7 %collective-permute-start.7 = (bf16[1136,128]{1,0:T(8,128)(2,1)S(1)}, bf16[1136,128]{1,0:T(8,128)(2,1)S(1)}, u32[]{:S(2)}, u32[]{:S(2)}) collective-permute-start(bf16[1136,128]{1,0:T(8,128)(2,1)S(1)} %slice.26), channel_id=1, source_target_pairs={{0,56},{8,0},{16,8},{24,16},{32,24},{40,32},{48,40},{56,48},{1,57}... | collective-permute-start | bytes 872456 | tf_op jit(solution)/shard_map/ppermute | solution.py:88
  63.8 7.9 %collective-permute-done.8.refs_1_ = bf16[8,80,384]{2,1,0:T(8,128)(2,1)S(1)} collective-permute-done((bf16[8,80,384]{2,1,0:T(8,128)(2,1)S(1)}, bf16[8,80,384]{2,1,0:T(8,128)(2,1)S(1)}, u32[]{:S(2)}, u32[]{:S(2)}) %collective-permute-start.8) | collective-permute-done | bytes 491552 | tf_op jit(solution)/shard_map/ppermute | solution.py:72
  71.8 3.2 %collective-permute-start.11 = (bf16[8,80,384]{2,1,0:T(8,128)(2,1)S(1)}, bf16[8,80,384]{2,1,0:T(8,128)(2,1)}, u32[]{:S(2)}, u32[]{:S(2)}) collective-permute-start(bf16[8,80,384]{2,1,0:T(8,128)(2,1)S(1)} %collective-permute-done.9.refs_4_), channel_id=1, source_target_pairs={{0,56},{8,0},{16,8},{24,16},{32,24},{40,32},{48,40},{56,48},{1,57}... | collective-permute-start | bytes 1474568 | tf_op jit(solution)/shard_map/ppermute | solution.py:73
  75.0 2.8 %collective-permute-done.6.refs_7_ = bf16[1120,128]{1,0:T(8,128)(2,1)S(1)} collective-permute-done((bf16[1120,128]{1,0:T(8,128)(2,1)S(1)}, bf16[1120,128]{1,0:T(8,128)(2,1)S(1)}, u32[]{:S(2)}, u32[]{:S(2)}) %collective-permute-start.6) | collective-permute-done | bytes 286752 | tf_op jit(solution)/shard_map/ppermute | solution.py:88
  77.9 9.1 %shard_map.132 = bf16[8,384,256]{2,1,0:T(8,128)(2,1)} custom-call(s32[7]{0:T(128)S(1)} %concatenate.3.where_ref, bf16[2256,128]{1,0:T(8,128)(2,1)S(1)} %copy-done.3, bf16[2256,128]{1,0:T(8,128)(2,1)S(1)} %collective-permute-done.refs_1_, bf16[2256,128]{1,0:T(8,128)(2,1)} %collective-permute-done.1.refs_2_, bf16[2256,128]{1,0:T(8,128)(2,1)} %copy-done.9, ...), custom_call_target="tpu_custom_call" | custom-call | flops 11000000512 | bytes 20000000 | tf_op jit(solution)/shard_map/pallas_call | solution.py:34
  87.1 5.9 %all-to-all-start.1 = ((bf16[8,384,256]{2,1,0:T(8,128)(2,1)}), bf16[8,384,256]{2,1,0:T(8,128)(2,1)}, u32[]{:S(2)}, u32[]{:S(2)}) async-start(bf16[8,384,256]{2,1,0:T(8,128)(2,1)} %shard_map.132), calls=%async_computation.1 | async-start | bytes 3145728 | tf_op jit(solution)/shard_map/all_to_all | solution.py:60
  93.0 3.2 %collective-permute-start.13 = (bf16[8,80,384]{2,1,0:T(8,128)(2,1)}, bf16[8,80,384]{2,1,0:T(8,128)(2,1)S(1)}, u32[]{:S(2)}, u32[]{:S(2)}) collective-permute-start(bf16[8,80,384]{2,1,0:T(8,128)(2,1)} %collective-permute-done.11.refs_5_), channel_id=1, source_target_pairs={{0,56},{8,0},{16,8},{24,16},{32,24},{40,32},{48,40},{56,48},{1,57}... | collective-permute-start | bytes 1474568 | tf_op jit(solution)/shard_map/ppermute | solution.py:73
  96.2 9.5 %collective-permute-done.12.refs_3_ = bf16[8,80,384]{2,1,0:T(8,128)(2,1)S(1)} collective-permute-done((bf16[8,80,384]{2,1,0:T(8,128)(2,1)}, bf16[8,80,384]{2,1,0:T(8,128)(2,1)S(1)}, u32[]{:S(2)}, u32[]{:S(2)}) %collective-permute-start.12) | collective-permute-done | bytes 491552 | tf_op jit(solution)/shard_map/ppermute | solution.py:72
  106.7 3.2 %collective-permute-start.15 = (bf16[4,80,384]{2,1,0:T(8,128)(2,1)}, bf16[4,80,384]{2,1,0:T(8,128)(2,1)S(1)}, u32[]{:S(2)}, u32[]{:S(2)}) collective-permute-start(bf16[4,80,384]{2,1,0:T(8,128)(2,1)} %slice.29), channel_id=1, source_target_pairs={{0,56},{8,0},{16,8},{24,16},{32,24},{40,32},{48,40},{56,48},{1,57}... | collective-permute-start | bytes 737288 | tf_op jit(solution)/shard_map/ppermute | solution.py:88
  109.8 3.4 %collective-permute-done.14.refs_7_ = bf16[4,80,384]{2,1,0:T(8,128)(2,1)S(1)} collective-permute-done((bf16[4,80,384]{2,1,0:T(8,128)(2,1)S(1)}, bf16[4,80,384]{2,1,0:T(8,128)(2,1)S(1)}, u32[]{:S(2)}, u32[]{:S(2)}) %collective-permute-start.14) | collective-permute-done | bytes 245792 | tf_op jit(solution)/shard_map/ppermute | solution.py:88
  113.9 5.5 %shard_map.134 = bf16[32,48,128]{2,1,0:T(8,128)(2,1)} custom-call(s32[7]{0:T(128)S(1)} %concatenate.3.where_ref, bf16[64,256]{1,0:T(8,128)(2,1)S(1)} %copy-done.2, bf16[64,640]{1,0:T(8,128)(2,1)S(1)} %get-tuple-element.20.embed_ref, f32[5,1,640]{2,1,0:T(1,128)S(1)} %get-tuple-element.21.shifts_ref, bf16[64,640]{1,0:T(8,128)(2,1)S(1)} %get-tuple-element.22.head_ref, ...), custom_call_target="tpu_custom_call" | custom-call | tf_op jit(solution)/shard_map/pallas_call | solution.py:34
  119.5 7.3 %all-to-all-start.2 = ((bf16[32,48,128]{2,1,0:T(8,128)(2,1)}), bf16[32,48,128]{2,1,0:T(8,128)(2,1)S(1)}, u32[]{:S(2)}, u32[]{:S(2)}) async-start(bf16[32,48,128]{2,1,0:T(8,128)(2,1)} %shard_map.134), calls=%async_computation.2 | async-start | bytes 786432 | tf_op jit(solution)/shard_map/all_to_all | solution.py:60
  129.1 6.4 %all-to-all-done.2.partial_ref = bf16[32,48,128]{2,1,0:T(8,128)(2,1)S(1)} async-done(((bf16[32,48,128]{2,1,0:T(8,128)(2,1)}), bf16[32,48,128]{2,1,0:T(8,128)(2,1)S(1)}, u32[]{:S(2)}, u32[]{:S(2)}) %all-to-all-start.2) | async-done | bytes 393248 | tf_op jit(solution)/shard_map/all_to_all | solution.py:60
  138.2 9.2 %all_to_all.25.grad_ref = bf16[8,32,128]{2,1,0:T(8,128)(2,1)S(1)} all-to-all(bf16[8,32,128]{2,1,0:T(8,128)(2,1)S(1)} %get-tuple-element.30), channel_id=1, replica_groups=mesh['section'=4,'seq'=8,'fsdp'=8] {'fsdp'}, dimensions={0} | all-to-all | bytes 131072 | tf_op jit(solution)/shard_map/all_to_all | solution.py:60
  148.3 13.4 %all_to_all.26.part_ref = bf16[8,48,128]{2,1,0:T(8,128)(2,1)S(1)} all-to-all(bf16[8,48,128]{2,1,0:T(8,128)(2,1)S(1)} %shard_map.136), channel_id=1, replica_groups=mesh['section'=4,'seq'=8,'fsdp'=8] {'seq'}, dimensions={0} | all-to-all | bytes 196608 | tf_op jit(solution)/shard_map/all_to_all | solution.py:60
  (68 shorter events, 16.2 us)
Async XLA Ops:
  0.6 27.9 %copy-start.13 = (s32[3]{0:T(128)S(1)}, s32[3]{0:T(128)}, u32[]{:S(2)}) copy-start(s32[3]{0:T(128)} %steps_ref.1) | copy-start | bytes 40
  0.6 28.0 %copy-start.1 = (bf16[32,5120]{1,0:T(8,128)(2,1)S(1)}, bf16[32,5120]{1,0:T(8,128)(2,1)}, u32[]{:S(2)}) copy-start(bf16[32,5120]{1,0:T(8,128)(2,1)} %feature_ref.1) | copy-start | bytes 983044
  6.4 18.6 %collective-permute-start.3 = (bf16[2256,128]{1,0:T(8,128)(2,1)}, bf16[2256,128]{1,0:T(8,128)(2,1)S(1)}, u32[]{:S(2)}, u32[]{:S(2)}) collective-permute-start(bf16[2256,128]{1,0:T(8,128)(2,1)} %get-tuple-element.18.refs_0_), channel_id=1, source_target_pairs={{0,56},{8,0},{16,8},{24,16},{32,24},{40,32},{48,40},{56,48},{1,57}... | collective-permute-start | bytes 1732616 | tf_op jit(solution)/shard_map/ppermute | solution.py:73
  12.3 16.2 %collective-permute-start = (bf16[2256,128]{1,0:T(8,128)(2,1)}, bf16[2256,128]{1,0:T(8,128)(2,1)S(1)}, u32[]{:S(2)}, u32[]{:S(2)}) collective-permute-start(bf16[2256,128]{1,0:T(8,128)(2,1)} %get-tuple-element.18.refs_0_), channel_id=1, source_target_pairs={{0,8},{8,16},{16,24},{24,32},{32,40},{40,48},{48,56},{56,0},{1,9},... | collective-permute-start | bytes 1732616 | tf_op jit(solution)/shard_map/ppermute | solution.py:72
  24.9 15.0 %collective-permute-start.4 = (bf16[2256,128]{1,0:T(8,128)(2,1)S(1)}, bf16[2256,128]{1,0:T(8,128)(2,1)}, u32[]{:S(2)}, u32[]{:S(2)}) collective-permute-start(bf16[2256,128]{1,0:T(8,128)(2,1)S(1)} %collective-permute-done.3.refs_4_), channel_id=1, source_target_pairs={{0,56},{8,0},{16,8},{24,16},{32,24},{40,32},{48,40},{56,48},{1,57}... | collective-permute-start | bytes 1732616 | tf_op jit(solution)/shard_map/ppermute | solution.py:73
  28.5 15.2 %collective-permute-start.1 = (bf16[2256,128]{1,0:T(8,128)(2,1)S(1)}, bf16[2256,128]{1,0:T(8,128)(2,1)}, u32[]{:S(2)}, u32[]{:S(2)}) collective-permute-start(bf16[2256,128]{1,0:T(8,128)(2,1)S(1)} %collective-permute-done.refs_1_), channel_id=1, source_target_pairs={{0,8},{8,16},{16,24},{24,32},{32,40},{40,48},{48,56},{56,0},{1,9},... | collective-permute-start | bytes 1732616 | tf_op jit(solution)/shard_map/ppermute | solution.py:72
  31.4 30.0 %copy-start = (f32[1,5,5120]{2,0,1:T(1,128)S(1)}, f32[1,5,5120]{2,0,1:T(1,128)}, u32[]{:S(2)}) copy-start(f32[1,5,5120]{2,0,1:T(1,128)} %param.15) | copy-start | bytes 307204
  31.4 17.7 %all-to-all-start = ((bf16[8,144,384]{2,1,0:T(8,128)(2,1)}), bf16[8,144,384]{2,1,0:T(8,128)(2,1)S(1)}, u32[]{:S(2)}, u32[]{:S(2)}) async-start(bf16[8,144,384]{2,1,0:T(8,128)(2,1)} %shard_map.133), calls=%async_computation | async-start | bytes 1769472 | tf_op jit(solution)/shard_map/all_to_all | solution.py:60
  40.0 17.6 %collective-permute-start.5 = (bf16[2256,128]{1,0:T(8,128)(2,1)}, bf16[2256,128]{1,0:T(8,128)(2,1)S(1)}, u32[]{:S(2)}, u32[]{:S(2)}) collective-permute-start(bf16[2256,128]{1,0:T(8,128)(2,1)} %collective-permute-done.4.refs_5_), channel_id=1, source_target_pairs={{0,56},{8,0},{16,8},{24,16},{32,24},{40,32},{48,40},{56,48},{1,57}... | collective-permute-start | bytes 1732616 | tf_op jit(solution)/shard_map/ppermute | solution.py:73
  43.8 17.5 %collective-permute-start.2 = (bf16[2256,128]{1,0:T(8,128)(2,1)}, bf16[2256,128]{1,0:T(8,128)(2,1)S(1)}, u32[]{:S(2)}, u32[]{:S(2)}) collective-permute-start(bf16[2256,128]{1,0:T(8,128)(2,1)} %collective-permute-done.1.refs_2_), channel_id=1, source_target_pairs={{0,8},{8,16},{16,24},{24,32},{32,40},{40,48},{48,56},{56,0},{1,9},... | collective-permute-start | bytes 1732616 | tf_op jit(solution)/shard_map/ppermute | solution.py:72
  49.1 22.6 %collective-permute-start.8 = (bf16[8,80,384]{2,1,0:T(8,128)(2,1)S(1)}, bf16[8,80,384]{2,1,0:T(8,128)(2,1)S(1)}, u32[]{:S(2)}, u32[]{:S(2)}) collective-permute-start(bf16[8,80,384]{2,1,0:T(8,128)(2,1)S(1)} %slice.27.refs_0_), channel_id=1, source_target_pairs={{0,8},{8,16},{16,24},{24,32},{32,40},{40,48},{48,56},{56,0},{1,9},... | collective-permute-start | bytes 1474568 | tf_op jit(solution)/shard_map/ppermute | solution.py:72
  49.2 22.5 %collective-permute-start.9 = (bf16[8,80,384]{2,1,0:T(8,128)(2,1)S(1)}, bf16[8,80,384]{2,1,0:T(8,128)(2,1)S(1)}, u32[]{:S(2)}, u32[]{:S(2)}) collective-permute-start(bf16[8,80,384]{2,1,0:T(8,128)(2,1)S(1)} %slice.27.refs_0_), channel_id=1, source_target_pairs={{0,56},{8,0},{16,8},{24,16},{32,24},{40,32},{48,40},{56,48},{1,57}... | collective-permute-start | bytes 1474568 | tf_op jit(solution)/shard_map/ppermute | solution.py:73
  57.6 20.2 %collective-permute-start.7 = (bf16[1136,128]{1,0:T(8,128)(2,1)S(1)}, bf16[1136,128]{1,0:T(8,128)(2,1)S(1)}, u32[]{:S(2)}, u32[]{:S(2)}) collective-permute-start(bf16[1136,128]{1,0:T(8,128)(2,1)S(1)} %slice.26), channel_id=1, source_target_pairs={{0,56},{8,0},{16,8},{24,16},{32,24},{40,32},{48,40},{56,48},{1,57}... | collective-permute-start | bytes 872456 | tf_op jit(solution)/shard_map/ppermute | solution.py:88
  61.3 16.5 %collective-permute-start.6 = (bf16[1120,128]{1,0:T(8,128)(2,1)S(1)}, bf16[1120,128]{1,0:T(8,128)(2,1)S(1)}, u32[]{:S(2)}, u32[]{:S(2)}) collective-permute-start(bf16[1120,128]{1,0:T(8,128)(2,1)S(1)} %slice.25), channel_id=1, source_target_pairs={{0,8},{8,16},{16,24},{24,32},{32,40},{40,48},{48,56},{56,0},{1,9},... | collective-permute-start | bytes 860168 | tf_op jit(solution)/shard_map/ppermute | solution.py:88
  61.4 16.5 %copy-start.3 = (bf16[2256,128]{1,0:T(8,128)(2,1)S(1)}, bf16[2256,128]{1,0:T(8,128)(2,1)}, u32[]{:S(2)}) copy-start(bf16[2256,128]{1,0:T(8,128)(2,1)} %get-tuple-element.18.refs_0_) | copy-start | bytes 1732612
  71.7 15.3 %collective-permute-start.10 = (bf16[8,80,384]{2,1,0:T(8,128)(2,1)S(1)}, bf16[8,80,384]{2,1,0:T(8,128)(2,1)}, u32[]{:S(2)}, u32[]{:S(2)}) collective-permute-start(bf16[8,80,384]{2,1,0:T(8,128)(2,1)S(1)} %collective-permute-done.8.refs_1_), channel_id=1, source_target_pairs={{0,8},{8,16},{16,24},{24,32},{32,40},{40,48},{48,56},{56,0},{1,9},... | collective-permute-start | bytes 1474568 | tf_op jit(solution)/shard_map/ppermute | solution.py:72
  71.8 15.2 %collective-permute-start.11 = (bf16[8,80,384]{2,1,0:T(8,128)(2,1)S(1)}, bf16[8,80,384]{2,1,0:T(8,128)(2,1)}, u32[]{:S(2)}, u32[]{:S(2)}) collective-permute-start(bf16[8,80,384]{2,1,0:T(8,128)(2,1)S(1)} %collective-permute-done.9.refs_4_), channel_id=1, source_target_pairs={{0,56},{8,0},{16,8},{24,16},{32,24},{40,32},{48,40},{56,48},{1,57}... | collective-permute-start | bytes 1474568 | tf_op jit(solution)/shard_map/ppermute | solution.py:73
  87.0 26.9 %copy-start.2 = (bf16[64,256]{1,0:T(8,128)(2,1)S(1)}, bf16[64,256]{1,0:T(8,128)(2,1)}, u32[]{:S(2)}) copy-start(bf16[64,256]{1,0:T(8,128)(2,1)} %get-tuple-element.17.own_ref) | copy-start | bytes 98308
  87.1 26.8 %all-to-all-start.1 = ((bf16[8,384,256]{2,1,0:T(8,128)(2,1)}), bf16[8,384,256]{2,1,0:T(8,128)(2,1)}, u32[]{:S(2)}, u32[]{:S(2)}) async-start(bf16[8,384,256]{2,1,0:T(8,128)(2,1)} %shard_map.132), calls=%async_computation.1 | async-start | bytes 3145728 | tf_op jit(solution)/shard_map/all_to_all | solution.py:60
  93.0 12.7 %collective-permute-start.12 = (bf16[8,80,384]{2,1,0:T(8,128)(2,1)}, bf16[8,80,384]{2,1,0:T(8,128)(2,1)S(1)}, u32[]{:S(2)}, u32[]{:S(2)}) collective-permute-start(bf16[8,80,384]{2,1,0:T(8,128)(2,1)} %collective-permute-done.10.refs_2_), channel_id=1, source_target_pairs={{0,8},{8,16},{16,24},{24,32},{32,40},{40,48},{48,56},{56,0},{1,9},... | collective-permute-start | bytes 1474568 | tf_op jit(solution)/shard_map/ppermute | solution.py:72
  93.0 12.8 %collective-permute-start.13 = (bf16[8,80,384]{2,1,0:T(8,128)(2,1)}, bf16[8,80,384]{2,1,0:T(8,128)(2,1)S(1)}, u32[]{:S(2)}, u32[]{:S(2)}) collective-permute-start(bf16[8,80,384]{2,1,0:T(8,128)(2,1)} %collective-permute-done.11.refs_5_), channel_id=1, source_target_pairs={{0,56},{8,0},{16,8},{24,16},{32,24},{40,32},{48,40},{56,48},{1,57}... | collective-permute-start | bytes 1474568 | tf_op jit(solution)/shard_map/ppermute | solution.py:73
  105.7 7.5 %collective-permute-start.14 = (bf16[4,80,384]{2,1,0:T(8,128)(2,1)S(1)}, bf16[4,80,384]{2,1,0:T(8,128)(2,1)S(1)}, u32[]{:S(2)}, u32[]{:S(2)}) collective-permute-start(bf16[4,80,384]{2,1,0:T(8,128)(2,1)S(1)} %slice.28), channel_id=1, source_target_pairs={{0,8},{8,16},{16,24},{24,32},{32,40},{40,48},{48,56},{56,0},{1,9},... | collective-permute-start | bytes 737288 | tf_op jit(solution)/shard_map/ppermute | solution.py:88
  106.7 7.2 %collective-permute-start.15 = (bf16[4,80,384]{2,1,0:T(8,128)(2,1)}, bf16[4,80,384]{2,1,0:T(8,128)(2,1)S(1)}, u32[]{:S(2)}, u32[]{:S(2)}) collective-permute-start(bf16[4,80,384]{2,1,0:T(8,128)(2,1)} %slice.29), channel_id=1, source_target_pairs={{0,56},{8,0},{16,8},{24,16},{32,24},{40,32},{48,40},{56,48},{1,57}... | collective-permute-start | bytes 737288 | tf_op jit(solution)/shard_map/ppermute | solution.py:88
  119.5 16.1 %all-to-all-start.2 = ((bf16[32,48,128]{2,1,0:T(8,128)(2,1)}), bf16[32,48,128]{2,1,0:T(8,128)(2,1)S(1)}, u32[]{:S(2)}, u32[]{:S(2)}) async-start(bf16[32,48,128]{2,1,0:T(8,128)(2,1)} %shard_map.134), calls=%async_computation.2 | async-start | bytes 786432 | tf_op jit(solution)/shard_map/all_to_all | solution.py:60
  (10 other events, 101.4 us)

commit v9 on v8

--- a/solution.py
+++ b/solution.py
@@ -172,7 +172,8 @@
         out_ref[j, slot + rows :] = joined[:, feat:]
 
 
-def columns_kernel(where_ref, embed_ref, head_ref, shifts_ref, embed_out, head_out, shifts_out):
+def columns_kernel(where_ref, embed_ref, head_ref, shifts_ref, plain_ref, *refs):
+    hidden_out, gate_out, scaled_out, extra_out, embed_out, head_out, shifts_out = refs
     count = 8
     part = embed_ref.shape[2] // count
     slot = part // count
@@ -191,6 +192,21 @@
                     block = source[:, pl.ds(pl.multiple_of(owner * part, 128), part)]
                     pieces.append(block[:, f * slot : (f + 1) * slot])
                 target[...] = jnp.concatenate(pieces, axis=1)
+
+    latent_dim = embed_out.shape[0]
+    hidden_out[...] = dot(embed_out[...], plain_ref[...], ((0,), (0,)))
+    gate_out[...] = jnp.broadcast_to(shifts_out[2], (128, shifts_out.shape[2])).T
+    plain_head = head_out[...].astype(f32)
+    head = (plain_head * (1.0 + shifts_out[4])).astype(bf16)
+    scaled_out[...] = head
+    sums = jnp.sum(head.astype(f32), axis=1, keepdims=True)
+    consts = jnp.sum(plain_head * shifts_out[3], axis=1, keepdims=True)
+    place = lax.broadcasted_iota(jnp.int32, (latent_dim, 128), 1)
+    extra = jnp.zeros((latent_dim, 128), f32)
+    for n, column in enumerate(halves(sums) + halves(consts)):
+        extra = jnp.where(place == n, column, extra)
+    extra = jnp.concatenate([extra, jnp.zeros_like(extra)], axis=0).T
+    extra_out[...] = extra[:16].astype(bf16)
 
 
 def fold_keys(heads, carry, queries, keys, values):
@@ -297,33 +313,24 @@
     return high, value - high
 
 
-def head_kernel(sections, where_ref, own_ref, embed_ref, shifts_ref, head_ref, att_ref, *refs):
+def head_kernel(sections, where_ref, hidden_ref, gate_ref, head_ref, extra_ref, att_ref, *refs):
     weight_refs, out_ref = refs[:-1], refs[-1]
     n_fsdp, _, rows = att_ref.shape
-    latent_dim = embed_ref.shape[0]
+    latent_dim = head_ref.shape[0]
     mixed = None
     for f in range(n_fsdp):
         whole = [ref[f] for ref in weight_refs[:-2]]
         whole.append(weight_refs[-2][f] if f < n_fsdp // 2 else weight_refs[-1][f - n_fsdp // 2])
         part = dot(jnp.concatenate(whole, axis=0), att_ref[f], ((1,), (0,)))
         mixed = part if mixed is None else mixed + part
-    gate = jnp.broadcast_to(shifts_ref[2], (8, embed_ref.shape[1])).T[:, :1]
-    residual = dot(embed_ref[...], own_ref[...], ((0,), (0,))) + gate * mixed
+    residual = hidden_ref[...] + gate_ref[:, :1] * mixed
     centre = jnp.mean(residual, axis=0, keepdims=True)
     residual = residual - centre
     spread = jnp.sum(residual * residual, axis=0, keepdims=True)
-    plain_head = head_ref[...].astype(f32)
-    head = (plain_head * (1.0 + shifts_ref[4])).astype(bf16)
-    values = dot(head, residual.astype(bf16), ((1,), (0,)))
+    values = dot(head_ref[...], residual.astype(bf16), ((1,), (0,)))
     spare = jnp.zeros((latent_dim - 4, rows), f32)
     values = jnp.concatenate([values, *halves(centre), *halves(spread), spare], axis=0).T.astype(bf16)
-    sums = jnp.sum(head.astype(f32), axis=1, keepdims=True)
-    consts = jnp.sum(plain_head * shifts_ref[3], axis=1, keepdims=True)
-    place = lax.broadcasted_iota(jnp.int32, (latent_dim, 128), 1)
-    extra = jnp.zeros((latent_dim, 128), f32)
-    for n, column in enumerate(halves(sums) + halves(consts)):
-        extra = jnp.where(place == n, column, extra)
-    extra = jnp.concatenate([extra, jnp.zeros_like(extra)], axis=0).T[:16].astype(bf16)
+    extra = extra_ref[...]
     piece = rows // n_fsdp
     for f in range(n_fsdp):
         for s in range(sections):
@@ -448,14 +455,25 @@
     )
     cut = run(aside_kernel, together(where, own), [((n_fsdp, slot + 2 * piece, feat), bf16)], out_weight, saved_features, picked=(0,))
     aside = exchange(cut, "fsdp")
-    embed_here, head_here, shifts_here = run(
+    hidden, gate, head_here, extra = run(
         columns_kernel,
         together(where, own),
-        [((latent_dim, depth), bf16), ((latent_dim, depth), bf16), ((shifts.shape[0], 1, depth), f32)],
+        [
+            ((depth, rows), f32),
+            ((depth, 128), f32),
+            ((latent_dim, depth), bf16),
+            ((16, 128), bf16),
+        ],
         in_weight,
         head_weight.transpose(0, 2, 1),
         shifts,
+        plain,
         picked=(0, 1),
+        scratch=[
+            pltpu.VMEM((latent_dim, depth), bf16),
+            pltpu.VMEM((latent_dim, depth), bf16),
+            pltpu.VMEM((shifts.shape[0], 1, depth), f32),
+        ],
     )
     around = Ring(own, "seq", n_seq, 0, lines // 32 * 16)
     around.step()
@@ -470,7 +488,7 @@
     blocks = around.blocks()
     attended = run(
         functools.partial(attention_kernel, heads, latent_dim),
-        together(where, embed_here),
+        together(where, hidden),
         [((n_fsdp, feat, rows), bf16)],
         *blocks,
         scratch=[
@@ -488,10 +506,10 @@
         functools.partial(head_kernel, sections),
         where,
         [((sections * n_fsdp, piece + 16, 128), bf16)],
-        plain,
-        embed_here,
-        shifts_here,
+        hidden,
+        gate,
         head_here,
+        extra,
         attended,
         *weights.blocks(),
     )

time: 164 us -> 164 us (level)
  waiting for transfers between devices: 56.3 us -> 53.4 us
  local copies, waits for them, and re-layouts: 2.1 us -> 4.59 us
    ppermute x6, waiting for transfers between devices: 17.4 us -> 14.5 us  [step(): self.behind.append(lax.ppermute(self.behind[-1], self.axis, self.up))]
    slice x2, local copies, waits for them, and re-layouts: 0.04 us -> 1.75 us  [finish(): first = lax.slice_in_dim(self.behind[-1], 0, size, axis=self.split)]
  transfers between devices with their start and end apart: 19 -> 19, of which waited for: 10 -> 10; matrix products, arithmetic and copies ran while one was open for 2% -> 3% of each run, Pallas kernels for 9% -> 9%
where the time goes in v9:
time: 164 us; the launch traced here: 163 us
  waiting for transfers between devices  53.4 us (33%)
  starting transfers between devices  49.5 us (30%)
  Pallas kernels  30.7 us (19%)
  blocking collectives  22.6 us (14%)
  local copies, waits for them, and re-layouts  4.59 us (3%)
    pallas_call x8, Pallas kernels, run(): pl.pallas_call(kernel, grid_spec=pltpu.PrefetchScalarGridSpec(num_scalar_...  30.7 us
    ppermute x6, starting transfers between devices, step(): self.ahead.append(lax.ppermute(self.ahead[-1], self.axis, self.down))  23 us
    all_to_all x2, blocking collectives, exchange(): return lax.all_to_all(blocks, axis, 0, 0, tiled=True)  22.6 us
    ppermute x6, waiting for transfers between devices, step(): self.ahead.append(lax.ppermute(self.ahead[-1], self.axis, self.down))  20.4 us
    all_to_all x3, starting transfers between devices, exchange(): return lax.all_to_all(blocks, axis, 0, 0, tiled=True)  19.4 us
    ppermute x6, waiting for transfers between devices, step(): self.behind.append(lax.ppermute(self.behind[-1], self.axis, self.up))  14.5 us
    all_to_all x3, waiting for transfers between devices, exchange(): return lax.all_to_all(blocks, axis, 0, 0, tiled=True)  11.7 us
    ppermute x2, starting transfers between devices, finish(): lax.ppermute(second, self.axis, self.down)  6.89 us
  transfers between devices with their start and end apart: 19, of which 10 were waited for; matrix products, arithmetic and copies ran while one was open for 3% of the time, Pallas kernels for 9%

profile of v9, /device:TPU:2, one launch (start us, length us, event | category | flops | bytes accessed | tf_op | source)
XLA Modules:
  0.0 163.0 jit_solution(2384963193694463793)
XLA Ops:
  0.7 5.7 %shard_map.130 = (bf16[2256,128]{1,0:T(8,128)(2,1)}, bf16[64,256]{1,0:T(8,128)(2,1)}) custom-call(s32[3]{0:T(128)} %steps_ref.1, bf16[3,64,5120]{2,1,0:T(8,128)(2,1)} %embed_ref.1, bf16[3,3,640,384]{3,2,1,0:T(8,128)(2,1)} %bitcast.15, f32[5,1,5120]{2,1,0:T(1,128)} %bitcast.13, bf16[64,256]{1,0:T(8,128)(2,1)} %bitcast.18, bf16[64,256]{1,0:T(8,128)(2,1)} %bitcast.19, ...), custom_call_target="tpu_custom_call" | custom-call | tf_op jit(solution)/shard_map/pallas_call | solution.py:34
  6.4 5.9 %collective-permute-start.3 = (bf16[2256,128]{1,0:T(8,128)(2,1)}, bf16[2256,128]{1,0:T(8,128)(2,1)S(1)}, u32[]{:S(2)}, u32[]{:S(2)}) collective-permute-start(bf16[2256,128]{1,0:T(8,128)(2,1)} %get-tuple-element.18.refs_0_), channel_id=1, source_target_pairs={{0,56},{8,0},{16,8},{24,16},{32,24},{40,32},{48,40},{56,48},{1,57}... | collective-permute-start | bytes 1732616 | tf_op jit(solution)/shard_map/ppermute | solution.py:73
  12.3 12.6 %collective-permute-done.3.refs_4_ = bf16[2256,128]{1,0:T(8,128)(2,1)S(1)} collective-permute-done((bf16[2256,128]{1,0:T(8,128)(2,1)}, bf16[2256,128]{1,0:T(8,128)(2,1)S(1)}, u32[]{:S(2)}, u32[]{:S(2)}) %collective-permute-start.3) | collective-permute-done | bytes 577568 | tf_op jit(solution)/shard_map/ppermute | solution.py:73
  24.9 3.6 %collective-permute-start.4 = (bf16[2256,128]{1,0:T(8,128)(2,1)S(1)}, bf16[2256,128]{1,0:T(8,128)(2,1)}, u32[]{:S(2)}, u32[]{:S(2)}) collective-permute-start(bf16[2256,128]{1,0:T(8,128)(2,1)S(1)} %collective-permute-done.3.refs_4_), channel_id=1, source_target_pairs={{0,56},{8,0},{16,8},{24,16},{32,24},{40,32},{48,40},{56,48},{1,57}... | collective-permute-start | bytes 1732616 | tf_op jit(solution)/shard_map/ppermute | solution.py:73
  31.4 6.1 %all-to-all-start = ((bf16[8,144,384]{2,1,0:T(8,128)(2,1)}), bf16[8,144,384]{2,1,0:T(8,128)(2,1)S(1)}, u32[]{:S(2)}, u32[]{:S(2)}) async-start(bf16[8,144,384]{2,1,0:T(8,128)(2,1)} %shard_map.133), calls=%async_computation | async-start | bytes 1769472 | tf_op jit(solution)/shard_map/all_to_all | solution.py:60
  40.0 3.8 %collective-permute-start.5 = (bf16[2256,128]{1,0:T(8,128)(2,1)}, bf16[2256,128]{1,0:T(8,128)(2,1)S(1)}, u32[]{:S(2)}, u32[]{:S(2)}) collective-permute-start(bf16[2256,128]{1,0:T(8,128)(2,1)} %collective-permute-done.4.refs_5_), channel_id=1, source_target_pairs={{0,56},{8,0},{16,8},{24,16},{32,24},{40,32},{48,40},{56,48},{1,57}... | collective-permute-start | bytes 1732616 | tf_op jit(solution)/shard_map/ppermute | solution.py:73
  43.8 5.3 %all-to-all-done.feature_ref = bf16[8,144,384]{2,1,0:T(8,128)(2,1)S(1)} async-done(((bf16[8,144,384]{2,1,0:T(8,128)(2,1)}), bf16[8,144,384]{2,1,0:T(8,128)(2,1)S(1)}, u32[]{:S(2)}, u32[]{:S(2)}) %all-to-all-start) | async-done | bytes 884768 | tf_op jit(solution)/shard_map/all_to_all | solution.py:60
  49.2 3.2 %collective-permute-start.9 = (bf16[8,80,384]{2,1,0:T(8,128)(2,1)S(1)}, bf16[8,80,384]{2,1,0:T(8,128)(2,1)S(1)}, u32[]{:S(2)}, u32[]{:S(2)}) collective-permute-start(bf16[8,80,384]{2,1,0:T(8,128)(2,1)S(1)} %slice.27.refs_0_), channel_id=1, source_target_pairs={{0,56},{8,0},{16,8},{24,16},{32,24},{40,32},{48,40},{56,48},{1,57}... | collective-permute-start | bytes 1474568 | tf_op jit(solution)/shard_map/ppermute | solution.py:73
  52.4 5.2 %collective-permute-done.5.refs_6_ = bf16[2256,128]{1,0:T(8,128)(2,1)S(1)} collective-permute-done((bf16[2256,128]{1,0:T(8,128)(2,1)}, bf16[2256,128]{1,0:T(8,128)(2,1)S(1)}, u32[]{:S(2)}, u32[]{:S(2)}) %collective-permute-start.5) | collective-permute-done | bytes 577568 | tf_op jit(solution)/shard_map/ppermute | solution.py:73
  57.6 3.7 %collective-permute-start.7 = (bf16[1136,128]{1,0:T(8,128)(2,1)S(1)}, bf16[1136,128]{1,0:T(8,128)(2,1)S(1)}, u32[]{:S(2)}, u32[]{:S(2)}) collective-permute-start(bf16[1136,128]{1,0:T(8,128)(2,1)S(1)} %slice.26), channel_id=1, source_target_pairs={{0,56},{8,0},{16,8},{24,16},{32,24},{40,32},{48,40},{56,48},{1,57}... | collective-permute-start | bytes 872456 | tf_op jit(solution)/shard_map/ppermute | solution.py:88
  65.9 5.9 %collective-permute-done.8.refs_1_ = bf16[8,80,384]{2,1,0:T(8,128)(2,1)S(1)} collective-permute-done((bf16[8,80,384]{2,1,0:T(8,128)(2,1)S(1)}, bf16[8,80,384]{2,1,0:T(8,128)(2,1)S(1)}, u32[]{:S(2)}, u32[]{:S(2)}) %collective-permute-start.8) | collective-permute-done | bytes 491552 | tf_op jit(solution)/shard_map/ppermute | solution.py:72
  71.8 3.2 %collective-permute-start.11 = (bf16[8,80,384]{2,1,0:T(8,128)(2,1)S(1)}, bf16[8,80,384]{2,1,0:T(8,128)(2,1)}, u32[]{:S(2)}, u32[]{:S(2)}) collective-permute-start(bf16[8,80,384]{2,1,0:T(8,128)(2,1)S(1)} %collective-permute-done.9.refs_4_), channel_id=1, source_target_pairs={{0,56},{8,0},{16,8},{24,16},{32,24},{40,32},{48,40},{56,48},{1,57}... | collective-permute-start | bytes 1474568 | tf_op jit(solution)/shard_map/ppermute | solution.py:73
  75.1 2.8 %collective-permute-done.6.refs_7_ = bf16[1120,128]{1,0:T(8,128)(2,1)S(1)} collective-permute-done((bf16[1120,128]{1,0:T(8,128)(2,1)S(1)}, bf16[1120,128]{1,0:T(8,128)(2,1)S(1)}, u32[]{:S(2)}, u32[]{:S(2)}) %collective-permute-start.6) | collective-permute-done | bytes 286752 | tf_op jit(solution)/shard_map/ppermute | solution.py:88
  77.9 9.2 %shard_map.132 = bf16[8,384,256]{2,1,0:T(8,128)(2,1)} custom-call(s32[7]{0:T(128)S(1)} %concatenate.3.where_ref, bf16[2256,128]{1,0:T(8,128)(2,1)S(1)} %copy-done.4, bf16[2256,128]{1,0:T(8,128)(2,1)S(1)} %collective-permute-done.refs_1_, bf16[2256,128]{1,0:T(8,128)(2,1)} %collective-permute-done.1.refs_2_, bf16[2256,128]{1,0:T(8,128)(2,1)} %collective-permute-done.2.refs_3_, ...), custom_call_target="tpu_custom_call" | custom-call | flops 11000000512 | bytes 20000000 | tf_op jit(solution)/shard_map/pallas_call | solution.py:34
  87.1 5.9 %all-to-all-start.1 = ((bf16[8,384,256]{2,1,0:T(8,128)(2,1)}), bf16[8,384,256]{2,1,0:T(8,128)(2,1)}, u32[]{:S(2)}, u32[]{:S(2)}) async-start(bf16[8,384,256]{2,1,0:T(8,128)(2,1)} %shard_map.132), calls=%async_computation.1 | async-start | bytes 3145728 | tf_op jit(solution)/shard_map/all_to_all | solution.py:60
  93.0 3.2 %collective-permute-start.13 = (bf16[8,80,384]{2,1,0:T(8,128)(2,1)}, bf16[8,80,384]{2,1,0:T(8,128)(2,1)S(1)}, u32[]{:S(2)}, u32[]{:S(2)}) collective-permute-start(bf16[8,80,384]{2,1,0:T(8,128)(2,1)} %collective-permute-done.11.refs_5_), channel_id=1, source_target_pairs={{0,56},{8,0},{16,8},{24,16},{32,24},{40,32},{48,40},{56,48},{1,57}... | collective-permute-start | bytes 1474568 | tf_op jit(solution)/shard_map/ppermute | solution.py:73
  96.3 8.6 %collective-permute-done.12.refs_3_ = bf16[8,80,384]{2,1,0:T(8,128)(2,1)S(1)} collective-permute-done((bf16[8,80,384]{2,1,0:T(8,128)(2,1)}, bf16[8,80,384]{2,1,0:T(8,128)(2,1)S(1)}, u32[]{:S(2)}, u32[]{:S(2)}) %collective-permute-start.12) | collective-permute-done | bytes 491552 | tf_op jit(solution)/shard_map/ppermute | solution.py:72
  106.4 3.2 %collective-permute-start.15 = (bf16[4,80,384]{2,1,0:T(8,128)(2,1)}, bf16[4,80,384]{2,1,0:T(8,128)(2,1)S(1)}, u32[]{:S(2)}, u32[]{:S(2)}) collective-permute-start(bf16[4,80,384]{2,1,0:T(8,128)(2,1)} %slice.29), channel_id=1, source_target_pairs={{0,56},{8,0},{16,8},{24,16},{32,24},{40,32},{48,40},{56,48},{1,57}... | collective-permute-start | bytes 737288 | tf_op jit(solution)/shard_map/ppermute | solution.py:88
  109.7 3.6 %collective-permute-done.14.refs_7_ = bf16[4,80,384]{2,1,0:T(8,128)(2,1)S(1)} collective-permute-done((bf16[4,80,384]{2,1,0:T(8,128)(2,1)}, bf16[4,80,384]{2,1,0:T(8,128)(2,1)S(1)}, u32[]{:S(2)}, u32[]{:S(2)}) %collective-permute-start.14) | collective-permute-done | bytes 245792 | tf_op jit(solution)/shard_map/ppermute | solution.py:88
  113.7 5.6 %shard_map.134 = bf16[32,48,128]{2,1,0:T(8,128)(2,1)} custom-call(s32[7]{0:T(128)S(1)} %concatenate.3.where_ref, f32[640,256]{1,0:T(8,128)} %copy-done, f32[640,128]{1,0:T(8,128)S(1)} %get-tuple-element.22.gate_ref, bf16[64,640]{1,0:T(8,128)(2,1)S(1)} %get-tuple-element.23.head_ref, bf16[16,128]{1,0:T(8,128)(2,1)S(1)} %get-tuple-element.24.extra_ref, ...), custom_call_target="tpu_custom_call" | custom-call | tf_op jit(solution)/shard_map/pallas_call | solution.py:34
  119.4 7.4 %all-to-all-start.2 = ((bf16[32,48,128]{2,1,0:T(8,128)(2,1)}), bf16[32,48,128]{2,1,0:T(8,128)(2,1)S(1)}, u32[]{:S(2)}, u32[]{:S(2)}) async-start(bf16[32,48,128]{2,1,0:T(8,128)(2,1)} %shard_map.134), calls=%async_computation.2 | async-start | bytes 786432 | tf_op jit(solution)/shard_map/all_to_all | solution.py:60
  129.1 6.4 %all-to-all-done.2.partial_ref = bf16[32,48,128]{2,1,0:T(8,128)(2,1)S(1)} async-done(((bf16[32,48,128]{2,1,0:T(8,128)(2,1)}), bf16[32,48,128]{2,1,0:T(8,128)(2,1)S(1)}, u32[]{:S(2)}, u32[]{:S(2)}) %all-to-all-start.2) | async-done | bytes 393248 | tf_op jit(solution)/shard_map/all_to_all | solution.py:60
  138.2 9.2 %all_to_all.25.grad_ref = bf16[8,32,128]{2,1,0:T(8,128)(2,1)S(1)} all-to-all(bf16[8,32,128]{2,1,0:T(8,128)(2,1)S(1)} %get-tuple-element.32), channel_id=1, replica_groups=mesh['section'=4,'seq'=8,'fsdp'=8] {'fsdp'}, dimensions={0} | all-to-all | bytes 131072 | tf_op jit(solution)/shard_map/all_to_all | solution.py:60
  148.3 13.4 %all_to_all.26.part_ref = bf16[8,48,128]{2,1,0:T(8,128)(2,1)S(1)} all-to-all(bf16[8,48,128]{2,1,0:T(8,128)(2,1)S(1)} %shard_map.136), channel_id=1, replica_groups=mesh['section'=4,'seq'=8,'fsdp'=8] {'seq'}, dimensions={0} | all-to-all | bytes 196608 | tf_op jit(solution)/shard_map/all_to_all | solution.py:60
  (68 shorter events, 18.7 us)
Async XLA Ops:
  0.6 27.9 %copy-start.13 = (s32[3]{0:T(128)S(1)}, s32[3]{0:T(128)}, u32[]{:S(2)}) copy-start(s32[3]{0:T(128)} %steps_ref.1) | copy-start | bytes 40
  0.6 28.0 %copy-start.2 = (bf16[32,5120]{1,0:T(8,128)(2,1)S(1)}, bf16[32,5120]{1,0:T(8,128)(2,1)}, u32[]{:S(2)}) copy-start(bf16[32,5120]{1,0:T(8,128)(2,1)} %feature_ref.1) | copy-start | bytes 983044
  6.4 18.6 %collective-permute-start.3 = (bf16[2256,128]{1,0:T(8,128)(2,1)}, bf16[2256,128]{1,0:T(8,128)(2,1)S(1)}, u32[]{:S(2)}, u32[]{:S(2)}) collective-permute-start(bf16[2256,128]{1,0:T(8,128)(2,1)} %get-tuple-element.18.refs_0_), channel_id=1, source_target_pairs={{0,56},{8,0},{16,8},{24,16},{32,24},{40,32},{48,40},{56,48},{1,57}... | collective-permute-start | bytes 1732616 | tf_op jit(solution)/shard_map/ppermute | solution.py:73
  12.3 16.2 %collective-permute-start = (bf16[2256,128]{1,0:T(8,128)(2,1)}, bf16[2256,128]{1,0:T(8,128)(2,1)S(1)}, u32[]{:S(2)}, u32[]{:S(2)}) collective-permute-start(bf16[2256,128]{1,0:T(8,128)(2,1)} %get-tuple-element.18.refs_0_), channel_id=1, source_target_pairs={{0,8},{8,16},{16,24},{24,32},{32,40},{40,48},{48,56},{56,0},{1,9},... | collective-permute-start | bytes 1732616 | tf_op jit(solution)/shard_map/ppermute | solution.py:72
  24.9 15.0 %collective-permute-start.4 = (bf16[2256,128]{1,0:T(8,128)(2,1)S(1)}, bf16[2256,128]{1,0:T(8,128)(2,1)}, u32[]{:S(2)}, u32[]{:S(2)}) collective-permute-start(bf16[2256,128]{1,0:T(8,128)(2,1)S(1)} %collective-permute-done.3.refs_4_), channel_id=1, source_target_pairs={{0,56},{8,0},{16,8},{24,16},{32,24},{40,32},{48,40},{56,48},{1,57}... | collective-permute-start | bytes 1732616 | tf_op jit(solution)/shard_map/ppermute | solution.py:73
  28.5 15.2 %collective-permute-start.1 = (bf16[2256,128]{1,0:T(8,128)(2,1)S(1)}, bf16[2256,128]{1,0:T(8,128)(2,1)}, u32[]{:S(2)}, u32[]{:S(2)}) collective-permute-start(bf16[2256,128]{1,0:T(8,128)(2,1)S(1)} %collective-permute-done.refs_1_), channel_id=1, source_target_pairs={{0,8},{8,16},{16,24},{24,32},{32,40},{40,48},{48,56},{56,0},{1,9},... | collective-permute-start | bytes 1732616 | tf_op jit(solution)/shard_map/ppermute | solution.py:72
  31.4 31.0 %copy-start.1 = (f32[1,5,5120]{2,0,1:T(1,128)S(1)}, f32[1,5,5120]{2,0,1:T(1,128)}, u32[]{:S(2)}) copy-start(f32[1,5,5120]{2,0,1:T(1,128)} %param.15) | copy-start | bytes 307204
  31.4 31.0 %copy-start.3 = (bf16[64,256]{1,0:T(8,128)(2,1)S(1)}, bf16[64,256]{1,0:T(8,128)(2,1)}, u32[]{:S(2)}) copy-start(bf16[64,256]{1,0:T(8,128)(2,1)} %get-tuple-element.20.plain_ref) | copy-start | bytes 98308
  31.4 17.7 %all-to-all-start = ((bf16[8,144,384]{2,1,0:T(8,128)(2,1)}), bf16[8,144,384]{2,1,0:T(8,128)(2,1)S(1)}, u32[]{:S(2)}, u32[]{:S(2)}) async-start(bf16[8,144,384]{2,1,0:T(8,128)(2,1)} %shard_map.133), calls=%async_computation | async-start | bytes 1769472 | tf_op jit(solution)/shard_map/all_to_all | solution.py:60
  40.0 17.6 %collective-permute-start.5 = (bf16[2256,128]{1,0:T(8,128)(2,1)}, bf16[2256,128]{1,0:T(8,128)(2,1)S(1)}, u32[]{:S(2)}, u32[]{:S(2)}) collective-permute-start(bf16[2256,128]{1,0:T(8,128)(2,1)} %collective-permute-done.4.refs_5_), channel_id=1, source_target_pairs={{0,56},{8,0},{16,8},{24,16},{32,24},{40,32},{48,40},{56,48},{1,57}... | collective-permute-start | bytes 1732616 | tf_op jit(solution)/shard_map/ppermute | solution.py:73
  43.8 17.5 %collective-permute-start.2 = (bf16[2256,128]{1,0:T(8,128)(2,1)}, bf16[2256,128]{1,0:T(8,128)(2,1)}, u32[]{:S(2)}, u32[]{:S(2)}) collective-permute-start(bf16[2256,128]{1,0:T(8,128)(2,1)} %collective-permute-done.1.refs_2_), channel_id=1, source_target_pairs={{0,8},{8,16},{16,24},{24,32},{32,40},{40,48},{48,56},{56,0},{1,9},... | collective-permute-start | bytes 1732616 | tf_op jit(solution)/shard_map/ppermute | solution.py:72
  49.1 22.6 %collective-permute-start.8 = (bf16[8,80,384]{2,1,0:T(8,128)(2,1)S(1)}, bf16[8,80,384]{2,1,0:T(8,128)(2,1)S(1)}, u32[]{:S(2)}, u32[]{:S(2)}) collective-permute-start(bf16[8,80,384]{2,1,0:T(8,128)(2,1)S(1)} %slice.27.refs_0_), channel_id=1, source_target_pairs={{0,8},{8,16},{16,24},{24,32},{32,40},{40,48},{48,56},{56,0},{1,9},... | collective-permute-start | bytes 1474568 | tf_op jit(solution)/shard_map/ppermute | solution.py:72
  49.2 22.5 %collective-permute-start.9 = (bf16[8,80,384]{2,1,0:T(8,128)(2,1)S(1)}, bf16[8,80,384]{2,1,0:T(8,128)(2,1)S(1)}, u32[]{:S(2)}, u32[]{:S(2)}) collective-permute-start(bf16[8,80,384]{2,1,0:T(8,128)(2,1)S(1)} %slice.27.refs_0_), channel_id=1, source_target_pairs={{0,56},{8,0},{16,8},{24,16},{32,24},{40,32},{48,40},{56,48},{1,57}... | collective-permute-start | bytes 1474568 | tf_op jit(solution)/shard_map/ppermute | solution.py:73
  57.6 20.2 %collective-permute-start.7 = (bf16[1136,128]{1,0:T(8,128)(2,1)S(1)}, bf16[1136,128]{1,0:T(8,128)(2,1)S(1)}, u32[]{:S(2)}, u32[]{:S(2)}) collective-permute-start(bf16[1136,128]{1,0:T(8,128)(2,1)S(1)} %slice.26), channel_id=1, source_target_pairs={{0,56},{8,0},{16,8},{24,16},{32,24},{40,32},{48,40},{56,48},{1,57}... | collective-permute-start | bytes 872456 | tf_op jit(solution)/shard_map/ppermute | solution.py:88
  62.3 15.6 %collective-permute-start.6 = (bf16[1120,128]{1,0:T(8,128)(2,1)S(1)}, bf16[1120,128]{1,0:T(8,128)(2,1)S(1)}, u32[]{:S(2)}, u32[]{:S(2)}) collective-permute-start(bf16[1120,128]{1,0:T(8,128)(2,1)S(1)} %slice.25), channel_id=1, source_target_pairs={{0,8},{8,16},{16,24},{24,32},{32,40},{40,48},{48,56},{56,0},{1,9},... | collective-permute-start | bytes 860168 | tf_op jit(solution)/shard_map/ppermute | solution.py:88
  62.4 15.5 %copy-start.4 = (bf16[2256,128]{1,0:T(8,128)(2,1)S(1)}, bf16[2256,128]{1,0:T(8,128)(2,1)}, u32[]{:S(2)}) copy-start(bf16[2256,128]{1,0:T(8,128)(2,1)} %get-tuple-element.18.refs_0_) | copy-start | bytes 1732612
  71.7 15.3 %collective-permute-start.10 = (bf16[8,80,384]{2,1,0:T(8,128)(2,1)S(1)}, bf16[8,80,384]{2,1,0:T(8,128)(2,1)}, u32[]{:S(2)}, u32[]{:S(2)}) collective-permute-start(bf16[8,80,384]{2,1,0:T(8,128)(2,1)S(1)} %collective-permute-done.8.refs_1_), channel_id=1, source_target_pairs={{0,8},{8,16},{16,24},{24,32},{32,40},{40,48},{48,56},{56,0},{1,9},... | collective-permute-start | bytes 1474568 | tf_op jit(solution)/shard_map/ppermute | solution.py:72
  71.8 15.3 %collective-permute-start.11 = (bf16[8,80,384]{2,1,0:T(8,128)(2,1)S(1)}, bf16[8,80,384]{2,1,0:T(8,128)(2,1)}, u32[]{:S(2)}, u32[]{:S(2)}) collective-permute-start(bf16[8,80,384]{2,1,0:T(8,128)(2,1)S(1)} %collective-permute-done.9.refs_4_), channel_id=1, source_target_pairs={{0,56},{8,0},{16,8},{24,16},{32,24},{40,32},{48,40},{56,48},{1,57}... | collective-permute-start | bytes 1474568 | tf_op jit(solution)/shard_map/ppermute | solution.py:73
  87.1 26.6 %all-to-all-start.1 = ((bf16[8,384,256]{2,1,0:T(8,128)(2,1)}), bf16[8,384,256]{2,1,0:T(8,128)(2,1)}, u32[]{:S(2)}, u32[]{:S(2)}) async-start(bf16[8,384,256]{2,1,0:T(8,128)(2,1)} %shard_map.132), calls=%async_computation.1 | async-start | bytes 3145728 | tf_op jit(solution)/shard_map/all_to_all | solution.py:60
  93.0 11.9 %collective-permute-start.12 = (bf16[8,80,384]{2,1,0:T(8,128)(2,1)}, bf16[8,80,384]{2,1,0:T(8,128)(2,1)S(1)}, u32[]{:S(2)}, u32[]{:S(2)}) collective-permute-start(bf16[8,80,384]{2,1,0:T(8,128)(2,1)} %collective-permute-done.10.refs_2_), channel_id=1, source_target_pairs={{0,8},{8,16},{16,24},{24,32},{32,40},{40,48},{48,56},{56,0},{1,9},... | collective-permute-start | bytes 1474568 | tf_op jit(solution)/shard_map/ppermute | solution.py:72
  93.0 12.7 %collective-permute-start.13 = (bf16[8,80,384]{2,1,0:T(8,128)(2,1)}, bf16[8,80,384]{2,1,0:T(8,128)(2,1)S(1)}, u32[]{:S(2)}, u32[]{:S(2)}) collective-permute-start(bf16[8,80,384]{2,1,0:T(8,128)(2,1)} %collective-permute-done.11.refs_5_), channel_id=1, source_target_pairs={{0,56},{8,0},{16,8},{24,16},{32,24},{40,32},{48,40},{56,48},{1,57}... | collective-permute-start | bytes 1474568 | tf_op jit(solution)/shard_map/ppermute | solution.py:73
  105.7 7.6 %collective-permute-start.14 = (bf16[4,80,384]{2,1,0:T(8,128)(2,1)}, bf16[4,80,384]{2,1,0:T(8,128)(2,1)S(1)}, u32[]{:S(2)}, u32[]{:S(2)}) collective-permute-start(bf16[4,80,384]{2,1,0:T(8,128)(2,1)} %slice.28), channel_id=1, source_target_pairs={{0,8},{8,16},{16,24},{24,32},{32,40},{40,48},{48,56},{56,0},{1,9},... | collective-permute-start | bytes 737288 | tf_op jit(solution)/shard_map/ppermute | solution.py:88
  106.4 7.3 %collective-permute-start.15 = (bf16[4,80,384]{2,1,0:T(8,128)(2,1)}, bf16[4,80,384]{2,1,0:T(8,128)(2,1)S(1)}, u32[]{:S(2)}, u32[]{:S(2)}) collective-permute-start(bf16[4,80,384]{2,1,0:T(8,128)(2,1)} %slice.29), channel_id=1, source_target_pairs={{0,56},{8,0},{16,8},{24,16},{32,24},{40,32},{48,40},{56,48},{1,57}... | collective-permute-start | bytes 737288 | tf_op jit(solution)/shard_map/ppermute | solution.py:88
  119.4 16.2 %all-to-all-start.2 = ((bf16[32,48,128]{2,1,0:T(8,128)(2,1)}), bf16[32,48,128]{2,1,0:T(8,128)(2,1)S(1)}, u32[]{:S(2)}, u32[]{:S(2)}) async-start(bf16[32,48,128]{2,1,0:T(8,128)(2,1)} %shard_map.134), calls=%async_computation.2 | async-start | bytes 786432 | tf_op jit(solution)/shard_map/all_to_all | solution.py:60
  (10 other events, 102.2 us)
